TPU v7x, 32 devices: a whole 2x2x4 slice. The times are simulated.
32 devices in a mesh: wide: 8 (over y, x, core), narrow: 4 (over z).
Axes of the slice: x: 2, y: 2, z: 4, core: 2. Of those that a mesh axis runs over, the one named last changes fastest.
Arguments:
- tokens: bfloat16 [32768, 1024], P(('wide', 'narrow')), may hold values from -6 to 6
- memory: bfloat16 [16384, 1024], P(('wide', 'narrow')), may hold values from -6 to 6
- cotangent: bfloat16 [32768, 1024], P(('wide', 'narrow')), may hold values from -6 to 6
- live_length: int32 [32], P(('wide', 'narrow')), may hold values from 278 to 1024, as said below
- pair_starts: int32 [32, 8], P(('wide', 'narrow')), may hold values from 0 to 1023, as said below
- source_starts: int32 [32, 8], P(('wide', 'narrow')), may hold values from 0 to 511, as said below
- group_bounds: int32 [9], replicated, may hold values from 0 to 32, as said below
- group_counts: int32 [8], replicated, may hold values from 500 to 1499
- self_query: bfloat16 [1024, 1024], P(('wide', 'narrow')), may hold values from -0.1875 to 0.1875
- self_key: bfloat16 [1024, 1024], P(('wide', 'narrow')), may hold values from -0.1875 to 0.1875
- self_value: bfloat16 [1024, 1024], P(('wide', 'narrow')), may hold values from -0.1875 to 0.1875
- self_output: bfloat16 [1024, 1024], P(('wide', 'narrow')), may hold values from -1.5 to 1.5
- cross_query: bfloat16 [1024, 1024], P(('wide', 'narrow')), may hold values from -0.1875 to 0.1875
- cross_key: bfloat16 [1024, 1024], P(('wide', 'narrow')), may hold values from -0.1875 to 0.1875
- cross_value: bfloat16 [1024, 1024], P(('wide', 'narrow')), may hold values from -0.1875 to 0.1875
- cross_output: bfloat16 [1024, 1024], P(('wide', 'narrow')), may hold values from -1.5 to 1.5
- hidden_in: bfloat16 [1024, 4096], P(('wide', 'narrow')), may hold values from -0.1875 to 0.1875
- hidden_out: bfloat16 [4096, 1024], P(('wide', 'narrow')), may hold values from -0.09375 to 0.09375
- first_gain: bfloat16 [1024], P(('wide', 'narrow')), may hold values from 0.099609375 to 1.8984375
- first_shift: bfloat16 [1024], P(('wide', 'narrow')), may hold values from -3 to 3
- second_gain: bfloat16 [1024], P(('wide', 'narrow')), may hold values from 0.099609375 to 1.8984375
- second_shift: bfloat16 [1024], P(('wide', 'narrow')), may hold values from -3 to 3
- third_gain: bfloat16 [1024], P(('wide', 'narrow')), may hold values from 0.099609375 to 1.8984375
- third_shift: bfloat16 [1024], P(('wide', 'narrow')), may hold values from -3 to 3
Outputs:
- layer_output: bfloat16 [32768, 1024], P(('wide', 'narrow'))
- tokens_grad: bfloat16 [32768, 1024], P(('wide', 'narrow'))
- memory_grad: bfloat16 [16384, 1024], P(('wide', 'narrow'))
- self_query_grad: float32 [1024, 1024], P(('wide', 'narrow'))
- self_key_grad: float32 [1024, 1024], P(('wide', 'narrow'))
- self_value_grad: float32 [1024, 1024], P(('wide', 'narrow'))
- self_output_grad: float32 [1024, 1024], P(('wide', 'narrow'))
- cross_query_grad: float32 [1024, 1024], P(('wide', 'narrow'))
- cross_key_grad: float32 [1024, 1024], P(('wide', 'narrow'))
- cross_value_grad: float32 [1024, 1024], P(('wide', 'narrow'))
- cross_output_grad: float32 [1024, 1024], P(('wide', 'narrow'))
- hidden_in_grad: float32 [1024, 4096], P(('wide', 'narrow'))
- hidden_out_grad: float32 [4096, 1024], P(('wide', 'narrow'))
- first_gain_grad: float32 [1024], P(('wide', 'narrow'))
- first_shift_grad: float32 [1024], P(('wide', 'narrow'))
- second_gain_grad: float32 [1024], P(('wide', 'narrow'))
- second_shift_grad: float32 [1024], P(('wide', 'narrow'))
- third_gain_grad: float32 [1024], P(('wide', 'narrow'))
- third_shift_grad: float32 [1024], P(('wide', 'narrow'))
Inputs may be any that keep to these rules, and one draw needn't show every extreme that they name: `live_length`: positions at or after a row's live length are padding; the rows of the last device are full. `pair_starts`: strictly rising, the first 0, all below the row's live length; a sentence pair runs to the next start or to the live length. `source_starts`: strictly rising, the first 0, all below 512; a source runs to the next start or to 512. Strictly rising, the first 0, the last the number of devices; language pair g holds the devices group_bounds[g] to group_bounds[g + 1] - 1 of the joined index wide+narrow.
All inputs are finite; a program needn't handle non-finite values.
Results may differ from a plain program's by a relative error of at most 0.017.
Values may be sent and summed in bfloat16 or wider, within the bound.
A program may use at most 384 MiB of HBM per device.

v0:
```python
import jax
import jax.numpy as jnp
from jax import lax
from jax.sharding import PartitionSpec as P

HEADS = 16
HEAD_DIM = 64
SEQ = 1024
MEM = 512
NSEG = 8


EPSILON = 1e-05
FILLER = -1e30


def layer_norm(values, gain_vector, shift_vector):
    center = values - jnp.mean(values, axis=-1, keepdims=True)
    inverse = lax.rsqrt(jnp.mean(center * center, axis=-1, keepdims=True) + EPSILON)
    return center * inverse * gain_vector + shift_vector


def linear(left_side, right_side):
    return jnp.dot(left_side, right_side, preferred_element_type=jnp.float32)


def linear_back(gradient, right_side):
    return jnp.einsum("te,de->td", gradient, right_side, preferred_element_type=jnp.float32)


def outer_sum(left_side, gradient):
    return jnp.einsum("td,te->de", left_side, gradient, preferred_element_type=jnp.float32)


def segment_ids(starts, length, extent):
    places = jnp.arange(extent, dtype=jnp.int32)
    counted = jnp.sum((starts[None, :] <= places[:, None]).astype(jnp.int32), axis=1) - 1
    return jnp.where(places < length, counted, NSEG)


def masks_of(pair_row, source_row, length):
    places = jnp.arange(SEQ, dtype=jnp.int32)
    target_segment = segment_ids(pair_row, length, SEQ)
    memory_segment = segment_ids(source_row, MEM, MEM)
    self_allowed = (target_segment[:, None] == target_segment[None, :]) & (
        places[None, :] <= places[:, None]
    )
    cross_allowed = (target_segment[:, None] == memory_segment[None, :]) | (
        target_segment[:, None] == NSEG
    )
    return (self_allowed, cross_allowed)


def attend(queries, key_rows, value_rows, allowed):
    length = queries.shape[0]
    block_rows = min(512, length)
    block_count = length // block_rows
    score_scale = HEAD_DIM ** (-0.5)
    query_heads = queries.reshape(block_count, block_rows, HEADS, HEAD_DIM)
    key_heads = key_rows.reshape(-1, HEADS, HEAD_DIM)
    value_heads = value_rows.reshape(-1, HEADS, HEAD_DIM)
    allowed_blocks = allowed.reshape(block_count, block_rows, -1)

    def one_block(block_input):
        query_part, allowed_part = block_input
        scores = (
            jnp.einsum("qhd,khd->hqk", query_part, key_heads, preferred_element_type=jnp.float32)
            * score_scale
        )
        scores = jnp.where(allowed_part[None], scores, FILLER)
        row_peak = jnp.max(scores, axis=-1, keepdims=True)
        log_total = row_peak + jnp.log(jnp.sum(jnp.exp(scores - row_peak), axis=-1, keepdims=True))
        weights = jnp.exp(scores - log_total).astype(jnp.bfloat16)
        mixed_heads = jnp.einsum(
            "hqk,khd->qhd", weights, value_heads, preferred_element_type=jnp.float32
        )
        return (mixed_heads.reshape(block_rows, HEADS * HEAD_DIM), log_total)

    mixed_blocks, log_totals = lax.map(one_block, (query_heads, allowed_blocks))
    return (mixed_blocks.reshape(length, HEADS * HEAD_DIM), log_totals)


def attend_back(queries, key_rows, value_rows, allowed, log_totals, out_grad):
    length = queries.shape[0]
    block_rows = min(512, length)
    block_count = length // block_rows
    score_scale = HEAD_DIM ** (-0.5)
    query_heads = queries.reshape(block_count, block_rows, HEADS, HEAD_DIM)
    grad_heads = out_grad.reshape(block_count, block_rows, HEADS, HEAD_DIM)
    key_heads = key_rows.reshape(-1, HEADS, HEAD_DIM)
    value_heads = value_rows.reshape(-1, HEADS, HEAD_DIM)
    allowed_blocks = allowed.reshape(block_count, block_rows, -1)

    def one_block(running, block_input):
        key_grad, value_grad = running
        query_part, allowed_part, log_part, grad_part = block_input
        scores = (
            jnp.einsum("qhd,khd->hqk", query_part, key_heads, preferred_element_type=jnp.float32)
            * score_scale
        )
        scores = jnp.where(allowed_part[None], scores, FILLER)
        probs_full = jnp.exp(scores - log_part)
        value_grad = value_grad + jnp.einsum(
            "hqk,qhd->khd",
            probs_full.astype(jnp.bfloat16),
            grad_part,
            preferred_element_type=jnp.float32,
        )
        prob_grad = jnp.einsum(
            "qhd,khd->hqk", grad_part, value_heads, preferred_element_type=jnp.float32
        )
        row_dot = jnp.sum(prob_grad * probs_full, axis=-1, keepdims=True)
        score_grad = (probs_full * (prob_grad - row_dot)).astype(jnp.bfloat16)
        query_grad = (
            jnp.einsum("hqk,khd->qhd", score_grad, key_heads, preferred_element_type=jnp.float32)
            * score_scale
        )
        key_grad = (
            key_grad
            + jnp.einsum("hqk,qhd->khd", score_grad, query_part, preferred_element_type=jnp.float32)
            * score_scale
        )
        return ((key_grad, value_grad), query_grad.reshape(block_rows, HEADS * HEAD_DIM))

    empty_grad = jnp.zeros(key_heads.shape, jnp.float32)
    (key_grad, value_grad), query_grads = lax.scan(
        one_block, (empty_grad, empty_grad), (query_heads, allowed_blocks, log_totals, grad_heads)
    )
    return (
        query_grads.reshape(length, HEADS * HEAD_DIM).astype(jnp.bfloat16),
        key_grad.reshape(key_rows.shape).astype(jnp.bfloat16),
        value_grad.reshape(value_rows.shape).astype(jnp.bfloat16),
    )


def row_attention(queries, key_rows, value_rows, allowed, row_count):

    def one_row(row_items):
        return attend(row_items[0], row_items[1], row_items[2], row_items[3])

    mixed_rows, log_totals = lax.map(
        one_row,
        (
            queries.reshape(row_count, -1, queries.shape[-1]),
            key_rows.reshape(row_count, -1, key_rows.shape[-1]),
            value_rows.reshape(row_count, -1, value_rows.shape[-1]),
            allowed,
        ),
    )
    return (mixed_rows.reshape(queries.shape).astype(jnp.bfloat16), log_totals)


def row_attention_back(queries, key_rows, value_rows, allowed, log_totals, out_grad, row_count):

    def one_row(row_items):
        return attend_back(
            row_items[0], row_items[1], row_items[2], row_items[3], row_items[4], row_items[5]
        )

    query_grad, key_grad, value_grad = lax.map(
        one_row,
        (
            queries.reshape(row_count, -1, queries.shape[-1]),
            key_rows.reshape(row_count, -1, key_rows.shape[-1]),
            value_rows.reshape(row_count, -1, value_rows.shape[-1]),
            allowed,
            log_totals,
            out_grad.reshape(row_count, -1, out_grad.shape[-1]),
        ),
    )
    return (
        query_grad.reshape(queries.shape),
        key_grad.reshape(key_rows.shape),
        value_grad.reshape(value_rows.shape),
    )


def merge_grads(gradients):
    return lax.psum_scatter(gradients, ("wide", "narrow"), scatter_dimension=0, tiled=True)


def on_device(
    tokens,
    memory,
    cotangent,
    live_length,
    pair_starts,
    source_starts,
    group_bounds,
    group_counts,
    self_query,
    self_key,
    self_value,
    self_output,
    cross_query,
    cross_key,
    cross_value,
    cross_output,
    hidden_in,
    hidden_out,
    first_gain,
    first_shift,
    second_gain,
    second_shift,
    third_gain,
    third_shift,
):
    row_count = live_length.shape[0]
    live_total = lax.psum(jnp.sum(live_length), ("wide", "narrow"))
    (
        query_self,
        key_self,
        value_self,
        output_self,
        query_cross,
        key_cross,
        value_cross,
        output_cross,
        gain_one,
        shift_one,
        gain_two,
        shift_two,
    ) = (
        lax.all_gather(self_query, ("wide", "narrow"), axis=0, tiled=True),
        lax.all_gather(self_key, ("wide", "narrow"), axis=0, tiled=True),
        lax.all_gather(self_value, ("wide", "narrow"), axis=0, tiled=True),
        lax.all_gather(self_output, ("wide", "narrow"), axis=0, tiled=True),
        lax.all_gather(cross_query, ("wide", "narrow"), axis=0, tiled=True),
        lax.all_gather(cross_key, ("wide", "narrow"), axis=0, tiled=True),
        lax.all_gather(cross_value, ("wide", "narrow"), axis=0, tiled=True),
        lax.all_gather(cross_output, ("wide", "narrow"), axis=0, tiled=True),
        lax.all_gather(first_gain, ("wide", "narrow"), axis=0, tiled=True),
        lax.all_gather(first_shift, ("wide", "narrow"), axis=0, tiled=True),
        lax.all_gather(second_gain, ("wide", "narrow"), axis=0, tiled=True),
        lax.all_gather(second_shift, ("wide", "narrow"), axis=0, tiled=True),
    )
    self_allowed, cross_allowed = jax.vmap(masks_of)(pair_starts, source_starts, live_length)
    resident = tokens.astype(jnp.float32)
    normed_full, norm_back_one = jax.vjp(
        layer_norm, resident, gain_one.astype(jnp.float32), shift_one.astype(jnp.float32)
    )
    normed_one = normed_full.astype(jnp.bfloat16)
    self_queries = linear(normed_one, query_self).astype(jnp.bfloat16)
    self_keys = linear(normed_one, key_self).astype(jnp.bfloat16)
    self_values = linear(normed_one, value_self).astype(jnp.bfloat16)
    self_mixed, self_logs = row_attention(
        self_queries, self_keys, self_values, self_allowed, row_count
    )
    after_self = resident + linear(self_mixed, output_self)
    normed_full, norm_back_two = jax.vjp(
        layer_norm, after_self, gain_two.astype(jnp.float32), shift_two.astype(jnp.float32)
    )
    normed_two = normed_full.astype(jnp.bfloat16)
    cross_queries = linear(normed_two, query_cross).astype(jnp.bfloat16)
    cross_keys = linear(memory, key_cross).astype(jnp.bfloat16)
    cross_values = linear(memory, value_cross).astype(jnp.bfloat16)
    cross_mixed, cross_logs = row_attention(
        cross_queries, cross_keys, cross_values, cross_allowed, row_count
    )
    after_cross = after_self + linear(cross_mixed, output_cross)
    expand_whole, reduce_whole, gain_three, shift_three = (
        lax.all_gather(hidden_in, ("wide", "narrow"), axis=0, tiled=True),
        lax.all_gather(hidden_out, ("wide", "narrow"), axis=0, tiled=True),
        lax.all_gather(third_gain, ("wide", "narrow"), axis=0, tiled=True),
        lax.all_gather(third_shift, ("wide", "narrow"), axis=0, tiled=True),
    )
    normed_full, norm_back_three = jax.vjp(
        layer_norm, after_cross, gain_three.astype(jnp.float32), shift_three.astype(jnp.float32)
    )
    normed_three = normed_full.astype(jnp.bfloat16)
    hidden = linear(normed_three, expand_whole)
    activated, gelu_back = jax.vjp(jax.nn.gelu, hidden)
    activated = activated.astype(jnp.bfloat16)
    layer_output = (after_cross + linear(activated, reduce_whole)).astype(jnp.bfloat16)
    device = lax.axis_index(("wide", "narrow"))
    member = (group_bounds[:-1] <= device) & (device < group_bounds[1:])
    pair_tokens = jnp.sum(jnp.where(member, group_counts, 0))
    token_all = row_count * SEQ * lax.axis_size("wide") * lax.axis_size("narrow")
    row_weight = (
        pair_tokens.astype(jnp.float32) * (token_all / 1000.0) / live_total.astype(jnp.float32)
    )
    places = jnp.arange(SEQ, dtype=jnp.int32)
    live_mask = (places[None, :] < live_length[:, None]).astype(jnp.float32).reshape(-1, 1)
    out_grad = cotangent.astype(jnp.float32) * live_mask * row_weight
    expand_whole, reduce_whole = (
        lax.all_gather(hidden_in, ("wide", "narrow"), axis=0, tiled=True),
        lax.all_gather(hidden_out, ("wide", "narrow"), axis=0, tiled=True),
    )
    branch_three = out_grad.astype(jnp.bfloat16)
    reduce_grad = outer_sum(activated, branch_three)
    (reduce_shard,) = merge_grads((reduce_grad,))
    hidden_grad = gelu_back(linear_back(branch_three, reduce_whole))[0].astype(jnp.bfloat16)
    expand_grad = outer_sum(normed_three, hidden_grad)
    cross_part, gain_three_grad, shift_three_grad = norm_back_three(
        linear_back(hidden_grad, expand_whole)
    )
    expand_shard, gain_three_shard, shift_three_shard = merge_grads(
        (expand_grad, gain_three_grad, shift_three_grad)
    )
    cross_total = out_grad + cross_part
    (
        query_self,
        key_self,
        value_self,
        output_self,
        query_cross,
        key_cross,
        value_cross,
        output_cross,
    ) = (
        lax.all_gather(self_query, ("wide", "narrow"), axis=0, tiled=True),
        lax.all_gather(self_key, ("wide", "narrow"), axis=0, tiled=True),
        lax.all_gather(self_value, ("wide", "narrow"), axis=0, tiled=True),
        lax.all_gather(self_output, ("wide", "narrow"), axis=0, tiled=True),
        lax.all_gather(cross_query, ("wide", "narrow"), axis=0, tiled=True),
        lax.all_gather(cross_key, ("wide", "narrow"), axis=0, tiled=True),
        lax.all_gather(cross_value, ("wide", "narrow"), axis=0, tiled=True),
        lax.all_gather(cross_output, ("wide", "narrow"), axis=0, tiled=True),
    )
    branch_two = cross_total.astype(jnp.bfloat16)
    cross_output_grad = outer_sum(cross_mixed, branch_two)
    mixed_grad = linear_back(branch_two, output_cross).astype(jnp.bfloat16)
    cq_grad, ck_grad, cv_grad = row_attention_back(
        cross_queries, cross_keys, cross_values, cross_allowed, cross_logs, mixed_grad, row_count
    )
    cross_query_grad = outer_sum(normed_two, cq_grad)
    cross_key_grad = outer_sum(memory, ck_grad)
    cross_value_grad = outer_sum(memory, cv_grad)
    memory_grad = (linear_back(ck_grad, key_cross) + linear_back(cv_grad, value_cross)).astype(
        jnp.bfloat16
    )
    self_part, gain_two_grad, shift_two_grad = norm_back_two(linear_back(cq_grad, query_cross))
    cross_shards = merge_grads(
        (
            cross_query_grad,
            cross_key_grad,
            cross_value_grad,
            cross_output_grad,
            gain_two_grad,
            shift_two_grad,
        )
    )
    self_total = cross_total + self_part
    branch_one = self_total.astype(jnp.bfloat16)
    self_output_grad = outer_sum(self_mixed, branch_one)
    mixed_grad = linear_back(branch_one, output_self).astype(jnp.bfloat16)
    sq_grad, sk_grad, sv_grad = row_attention_back(
        self_queries, self_keys, self_values, self_allowed, self_logs, mixed_grad, row_count
    )
    self_query_grad = outer_sum(normed_one, sq_grad)
    self_key_grad = outer_sum(normed_one, sk_grad)
    self_value_grad = outer_sum(normed_one, sv_grad)
    normed_grad = (
        linear_back(sq_grad, query_self)
        + linear_back(sk_grad, key_self)
        + linear_back(sv_grad, value_self)
    )
    input_part, gain_one_grad, shift_one_grad = norm_back_one(normed_grad)
    self_shards = merge_grads(
        (
            self_query_grad,
            self_key_grad,
            self_value_grad,
            self_output_grad,
            gain_one_grad,
            shift_one_grad,
        )
    )
    tokens_grad = (self_total + input_part).astype(jnp.bfloat16)
    return (
        layer_output,
        tokens_grad,
        memory_grad,
        self_shards[0],
        self_shards[1],
        self_shards[2],
        self_shards[3],
        cross_shards[0],
        cross_shards[1],
        cross_shards[2],
        cross_shards[3],
        expand_shard,
        reduce_shard,
        self_shards[4],
        self_shards[5],
        cross_shards[4],
        cross_shards[5],
        gain_three_shard,
        shift_three_shard,
    )


def solution(mesh):
    return jax.shard_map(
        on_device,
        mesh=mesh,
        in_specs=(
            P(("wide", "narrow"), None),
            P(("wide", "narrow"), None),
            P(("wide", "narrow"), None),
            P(("wide", "narrow")),
            P(("wide", "narrow"), None),
            P(("wide", "narrow"), None),
            P(),
            P(),
            P(("wide", "narrow"), None),
            P(("wide", "narrow"), None),
            P(("wide", "narrow"), None),
            P(("wide", "narrow"), None),
            P(("wide", "narrow"), None),
            P(("wide", "narrow"), None),
            P(("wide", "narrow"), None),
            P(("wide", "narrow"), None),
            P(("wide", "narrow"), None),
            P(("wide", "narrow"), None),
            P(("wide", "narrow")),
            P(("wide", "narrow")),
            P(("wide", "narrow")),
            P(("wide", "narrow")),
            P(("wide", "narrow")),
            P(("wide", "narrow")),
        ),
        out_specs=(
            P(("wide", "narrow"), None),
            P(("wide", "narrow"), None),
            P(("wide", "narrow"), None),
            P(("wide", "narrow"), None),
            P(("wide", "narrow"), None),
            P(("wide", "narrow"), None),
            P(("wide", "narrow"), None),
            P(("wide", "narrow"), None),
            P(("wide", "narrow"), None),
            P(("wide", "narrow"), None),
            P(("wide", "narrow"), None),
            P(("wide", "narrow"), None),
            P(("wide", "narrow"), None),
            P(("wide", "narrow")),
            P(("wide", "narrow")),
            P(("wide", "narrow")),
            P(("wide", "narrow")),
            P(("wide", "narrow")),
            P(("wide", "narrow")),
        ),
        check_vma=False,
    )
```

profile of v0, /device:TPU:0, one launch (start us, length us, event | category | flops | bytes accessed | tf_op | source)
XLA Modules:
  0.0 2628.1 jit_solution(7954906421532620663)
XLA Ops:
  14.7 42.3 %psum.7 = s32[]{:T(128)} all-reduce(s32[]{:T(128)} %bitcast.10), channel_id=1, replica_groups=mesh['wide'=8,'narrow'=4] {'wide','narrow'}, use_global_device_ids=true, to_apply=%region_17.18 | all-reduce | flops 1 | bytes 8 | tf_op jit(solution)/shard_map/psum | solution.py:209
  65.6 40.7 %all-reduce.13 = (bf16[1024]{0:T(1024)(128)(2,1)S(1)}, bf16[1024]{0:T(1024)(128)(2,1)S(1)}, bf16[1024]{0:T(1024)(128)(2,1)S(1)}, bf16[1024]{0:T(1024)(128)(2,1)S...) all-reduce(bf16[1024]{0:T(1024)(128)(2,1)S(1)} %dynamic-update-slic, ...), channel_id=1, replica_groups=mesh['wide'=8,'narrow'=4] {'wide','narrow'}, use_global_device_ids=true, to_apply=%add.1 | all-reduce | flops 6144 | bytes 24576
  145.2 41.8 %all-gather.13.cloned.1.call-done = bf16[1024,1024]{1,0:T(8,128)(2,1)} async-done(((bf16[32,1024]{1,0:T(8,128)(2,1)}), bf16[1024,1024]{1,0:T(8,128)(2,1)}) %all-gather.13.cloned.1.call-update) | async-done | bytes 2097168 | tf_op jit(solution)/shard_map/all_gather | solution.py:225
  194.1 106.3 %while.94 = (s32[]{:T(128)}, bf16[2,512,1024]{2,1,0:T(8,128)(2,1)}, f32[2,16,512,1]{2,1,3,0:T(8,128)}, pred[2,512,1024]{2,1,0:T(8,128)(4,1)}, bf16[2,512,16,64]{...) while((s32[]{:T(128)}, bf16[2,512,1024]{2,1,0:T(8,128)(2,1)}, ...), condition=%wide.region_6.7_spmd, body=%wide.region_3.6_spmd.sunk | while | flops 2239750144 | bytes 116129928 | solution.py:79
  226.4 16.4 fusion.205
  279.5 16.4 fusion.205
  311.0 50.6 %all-gather.17.cloned.1.call-done = bf16[1024,1024]{1,0:T(8,128)(2,1)} async-done(((bf16[32,1024]{1,0:T(8,128)(2,1)}), bf16[1024,1024]{1,0:T(8,128)(2,1)}) %all-gather.17.cloned.1.call-update) | async-done | bytes 2097168 | tf_op jit(solution)/shard_map/all_gather | solution.py:227
  370.1 49.8 %all-gather.19.cloned.1.call-done = bf16[1024,1024]{1,0:T(8,128)(2,1)} async-done(((bf16[32,1024]{1,0:T(8,128)(2,1)}), bf16[1024,1024]{1,0:T(8,128)(2,1)}) %all-gather.19.cloned.1.call-update) | async-done | bytes 2097168 | tf_op jit(solution)/shard_map/all_gather | solution.py:228
  440.2 65.9 %while.95 = (s32[]{:T(128)}, bf16[2,512,1024]{2,1,0:T(8,128)(2,1)}, f32[2,16,512,1]{2,1,3,0:T(8,128)S(1)}, pred[2,512,512]{1,2,0:T(8,128)(4,1)}, bf16[2,512,16,6...) while((s32[]{:T(128)}, bf16[2,512,1024]{2,1,0:T(8,128)(2,1)}, ...), condition=%wide.region_13.14_spmd, body=%wide.region_10.13_spmd.sunk | while | flops 1119870976 | bytes 60293228 | solution.py:79
  514.8 42.6 %all-gather.27.cloned.1.call-done = bf16[1024,4096]{1,0:T(8,128)(2,1)} async-done(((bf16[32,4096]{1,0:T(8,128)(2,1)}), bf16[1024,4096]{1,0:T(8,128)(2,1)}) %all-gather.27.cloned.1.call-update) | async-done | bytes 8388624 | tf_op jit(solution)/shard_map/all_gather | solution.py:262
  557.4 16.9 fusion.96
  574.3 61.9 %all-gather.29.cloned.1.call-done = bf16[4096,1024]{1,0:T(8,128)(2,1)} async-done(((bf16[128,1024]{1,0:T(8,128)(2,1)}), bf16[4096,1024]{1,0:T(8,128)(2,1)}) %all-gather.29.cloned.1.call-update) | async-done | bytes 8388624 | tf_op jit(solution)/shard_map/all_gather | solution.py:263
  636.2 26.8 %fusion.63 = bf16[1024,4096]{1,0:T(8,128)(2,1)} fusion(f32[1024,4096]{1,0:T(8,128)} %fusion.96, bf16[4096,1024]{1,0:T(8,128)(2,1)} %all-gather.29.cloned.1.call-done, bf16[1024,1024]{0,1:T(8,128)(2,1)} %copy.153, f32[]{:T(128)S(6)} %div.63, f32[1024]{0:T(1024)S(1)} %copy-done.48), kind=kOutput, calls=%fused_computation.92 | convolution fusion | flops 8678014976 | bytes 35655684 | tf_op jit(solution)/shard_map/te,de->td/dot_general | solution.py:28
  663.0 15.9 fusion.112
  718.8 105.6 %while.96 = (s32[]{:T(128)}, f32[512,16,64]{0,2,1:T(8,128)}, f32[512,16,64]{0,2,1:T(8,128)}, bf16[2,512,1024]{2,1,0:T(8,128)(2,1)}, bf16[2,512,16,64]{1,3,2,0:T(...) while((s32[]{:T(128)}, f32[512,16,64]{0,2,1:T(8,128)}, ...), condition=%wide.region_22.23_spmd.clone, body=%wide.region_20.22_spmd.clone.sunk | while | flops 2725765120 | bytes 198082896 | solution.py:126
  894.3 220.1 %while.97 = (s32[]{:T(128)}, f32[1024,16,64]{0,2,1:T(8,128)}, f32[1024,16,64]{0,2,1:T(8,128)}, bf16[2,512,1024]{2,1,0:T(8,128)(2,1)}, bf16[2,512,16,64]{1,3,2,0:...) while((s32[]{:T(128)}, f32[1024,16,64]{0,2,1:T(8,128)}, ...), condition=%wide.region_27.28_spmd.clone, body=%wide.region_25.27_spmd.clone.sunk | while | flops 5500821504 | bytes 370901216 | solution.py:126
  911.1 17.7 bitcast_add_fusion.11
  928.8 25.5 multiply_reduce_fusion.11
  954.3 28.1 %multiply_convert_fusion.8 = bf16[16,512,1024]{2,1,0:T(8,128)(2,1)} fusion(f32[16,512,1024]{2,1,0:T(8,128)} %get-tuple-element.938, f32[16,512,1024]{2,1,0:T(8,128)} %fusion.228, f32[16,512]{1,0:T(8,128)S(1)} %get-tuple-element.939, f32[16,512]{1,0:T(8,128)S(1)} %dynamic-slice_bitcast_fusion.16, pred[512,1024]{1,0:T(8,128)(4,1)S(1)} %dynamic-slice_bitcast_fusion.17), kind=kLoop, calls=%fused_computation.56.clone.1 | loop fusion | flops 50331648 | bytes 84475904 | tf_op jit(solution)/shard_map/while/body/eval_jaxpr/while/body/eval_jaxpr/convert_element_type | solution.py:113
  1019.6 18.9 bitcast_add_fusion.11
  1038.5 25.5 multiply_reduce_fusion.11
  1064.0 28.2 %multiply_convert_fusion.8 = bf16[16,512,1024]{2,1,0:T(8,128)(2,1)} fusion(f32[16,512,1024]{2,1,0:T(8,128)} %get-tuple-element.938, f32[16,512,1024]{2,1,0:T(8,128)} %fusion.228, f32[16,512]{1,0:T(8,128)S(1)} %get-tuple-element.939, f32[16,512]{1,0:T(8,128)S(1)} %dynamic-slice_bitcast_fusion.16, pred[512,1024]{1,0:T(8,128)(4,1)S(1)} %dynamic-slice_bitcast_fusion.17), kind=kLoop, calls=%fused_computation.56.clone.1 | loop fusion | flops 50331648 | bytes 84475904 | tf_op jit(solution)/shard_map/while/body/eval_jaxpr/while/body/eval_jaxpr/convert_element_type | solution.py:113
  1146.0 20.1 fusion.78
  1166.9 16.9 fusion.95
  1183.8 16.7 add_convert_fusion.1
  1219.5 40.1 %all-reduce.12 = (f32[1024]{0:T(1024)S(1)}, f32[1024]{0:T(1024)S(1)}, f32[1024]{0:T(1024)S(1)}, f32[1024]{0:T(1024)S(1)}, f32[1024]{0:T(1024)S(1)}, /*index=5*/f32[1024]{0:T(1024)S(1)}) all-reduce(f32[1024]{0:T(1024)S(1)} %get-tuple-element.597, ...), channel_id=12, replica_groups=mesh['wide'=8,'narrow'=4] {'wide','narrow'}, use_global_device_ids=true, to_apply=%region_41.42.clone | all-reduce | flops 6144 | bytes 49152
  1293.4 149.0 %reduce-scatter.15.cloned.1.call-done = f32[32,1024]{1,0:T(8,128)} async-done(((f32[1024,1024]{1,0:T(8,128)}), f32[32,1024]{1,0:T(8,128)}) %reduce-scatter.15.cloned.1.call-update) | async-done | bytes 131088 | tf_op jit(solution)/shard_map/reduce_scatter | solution.py:179
  1442.4 149.4 %reduce-scatter.17.cloned.1.call-done = f32[32,1024]{1,0:T(8,128)} async-done(((f32[1024,1024]{1,0:T(8,128)}), f32[32,1024]{1,0:T(8,128)}) %reduce-scatter.17.cloned.1.call-update) | async-done | bytes 131088 | tf_op jit(solution)/shard_map/reduce_scatter | solution.py:179
  1591.8 149.8 %reduce-scatter.19.cloned.1.call-done = f32[32,1024]{1,0:T(8,128)} async-done(((f32[1024,1024]{1,0:T(8,128)}), f32[32,1024]{1,0:T(8,128)}) %reduce-scatter.19.cloned.1.call-update) | async-done | bytes 131088 | tf_op jit(solution)/shard_map/reduce_scatter | solution.py:179
  1741.6 148.8 %reduce-scatter.21.cloned.1.call-done = f32[32,1024]{1,0:T(8,128)} async-done(((f32[1024,1024]{1,0:T(8,128)}), f32[32,1024]{1,0:T(8,128)}) %reduce-scatter.21.cloned.1.call-update) | async-done | bytes 131088 | tf_op jit(solution)/shard_map/reduce_scatter | solution.py:179
  1890.4 365.8 %reduce-scatter.29.cloned.1.call-done = f32[128,1024]{1,0:T(8,128)} async-done(((f32[4096,1024]{1,0:T(8,128)}), f32[128,1024]{1,0:T(8,128)}) %reduce-scatter.29.cloned.1.call-update) | async-done | bytes 524304 | tf_op jit(solution)/shard_map/reduce_scatter | solution.py:179
  2256.1 364.9 %reduce-scatter.27.cloned.1.call-done = f32[32,4096]{1,0:T(8,128)} async-done(((f32[1024,4096]{1,0:T(8,128)}), f32[32,4096]{1,0:T(8,128)}) %reduce-scatter.27.cloned.1.call-update) | async-done | bytes 524304 | tf_op jit(solution)/shard_map/reduce_scatter | solution.py:179
  (406 shorter events, 621.8 us)
Async XLA Ops:
  7.2 293.3 %copy-start = (bf16[512,1024]{1,0:T(8,128)(2,1)S(1)}, bf16[512,1024]{1,0:T(8,128)(2,1)}, u32[]{:S(2)}) copy-start(bf16[512,1024]{1,0:T(8,128)(2,1)} %param.33) | copy-start | bytes 3145732
  7.2 114.5 %all-gather.11.cloned.1.call-start = ((), (), s32[]{:S(2)}) async-start(), calls=%async_computation.10 | async-start | bytes 2162688 | tf_op jit(solution)/shard_map/all_gather | solution.py:224
  7.9 131.6 %all-gather.15.cloned.1.call-start = ((), (), s32[]{:S(2)}) async-start(), calls=%async_computation.12 | async-start | bytes 2162688 | tf_op jit(solution)/shard_map/all_gather | solution.py:226
  8.7 178.3 %all-gather.13.cloned.1.call-start = ((), (), s32[]{:S(2)}) async-start(), calls=%async_computation.11 | async-start | bytes 2162688 | tf_op jit(solution)/shard_map/all_gather | solution.py:225
  9.4 291.1 %all-gather.23.cloned.1.call-start = ((), (), s32[]{:S(2)}) async-start(), calls=%async_computation.16 | async-start | bytes 2162688 | tf_op jit(solution)/shard_map/all_gather | solution.py:230
  10.0 297.4 %all-gather.21.cloned.1.call-start = ((), (), s32[]{:S(2)}) async-start(), calls=%async_computation.15 | async-start | bytes 2162688 | tf_op jit(solution)/shard_map/all_gather | solution.py:229
  10.6 351.0 %all-gather.17.cloned.1.call-start = ((), (), s32[]{:S(2)}) async-start(), calls=%async_computation.13 | async-start | bytes 2162688 | tf_op jit(solution)/shard_map/all_gather | solution.py:227
  11.2 408.7 %all-gather.19.cloned.1.call-start = ((), (), s32[]{:S(2)}) async-start(), calls=%async_computation.14 | async-start | bytes 2162688 | tf_op jit(solution)/shard_map/all_gather | solution.py:228
  11.9 494.2 %all-gather.25.cloned.1.call-start = ((), (), s32[]{:S(2)}) async-start(), calls=%async_computation.17 | async-start | bytes 2162688 | tf_op jit(solution)/shard_map/all_gather | solution.py:231
  12.7 544.8 %all-gather.27.cloned.1.call-start = ((), (), s32[]{:S(2)}) async-start(), calls=%async_computation.18 | async-start | bytes 8650752 | tf_op jit(solution)/shard_map/all_gather | solution.py:262
  13.4 622.8 %all-gather.29.cloned.1.call-start = ((), (), s32[]{:S(2)}) async-start(), calls=%async_computation.19 | async-start | bytes 8650752 | tf_op jit(solution)/shard_map/all_gather | solution.py:263
  14.0 1264.9 %reduce-scatter.25.cloned.1.call-start = ((), (), s32[]{:S(2)}) async-start(), calls=%async_computation.25 | async-start | bytes 4325376 | tf_op jit(solution)/shard_map/reduce_scatter | solution.py:179
  512.3 177.4 %copy-start.46 = (f32[1024]{0:T(1024)}, f32[1024]{0:T(1024)S(1)}, u32[]{:S(2)}) copy-start(f32[1024]{0:T(1024)S(1)} %broadcast_multiply_fusion) | copy-start | bytes 12292
  514.8 174.9 %copy-start.61 = (f32[1024]{0:T(1024)}, f32[1024]{0:T(1024)S(1)}, u32[]{:S(2)}) copy-start(f32[1024]{0:T(1024)S(1)} %fusion.92) | copy-start | bytes 12292
  514.8 121.4 %copy-start.48 = (f32[1024]{0:T(1024)S(1)}, f32[1024]{0:T(1024)}, u32[]{:S(2)}) copy-start(f32[1024]{0:T(1024)} %fusion.88) | copy-start | bytes 12292
  698.9 580.0 %reduce-scatter.23.cloned.1.call-start = ((), (), s32[]{:S(2)}) async-start(), calls=%async_computation.24 | async-start | bytes 4325376 | tf_op jit(solution)/shard_map/reduce_scatter | solution.py:179
  718.8 105.6 %copy-start.41 = (f32[1024]{0:T(1024)S(1)}, f32[1024]{0:T(1024)}, u32[]{:S(2)}) copy-start(f32[1024]{0:T(1024)} %copy-done.40) | copy-start | bytes 12292
  718.8 105.6 %copy-start.43 = (f32[1024]{0:T(1024)S(1)}, f32[1024]{0:T(1024)}, u32[]{:S(2)}) copy-start(f32[1024]{0:T(1024)} %convert_element_type.201) | copy-start | bytes 12292
  718.8 105.6 %copy-start.52 = (f32[1024]{0:T(1024)S(1)}, f32[1024]{0:T(1024)}, u32[]{:S(2)}) copy-start(f32[1024]{0:T(1024)} %copy-done.51) | copy-start | bytes 12292
  718.8 105.6 %copy-start.74 = (f32[1024]{0:T(1024)S(1)}, f32[1024]{0:T(1024)}, u32[]{:S(2)}) copy-start(f32[1024]{0:T(1024)} %convert_element_type.202) | copy-start | bytes 12292
  831.7 447.2 %reduce-scatter.33.cloned.1.call-start = ((), (), s32[]{:S(2)}) async-start(), calls=%async_computation.29 | async-start | bytes 4325376
  843.1 450.3 %reduce-scatter.31.cloned.1.call-start = ((), (), s32[]{:S(2)}) async-start(), calls=%async_computation.28 | async-start | bytes 4325376
  892.1 550.3 %reduce-scatter.15.cloned.1.call-start = ((), (), s32[]{:S(2)}) async-start(), calls=%async_computation.20 | async-start | bytes 4325376 | tf_op jit(solution)/shard_map/reduce_scatter | solution.py:179
  894.3 220.2 %copy-start.45 = (f32[1024]{0:T(1024)S(1)}, f32[1024]{0:T(1024)}, u32[]{:S(2)}) copy-start(f32[1024]{0:T(1024)} %copy-done.44) | copy-start | bytes 12292
  894.3 220.2 %copy-start.56 = (f32[1024]{0:T(1024)S(1)}, f32[1024]{0:T(1024)}, u32[]{:S(2)}) copy-start(f32[1024]{0:T(1024)} %copy-done.55) | copy-start | bytes 12292
  894.3 220.2 %copy-start.58 = (f32[1024]{0:T(1024)S(1)}, f32[1024]{0:T(1024)}, u32[]{:S(2)}) copy-start(f32[1024]{0:T(1024)} %copy-done.57) | copy-start | bytes 12292
  1121.2 470.6 %reduce-scatter.17.cloned.1.call-start = ((), (), s32[]{:S(2)}) async-start(), calls=%async_computation.21 | async-start | bytes 4325376 | tf_op jit(solution)/shard_map/reduce_scatter | solution.py:179
  1129.6 612.0 %reduce-scatter.19.cloned.1.call-start = ((), (), s32[]{:S(2)}) async-start(), calls=%async_computation.22 | async-start | bytes 4325376 | tf_op jit(solution)/shard_map/reduce_scatter | solution.py:179
  1138.1 752.3 %reduce-scatter.21.cloned.1.call-start = ((), (), s32[]{:S(2)}) async-start(), calls=%async_computation.23 | async-start | bytes 4325376 | tf_op jit(solution)/shard_map/reduce_scatter | solution.py:179
  1145.4 1110.8 %reduce-scatter.29.cloned.1.call-start = ((), (), s32[]{:S(2)}) async-start(), calls=%async_computation.27 | async-start | bytes 17301504 | tf_op jit(solution)/shard_map/reduce_scatter | solution.py:179
  1166.2 1454.8 %reduce-scatter.27.cloned.1.call-start = ((), (), s32[]{:S(2)}) async-start(), calls=%async_computation.26 | async-start | bytes 17301504 | tf_op jit(solution)/shard_map/reduce_scatter | solution.py:179
  1273.3 1347.8 %copy-start.1 = (bf16[512,1024]{1,0:T(8,128)(2,1)S(1)}, bf16[512,1024]{1,0:T(8,128)(2,1)}, u32[]{:S(2)}) copy-start(bf16[512,1024]{1,0:T(8,128)(2,1)} %param.33) | copy-start | bytes 3145732
  (79 other events, 952.3 us)
Sparse Core Ops, SparseCore 0:
  11.0 59.2 all-gather.10
  73.2 55.4 all-gather.14
  131.6 55.3 all-gather.12
  189.8 55.3 all-gather.22
  247.9 55.4 all-gather.20
  306.2 55.3 all-gather.16
  364.5 55.3 all-gather.18
  422.8 55.3 all-gather.24
  481.1 76.2 all-gather.26
  560.2 75.9 all-gather.28
  699.1 146.8 reduce-scatter.24
  848.7 146.0 reduce-scatter.22
  997.6 146.2 reduce-scatter.32
  1146.6 146.7 reduce-scatter.30
  1296.1 146.2 reduce-scatter.14
  1445.1 146.6 reduce-scatter.16
  1594.5 147.0 reduce-scatter.18
  1744.3 146.0 reduce-scatter.20
  1893.2 362.8 reduce-scatter.28
  2258.9 362.1 reduce-scatter.26
where the time goes:
time: 2640 us; the launch traced here: 2630 us
  waiting for transfers between devices  1600 us (61%)
  matrix products  551 us (21%)
  other arithmetic  171 us (6%)
  local copies, waits for them, and re-layouts  168 us (6%)
  blocking collectives  123 us (5%)
    reduce_scatter x8, waiting for transfers between devices, merge_grads(): lax.psum_scatter(gradients, ('wide', 'narrow'), scatter_dimension=0, tile...  1330 us
    dot_general x8, matrix products, one_block(): jnp.einsum('qhd,khd->hqk', query_part, key_heads, preferred_element_type=...  95.7 us
    unnamed x2, blocking collectives  80.8 us
    convert_element_type x4, other arithmetic, one_block(): score_grad = (probs_full * (prob_grad - row_dot)).astype(jnp.bfloat16)  79.5 us
    dot_general x10, matrix products, outer_sum(): jnp.einsum('td,te->de', left_side, gradient, preferred_element_type=jnp.f...  77.8 us
    dot_general x10, matrix products, linear(): return jnp.dot(left_side, right_side, preferred_element_type=jnp.float32)  75.4 us
    dot_general x4, matrix products, one_block(): jnp.einsum('qhd,khd->hqk', grad_part, value_heads, preferred_element_type...  75 us
    dot_general x10, matrix products, linear_back(): jnp.einsum('te,de->td', gradient, right_side, preferred_element_type=jnp....  73.5 us
  transfers between devices with their start and end apart: 20, of which 12 were waited for; matrix products, arithmetic and copies ran while one was open for 30% of the time, Pallas kernels for 0%

commit v1 on v0

v1 whole, which is shorter than its diff:
```python
import functools
import jax
import jax.numpy as jnp
from jax import lax
from jax.experimental import pallas as pl
from jax.experimental.pallas import tpu as pltpu
from jax.sharding import PartitionSpec as P

SEQ = 1024
MEM = 512
HEADS = 16
HEAD_DIM = 64
EPSILON = 1e-05
BQ = 256
LOG2E = 1.4426950408889634
SCALE2 = HEAD_DIM**-0.5 * LOG2E
FILLER = -1e30
F32, BF16 = jnp.float32, jnp.bfloat16


def mm(a, b):
    return jnp.dot(a, b, preferred_element_type=F32)


def halves(x):
    low = lax.broadcasted_iota(jnp.int32, x.shape, 1) < HEAD_DIM
    zero = jnp.zeros_like(x)
    return (jnp.where(low, x, zero), jnp.where(low, zero, x))


def self_allowed_of(i, j, first_row):
    shape = (BQ, BQ)
    key = lax.broadcasted_iota(jnp.int32, shape, 0)
    allowed = key >= first_row - j * BQ
    if i == j:
        allowed = allowed & (key <= lax.broadcasted_iota(jnp.int32, shape, 1))
    return allowed


def self_forward_kernel(low_ref, first_ref, qkv_ref, out_ref, log_ref, m_ref, l_ref, acc_ref):
    row = pl.program_id(0)
    blocks = SEQ // BQ
    for i in range(blocks):
        rows = slice(i * BQ, (i + 1) * BQ)
        q_t = qkv_ref[rows, 0:128].T
        first_row = first_ref[0, :, rows]

        def step(j, fresh):
            keys = slice(j * BQ, (j + 1) * BQ)
            k_parts = halves(qkv_ref[keys, 128:256])
            v_t = qkv_ref[keys, 256:384].T
            allowed = self_allowed_of(i, j, first_row)
            for h in range(2):
                feats = slice(h * 64, (h + 1) * 64)
                s = jnp.where(allowed, mm(k_parts[h], q_t) * SCALE2, FILLER)
                peak = jnp.max(s, axis=0, keepdims=True)
                if fresh:
                    p = jnp.exp2(s - peak)
                    m_ref[h : h + 1, :] = peak
                    l_ref[h : h + 1, :] = jnp.sum(p, axis=0, keepdims=True)
                    acc_ref[feats, :] = mm(v_t[feats, :], p.astype(BF16))
                else:
                    old = m_ref[h : h + 1, :]
                    peak = jnp.maximum(old, peak)
                    p = jnp.exp2(s - peak)
                    fade = jnp.exp2(old - peak)
                    m_ref[h : h + 1, :] = peak
                    l_ref[h : h + 1, :] = l_ref[h : h + 1, :] * fade + jnp.sum(p, axis=0, keepdims=True)
                    acc_ref[feats, :] = acc_ref[feats, :] * fade + mm(v_t[feats, :], p.astype(BF16))

        step(i, True)
        for j in reversed(range(i)):
            pl.when(j >= low_ref[row * blocks + i])(functools.partial(step, j, False))
        total = l_ref[0:2, :]
        log_ref[0, 0, 0:2, rows] = m_ref[0:2, :] + jnp.log2(total)
        inv = 1.0 / total
        o_t = jnp.concatenate([acc_ref[0:64, :] * inv[0:1], acc_ref[64:128, :] * inv[1:2]], axis=0)
        out_ref[rows, :] = o_t.T.astype(BF16)


def self_forward(low, first, qkv, row_count):
    pairs = HEADS // 2
    return pl.pallas_call(
        self_forward_kernel,
        grid_spec=pltpu.PrefetchScalarGridSpec(
            num_scalar_prefetch=1,
            grid=(row_count, pairs),
            in_specs=[
                pl.BlockSpec((1, 1, SEQ), lambda r, p, low: (r, 0, 0)),
                pl.BlockSpec((SEQ, 384), lambda r, p, low: (r, p)),
            ],
            out_specs=[
                pl.BlockSpec((SEQ, 128), lambda r, p, low: (r, p)),
                pl.BlockSpec((1, 1, 8, SEQ), lambda r, p, low: (r, p, 0, 0)),
            ],
            scratch_shapes=[pltpu.VMEM((8, BQ), F32), pltpu.VMEM((8, BQ), F32), pltpu.VMEM((128, BQ), F32)],
        ),
        out_shape=[
            jax.ShapeDtypeStruct((row_count * SEQ, HEADS * HEAD_DIM), BF16),
            jax.ShapeDtypeStruct((row_count, pairs, 8, SEQ), F32),
        ],
        name="self_forward",
        compiler_params=pltpu.CompilerParams(vmem_limit_bytes=32 << 20),
        cost_estimate=pl.CostEstimate(flops=20 << 30, bytes_accessed=row_count * (8 << 20), transcendentals=8 << 20),
    )(low, first, qkv)


def self_backward_kernel(low_ref, first_ref, log_ref, qkv_ref, out_ref, grad_ref, dqkv_ref, dk_ref, dv_ref, dq_ref):
    row = pl.program_id(0)
    blocks = SEQ // BQ
    dk_ref[...] = jnp.zeros_like(dk_ref)
    dv_ref[...] = jnp.zeros_like(dv_ref)
    for i in range(blocks):
        rows = slice(i * BQ, (i + 1) * BQ)
        q, g = qkv_ref[rows, 0:128], grad_ref[rows, :]
        q_t, g_t = q.T, g.T
        prod = g_t.astype(F32) * out_ref[rows, :].T.astype(F32)
        delta = [jnp.sum(prod[h * 64 : (h + 1) * 64], axis=0, keepdims=True) for h in range(2)]
        q_parts, g_parts = halves(q), halves(g)
        first_row = first_ref[0, :, rows]

        def step(j, fresh):
            keys = slice(j * BQ, (j + 1) * BQ)
            k = qkv_ref[keys, 128:256]
            k_parts, k_t = halves(k), k.T
            v_parts = halves(qkv_ref[keys, 256:384])
            allowed = self_allowed_of(i, j, first_row)
            dv, dk = [], []
            for h in range(2):
                feats = slice(h * 64, (h + 1) * 64)
                s = jnp.where(allowed, mm(k_parts[h], q_t) * SCALE2, FILLER)
                p = jnp.exp2(s - log_ref[0, 0, h : h + 1, rows])
                dp = mm(v_parts[h], g_t)
                ds = (p * (dp - delta[h])).astype(BF16)
                dv.append(mm(p.astype(BF16), g_parts[h]))
                dk.append(mm(ds, q_parts[h]))
                part = mm(k_t[feats, :], ds)
                dq_ref[feats, :] = part if fresh else dq_ref[feats, :] + part
            dv_ref[keys, :] += dv[0] + dv[1]
            dk_ref[keys, :] += dk[0] + dk[1]

        step(i, True)
        for j in reversed(range(i)):
            pl.when(j >= low_ref[row * blocks + i])(functools.partial(step, j, False))
        dqkv_ref[rows, 0:128] = (dq_ref[...] * HEAD_DIM**-0.5).T.astype(BF16)
    dqkv_ref[:, 128:256] = (dk_ref[...] * HEAD_DIM**-0.5).astype(BF16)
    dqkv_ref[:, 256:384] = dv_ref[...].astype(BF16)


def self_backward(low, first, logs, qkv, out, grad, row_count):
    pairs = HEADS // 2
    return pl.pallas_call(
        self_backward_kernel,
        grid_spec=pltpu.PrefetchScalarGridSpec(
            num_scalar_prefetch=1,
            grid=(row_count, pairs),
            in_specs=[
                pl.BlockSpec((1, 1, SEQ), lambda r, p, low: (r, 0, 0)),
                pl.BlockSpec((1, 1, 8, SEQ), lambda r, p, low: (r, p, 0, 0)),
                pl.BlockSpec((SEQ, 384), lambda r, p, low: (r, p)),
                pl.BlockSpec((SEQ, 128), lambda r, p, low: (r, p)),
                pl.BlockSpec((SEQ, 128), lambda r, p, low: (r, p)),
            ],
            out_specs=pl.BlockSpec((SEQ, 384), lambda r, p, low: (r, p)),
            scratch_shapes=[pltpu.VMEM((SEQ, 128), F32), pltpu.VMEM((SEQ, 128), F32), pltpu.VMEM((128, BQ), F32)],
        ),
        out_shape=jax.ShapeDtypeStruct((row_count * SEQ, 3 * HEADS * HEAD_DIM), BF16),
        name="self_backward",
        compiler_params=pltpu.CompilerParams(vmem_limit_bytes=32 << 20),
        cost_estimate=pl.CostEstimate(flops=40 << 30, bytes_accessed=row_count * (16 << 20), transcendentals=8 << 20),
    )(low, first, logs, qkv, out, grad)


def cross_allowed_of(bounds_ref, rows):
    key = lax.broadcasted_iota(jnp.int32, (MEM, BQ), 0)
    return (key >= bounds_ref[0, 0:1, rows]) & (key < bounds_ref[0, 1:2, rows])


def cross_forward_kernel(bounds_ref, q_ref, kv_ref, out_ref, log_ref):
    k_parts = halves(kv_ref[:, 0:128])
    v_t = kv_ref[:, 128:256].T
    for i in range(SEQ // BQ):
        rows = slice(i * BQ, (i + 1) * BQ)
        q_t = q_ref[rows, :].T
        allowed = cross_allowed_of(bounds_ref, rows)
        outs = []
        for h in range(2):
            s = jnp.where(allowed, mm(k_parts[h], q_t) * SCALE2, FILLER)
            peak = jnp.max(s, axis=0, keepdims=True)
            p = jnp.exp2(s - peak)
            total = jnp.sum(p, axis=0, keepdims=True)
            log_ref[0, 0, h : h + 1, rows] = peak + jnp.log2(total)
            outs.append(mm(v_t[h * 64 : (h + 1) * 64, :], p.astype(BF16)) * (1.0 / total))
        out_ref[rows, :] = jnp.concatenate(outs, axis=0).T.astype(BF16)


def cross_forward(bounds, q, kv, row_count):
    pairs = HEADS // 2
    return pl.pallas_call(
        cross_forward_kernel,
        grid=(row_count, pairs),
        in_specs=[
            pl.BlockSpec((1, 8, SEQ), lambda r, p: (r, 0, 0)),
            pl.BlockSpec((SEQ, 128), lambda r, p: (r, p)),
            pl.BlockSpec((MEM, 256), lambda r, p: (r, p)),
        ],
        out_specs=[
            pl.BlockSpec((SEQ, 128), lambda r, p: (r, p)),
            pl.BlockSpec((1, 1, 8, SEQ), lambda r, p: (r, p, 0, 0)),
        ],
        out_shape=[
            jax.ShapeDtypeStruct((row_count * SEQ, HEADS * HEAD_DIM), BF16),
            jax.ShapeDtypeStruct((row_count, pairs, 8, SEQ), F32),
        ],
        name="cross_forward",
        compiler_params=pltpu.CompilerParams(vmem_limit_bytes=32 << 20),
        cost_estimate=pl.CostEstimate(flops=20 << 30, bytes_accessed=row_count * (6 << 20), transcendentals=8 << 20),
    )(bounds, q, kv)


def cross_backward_kernel(bounds_ref, log_ref, q_ref, kv_ref, out_ref, grad_ref, dq_ref, dkv_ref, dk_ref, dv_ref):
    k = kv_ref[:, 0:128]
    k_parts, k_t = halves(k), k.T
    v_parts = halves(kv_ref[:, 128:256])
    for i in range(SEQ // BQ):
        rows = slice(i * BQ, (i + 1) * BQ)
        q, g = q_ref[rows, :], grad_ref[rows, :]
        q_t, g_t = q.T, g.T
        prod = g_t.astype(F32) * out_ref[rows, :].T.astype(F32)
        q_parts, g_parts = halves(q), halves(g)
        allowed = cross_allowed_of(bounds_ref, rows)
        dv, dk, dq = [], [], []
        for h in range(2):
            feats = slice(h * 64, (h + 1) * 64)
            delta = jnp.sum(prod[feats], axis=0, keepdims=True)
            s = jnp.where(allowed, mm(k_parts[h], q_t) * SCALE2, FILLER)
            p = jnp.exp2(s - log_ref[0, 0, h : h + 1, rows])
            dp = mm(v_parts[h], g_t)
            ds = (p * (dp - delta)).astype(BF16)
            dv.append(mm(p.astype(BF16), g_parts[h]))
            dk.append(mm(ds, q_parts[h]))
            dq.append(mm(k_t[feats, :], ds))
        if i == 0:
            dv_ref[...] = dv[0] + dv[1]
            dk_ref[...] = dk[0] + dk[1]
        else:
            dv_ref[...] += dv[0] + dv[1]
            dk_ref[...] += dk[0] + dk[1]
        dq_ref[rows, :] = (jnp.concatenate(dq, axis=0) * HEAD_DIM**-0.5).T.astype(BF16)
    dkv_ref[:, 0:128] = (dk_ref[...] * HEAD_DIM**-0.5).astype(BF16)
    dkv_ref[:, 128:256] = dv_ref[...].astype(BF16)


def cross_backward(bounds, logs, q, kv, out, grad, row_count):
    pairs = HEADS // 2
    return pl.pallas_call(
        cross_backward_kernel,
        grid=(row_count, pairs),
        in_specs=[
            pl.BlockSpec((1, 8, SEQ), lambda r, p: (r, 0, 0)),
            pl.BlockSpec((1, 1, 8, SEQ), lambda r, p: (r, p, 0, 0)),
            pl.BlockSpec((SEQ, 128), lambda r, p: (r, p)),
            pl.BlockSpec((MEM, 256), lambda r, p: (r, p)),
            pl.BlockSpec((SEQ, 128), lambda r, p: (r, p)),
            pl.BlockSpec((SEQ, 128), lambda r, p: (r, p)),
        ],
        out_specs=[
            pl.BlockSpec((SEQ, 128), lambda r, p: (r, p)),
            pl.BlockSpec((MEM, 256), lambda r, p: (r, p)),
        ],
        scratch_shapes=[pltpu.VMEM((MEM, 128), F32), pltpu.VMEM((MEM, 128), F32)],
        out_shape=[
            jax.ShapeDtypeStruct((row_count * SEQ, HEADS * HEAD_DIM), BF16),
            jax.ShapeDtypeStruct((row_count * MEM, 2 * HEADS * HEAD_DIM), BF16),
        ],
        name="cross_backward",
        compiler_params=pltpu.CompilerParams(vmem_limit_bytes=32 << 20),
        cost_estimate=pl.CostEstimate(flops=40 << 30, bytes_accessed=row_count * (12 << 20), transcendentals=8 << 20),
    )(bounds, logs, q, kv, out, grad)


def row_bounds(pair_starts, source_starts, live_length):
    places = jnp.arange(SEQ, dtype=jnp.int32)
    counted = jnp.sum((pair_starts[:, :, None] <= places).astype(jnp.int32), axis=1)
    live = places < live_length[:, None]
    begun = jnp.max(jnp.where(pair_starts[:, :, None] <= places, pair_starts[:, :, None], 0), axis=1)
    first = jnp.where(live, begun, live_length[:, None])
    nseg = pair_starts.shape[1]
    pick = jnp.arange(nseg)[None, :, None] == (counted - 1)[:, None, :]
    ends = jnp.concatenate([source_starts[:, 1:], jnp.full_like(source_starts[:, :1], MEM)], axis=1)
    start = jnp.sum(jnp.where(pick, source_starts[:, :, None], 0), axis=1)
    end = jnp.sum(jnp.where(pick, ends[:, :, None], 0), axis=1)
    start = jnp.where(live, start, 0)
    end = jnp.where(live, end, MEM)
    bounds = jnp.pad(jnp.stack([start, end], axis=1), ((0, 0), (0, 6), (0, 0)))
    low = (first[:, ::BQ] // BQ).reshape(-1)
    return low, first[:, None, :], bounds


def stages_of(mesh_axes):
    plan = []
    for axis, size in mesh_axes:
        bits = size.bit_length() - 1
        at = 0
        while at < bits:
            take = 1 if (bits - at) % 2 else 2
            plan.append((axis, at, take))
            at += take
    return plan


def trade(value, axis, size, mask):
    return lax.ppermute(value, axis, [(i, i ^ mask) for i in range(size)])


def digit_of(axis, at, take):
    return (lax.axis_index(axis) >> at) & ((1 << take) - 1)


def sum_to_owner(partial, mesh_axes):
    rows, columns = partial.shape
    sizes = dict(mesh_axes)
    plan = stages_of(mesh_axes)
    groups = []
    for axis, _ in mesh_axes:
        groups += sorted((s for s in plan if s[0] == axis), key=lambda s: -s[1])
    extents = [1 << s[2] for s in groups]
    value = partial.reshape(*extents, -1, columns)
    for number, stage in enumerate(plan):
        axis, at, take = stage
        place = groups.index(stage)
        digit = digit_of(axis, at, take)

        def chunk(mask):
            return lax.dynamic_index_in_dim(value, digit ^ mask, place, keepdims=False)

        arrived = [trade(chunk(mask), axis, sizes[axis], mask << at) for mask in range(1, 1 << take)]
        total = chunk(0).astype(F32)
        for piece in arrived:
            total = total + piece.astype(F32)
        groups = [g for g in groups if g != stage]
        value = total if number == len(plan) - 1 else total.astype(BF16)
    return value.reshape(-1, columns)


def sum_everywhere(value, mesh_axes):
    sizes = dict(mesh_axes)
    for axis, at, take in stages_of(mesh_axes):
        arrived = [trade(value, axis, sizes[axis], mask << at) for mask in range(1, 1 << take)]
        for piece in arrived:
            value = value + piece
    return value


def norm_parts(values):
    center = values - jnp.mean(values, axis=-1, keepdims=True)
    inverse = lax.rsqrt(jnp.mean(center * center, axis=-1, keepdims=True) + EPSILON)
    return center * inverse, inverse


def norm_back(values, gain, gradient):
    unit, inverse = norm_parts(values)
    gain_grad = jnp.sum(gradient * unit, axis=0)
    shift_grad = jnp.sum(gradient, axis=0)
    scaled = gradient * gain
    back = inverse * (
        scaled
        - jnp.mean(scaled, axis=-1, keepdims=True)
        - unit * jnp.mean(scaled * unit, axis=-1, keepdims=True)
    )
    return back, gain_grad, shift_grad


def by_pairs(*parts):
    rows = parts[0].shape[0]
    return jnp.stack([p.reshape(rows, -1, 128) for p in parts], axis=2).reshape(rows, -1)


def from_pairs(value, count):
    rows = value.shape[0]
    split = value.reshape(rows, -1, count, 128)
    return [split[:, :, c].reshape(rows, -1) for c in range(count)]


def linear_back(gradient, weight):
    return jnp.einsum("te,de->td", gradient, weight, preferred_element_type=F32)


def outer_sum(left_side, gradient):
    return jnp.einsum("td,te->de", left_side, gradient, preferred_element_type=F32).astype(BF16)


def on_device(
    mesh_axes,
    tokens,
    memory,
    cotangent,
    live_length,
    pair_starts,
    source_starts,
    group_bounds,
    group_counts,
    self_query,
    self_key,
    self_value,
    self_output,
    cross_query,
    cross_key,
    cross_value,
    cross_output,
    hidden_in,
    hidden_out,
    first_gain,
    first_shift,
    second_gain,
    second_shift,
    third_gain,
    third_shift,
):
    names = tuple(axis for axis, _ in mesh_axes)
    row_count = live_length.shape[0]
    shard_rows = self_query.shape[0]
    reduce_sum = functools.partial(sum_to_owner, mesh_axes=mesh_axes)

    def gather(shard):
        return lax.all_gather(shard, names, axis=0, tiled=True)

    digits = jnp.stack([live_length // 256, live_length % 256], axis=1).astype(BF16)
    digits = jnp.pad(digits, ((0, shard_rows - row_count), (0, 0)))
    norms = jnp.stack([first_gain, first_shift, second_gain, second_shift, third_gain, third_shift], axis=1)
    extra = jnp.pad(jnp.concatenate([norms, digits], axis=1), ((0, 0), (0, 120)))
    early = gather(jnp.concatenate([by_pairs(self_query, self_key, self_value), extra], axis=1))
    d = early.shape[0]
    qkv_weight = early[:, : 3 * d]
    extra = early[:, 3 * d : 3 * d + 8].astype(F32).T
    gain_one, shift_one, gain_two, shift_two, gain_three, shift_three = [extra[n] for n in range(6)]
    live_total = jnp.sum(extra[6]) * 256.0 + jnp.sum(extra[7])
    later = gather(
        jnp.concatenate([self_output, cross_query, by_pairs(cross_key, cross_value), cross_output, hidden_in], axis=1)
    )
    output_self = later[:, :d]
    query_cross = later[:, d : 2 * d]
    kv_cross = later[:, 2 * d : 4 * d]
    output_cross = later[:, 4 * d : 5 * d]
    expand_whole = later[:, 5 * d :]
    reduce_whole = gather(hidden_out)

    low, first, bounds = row_bounds(pair_starts, source_starts, live_length)
    resident = tokens.astype(F32)
    normed_one = (norm_parts(resident)[0] * gain_one + shift_one).astype(BF16)
    qkv = mm(normed_one, qkv_weight).astype(BF16)
    self_mixed, self_logs = self_forward(low, first, qkv, row_count)
    after_self = resident + mm(self_mixed, output_self)
    normed_two = (norm_parts(after_self)[0] * gain_two + shift_two).astype(BF16)
    cross_q = mm(normed_two, query_cross).astype(BF16)
    cross_kv = mm(memory, kv_cross).astype(BF16)
    cross_mixed, cross_logs = cross_forward(bounds, cross_q, cross_kv, row_count)
    after_cross = after_self + mm(cross_mixed, output_cross)
    normed_three = (norm_parts(after_cross)[0] * gain_three + shift_three).astype(BF16)
    hidden = mm(normed_three, expand_whole)
    activated, gelu_back = jax.vjp(jax.nn.gelu, hidden)
    activated = activated.astype(BF16)
    layer_output = (after_cross + mm(activated, reduce_whole)).astype(BF16)

    device = lax.axis_index(names)
    member = (group_bounds[:-1] <= device) & (device < group_bounds[1:])
    pair_tokens = jnp.sum(jnp.where(member, group_counts, 0))
    device_count = 1
    for _, size in mesh_axes:
        device_count *= size
    token_all = row_count * SEQ * device_count
    row_weight = pair_tokens.astype(F32) * (token_all / 1000.0) / live_total
    places = jnp.arange(SEQ, dtype=jnp.int32)
    live_mask = (places[None, :] < live_length[:, None]).astype(F32).reshape(-1, 1)
    out_grad = cotangent.astype(F32) * live_mask * row_weight

    branch_three = out_grad.astype(BF16)
    reduce_shard = reduce_sum(outer_sum(activated, branch_three))
    hidden_grad = gelu_back(linear_back(branch_three, reduce_whole))[0].astype(BF16)
    expand_shard = reduce_sum(outer_sum(normed_three, hidden_grad))
    cross_part, gain_three_grad, shift_three_grad = norm_back(
        after_cross, gain_three, linear_back(hidden_grad, expand_whole)
    )
    cross_total = out_grad + cross_part

    branch_two = cross_total.astype(BF16)
    mixed_grad = linear_back(branch_two, output_cross).astype(BF16)
    cq_grad, ckv_grad = cross_backward(bounds, cross_logs, cross_q, cross_kv, cross_mixed, mixed_grad, row_count)
    cross_shard = reduce_sum(
        jnp.concatenate(
            [outer_sum(cross_mixed, branch_two), outer_sum(normed_two, cq_grad), outer_sum(memory, ckv_grad)], axis=1
        )
    )
    memory_grad = linear_back(ckv_grad, kv_cross).astype(BF16)
    self_part, gain_two_grad, shift_two_grad = norm_back(after_self, gain_two, linear_back(cq_grad, query_cross))
    self_total = cross_total + self_part

    branch_one = self_total.astype(BF16)
    self_output_shard = reduce_sum(outer_sum(self_mixed, branch_one))
    mixed_grad = linear_back(branch_one, output_self).astype(BF16)
    qkv_grad = self_backward(low, first, self_logs, qkv, self_mixed, mixed_grad, row_count)
    qkv_shard = reduce_sum(outer_sum(normed_one, qkv_grad))
    input_part, gain_one_grad, shift_one_grad = norm_back(resident, gain_one, linear_back(qkv_grad, qkv_weight))
    tokens_grad = (self_total + input_part).astype(BF16)

    norm_grads = sum_everywhere(
        jnp.stack([gain_one_grad, shift_one_grad, gain_two_grad, shift_two_grad, gain_three_grad, shift_three_grad]),
        mesh_axes,
    )
    norm_shards = lax.dynamic_slice_in_dim(norm_grads, device * shard_rows, shard_rows, axis=1)
    query_shard, key_shard, value_shard = from_pairs(qkv_shard, 3)
    cross_key_shard, cross_value_shard = from_pairs(cross_shard[:, 2 * d :], 2)
    return (
        layer_output,
        tokens_grad,
        memory_grad,
        query_shard,
        key_shard,
        value_shard,
        self_output_shard,
        cross_shard[:, d : 2 * d],
        cross_key_shard,
        cross_value_shard,
        cross_shard[:, :d],
        expand_shard,
        reduce_shard,
        *[norm_shards[n] for n in range(6)],
    )


def solution(mesh):
    names = ("wide", "narrow")
    mesh_axes = tuple((axis, mesh.shape[axis]) for axis in names)
    split, vector = P(names, None), P(names)
    return jax.shard_map(
        functools.partial(on_device, mesh_axes),
        mesh=mesh,
        in_specs=(split,) * 3 + (vector,) + (split,) * 2 + (P(), P()) + (split,) * 10 + (vector,) * 6,
        out_specs=(split,) * 13 + (vector,) * 6,
        check_vma=False,
    )
```

time: 2640 us -> 904 us (0.34)
  waiting for transfers between devices: 1600 us -> 305 us
  matrix products: 551 us -> 191 us
  Pallas kernels: 0 us -> 167 us
  blocking collectives: 123 us -> 0 us
  other arithmetic: 171 us -> 67.9 us
  local copies, waits for them, and re-layouts: 168 us -> 92.8 us
  starting transfers between devices: 0.79 us -> 52 us
    reduce_scatter x8 -> x0, waiting for transfers between devices: 1330 us -> none  [merge_grads(): lax.psum_scatter(gradients, ('wide', 'narrow'), scatter_dimension=0, tile...]
    dot_general x58 -> x21, matrix products: 551 us -> 191 us  [the longest x7 70.9 us: linear_back(): return jnp.einsum('te,de->td', gradient, weight, preferred_element_type=F32)]
    ppermute x0 -> x42, waiting for transfers between devices: none -> 185 us  [trade(): return lax.ppermute(value, axis, [(i, i ^ mask) for i in range(size)])]
    pallas_call x0 -> x4, Pallas kernels: none -> 167 us  [the longest x1 46.4 us: self_backward(): pl.pallas_call(self_backward_kernel, grid_spec=pltpu.PrefetchScalarGridSp...]
    all_gather x10 -> x3, waiting for transfers between devices: 247 us -> 120 us  [gather(): return lax.all_gather(shard, names, axis=0, tiled=True)]
    unnamed x2 -> x0, blocking collectives: 80.8 us -> none
    convert_element_type x17 -> x12, other arithmetic: 95.1 us -> 29.5 us  [the longest x10 28.2 us: sum_to_owner(): value = total if number == len(plan) - 1 else total.astype(BF16)]
    ppermute x0 -> x42, starting transfers between devices: none -> 51.9 us  [trade(): return lax.ppermute(value, axis, [(i, i ^ mask) for i in range(size)])]
  transfers between devices with their start and end apart: 20 -> 45, of which waited for: 12 -> 20; matrix products, arithmetic and copies ran while one was open for 30% -> 24% of each run, Pallas kernels for 0% -> 10%
where the time goes in v1:
time: 904 us; the launch traced here: 894 us
  waiting for transfers between devices  305 us (34%)
  matrix products  191 us (21%)
  Pallas kernels  167 us (18%)
  local copies, waits for them, and re-layouts  92.8 us (10%)
  other arithmetic  67.9 us (8%)
  starting transfers between devices  52 us (6%)
  between operations  18.3 us (2%)
    ppermute x42, waiting for transfers between devices, trade(): return lax.ppermute(value, axis, [(i, i ^ mask) for i in range(size)])  185 us
    all_gather x3, waiting for transfers between devices, gather(): return lax.all_gather(shard, names, axis=0, tiled=True)  120 us
    dot_general x7, matrix products, linear_back(): return jnp.einsum('te,de->td', gradient, weight, preferred_element_type=F32)  70.9 us
    dot_general x7, matrix products, mm(): return jnp.dot(a, b, preferred_element_type=F32)  63.3 us
    dot_general x7, matrix products, outer_sum(): jnp.einsum('td,te->de', left_side, gradient, preferred_element_type=F32)  56.8 us
    ppermute x42, starting transfers between devices, trade(): return lax.ppermute(value, axis, [(i, i ^ mask) for i in range(size)])  51.9 us
    pallas_call x1, Pallas kernels, self_backward(): pl.pallas_call(self_backward_kernel, grid_spec=pltpu.PrefetchScalarGridSp...  46.4 us
    pallas_call x1, Pallas kernels, self_forward(): pl.pallas_call(self_forward_kernel, grid_spec=pltpu.PrefetchScalarGridSpe...  45.6 us
  transfers between devices with their start and end apart: 45, of which 20 were waited for; matrix products, arithmetic and copies ran while one was open for 24% of the time, Pallas kernels for 10%

profile of v1, /device:TPU:0, one launch (start us, length us, event | category | flops | bytes accessed | tf_op | source)
XLA Modules:
  0.0 893.9 jit_solution(7077470439866370093)
XLA Ops:
  29.9 56.8 %all-gather.4.cloned.1.call-done = bf16[1024,3200]{1,0:T(8,128)(2,1)} async-done(((bf16[32,3200]{1,0:T(8,128)(2,1)}), bf16[1024,3200]{1,0:T(8,128)(2,1)}) %all-gather.4.cloned.1.call-update) | async-done | bytes 6553616 | tf_op jit(solution)/shard_map/all_gather | solution.py:426
  91.4 10.3 %convolution_convert_fusion.3.qkv_ref = bf16[1024,3072]{1,0:T(8,128)(2,1)S(1)} fusion(bf16[1024,3200]{1,0:T(8,128)(2,1)} %all-gather.4.cloned.1.call-done, bf16[1024,1024]{0,1:T(8,128)(2,1)S(1)} %copy.122, f32[1024]{0:T(1024)S(1)} %get-tuple-element.125, f32[1024]{0:T(1024)S(1)} %get-tuple-element.126, f32[1024]{0:T(1024)S(1)} %add_rsqrt_fusion.2, ...), kind=kOutput, calls=%fused_computation.29 | convolution fusion | flops 6451888128 | bytes 14696448 | tf_op jit(solution)/shard_map/dot_general | solution.py:22
  101.8 45.6 %self_forward.1 = (bf16[1024,1024]{1,0:T(8,128)(2,1)S(1)}, f32[1,8,8,1024]{3,2,1,0:T(8,128)S(1)}) custom-call(s32[4]{0:T(128)S(1)} %fusion.101.low_ref, s32[1,1,1024]{2,1,0:T(1,128)S(1)} %fusion.96.first_ref, bf16[1024,3072]{1,0:T(8,128)(2,1)S(1)} %convolution_convert_fusion.3.qkv_ref), custom_call_target="tpu_custom_call" | custom-call | flops 21474836480 | bytes 8388608 | tf_op jit(solution)/shard_map/self_forward/pallas_call | solution.py:83
  150.1 62.8 %all-gather.6.cloned.1.call-done = bf16[1024,9216]{1,0:T(8,128)(2,1)} async-done(((bf16[32,9216]{1,0:T(8,128)(2,1)}), bf16[1024,9216]{1,0:T(8,128)(2,1)}) %all-gather.6.cloned.1.call-update) | async-done | bytes 18874384 | tf_op jit(solution)/shard_map/all_gather | solution.py:426
  218.4 5.5 fusion.41.kv_ref
  229.1 43.1 %cross_forward.1 = (bf16[1024,1024]{1,0:T(8,128)(2,1)S(1)}, f32[1,8,8,1024]{3,2,1,0:T(8,128)S(1)}) custom-call(s32[1,8,1024]{2,1,0:T(8,128)S(1)} %pad.14.bounds_ref, bf16[1024,1024]{1,0:T(8,128)(2,1)S(1)} %convolution_convert_fusion.9.q_ref, bf16[512,2048]{1,0:T(8,128)(2,1)S(1)} %fusion.41.kv_ref), custom_call_target="tpu_custom_call" | custom-call | flops 21474836480 | bytes 6291456 | tf_op jit(solution)/shard_map/cross_forward/pallas_call | solution.py:199
  279.3 15.7 %fusion.12 = f32[1024,4096]{1,0:T(8,128)} fusion(bf16[1024,9216]{1,0:T(8,128)(2,1)} %all-gather.6.cloned.1.call-done, f32[1024,1024]{0,1:T(8,128)S(1)} %get-tuple-element.174, f32[1024]{0:T(1024)S(1)} %get-tuple-element.121, f32[1024]{0:T(1024)S(1)} %get-tuple-element.122, f32[1024]{0:T(1024)S(1)} %add_rsqrt_fusion, f32[1024]{0:T(1024)S(1)} %broadcast_multiply_fusion.6), kind=kOutput, calls=%fused_computation.21 | convolution fusion | flops 8595177472 | bytes 29376512 | tf_op jit(solution)/shard_map/dot_general | solution.py:22
  295.0 18.5 %convolution_convert_fusion = bf16[4096,1024]{1,0:T(8,128)(2,1)} fusion(bf16[1024,1024]{0,1:T(8,128)(2,1)S(1)} %copy-done.27, f32[]{:T(128)S(6)} %div.80, f32[1024]{0:T(1024)S(1)} %fusion.97, f32[1024,4096]{1,0:T(8,128)} %fusion.12), kind=kOutput, calls=%fused_computation.17 | convolution fusion | flops 8636071936 | bytes 27267076 | tf_op jit(solution)/shard_map/td,te->de/dot_general | solution.py:390
  313.5 26.4 %fusion.6 = bf16[1024,4096]{1,0:T(8,128)(2,1)} fusion(f32[1024,4096]{1,0:T(8,128)} %fusion.12, bf16[4096,1024]{1,0:T(8,128)(2,1)} %all-gather.8.cloned.1.call-done, bf16[1024,1024]{0,1:T(8,128)(2,1)} %copy.131, f32[]{:T(128)S(6)} %div.80, f32[1024]{0:T(1024)S(1)} %fusion.97), kind=kOutput, calls=%fused_computation.8 | convolution fusion | flops 8678014976 | bytes 35655684 | tf_op jit(solution)/shard_map/te,de->td/dot_general | solution.py:386
  339.9 16.3 %convolution_convert_fusion.1 = bf16[1024,4096]{1,0:T(8,128)(2,1)} fusion(bf16[1024,4096]{1,0:T(8,128)(2,1)} %fusion.6, f32[1024,1024]{0,1:T(8,128)} %copy-done.15, f32[1024]{0:T(1024)S(1)} %get-tuple-element.121, f32[1024]{0:T(1024)S(1)} %get-tuple-element.122, f32[1024]{0:T(1024)S(1)} %add_rsqrt_fusion, f32[1024]{0:T(1024)S(1)} %broadcast_multiply_fusion.6), kind=kOutput, calls=%fused_computation.18 | convolution fusion | flops 8599371776 | bytes 20987904 | tf_op jit(solution)/shard_map/td,te->de/dot_general | solution.py:390
  356.3 13.2 %fusion.110 = (f32[1024]{0:T(1024)}, f32[1024,1024]{1,0:T(8,128)}) fusion(bf16[1024,4096]{1,0:T(8,128)(2,1)S(1)} %copy-done.60, bf16[1024,9216]{1,0:T(8,128)(2,1)} %all-gather.6.cloned.1.call-done), kind=kOutput, calls=%fused_computation.252 | convolution fusion | flops 8590982144 | bytes 20975616 | tf_op jit(solution)/shard_map/te,de->td/dot_general | solution.py:386
  369.5 5.3 copy.132
  392.2 31.5 %cross_backward.1 = (bf16[1024,1024]{1,0:T(8,128)(2,1)S(1)}, bf16[512,2048]{1,0:T(8,128)(2,1)S(1)}) custom-call(s32[1,8,1024]{2,1,0:T(8,128)S(1)} %pad.14.bounds_ref, f32[1,8,8,1024]{3,2,1,0:T(8,128)S(1)} %copy-done.11, bf16[1024,1024]{1,0:T(8,128)(2,1)S(1)} %copy-done.9, bf16[512,2048]{1,0:T(8,128)(2,1)S(1)} %copy-done.5, bf16[1024,1024]{1,0:T(8,128)(2,1)S(1)} %copy-done.3, ...), custom_call_target="tpu_custom_call" | custom-call | flops 42949672960 | bytes 12582912 | tf_op jit(solution)/shard_map/cross_backward/pallas_call | solution.py:256
  432.3 6.1 fusion.109
  438.4 5.3 copy.133
  460.9 46.4 %self_backward.1 = bf16[1024,3072]{1,0:T(8,128)(2,1)S(1)} custom-call(s32[4]{0:T(128)S(1)} %fusion.101.low_ref, s32[1,1,1024]{2,1,0:T(1,128)S(1)} %fusion.96.first_ref, f32[1,8,8,1024]{3,2,1,0:T(8,128)S(1)} %get-tuple-element.29.log_ref, bf16[1024,3072]{1,0:T(8,128)(2,1)S(1)} %bitcast.212, bf16[1024,1024]{1,0:T(8,128)(2,1)S(1)} %copy-done.7, ...), custom_call_target="tpu_custom_call" | custom-call | flops 42949672960 | bytes 16777216 | tf_op jit(solution)/shard_map/self_backward/pallas_call | solution.py:152
  507.4 7.4 convolution_convert_fusion.2
  518.8 10.2 %fusion.108 = (f32[1024]{0:T(1024)S(1)}, f32[1024,1024]{1,0:T(8,128)}) fusion(bf16[1024,3072]{1,0:T(8,128)(2,1)S(1)} %self_backward.1, bf16[1024,3200]{1,0:T(8,128)(2,1)} %all-gather.4.cloned.1.call-done), kind=kOutput, calls=%fused_computation.250 | convolution fusion | flops 6443498496 | bytes 16781312 | tf_op jit(solution)/shard_map/te,de->td/dot_general | solution.py:386
  538.6 16.9 %add_convert_fusion = bf16[1024,1024]{0,1:T(8,128)(2,1)} fusion(f32[1024,1024]{0,1:T(8,128)} %copy-done.15, bf16[4096,1024]{1,0:T(8,128)(2,1)} %all-gather.8.cloned.1.call-done, f32[1024,4096]{1,0:T(8,128)} %fusion.12), kind=kOutput, calls=%fused_computation.60 | convolution fusion | flops 8629780480 | bytes 31457280 | tf_op jit(solution)/shard_map/dot_general | solution.py:22
  555.5 5.7 fusion.69
  575.6 11.3 %copy.137 = bf16[1024,4096]{1,0:T(8,128)(2,1)} copy(bf16[1024,4096]{0,1:T(8,128)(2,1)} %pad_maximum_fusion) | data formatting | bytes 16777216 | tf_op jit(solution)/shard_map/concatenate | solution.py:490
  623.2 28.5 %collective-permute-done.9 = bf16[4,32,1024]{2,1,0:T(8,128)(2,1)S(1)} collective-permute-done((bf16[4,32,1024]{2,1,0:T(8,128)(2,1)}, bf16[4,32,1024]{2,1,0:T(8,128)(2,1)S(1)}, u32[]{:S(2)}, u32[]{:S(2)}) %collective-permute-start.9) | collective-permute-done | bytes 262176 | tf_op jit(solution)/shard_map/ppermute | solution.py:313
  672.8 9.4 %collective-permute-done.5 = bf16[32,3072]{1,0:T(8,128)(2,1)S(1)} collective-permute-done((bf16[32,3072]{1,0:T(8,128)(2,1)S(1)}, bf16[32,3072]{1,0:T(8,128)(2,1)S(1)}, u32[]{:S(2)}, u32[]{:S(2)}) %collective-permute-start.5) | collective-permute-done | bytes 196640 | tf_op jit(solution)/shard_map/ppermute | solution.py:313
  702.9 5.6 fusion.7
  708.9 10.0 %collective-permute-done.22 = bf16[4,32,4096]{2,1,0:T(8,128)(2,1)S(1)} collective-permute-done((bf16[4,32,4096]{2,1,0:T(8,128)(2,1)}, bf16[4,32,4096]{2,1,0:T(8,128)(2,1)S(1)}, u32[]{:S(2)}, u32[]{:S(2)}) %collective-permute-start.22) | collective-permute-done | bytes 1048608 | tf_op jit(solution)/shard_map/ppermute | solution.py:313
  718.9 22.0 %collective-permute-done.24 = bf16[4,32,4096]{2,1,0:T(8,128)(2,1)S(1)} collective-permute-done((bf16[4,32,4096]{2,1,0:T(8,128)(2,1)}, bf16[4,32,4096]{2,1,0:T(8,128)(2,1)S(1)}, u32[]{:S(2)}, u32[]{:S(2)}) %collective-permute-start.24) | collective-permute-done | bytes 1048608 | tf_op jit(solution)/shard_map/ppermute | solution.py:313
  748.1 15.7 %collective-permute-done.15 = bf16[4,32,4096]{2,1,0:T(8,128)(2,1)S(1)} collective-permute-done((bf16[4,32,4096]{2,1,0:T(8,128)(2,1)}, bf16[4,32,4096]{2,1,0:T(8,128)(2,1)S(1)}, u32[]{:S(2)}, u32[]{:S(2)}) %collective-permute-start.15) | collective-permute-done | bytes 1048608 | tf_op jit(solution)/shard_map/ppermute | solution.py:313
  763.8 22.0 %collective-permute-done.17 = bf16[4,32,4096]{2,1,0:T(8,128)(2,1)S(1)} collective-permute-done((bf16[4,32,4096]{2,1,0:T(8,128)(2,1)}, bf16[4,32,4096]{2,1,0:T(8,128)(2,1)S(1)}, u32[]{:S(2)}, u32[]{:S(2)}) %collective-permute-start.17) | collective-permute-done | bytes 1048608 | tf_op jit(solution)/shard_map/ppermute | solution.py:313
  789.9 18.9 %collective-permute-done.29 = bf16[4,128,1024]{2,1,0:T(8,128)(2,1)S(1)} collective-permute-done((bf16[4,128,1024]{2,1,0:T(8,128)(2,1)S(1)}, bf16[4,128,1024]{2,1,0:T(8,128)(2,1)S(1)}, u32[]{:S(2)}, u32[]{:S(2)}) %collective-permute-start.29) | collective-permute-done | bytes 1048608 | tf_op jit(solution)/shard_map/ppermute | solution.py:313
  808.8 20.8 %collective-permute-done.31 = bf16[4,128,1024]{2,1,0:T(8,128)(2,1)S(1)} collective-permute-done((bf16[4,128,1024]{2,1,0:T(8,128)(2,1)S(1)}, bf16[4,128,1024]{2,1,0:T(8,128)(2,1)S(1)}, u32[]{:S(2)}, u32[]{:S(2)}) %collective-permute-start.31) | collective-permute-done | bytes 1048608 | tf_op jit(solution)/shard_map/ppermute | solution.py:313
  840.7 12.7 %collective-permute-start.32 = (bf16[128,1024]{1,0:T(8,128)(2,1)}, bf16[128,1024]{1,0:T(8,128)(2,1)}, u32[]{:S(2)}, u32[]{:S(2)}) collective-permute-start(bf16[128,1024]{1,0:T(8,128)(2,1)} %get-tuple-element.145), channel_id=1, source_target_pairs={{0,1},{1,0},{2,3},{3,2},{4,5},{5,4},{6,7},{7,6},{8,9},{9,8},{10,11... | collective-permute-start | bytes 786440 | tf_op jit(solution)/shard_map/ppermute | solution.py:313
  864.7 10.6 %collective-permute-done.26 = bf16[32,4096]{1,0:T(8,128)(2,1)} collective-permute-done((bf16[32,4096]{1,0:T(8,128)(2,1)}, bf16[32,4096]{1,0:T(8,128)(2,1)}, u32[]{:S(2)}, u32[]{:S(2)}) %collective-permute-start.26) | collective-permute-done | bytes 262176 | tf_op jit(solution)/shard_map/ppermute | solution.py:313
  (339 shorter events, 238.9 us)
Async XLA Ops:
  7.3 79.4 %all-gather.4.cloned.1.call-start = ((), (), s32[]{:S(2)}) async-start(), calls=%async_computation | async-start | bytes 6758400 | tf_op jit(solution)/shard_map/all_gather | solution.py:426
  13.0 200.0 %all-gather.6.cloned.1.call-start = ((), (), s32[]{:S(2)}) async-start(), calls=%async_computation.1 | async-start | bytes 19464192 | tf_op jit(solution)/shard_map/all_gather | solution.py:426
  18.7 294.8 %all-gather.8.cloned.1.call-start = ((), (), s32[]{:S(2)}) async-start(), calls=%async_computation.2 | async-start | bytes 8650752 | tf_op jit(solution)/shard_map/all_gather | solution.py:426
  516.0 72.6 %collective-permute-start.7 = (bf16[4,4,32,1024]{3,2,1,0:T(8,128)(2,1)}, bf16[4,4,32,1024]{3,2,1,0:T(8,128)(2,1)}, u32[]{:S(2)}, u32[]{:S(2)}) collective-permute-start(bf16[4,4,32,1024]{3,2,1,0:T(8,128)(2,1)} %dynamic-slice_bitcast_fusion.13), channel_id=1, source_target_pairs={{0,4},{4,0},{8,12},{12,8},{16,20},{20,16},{24,28},{28,24},{1,5},{5... | collective-permute-start | bytes 3145736 | tf_op jit(solution)/shard_map/ppermute | solution.py:313
  518.6 75.6 %collective-permute-start = (bf16[4,4,32,3072]{3,2,1,0:T(8,128)(2,1)}, bf16[4,4,32,3072]{3,2,1,0:T(8,128)(2,1)}, u32[]{:S(2)}, u32[]{:S(2)}) collective-permute-start(bf16[4,4,32,3072]{3,2,1,0:T(8,128)(2,1)} %dynamic-slice_bitcast_fusion.3), channel_id=1, source_target_pairs={{0,4},{4,0},{8,12},{12,8},{16,20},{20,16},{24,28},{28,24},{1,5},{5... | collective-permute-start | bytes 9437192 | tf_op jit(solution)/shard_map/ppermute | solution.py:313
  538.2 31.3 %collective-permute-start.35 = (f32[6,1024]{1,0:T(8,128)S(1)}, f32[6,1024]{1,0:T(8,128)S(1)}, u32[]{:S(2)}, u32[]{:S(2)}) collective-permute-start(f32[6,1024]{1,0:T(8,128)S(1)} %stack.77), channel_id=1, source_target_pairs={{0,4},{4,0},{8,12},{12,8},{16,20},{20,16},{24,28},{28,24},{1,5},{5... | collective-permute-start | bytes 73736 | tf_op jit(solution)/shard_map/ppermute | solution.py:313
  569.6 17.3 %collective-permute-start.38 = (f32[6,1024]{1,0:T(8,128)S(1)}, f32[6,1024]{1,0:T(8,128)S(1)}, u32[]{:S(2)}, u32[]{:S(2)}) collective-permute-start(f32[6,1024]{1,0:T(8,128)S(1)} %add.388), channel_id=1, source_target_pairs={{0,24},{4,28},{8,16},{12,20},{16,8},{20,12},{24,0},{28,4},{1,25},{... | collective-permute-start | bytes 73736 | tf_op jit(solution)/shard_map/ppermute | solution.py:313
  569.6 17.3 %collective-permute-start.37 = (f32[6,1024]{1,0:T(8,128)S(1)}, f32[6,1024]{1,0:T(8,128)S(1)}, u32[]{:S(2)}, u32[]{:S(2)}) collective-permute-start(f32[6,1024]{1,0:T(8,128)S(1)} %add.388), channel_id=1, source_target_pairs={{0,16},{4,20},{8,24},{12,28},{16,0},{20,4},{24,8},{28,12},{1,17},{... | collective-permute-start | bytes 73736 | tf_op jit(solution)/shard_map/ppermute | solution.py:313
  586.9 98.8 %collective-permute-start.21 = (bf16[4,4,32,4096]{3,2,1,0:T(8,128)(2,1)}, bf16[4,4,32,4096]{3,2,1,0:T(8,128)(2,1)}, u32[]{:S(2)}, u32[]{:S(2)}) collective-permute-start(bf16[4,4,32,4096]{3,2,1,0:T(8,128)(2,1)} %dynamic-slice_bitcast_fusion.1), channel_id=1, source_target_pairs={{0,4},{4,0},{8,12},{12,8},{16,20},{20,16},{24,28},{28,24},{1,5},{5... | collective-permute-start | bytes 12582920 | tf_op jit(solution)/shard_map/ppermute | solution.py:313
  603.9 49.2 %collective-permute-start.1 = (bf16[4,32,3072]{2,1,0:T(8,128)(2,1)}, bf16[4,32,3072]{2,1,0:T(8,128)(2,1)}, u32[]{:S(2)}, u32[]{:S(2)}) collective-permute-start(bf16[4,32,3072]{2,1,0:T(8,128)(2,1)} %get-tuple-element.142), channel_id=1, source_target_pairs={{0,8},{4,12},{8,0},{12,4},{16,24},{20,28},{24,16},{28,20},{1,9},{5... | collective-permute-start | bytes 2359304 | tf_op jit(solution)/shard_map/ppermute | solution.py:313
  605.0 48.4 %collective-permute-start.3 = (bf16[4,32,3072]{2,1,0:T(8,128)(2,1)}, bf16[4,32,3072]{2,1,0:T(8,128)(2,1)}, u32[]{:S(2)}, u32[]{:S(2)}) collective-permute-start(bf16[4,32,3072]{2,1,0:T(8,128)(2,1)} %get-tuple-element.143), channel_id=1, source_target_pairs={{0,24},{4,28},{8,16},{12,20},{16,8},{20,12},{24,0},{28,4},{1,25},{... | collective-permute-start | bytes 2359304 | tf_op jit(solution)/shard_map/ppermute | solution.py:313
  607.3 47.8 %collective-permute-start.2 = (bf16[4,32,3072]{2,1,0:T(8,128)(2,1)}, bf16[4,32,3072]{2,1,0:T(8,128)(2,1)}, u32[]{:S(2)}, u32[]{:S(2)}) collective-permute-start(bf16[4,32,3072]{2,1,0:T(8,128)(2,1)} %get-tuple-element.144), channel_id=1, source_target_pairs={{0,16},{4,20},{8,24},{12,28},{16,0},{20,4},{24,8},{28,12},{1,17},{... | collective-permute-start | bytes 2359304 | tf_op jit(solution)/shard_map/ppermute | solution.py:313
  616.2 35.5 %collective-permute-start.9 = (bf16[4,32,1024]{2,1,0:T(8,128)(2,1)}, bf16[4,32,1024]{2,1,0:T(8,128)(2,1)S(1)}, u32[]{:S(2)}, u32[]{:S(2)}) collective-permute-start(bf16[4,32,1024]{2,1,0:T(8,128)(2,1)} %get-tuple-element.156), channel_id=1, source_target_pairs={{0,16},{4,20},{8,24},{12,28},{16,0},{20,4},{24,8},{28,12},{1,17},{... | collective-permute-start | bytes 786440 | tf_op jit(solution)/shard_map/ppermute | solution.py:313
  651.8 44.3 %collective-permute-start.14 = (bf16[4,4,32,4096]{3,2,1,0:T(8,128)(2,1)}, bf16[4,4,32,4096]{3,2,1,0:T(8,128)(2,1)}, u32[]{:S(2)}, u32[]{:S(2)}) collective-permute-start(bf16[4,4,32,4096]{3,2,1,0:T(8,128)(2,1)} %dynamic-slice_bitcast_fusion.2), channel_id=1, source_target_pairs={{0,4},{4,0},{8,12},{12,8},{16,20},{20,16},{24,28},{28,24},{1,5},{5... | collective-permute-start | bytes 12582920 | tf_op jit(solution)/shard_map/ppermute | solution.py:313
  660.8 41.3 %collective-permute-start.28 = (bf16[4,4,128,1024]{3,2,1,0:T(8,128)(2,1)}, bf16[4,4,128,1024]{3,2,1,0:T(8,128)(2,1)}, u32[]{:S(2)}, u32[]{:S(2)}) collective-permute-start(bf16[4,4,128,1024]{3,2,1,0:T(8,128)(2,1)} %dynamic-slice_bitcast_fusion), channel_id=1, source_target_pairs={{0,4},{4,0},{8,12},{12,8},{16,20},{20,16},{24,28},{28,24},{1,5},{5... | collective-permute-start | bytes 12582920 | tf_op jit(solution)/shard_map/ppermute | solution.py:313
  692.6 26.3 %collective-permute-start.22 = (bf16[4,32,4096]{2,1,0:T(8,128)(2,1)}, bf16[4,32,4096]{2,1,0:T(8,128)(2,1)S(1)}, u32[]{:S(2)}, u32[]{:S(2)}) collective-permute-start(bf16[4,32,4096]{2,1,0:T(8,128)(2,1)} %get-tuple-element.136), channel_id=1, source_target_pairs={{0,8},{4,12},{8,0},{12,4},{16,24},{20,28},{24,16},{28,20},{1,9},{5... | collective-permute-start | bytes 3145736 | tf_op jit(solution)/shard_map/ppermute | solution.py:313
  693.2 47.6 %collective-permute-start.24 = (bf16[4,32,4096]{2,1,0:T(8,128)(2,1)}, bf16[4,32,4096]{2,1,0:T(8,128)(2,1)S(1)}, u32[]{:S(2)}, u32[]{:S(2)}) collective-permute-start(bf16[4,32,4096]{2,1,0:T(8,128)(2,1)} %get-tuple-element.137), channel_id=1, source_target_pairs={{0,24},{4,28},{8,16},{12,20},{16,8},{20,12},{24,0},{28,4},{1,25},{... | collective-permute-start | bytes 3145736 | tf_op jit(solution)/shard_map/ppermute | solution.py:313
  694.1 48.8 %collective-permute-start.23 = (bf16[4,32,4096]{2,1,0:T(8,128)(2,1)}, bf16[4,32,4096]{2,1,0:T(8,128)(2,1)}, u32[]{:S(2)}, u32[]{:S(2)}) collective-permute-start(bf16[4,32,4096]{2,1,0:T(8,128)(2,1)} %get-tuple-element.138), channel_id=1, source_target_pairs={{0,16},{4,20},{8,24},{12,28},{16,0},{20,4},{24,8},{28,12},{1,17},{... | collective-permute-start | bytes 3145736 | tf_op jit(solution)/shard_map/ppermute | solution.py:313
  701.4 62.4 %collective-permute-start.15 = (bf16[4,32,4096]{2,1,0:T(8,128)(2,1)}, bf16[4,32,4096]{2,1,0:T(8,128)(2,1)S(1)}, u32[]{:S(2)}, u32[]{:S(2)}) collective-permute-start(bf16[4,32,4096]{2,1,0:T(8,128)(2,1)} %get-tuple-element.139), channel_id=1, source_target_pairs={{0,8},{4,12},{8,0},{12,4},{16,24},{20,28},{24,16},{28,20},{1,9},{5... | collective-permute-start | bytes 3145736 | tf_op jit(solution)/shard_map/ppermute | solution.py:313
  702.1 83.7 %collective-permute-start.17 = (bf16[4,32,4096]{2,1,0:T(8,128)(2,1)}, bf16[4,32,4096]{2,1,0:T(8,128)(2,1)S(1)}, u32[]{:S(2)}, u32[]{:S(2)}) collective-permute-start(bf16[4,32,4096]{2,1,0:T(8,128)(2,1)} %get-tuple-element.140), channel_id=1, source_target_pairs={{0,24},{4,28},{8,16},{12,20},{16,8},{20,12},{24,0},{28,4},{1,25},{... | collective-permute-start | bytes 3145736 | tf_op jit(solution)/shard_map/ppermute | solution.py:313
  718.8 68.9 %collective-permute-start.16 = (bf16[4,32,4096]{2,1,0:T(8,128)(2,1)S(1)}, bf16[4,32,4096]{2,1,0:T(8,128)(2,1)S(1)}, u32[]{:S(2)}, u32[]{:S(2)}) collective-permute-start(bf16[4,32,4096]{2,1,0:T(8,128)(2,1)S(1)} %get-tuple-element.141), channel_id=1, source_target_pairs={{0,16},{4,20},{8,24},{12,28},{16,0},{20,4},{24,8},{28,12},{1,17},{... | collective-permute-start | bytes 3145736 | tf_op jit(solution)/shard_map/ppermute | solution.py:313
  740.8 68.0 %collective-permute-start.29 = (bf16[4,128,1024]{2,1,0:T(8,128)(2,1)S(1)}, bf16[4,128,1024]{2,1,0:T(8,128)(2,1)S(1)}, u32[]{:S(2)}, u32[]{:S(2)}) collective-permute-start(bf16[4,128,1024]{2,1,0:T(8,128)(2,1)S(1)} %get-tuple-element.133), channel_id=1, source_target_pairs={{0,8},{4,12},{8,0},{12,4},{16,24},{20,28},{24,16},{28,20},{1,9},{5... | collective-permute-start | bytes 3145736 | tf_op jit(solution)/shard_map/ppermute | solution.py:313
  742.9 86.7 %collective-permute-start.31 = (bf16[4,128,1024]{2,1,0:T(8,128)(2,1)S(1)}, bf16[4,128,1024]{2,1,0:T(8,128)(2,1)S(1)}, u32[]{:S(2)}, u32[]{:S(2)}) collective-permute-start(bf16[4,128,1024]{2,1,0:T(8,128)(2,1)S(1)} %get-tuple-element.134), channel_id=1, source_target_pairs={{0,24},{4,28},{8,16},{12,20},{16,8},{20,12},{24,0},{28,4},{1,25},{... | collective-permute-start | bytes 3145736 | tf_op jit(solution)/shard_map/ppermute | solution.py:313
  763.8 67.3 %collective-permute-start.30 = (bf16[4,128,1024]{2,1,0:T(8,128)(2,1)S(1)}, bf16[4,128,1024]{2,1,0:T(8,128)(2,1)S(1)}, u32[]{:S(2)}, u32[]{:S(2)}) collective-permute-start(bf16[4,128,1024]{2,1,0:T(8,128)(2,1)S(1)} %get-tuple-element.135), channel_id=1, source_target_pairs={{0,16},{4,20},{8,24},{12,28},{16,0},{20,4},{24,8},{28,12},{1,17},{... | collective-permute-start | bytes 3145736 | tf_op jit(solution)/shard_map/ppermute | solution.py:313
  785.8 78.8 %collective-permute-start.25 = (bf16[32,4096]{1,0:T(8,128)(2,1)}, bf16[32,4096]{1,0:T(8,128)(2,1)}, u32[]{:S(2)}, u32[]{:S(2)}) collective-permute-start(bf16[32,4096]{1,0:T(8,128)(2,1)} %get-tuple-element.148), channel_id=1, source_target_pairs={{0,1},{1,0},{2,3},{3,2},{4,5},{5,4},{6,7},{7,6},{8,9},{9,8},{10,11... | collective-permute-start | bytes 786440 | tf_op jit(solution)/shard_map/ppermute | solution.py:313
  787.7 77.0 %collective-permute-start.27 = (bf16[32,4096]{1,0:T(8,128)(2,1)}, bf16[32,4096]{1,0:T(8,128)(2,1)}, u32[]{:S(2)}, u32[]{:S(2)}) collective-permute-start(bf16[32,4096]{1,0:T(8,128)(2,1)} %get-tuple-element.149), channel_id=1, source_target_pairs={{0,3},{1,2},{2,1},{3,0},{4,7},{5,6},{6,5},{7,4},{8,11},{9,10},{10,... | collective-permute-start | bytes 786440 | tf_op jit(solution)/shard_map/ppermute | solution.py:313
  808.8 24.2 %collective-permute-start.18 = (bf16[32,4096]{1,0:T(8,128)(2,1)S(1)}, bf16[32,4096]{1,0:T(8,128)(2,1)S(1)}, u32[]{:S(2)}, u32[]{:S(2)}) collective-permute-start(bf16[32,4096]{1,0:T(8,128)(2,1)S(1)} %get-tuple-element.151), channel_id=1, source_target_pairs={{0,1},{1,0},{2,3},{3,2},{4,5},{5,4},{6,7},{7,6},{8,9},{9,8},{10,11... | collective-permute-start | bytes 786440 | tf_op jit(solution)/shard_map/ppermute | solution.py:313
  831.1 27.4 %collective-permute-start.19 = (bf16[32,4096]{1,0:T(8,128)(2,1)S(1)}, bf16[32,4096]{1,0:T(8,128)(2,1)S(1)}, u32[]{:S(2)}, u32[]{:S(2)}) collective-permute-start(bf16[32,4096]{1,0:T(8,128)(2,1)S(1)} %get-tuple-element.153), channel_id=1, source_target_pairs={{0,2},{1,3},{2,0},{3,1},{4,6},{5,7},{6,4},{7,5},{8,10},{9,11},{10,... | collective-permute-start | bytes 786440 | tf_op jit(solution)/shard_map/ppermute | solution.py:313
  833.0 42.4 %collective-permute-start.26 = (bf16[32,4096]{1,0:T(8,128)(2,1)}, bf16[32,4096]{1,0:T(8,128)(2,1)}, u32[]{:S(2)}, u32[]{:S(2)}) collective-permute-start(bf16[32,4096]{1,0:T(8,128)(2,1)} %get-tuple-element.150), channel_id=1, source_target_pairs={{0,2},{1,3},{2,0},{3,1},{4,6},{5,7},{6,4},{7,5},{8,10},{9,11},{10,... | collective-permute-start | bytes 786440 | tf_op jit(solution)/shard_map/ppermute | solution.py:313
  840.7 40.5 %collective-permute-start.32 = (bf16[128,1024]{1,0:T(8,128)(2,1)}, bf16[128,1024]{1,0:T(8,128)(2,1)}, u32[]{:S(2)}, u32[]{:S(2)}) collective-permute-start(bf16[128,1024]{1,0:T(8,128)(2,1)} %get-tuple-element.145), channel_id=1, source_target_pairs={{0,1},{1,0},{2,3},{3,2},{4,5},{5,4},{6,7},{7,6},{8,9},{9,8},{10,11... | collective-permute-start | bytes 786440 | tf_op jit(solution)/shard_map/ppermute | solution.py:313
  858.5 22.7 %collective-permute-start.34 = (bf16[128,1024]{1,0:T(8,128)(2,1)}, bf16[128,1024]{1,0:T(8,128)(2,1)}, u32[]{:S(2)}, u32[]{:S(2)}) collective-permute-start(bf16[128,1024]{1,0:T(8,128)(2,1)} %get-tuple-element.146), channel_id=1, source_target_pairs={{0,3},{1,2},{2,1},{3,0},{4,7},{5,6},{6,5},{7,4},{8,11},{9,10},{10,... | collective-permute-start | bytes 786440 | tf_op jit(solution)/shard_map/ppermute | solution.py:313
  864.7 20.3 %collective-permute-start.33 = (bf16[128,1024]{1,0:T(8,128)(2,1)}, bf16[128,1024]{1,0:T(8,128)(2,1)S(1)}, u32[]{:S(2)}, u32[]{:S(2)}) collective-permute-start(bf16[128,1024]{1,0:T(8,128)(2,1)} %get-tuple-element.147), channel_id=1, source_target_pairs={{0,2},{1,3},{2,0},{3,1},{4,6},{5,7},{6,4},{7,5},{8,10},{9,11},{10,... | collective-permute-start | bytes 786440 | tf_op jit(solution)/shard_map/ppermute | solution.py:313
  (82 other events, 1874.9 us)
Sparse Core Ops, SparseCore 0:
  13.1 73.4 all-gather.3
  90.0 122.9 all-gather.5
  215.9 75.5 all-gather.7

commit v2 on v1

--- a/solution.py
+++ b/solution.py
@@ -10,6 +10,7 @@
 MEM = 512
 HEADS = 16
 HEAD_DIM = 64
+WIDTH = HEADS * HEAD_DIM
 EPSILON = 1e-05
 BQ = 256
 LOG2E = 1.4426950408889634
@@ -147,8 +148,9 @@
     dqkv_ref[:, 256:384] = dv_ref[...].astype(BF16)
 
 
-def self_backward(low, first, logs, qkv, out, grad, row_count):
-    pairs = HEADS // 2
+def self_backward(low, first, logs, qkv, out, grad, row_count, part):
+    pairs = HEADS // 4
+    skip = part * pairs
     return pl.pallas_call(
         self_backward_kernel,
         grid_spec=pltpu.PrefetchScalarGridSpec(
@@ -156,18 +158,18 @@
             grid=(row_count, pairs),
             in_specs=[
                 pl.BlockSpec((1, 1, SEQ), lambda r, p, low: (r, 0, 0)),
-                pl.BlockSpec((1, 1, 8, SEQ), lambda r, p, low: (r, p, 0, 0)),
-                pl.BlockSpec((SEQ, 384), lambda r, p, low: (r, p)),
-                pl.BlockSpec((SEQ, 128), lambda r, p, low: (r, p)),
-                pl.BlockSpec((SEQ, 128), lambda r, p, low: (r, p)),
+                pl.BlockSpec((1, 1, 8, SEQ), lambda r, p, low: (r, p + skip, 0, 0)),
+                pl.BlockSpec((SEQ, 384), lambda r, p, low: (r, p + skip)),
+                pl.BlockSpec((SEQ, 128), lambda r, p, low: (r, p + skip)),
+                pl.BlockSpec((SEQ, 128), lambda r, p, low: (r, p + skip)),
             ],
             out_specs=pl.BlockSpec((SEQ, 384), lambda r, p, low: (r, p)),
             scratch_shapes=[pltpu.VMEM((SEQ, 128), F32), pltpu.VMEM((SEQ, 128), F32), pltpu.VMEM((128, BQ), F32)],
         ),
-        out_shape=jax.ShapeDtypeStruct((row_count * SEQ, 3 * HEADS * HEAD_DIM), BF16),
+        out_shape=jax.ShapeDtypeStruct((row_count * SEQ, pairs * 384), BF16),
         name="self_backward",
         compiler_params=pltpu.CompilerParams(vmem_limit_bytes=32 << 20),
-        cost_estimate=pl.CostEstimate(flops=40 << 30, bytes_accessed=row_count * (16 << 20), transcendentals=8 << 20),
+        cost_estimate=pl.CostEstimate(flops=(5 << 30) * pairs, bytes_accessed=row_count * (16 << 20), transcendentals=8 << 20),
     )(low, first, logs, qkv, out, grad)
 
 
@@ -297,6 +299,417 @@
     return low, first[:, None, :], bounds
 
 
+TB = 256
+
+
+def mm_t(a, b):
+    return lax.dot_general(a, b, (((1,), (1,)), ((), ())), preferred_element_type=F32)
+
+
+def norm_parts(values):
+    center = values - jnp.mean(values, axis=-1, keepdims=True)
+    inverse = lax.rsqrt(jnp.mean(center * center, axis=-1, keepdims=True) + EPSILON)
+    return center * inverse, inverse
+
+
+def norm_back(unit, inverse, gain, gradient):
+    scaled = gradient * gain
+    return inverse * (
+        scaled
+        - jnp.mean(scaled, axis=-1, keepdims=True)
+        - unit * jnp.mean(scaled * unit, axis=-1, keepdims=True)
+    )
+
+
+def add_norm_grads(ref, unit, gradient):
+    @pl.when(pl.program_id(0) == 0)
+    def _():
+        ref[...] = jnp.zeros_like(ref)
+
+    ref[0:1, :] += jnp.sum(gradient * unit, axis=0, keepdims=True)
+    ref[1:2, :] += jnp.sum(gradient, axis=0, keepdims=True)
+
+
+def tile(rows, columns, at=0):
+    return pl.BlockSpec((rows, columns), lambda b: (b, at))
+
+
+def whole(rows, columns, at=0):
+    return pl.BlockSpec((rows, columns), lambda b: (0, at), pipeline_mode=pl.Buffered(1))
+
+
+def shape(rows, columns, dtype):
+    return jax.ShapeDtypeStruct((rows, columns), dtype)
+
+
+def params(mib):
+    return pltpu.CompilerParams(vmem_limit_bytes=mib << 20)
+
+
+def cost(flops, moved):
+    return pl.CostEstimate(flops=int(flops), bytes_accessed=int(moved), transcendentals=0)
+
+
+def project_kernel(tokens_ref, norms_ref, weight_ref, normed_ref, out_ref):
+    unit, _ = norm_parts(tokens_ref[...].astype(F32))
+    normed = (unit * norms_ref[0:1, :] + norms_ref[1:2, :]).astype(BF16)
+    normed_ref[...] = normed
+    for part in range(3):
+        at = slice(part * 1024, (part + 1) * 1024)
+        out_ref[:, at] = mm(normed, weight_ref[:, at]).astype(BF16)
+
+
+def project(tokens, norms, early):
+    rows, d = tokens.shape
+    return pl.pallas_call(
+        project_kernel,
+        grid=(rows // TB,),
+        in_specs=[tile(TB, d), whole(8, d), whole(d, 3 * d)],
+        out_specs=[tile(TB, d), tile(TB, 3 * d)],
+        out_shape=[shape(rows, d, BF16), shape(rows, 3 * d, BF16)],
+        name="project",
+        compiler_params=params(40),
+        cost_estimate=cost(6 * rows * d * d, 16 << 20),
+    )(tokens, norms, early)
+
+
+def middle_kernel(
+    mixed_ref, tokens_ref, memory_ref, norms_ref, wo_ref, wq_ref, wkv_ref, after_ref, normed_ref, q_ref, kv_ref
+):
+    after = tokens_ref[...].astype(F32) + mm(mixed_ref[...], wo_ref[...])
+    after_ref[...] = after
+    kv_ref[...] = mm(memory_ref[...], wkv_ref[...]).astype(BF16)
+    unit, _ = norm_parts(after)
+    normed = (unit * norms_ref[2:3, :] + norms_ref[3:4, :]).astype(BF16)
+    normed_ref[...] = normed
+    q_ref[...] = mm(normed, wq_ref[...]).astype(BF16)
+
+
+def middle(mixed, tokens, memory, norms, early):
+    rows, d = tokens.shape
+    mem_rows = memory.shape[0]
+    steps = rows // TB
+    mb = mem_rows // steps
+    return pl.pallas_call(
+        middle_kernel,
+        grid=(steps,),
+        in_specs=[
+            tile(TB, d),
+            tile(TB, d),
+            tile(mb, d),
+            whole(8, d),
+            whole(d, d, OUT_SELF),
+            whole(d, d, QUERY_CROSS),
+            whole(d, 2 * d, KV_CROSS),
+        ],
+        out_specs=[tile(TB, d), tile(TB, d), tile(TB, d), tile(mb, 2 * d)],
+        out_shape=[shape(rows, d, F32), shape(rows, d, BF16), shape(rows, d, BF16), shape(mem_rows, 2 * d, BF16)],
+        name="middle",
+        compiler_params=params(40),
+        cost_estimate=cost(6 * rows * d * d, 20 << 20),
+    )(mixed, tokens, memory, norms, early, early, early)
+
+
+GELU_A = 0.7978845608028654
+GELU_B = 0.044715
+
+
+def feed_kernel(
+    live_ref,
+    weight_ref,
+    mixed_ref,
+    before_ref,
+    cot_ref,
+    norms_ref,
+    wo_ref,
+    win_ref,
+    wout_ref,
+    out_ref,
+    normed_ref,
+    act_ref,
+    hid_ref,
+    b3_ref,
+    total_ref,
+    b2_ref,
+    grad_ref,
+    ngrad_ref,
+):
+    block = pl.program_id(0)
+    per_row = SEQ // TB
+    row = block // per_row
+    places = lax.broadcasted_iota(jnp.int32, (TB, 1), 0) + (block % per_row) * TB
+    live = (places < live_ref[row]).astype(F32)
+    out_grad = cot_ref[...].astype(F32) * live * weight_ref[0]
+    branch = out_grad.astype(BF16)
+    b3_ref[...] = branch
+    after = before_ref[...] + mm(mixed_ref[...], wo_ref[...])
+    unit, inverse = norm_parts(after)
+    normed = (unit * norms_ref[4:5, :] + norms_ref[5:6, :]).astype(BF16)
+    normed_ref[...] = normed
+    d = normed.shape[1]
+    result, back = after, None
+    for part in range(win_ref.shape[1] // d):
+        at = slice(part * d, (part + 1) * d)
+        x = mm(normed, win_ref[:, at])
+        square = x * x
+        t = jnp.tanh(GELU_A * x * (1.0 + GELU_B * square))
+        half = 0.5 * (1.0 + t)
+        act = (x * half).astype(BF16)
+        slope = half + (0.5 * GELU_A) * x * (1.0 - t * t) * (1.0 + (3.0 * GELU_B) * square)
+        act_ref[:, at] = act
+        hid = (mm_t(branch, wout_ref[:, at]) * slope).astype(BF16)
+        hid_ref[:, at] = hid
+        result = result + mm(act, wout_ref[:, at])
+        term = mm_t(hid, win_ref[:, at])
+        back = term if back is None else back + term
+    out_ref[...] = result.astype(BF16)
+    total = out_grad + norm_back(unit, inverse, norms_ref[4:5, :], back)
+    total_ref[...] = total
+    b2 = total.astype(BF16)
+    b2_ref[...] = b2
+    grad_ref[...] = mm_t(b2, wo_ref[...]).astype(BF16)
+    add_norm_grads(ngrad_ref, unit, back)
+
+
+def feed(live_length, row_weight, mixed, before, cotangent, norms, early, late):
+    rows, d = cotangent.shape
+    ff = late.shape[1] // 2
+    smem = pl.BlockSpec(memory_space=pltpu.SMEM)
+    return pl.pallas_call(
+        feed_kernel,
+        grid=(rows // TB,),
+        in_specs=[
+            smem,
+            smem,
+            tile(TB, d),
+            tile(TB, d),
+            tile(TB, d),
+            whole(8, d),
+            whole(d, d, OUT_CROSS),
+            whole(d, ff, 0),
+            whole(d, ff, 1),
+        ],
+        out_specs=[
+            tile(TB, d),
+            tile(TB, d),
+            tile(TB, ff),
+            tile(TB, ff),
+            tile(TB, d),
+            tile(TB, d),
+            tile(TB, d),
+            tile(TB, d),
+            whole(8, d),
+        ],
+        out_shape=[
+            shape(rows, d, BF16),
+            shape(rows, d, BF16),
+            shape(rows, ff, BF16),
+            shape(rows, ff, BF16),
+            shape(rows, d, BF16),
+            shape(rows, d, F32),
+            shape(rows, d, BF16),
+            shape(rows, d, BF16),
+            shape(8, d, F32),
+        ],
+        name="feed",
+        compiler_params=params(58),
+        cost_estimate=cost(38 * rows * d * d, 50 << 20),
+    )(live_length, row_weight, mixed, before, cotangent, norms, early, late, late)
+
+
+def cross_close_kernel(
+    dq_ref, dkv_ref, before_ref, total_ref, norms_ref, wq_ref, wkv_ref, wo_ref, out_ref, b1_ref, grad_ref, mem_ref, ngrad_ref
+):
+    gradient = mm_t(dq_ref[...], wq_ref[...])
+    mem_ref[...] = mm_t(dkv_ref[...], wkv_ref[...]).astype(BF16)
+    unit, inverse = norm_parts(before_ref[...])
+    total = total_ref[...] + norm_back(unit, inverse, norms_ref[2:3, :], gradient)
+    out_ref[...] = total
+    b1 = total.astype(BF16)
+    b1_ref[...] = b1
+    grad_ref[...] = mm_t(b1, wo_ref[...]).astype(BF16)
+    add_norm_grads(ngrad_ref, unit, gradient)
+
+
+def cross_close(dq, dkv, before, total, norms, early):
+    rows, d = dq.shape
+    mem_rows = dkv.shape[0]
+    steps = rows // TB
+    mb = mem_rows // steps
+    return pl.pallas_call(
+        cross_close_kernel,
+        grid=(steps,),
+        in_specs=[
+            tile(TB, d),
+            tile(mb, 2 * d),
+            tile(TB, d),
+            tile(TB, d),
+            whole(8, d),
+            whole(d, d, QUERY_CROSS),
+            whole(d, 2 * d, KV_CROSS),
+            whole(d, d, OUT_SELF),
+        ],
+        out_specs=[tile(TB, d), tile(TB, d), tile(TB, d), tile(mb, d), whole(8, d)],
+        out_shape=[
+            shape(rows, d, F32),
+            shape(rows, d, BF16),
+            shape(rows, d, BF16),
+            shape(mem_rows, d, BF16),
+            shape(8, d, F32),
+        ],
+        name="cross_close",
+        compiler_params=params(40),
+        cost_estimate=cost(6 * rows * d * d, 24 << 20),
+    )(dq, dkv, before, total, norms, early, early, early)
+
+
+def self_close_kernel(dqkv_ref, before_ref, total_ref, norms_ref, w_ref, out_ref, ngrad_ref):
+    gradient = mm_t(dqkv_ref[...], w_ref[...])
+    unit, inverse = norm_parts(before_ref[...].astype(F32))
+    total = total_ref[...] + norm_back(unit, inverse, norms_ref[0:1, :], gradient)
+    out_ref[...] = total.astype(BF16)
+    add_norm_grads(ngrad_ref, unit, gradient)
+
+
+def self_close(dqkv, before, total, norms, early):
+    rows, d = total.shape
+    return pl.pallas_call(
+        self_close_kernel,
+        grid=(rows // TB,),
+        in_specs=[tile(TB, 3 * d), tile(TB, d), tile(TB, d), whole(8, d), whole(d, 3 * d)],
+        out_specs=[tile(TB, d), whole(8, d)],
+        out_shape=[shape(rows, d, BF16), shape(8, d, F32)],
+        name="self_close",
+        compiler_params=params(40),
+        cost_estimate=cost(6 * rows * d * d, 20 << 20),
+    )(dqkv, before, total, norms, early)
+
+
+OUT_SELF, KV_CROSS, QUERY_CROSS, OUT_CROSS, EXTRA = 3, 2, 6, 7, 64
+
+
+def greet_all(narrow):
+    w, z = lax.axis_index("wide"), lax.axis_index("narrow")
+    barrier = pltpu.get_barrier_semaphore()
+    others = [(w ^ 1, z), (w ^ 2, z), (w ^ 4, z)] + [(w, z ^ mask) for mask in range(1, narrow)]
+    for other in others:
+        pl.semaphore_signal(barrier, inc=1, device_id=other, device_id_type=pl.DeviceIdType.MESH)
+    pl.semaphore_wait(barrier, len(others))
+
+
+def early_gather_kernel(wide, narrow, shard_ref, out_ref, send_sems, recv_sems, own_sem):
+    rows = shard_ref.shape[0]
+    half = rows // 2
+    w, z = lax.axis_index("wide"), lax.axis_index("narrow")
+    core, x, y = w ^ 1, w ^ 2, w ^ 4
+    up, down, to_x, to_y, on_y, on_x, to_core = [k * narrow for k in range(7)]
+
+    def start_of(holder, s):
+        return pl.multiple_of((holder * narrow + s) * rows, rows)
+
+    def move(holder, s, number, target, first=0, count=rows, own=False):
+        at = pl.multiple_of(start_of(holder, s) + first, half)
+        place = out_ref.at[pl.ds(at, count)]
+        return pltpu.make_async_remote_copy(
+            src_ref=shard_ref.at[pl.ds(first, count)] if own else place,
+            dst_ref=place,
+            send_sem=send_sems.at[number],
+            recv_sem=recv_sems.at[number],
+            device_id=target,
+            device_id_type=pl.DeviceIdType.MESH,
+        )
+
+    above, below = (w, z + 1), (w, z - 1)
+    greet_all(narrow)
+
+    keep = pltpu.make_async_copy(shard_ref, out_ref.at[pl.ds(start_of(w, z), rows)], own_sem)
+    keep.start()
+
+    def spread(s, own=False):
+        move(w, s, to_x + s, (x, z), own=own).start()
+        move(w, s, to_y + s, (y, z), own=own).start()
+        move(w, s, to_core + s, (core, z), own=own).start()
+
+    def relay(s):
+        move(x, s, to_x + s, (x, z)).wait_recv()
+        move(x, s, on_y + s, (y, z), 0, half).start()
+        move(x, s, to_core + narrow + s, (core, z)).start()
+        move(y, s, to_y + s, (y, z)).wait_recv()
+        move(y, s, on_x + s, (x, z), half, half).start()
+        move(y, s, to_core + 2 * narrow + s, (core, z)).start()
+
+    def at_distance(r, action):
+        if r == 0:
+            action(z)
+        else:
+            pl.when(z - r >= 0)(lambda: action(z - r))
+            pl.when(z + r < narrow)(lambda: action(z + r))
+
+    pl.when(z < narrow - 1)(lambda: move(w, z, up + z, above, own=True).start())
+    pl.when(z > 0)(lambda: move(w, z, down + z, below, own=True).start())
+    spread(z, own=True)
+    for r in range(1, narrow):
+
+        def from_below(r=r):
+            s = z - r
+            move(w, s, up + s, above).wait_recv()
+            pl.when(z < narrow - 1)(lambda: move(w, s, up + s, above).start())
+            spread(s)
+
+        def from_above(r=r):
+            s = z + r
+            move(w, s, down + s, below).wait_recv()
+            pl.when(z > 0)(lambda: move(w, s, down + s, below).start())
+            spread(s)
+
+        pl.when(z - r >= 0)(from_below)
+        pl.when(z + r < narrow)(from_above)
+        at_distance(r - 1, relay)
+    at_distance(narrow - 1, relay)
+
+    def corner(s):
+        move(x ^ 4, s, on_y + s, (y, z), 0, half).wait_recv()
+        move(x ^ 4, s, on_x + s, (x, z), half, half).wait_recv()
+        move(x ^ 4, s, to_core + 3 * narrow + s, (core, z)).start()
+
+    for r in range(narrow):
+        at_distance(r, corner)
+    for s in range(narrow):
+        for k, holder in enumerate((w, x, y, x ^ 4)):
+            move(holder ^ 1, s, to_core + k * narrow + s, (core, z)).wait_recv()
+    for s in range(narrow):
+        pl.when((s <= z) & (z < narrow - 1))(lambda s=s: move(w, s, up + s, above).wait_send())
+        pl.when((s >= z) & (z > 0))(lambda s=s: move(w, s, down + s, below).wait_send())
+        move(w, s, to_x + s, (x, z)).wait_send()
+        move(w, s, to_y + s, (y, z)).wait_send()
+        move(x, s, on_y + s, (y, z), 0, half).wait_send()
+        move(y, s, on_x + s, (x, z), half, half).wait_send()
+        for k, holder in enumerate((w, x, y, x ^ 4)):
+            move(holder, s, to_core + k * narrow + s, (core, z)).wait_send()
+    keep.wait()
+
+
+def early_gather(shard, mesh_axes):
+    (_, wide), (_, narrow) = mesh_axes
+    rows, columns = shard.shape
+    if wide != 8 or rows % 32:
+        return lax.all_gather(shard, tuple(axis for axis, _ in mesh_axes), axis=0, tiled=True)
+    return pl.pallas_call(
+        functools.partial(early_gather_kernel, wide, narrow),
+        in_specs=[pl.BlockSpec(memory_space=pl.ANY)],
+        out_specs=pl.BlockSpec(memory_space=pl.ANY),
+        out_shape=jax.ShapeDtypeStruct((rows * wide * narrow, columns), BF16),
+        scratch_shapes=[
+            pltpu.SemaphoreType.DMA((10 * narrow,)),
+            pltpu.SemaphoreType.DMA((10 * narrow,)),
+            pltpu.SemaphoreType.DMA,
+        ],
+        name="early_gather",
+        compiler_params=pltpu.CompilerParams(collective_id=0, has_side_effects=True),
+        cost_estimate=pl.CostEstimate(flops=0, bytes_accessed=200 << 20, transcendentals=0),
+    )(shard)
+
+
 def stages_of(mesh_axes):
     plan = []
     for axis, size in mesh_axes:
@@ -317,30 +730,88 @@
     return (lax.axis_index(axis) >> at) & ((1 << take) - 1)
 
 
-def sum_to_owner(partial, mesh_axes):
-    rows, columns = partial.shape
+def pick(value, digit, place):
+    if isinstance(value, list):
+        return jnp.concatenate([pick(v, digit, place) for v in value], axis=0)
+    return lax.dynamic_index_in_dim(value, digit, place, keepdims=False)
+
+
+def add_up(own, pieces):
+    total = own.astype(F32)
+    for piece in pieces:
+        total = total + piece.astype(F32)
+    return total
+
+
+def sum_steps(partial, mesh_axes):
     sizes = dict(mesh_axes)
     plan = stages_of(mesh_axes)
     groups = []
     for axis, _ in mesh_axes:
         groups += sorted((s for s in plan if s[0] == axis), key=lambda s: -s[1])
+    devices = 1
+    for _, size in mesh_axes:
+        devices *= size
+    columns = partial[0].shape[1]
     extents = [1 << s[2] for s in groups]
-    value = partial.reshape(*extents, -1, columns)
+    value = [p.reshape(p.shape[0] // WIDTH, *extents, -1, columns) for p in partial]
     for number, stage in enumerate(plan):
         axis, at, take = stage
-        place = groups.index(stage)
+        place = 1 + groups.index(stage)
+        groups.remove(stage)
+        if axis == "wide" and take == 2:
+            if isinstance(value, list):
+                value = jnp.concatenate(value, axis=0)
+            split = value.reshape(*value.shape[:place], 2, 2, *value.shape[place + 1 :])
+            a, b = split[..., : columns // 2], split[..., columns // 2 :]
+            low, high = digit_of(axis, at, 1), digit_of(axis, at + 1, 1)
+            step = ((high, place, 2 << at), (low, place + 1, 1 << at))
+            for (digit_a, place_a, mask_a), (digit_b, place_b, mask_b) in (
+                step,
+                ((low, place, 1 << at), (high, place, 2 << at)),
+            ):
+                pieces = yield [
+                    trade(pick(a, digit_a ^ 1, place_a), axis, sizes[axis], mask_a),
+                    trade(pick(b, digit_b ^ 1, place_b), axis, sizes[axis], mask_b),
+                ]
+                a = add_up(pick(a, digit_a, place_a), pieces[:1]).astype(BF16)
+                b = add_up(pick(b, digit_b, place_b), pieces[1:]).astype(BF16)
+            value = jnp.concatenate([a, b], axis=-1)
+            continue
         digit = digit_of(axis, at, take)
-
-        def chunk(mask):
-            return lax.dynamic_index_in_dim(value, digit ^ mask, place, keepdims=False)
-
-        arrived = [trade(chunk(mask), axis, sizes[axis], mask << at) for mask in range(1, 1 << take)]
-        total = chunk(0).astype(F32)
-        for piece in arrived:
-            total = total + piece.astype(F32)
-        groups = [g for g in groups if g != stage]
-        value = total if number == len(plan) - 1 else total.astype(BF16)
-    return value.reshape(-1, columns)
+        pieces = yield [
+            trade(pick(value, digit ^ mask, place), axis, sizes[axis], mask << at) for mask in range(1, 1 << take)
+        ]
+        value = add_up(pick(value, digit, place), pieces)
+        if number < len(plan) - 1:
+            value = value.astype(BF16)
+    return value.astype(F32).reshape(-1, columns)
+
+
+class StagedSum:
+    def __init__(self, partial, mesh_axes):
+        self.steps = sum_steps(partial, mesh_axes)
+        self.under_way = next(self.steps)
+        self.value = None
+
+    def go_on(self, pieces):
+        try:
+            self.under_way = self.steps.send(pieces)
+        except StopIteration as stop:
+            self.under_way, self.value = None, stop.value
+
+    def result(self):
+        while self.under_way is not None:
+            self.go_on(self.under_way)
+        return self.value
+
+
+def fence(value, *sums):
+    held = [s for s in sums if s.under_way is not None]
+    value, arrived = lax.optimization_barrier((value, [s.under_way for s in held]))
+    for s, pieces in zip(held, arrived):
+        s.go_on(pieces)
+    return value
 
 
 def sum_everywhere(value, mesh_axes):
@@ -352,25 +823,6 @@
     return value
 
 
-def norm_parts(values):
-    center = values - jnp.mean(values, axis=-1, keepdims=True)
-    inverse = lax.rsqrt(jnp.mean(center * center, axis=-1, keepdims=True) + EPSILON)
-    return center * inverse, inverse
-
-
-def norm_back(values, gain, gradient):
-    unit, inverse = norm_parts(values)
-    gain_grad = jnp.sum(gradient * unit, axis=0)
-    shift_grad = jnp.sum(gradient, axis=0)
-    scaled = gradient * gain
-    back = inverse * (
-        scaled
-        - jnp.mean(scaled, axis=-1, keepdims=True)
-        - unit * jnp.mean(scaled * unit, axis=-1, keepdims=True)
-    )
-    return back, gain_grad, shift_grad
-
-
 def by_pairs(*parts):
     rows = parts[0].shape[0]
     return jnp.stack([p.reshape(rows, -1, 128) for p in parts], axis=2).reshape(rows, -1)
@@ -382,12 +834,325 @@
     return [split[:, :, c].reshape(rows, -1) for c in range(count)]
 
 
-def linear_back(gradient, weight):
-    return jnp.einsum("te,de->td", gradient, weight, preferred_element_type=F32)
-
-
 def outer_sum(left_side, gradient):
     return jnp.einsum("td,te->de", left_side, gradient, preferred_element_type=F32).astype(BF16)
+
+
+CHUNKS = 4
+
+
+class Scatter:
+    def __init__(self, share, buffers, out_ref, send_sems, recv_sems, narrow, base=0):
+        self.share, self.out_ref = share, out_ref
+        self.from_core, self.a1, self.b1, self.a2, self.b2, self.from_line = buffers
+        self.send_sems, self.recv_sems, self.base = send_sems, recv_sems, base
+        self.narrow = narrow
+        self.half = share.shape[-1] // 2
+        self.w, self.z = lax.axis_index("wide"), lax.axis_index("narrow")
+        self.c, self.x, self.y = self.w & 1, (self.w >> 1) & 1, (self.w >> 2) & 1
+        self.per_chunk = 4 + narrow
+
+    def move(self, i, number, src, dst, target):
+        at = self.base + i * self.per_chunk + number
+        return pltpu.make_async_remote_copy(
+            src_ref=src,
+            dst_ref=dst,
+            send_sem=self.send_sems.at[at],
+            recv_sem=self.recv_sems.at[at],
+            device_id=target,
+            device_id_type=pl.DeviceIdType.MESH,
+        )
+
+    def to_core(self, i):
+        return self.move(i, 0, self.share.at[i, :, :, 1 - self.c], self.from_core.at[i], (self.w ^ 1, self.z))
+
+    def first(self, i):
+        left, right = pl.ds(0, self.half), pl.ds(self.half, self.half)
+        return (
+            self.move(
+                i, 1, self.share.at[i, :, 1 - self.x, self.c, :, :, left], self.a1.at[i], (self.w ^ 2, self.z)
+            ),
+            self.move(
+                i, 2, self.share.at[i, 1 - self.y, :, self.c, :, :, right], self.b1.at[i], (self.w ^ 4, self.z)
+            ),
+        )
+
+    def second(self, i):
+        left, right = pl.ds(0, self.half), pl.ds(self.half, self.half)
+        return (
+            self.move(
+                i, 3, self.share.at[i, 1 - self.y, self.x, self.c, :, :, left], self.a2.at[i], (self.w ^ 4, self.z)
+            ),
+            self.move(
+                i, 4, self.share.at[i, self.y, 1 - self.x, self.c, :, :, right], self.b2.at[i], (self.w ^ 2, self.z)
+            ),
+        )
+
+    def along(self, i):
+        return [
+            self.move(
+                i,
+                4 + mask,
+                self.share.at[i, self.y, self.x, self.c, self.z ^ mask],
+                self.from_line.at[i, mask - 1],
+                (self.w, self.z ^ mask),
+            )
+            for mask in range(1, self.narrow)
+        ]
+
+    def begin(self, i):
+        self.to_core(i).start()
+
+    def add(self, place, columns, piece):
+        now = self.share[(*place, slice(None), slice(None), columns)]
+        self.share[(*place, slice(None), slice(None), columns)] = (now.astype(F32) + piece.astype(F32)).astype(BF16)
+
+    def step(self, i, stage):
+        both, left, right = slice(None), slice(0, self.half), slice(self.half, None)
+        if stage == 0:
+            self.to_core(i).wait_recv()
+            for a in range(2):
+                for b in range(2):
+                    self.add((i, a, b, self.c), both, self.from_core[i, a, b])
+            for copy in self.first(i):
+                copy.start()
+        elif stage == 1:
+            for copy in self.first(i):
+                copy.wait_recv()
+            for a in range(2):
+                self.add((i, a, self.x, self.c), left, self.a1[i, a])
+                self.add((i, self.y, a, self.c), right, self.b1[i, a])
+            for copy in self.second(i):
+                copy.start()
+        elif stage == 2:
+            for copy in self.second(i):
+                copy.wait_recv()
+            self.add((i, self.y, self.x, self.c), left, self.a2[i])
+            self.add((i, self.y, self.x, self.c), right, self.b2[i])
+            for copy in self.along(i):
+                copy.start()
+        else:
+            for copy in self.along(i):
+                copy.wait_recv()
+            total = self.share[i, self.y, self.x, self.c, self.z].astype(F32)
+            for mask in range(1, self.narrow):
+                total = total + self.from_line[i, mask - 1].astype(F32)
+            width = 2 * self.half
+            self.out_ref[:, i * width : (i + 1) * width] = total
+
+    def close(self, i):
+        for copy in (self.to_core(i), *self.first(i), *self.second(i), *self.along(i)):
+            copy.wait_send()
+
+
+def scatter_scratch(chunks, narrow, rows, width):
+    return [
+        pltpu.VMEM((chunks, 2, 2, narrow, rows, width), BF16),
+        pltpu.VMEM((chunks, 2, narrow, rows, width // 2), BF16),
+        pltpu.VMEM((chunks, 2, narrow, rows, width // 2), BF16),
+        pltpu.VMEM((chunks, narrow, rows, width // 2), BF16),
+        pltpu.VMEM((chunks, narrow, rows, width // 2), BF16),
+        pltpu.VMEM((chunks, narrow - 1, rows, width), BF16),
+    ]
+
+
+def tail_kernel(
+    narrow,
+    share_any,
+    normed_any,
+    low_any,
+    high_any,
+    weight_any,
+    tokens_any,
+    total_any,
+    norms_ref,
+    norm_two_ref,
+    norm_three_ref,
+    out_ref,
+    shard_ref,
+    norm_out_ref,
+    normed,
+    normed_t,
+    grads,
+    weight,
+    tokens,
+    total,
+    share,
+    from_core,
+    a1,
+    b1,
+    a2,
+    b2,
+    from_line,
+    nval,
+    nin,
+    send_sems,
+    recv_sems,
+    load_sems,
+):
+    d = normed.shape[1]
+    width = share.shape[-1]
+    part = low_any.shape[1]
+    loads = [
+        pltpu.make_async_copy(share_any, share.at[0], load_sems.at[0]),
+        pltpu.make_async_copy(normed_any, normed, load_sems.at[1]),
+        pltpu.make_async_copy(low_any, grads.at[:, pl.ds(0, part)], load_sems.at[2]),
+        pltpu.make_async_copy(high_any, grads.at[:, pl.ds(part, part)], load_sems.at[3]),
+        pltpu.make_async_copy(weight_any.at[:, pl.ds(0, 3 * d)], weight, load_sems.at[4]),
+        pltpu.make_async_copy(tokens_any, tokens, load_sems.at[5]),
+        pltpu.make_async_copy(total_any, total, load_sems.at[6]),
+    ]
+    for load in loads:
+        load.start()
+    greet_all(narrow)
+    scatter = Scatter(share, (from_core, a1, b1, a2, b2, from_line), shard_ref, send_sems, recv_sems, narrow)
+    w, z = scatter.w, scatter.z
+    rows = share.shape[5]
+    group = 2 * narrow * rows
+
+    loads[0].wait()
+    scatter.begin(0)
+    loads[1].wait()
+    for t in range(d // TB):
+        normed_t[:, t * TB : (t + 1) * TB] = normed[t * TB : (t + 1) * TB, :].T
+
+    def multiply(i):
+        if i < 3:
+            loads[1 + i].wait()
+        for a in range(2):
+            for b in range(2):
+                at = (2 * a + b) * group
+                product = mm(normed_t[at : at + group, :], grads[:, (i - 1) * width : i * width])
+                share[i, a, b] = product.astype(BF16).reshape(2, narrow, rows, width)
+        scatter.begin(i)
+
+    def close_tokens(t):
+        if t == 0:
+            for load in loads[4:]:
+                load.wait()
+        at = slice(t * TB, (t + 1) * TB)
+        gradient = mm_t(grads[at, :], weight[...])
+        unit, inverse = norm_parts(tokens[at, :].astype(F32))
+        out_ref[at, :] = (total[at, :] + norm_back(unit, inverse, norms_ref[0:1, :], gradient)).astype(BF16)
+        gain, shift = jnp.sum(gradient * unit, axis=0, keepdims=True), jnp.sum(gradient, axis=0, keepdims=True)
+        if t == 0:
+            nval[0, 0:1, :] = gain
+            nval[0, 1:2, :] = shift
+        else:
+            nval[0, 0:1, :] += gain
+            nval[0, 1:2, :] += shift
+
+    first_sem = CHUNKS * scatter.per_chunk
+
+    def norm_copy(stage, number, target):
+        return pltpu.make_async_remote_copy(
+            src_ref=nval.at[stage],
+            dst_ref=nin.at[number],
+            send_sem=send_sems.at[first_sem + number],
+            recv_sem=recv_sems.at[first_sem + number],
+            device_id=target,
+            device_id_type=pl.DeviceIdType.MESH,
+        )
+
+    norm_copies = [[norm_copy(0, 0, (w ^ 1, z))], [norm_copy(1, 1, (w ^ 2, z))], [norm_copy(2, 2, (w ^ 4, z))]]
+    norm_copies.append([norm_copy(3, 2 + mask, (w, z ^ mask)) for mask in range(1, narrow)])
+
+    def norm_step(stage):
+        if stage == 0:
+            nval[0, 2:4, :] = norm_two_ref[0:2, :]
+            nval[0, 4:6, :] = norm_three_ref[0:2, :]
+            nval[0, 6:8, :] = jnp.zeros_like(norm_two_ref[0:2, :])
+        else:
+            for copy in norm_copies[stage - 1]:
+                copy.wait_recv()
+            value = nval[stage - 1]
+            if stage < 4:
+                nval[stage] = value + nin[stage - 1]
+            else:
+                for mask in range(1, narrow):
+                    value = value + nin[2 + mask]
+                norm_out_ref[...] = value
+        if stage < 4:
+            for copy in norm_copies[stage]:
+                copy.start()
+
+    multiply(1)
+    scatter.step(0, 0)
+    multiply(2)
+    scatter.step(1, 0)
+    multiply(3)
+    scatter.step(2, 0)
+    scatter.step(0, 1)
+    close_tokens(0)
+    scatter.step(3, 0)
+    scatter.step(1, 1)
+    scatter.step(0, 2)
+    close_tokens(1)
+    scatter.step(2, 1)
+    scatter.step(1, 2)
+    close_tokens(2)
+    scatter.step(3, 1)
+    scatter.step(0, 3)
+    close_tokens(3)
+    norm_step(0)
+    scatter.step(2, 2)
+    norm_step(1)
+    scatter.step(1, 3)
+    norm_step(2)
+    scatter.step(3, 2)
+    norm_step(3)
+    scatter.step(2, 3)
+    norm_step(4)
+    scatter.step(3, 3)
+    for i in range(CHUNKS):
+        scatter.close(i)
+    for copies in norm_copies:
+        for copy in copies:
+            copy.wait_send()
+
+
+def tail(output_share, normed, low_grads, high_grads, tokens, total, norms, norm_two, norm_three, early, mesh_axes):
+    (_, wide), (_, narrow) = mesh_axes
+    rows, d = tokens.shape
+    shard_rows = d // (wide * narrow)
+    width = 4 * d // CHUNKS
+    anywhere, vmem = pl.BlockSpec(memory_space=pl.ANY), pl.BlockSpec(memory_space=pltpu.VMEM)
+    copies = CHUNKS * (4 + narrow) + 2 + narrow
+    return pl.pallas_call(
+        functools.partial(tail_kernel, narrow),
+        in_specs=[anywhere] * 7 + [vmem] * 3,
+        out_specs=[vmem] * 3,
+        out_shape=[shape(rows, d, BF16), shape(shard_rows, 4 * d, F32), shape(8, d, F32)],
+        scratch_shapes=[
+            pltpu.VMEM((rows, d), BF16),
+            pltpu.VMEM((d, rows), BF16),
+            pltpu.VMEM((rows, 3 * d), BF16),
+            pltpu.VMEM((d, 3 * d), BF16),
+            pltpu.VMEM((rows, d), BF16),
+            pltpu.VMEM((rows, d), F32),
+            pltpu.VMEM((CHUNKS, 2, 2, 2, narrow, shard_rows, width), BF16),
+            *scatter_scratch(CHUNKS, narrow, shard_rows, width),
+            pltpu.VMEM((4, 8, d), F32),
+            pltpu.VMEM((2 + narrow, 8, d), F32),
+            pltpu.SemaphoreType.DMA((copies,)),
+            pltpu.SemaphoreType.DMA((copies,)),
+            pltpu.SemaphoreType.DMA((7,)),
+        ],
+        name="tail",
+        compiler_params=pltpu.CompilerParams(collective_id=1, has_side_effects=True, vmem_limit_bytes=58 << 20),
+        cost_estimate=cost(12 * rows * d * d, 100 << 20),
+    )(
+        output_share.reshape(2, 2, 2, narrow, shard_rows, d),
+        normed,
+        low_grads,
+        high_grads,
+        early,
+        tokens,
+        total,
+        norms,
+        norm_two,
+        norm_three,
+    )
 
 
 def on_device(
@@ -420,96 +1185,101 @@
     names = tuple(axis for axis, _ in mesh_axes)
     row_count = live_length.shape[0]
     shard_rows = self_query.shape[0]
-    reduce_sum = functools.partial(sum_to_owner, mesh_axes=mesh_axes)
-
-    def gather(shard):
-        return lax.all_gather(shard, names, axis=0, tiled=True)
+    device_count = 1
+    for _, size in mesh_axes:
+        device_count *= size
+
+    def staged(*partial):
+        return StagedSum(partial, mesh_axes)
 
     digits = jnp.stack([live_length // 256, live_length % 256], axis=1).astype(BF16)
     digits = jnp.pad(digits, ((0, shard_rows - row_count), (0, 0)))
     norms = jnp.stack([first_gain, first_shift, second_gain, second_shift, third_gain, third_shift], axis=1)
     extra = jnp.pad(jnp.concatenate([norms, digits], axis=1), ((0, 0), (0, 120)))
-    early = gather(jnp.concatenate([by_pairs(self_query, self_key, self_value), extra], axis=1))
-    d = early.shape[0]
-    qkv_weight = early[:, : 3 * d]
-    extra = early[:, 3 * d : 3 * d + 8].astype(F32).T
-    gain_one, shift_one, gain_two, shift_two, gain_three, shift_three = [extra[n] for n in range(6)]
-    live_total = jnp.sum(extra[6]) * 256.0 + jnp.sum(extra[7])
-    later = gather(
-        jnp.concatenate([self_output, cross_query, by_pairs(cross_key, cross_value), cross_output, hidden_in], axis=1)
+    early = early_gather(
+        jnp.concatenate(
+            [
+                by_pairs(self_query, self_key, self_value),
+                self_output,
+                by_pairs(cross_key, cross_value),
+                cross_query,
+                cross_output,
+                extra,
+            ],
+            axis=1,
+        ),
+        mesh_axes,
     )
-    output_self = later[:, :d]
-    query_cross = later[:, d : 2 * d]
-    kv_cross = later[:, 2 * d : 4 * d]
-    output_cross = later[:, 4 * d : 5 * d]
-    expand_whole = later[:, 5 * d :]
-    reduce_whole = gather(hidden_out)
-
-    low, first, bounds = row_bounds(pair_starts, source_starts, live_length)
-    resident = tokens.astype(F32)
-    normed_one = (norm_parts(resident)[0] * gain_one + shift_one).astype(BF16)
-    qkv = mm(normed_one, qkv_weight).astype(BF16)
-    self_mixed, self_logs = self_forward(low, first, qkv, row_count)
-    after_self = resident + mm(self_mixed, output_self)
-    normed_two = (norm_parts(after_self)[0] * gain_two + shift_two).astype(BF16)
-    cross_q = mm(normed_two, query_cross).astype(BF16)
-    cross_kv = mm(memory, kv_cross).astype(BF16)
-    cross_mixed, cross_logs = cross_forward(bounds, cross_q, cross_kv, row_count)
-    after_cross = after_self + mm(cross_mixed, output_cross)
-    normed_three = (norm_parts(after_cross)[0] * gain_three + shift_three).astype(BF16)
-    hidden = mm(normed_three, expand_whole)
-    activated, gelu_back = jax.vjp(jax.nn.gelu, hidden)
-    activated = activated.astype(BF16)
-    layer_output = (after_cross + mm(activated, reduce_whole)).astype(BF16)
-
+    quarters = hidden_out.shape[0] // shard_rows
+    late = lax.all_gather(
+        jnp.concatenate(
+            [hidden_in.reshape(shard_rows, device_count, quarters, -1).transpose(0, 2, 1, 3).reshape(shard_rows, -1)]
+            + [hidden_out[n * shard_rows : (n + 1) * shard_rows] for n in range(quarters)],
+            axis=1,
+        ),
+        names,
+        axis=0,
+        tiled=True,
+    )
+
+    norms = early[:, EXTRA * 128 : EXTRA * 128 + 8].astype(F32).T
+    live_total = jnp.sum(norms[6]) * 256.0 + jnp.sum(norms[7])
     device = lax.axis_index(names)
     member = (group_bounds[:-1] <= device) & (device < group_bounds[1:])
     pair_tokens = jnp.sum(jnp.where(member, group_counts, 0))
-    device_count = 1
-    for _, size in mesh_axes:
-        device_count *= size
     token_all = row_count * SEQ * device_count
     row_weight = pair_tokens.astype(F32) * (token_all / 1000.0) / live_total
-    places = jnp.arange(SEQ, dtype=jnp.int32)
-    live_mask = (places[None, :] < live_length[:, None]).astype(F32).reshape(-1, 1)
-    out_grad = cotangent.astype(F32) * live_mask * row_weight
-
-    branch_three = out_grad.astype(BF16)
-    reduce_shard = reduce_sum(outer_sum(activated, branch_three))
-    hidden_grad = gelu_back(linear_back(branch_three, reduce_whole))[0].astype(BF16)
-    expand_shard = reduce_sum(outer_sum(normed_three, hidden_grad))
-    cross_part, gain_three_grad, shift_three_grad = norm_back(
-        after_cross, gain_three, linear_back(hidden_grad, expand_whole)
+    low, first, bounds = row_bounds(pair_starts, source_starts, live_length)
+
+    normed_one, qkv = project(tokens, norms, early)
+    self_mixed, self_logs = self_forward(low, first, qkv, row_count)
+    after_self, normed_two, cross_q, cross_kv = middle(self_mixed, tokens, memory, norms, early)
+    cross_mixed, cross_logs = cross_forward(bounds, cross_q, cross_kv, row_count)
+    layer_output, normed_three, activated, hidden_grad, branch_three, cross_total, branch_two, mixed_grad, norm_three = feed(
+        live_length, row_weight[None], cross_mixed, after_self, cotangent, norms, early, late
     )
-    cross_total = out_grad + cross_part
-
-    branch_two = cross_total.astype(BF16)
-    mixed_grad = linear_back(branch_two, output_cross).astype(BF16)
+
+    reduce_sum = staged(outer_sum(activated, branch_three))
+    mixed_grad, expand_share = lax.optimization_barrier((mixed_grad, outer_sum(normed_three, hidden_grad)))
+    mixed_grad = fence(mixed_grad, reduce_sum)
+    expand_sum = staged(expand_share)
     cq_grad, ckv_grad = cross_backward(bounds, cross_logs, cross_q, cross_kv, cross_mixed, mixed_grad, row_count)
-    cross_shard = reduce_sum(
-        jnp.concatenate(
-            [outer_sum(cross_mixed, branch_two), outer_sum(normed_two, cq_grad), outer_sum(memory, ckv_grad)], axis=1
+    cq_grad, ckv_grad = fence((cq_grad, ckv_grad), reduce_sum, expand_sum)
+    shares = [outer_sum(cross_mixed, branch_two), outer_sum(normed_two, cq_grad)]
+    shares += [outer_sum(memory, part) for part in (ckv_grad[:, :WIDTH], ckv_grad[:, WIDTH:])]
+    cq_grad, shares = lax.optimization_barrier((cq_grad, shares))
+    cross_sum = staged(*shares)
+    self_total, branch_one, mixed_grad, memory_grad, norm_two = cross_close(
+        cq_grad, ckv_grad, after_self, cross_total, norms, early
+    )
+    mixed_grad = fence(mixed_grad, reduce_sum, expand_sum, cross_sum)
+    output_share = outer_sum(self_mixed, branch_one)
+    low_grads = self_backward(low, first, self_logs, qkv, self_mixed, mixed_grad, row_count, 0)
+    low_grads, mixed_grad = fence((low_grads, mixed_grad), reduce_sum, expand_sum)
+    high_grads = self_backward(low, first, self_logs, qkv, self_mixed, mixed_grad, row_count, 1)
+    high_grads = fence(high_grads, expand_sum, cross_sum)
+    if mesh_axes[0][1] == 8 and row_count == 1:
+        high_grads = fence(high_grads, cross_sum)
+        tokens_grad, last_shard, norm_grads = tail(
+            output_share, normed_one, low_grads, high_grads, tokens, self_total, norms, norm_two, norm_three, early, mesh_axes
         )
+        output_shard, qkv_shard = last_shard[:, :WIDTH], last_shard[:, WIDTH:]
+    else:
+        qkv_grad = jnp.concatenate([low_grads, high_grads], axis=1)
+        last_sum = staged(output_share, *[outer_sum(normed_one, qkv_grad[:, n * WIDTH : (n + 1) * WIDTH]) for n in range(3)])
+        tokens_grad, norm_one = self_close(qkv_grad, tokens, self_total, norms, early)
+        norm_grads = sum_everywhere(jnp.concatenate([norm_one[:2], norm_two[:2], norm_three[:2]]), mesh_axes)
+        output_shard, *qkv_shards = last_sum.result().reshape(4, shard_rows, WIDTH)
+        qkv_shard = jnp.concatenate(qkv_shards, axis=1)
+    norm_shards = lax.dynamic_slice_in_dim(norm_grads, device * shard_rows, shard_rows, axis=1)
+    reduce_shard = reduce_sum.result()
+    expand_shard = expand_sum.result()
+    expand_shard = (
+        expand_shard.reshape(shard_rows, quarters, device_count, -1).transpose(0, 2, 1, 3).reshape(shard_rows, -1)
     )
-    memory_grad = linear_back(ckv_grad, kv_cross).astype(BF16)
-    self_part, gain_two_grad, shift_two_grad = norm_back(after_self, gain_two, linear_back(cq_grad, query_cross))
-    self_total = cross_total + self_part
-
-    branch_one = self_total.astype(BF16)
-    self_output_shard = reduce_sum(outer_sum(self_mixed, branch_one))
-    mixed_grad = linear_back(branch_one, output_self).astype(BF16)
-    qkv_grad = self_backward(low, first, self_logs, qkv, self_mixed, mixed_grad, row_count)
-    qkv_shard = reduce_sum(outer_sum(normed_one, qkv_grad))
-    input_part, gain_one_grad, shift_one_grad = norm_back(resident, gain_one, linear_back(qkv_grad, qkv_weight))
-    tokens_grad = (self_total + input_part).astype(BF16)
-
-    norm_grads = sum_everywhere(
-        jnp.stack([gain_one_grad, shift_one_grad, gain_two_grad, shift_two_grad, gain_three_grad, shift_three_grad]),
-        mesh_axes,
-    )
-    norm_shards = lax.dynamic_slice_in_dim(norm_grads, device * shard_rows, shard_rows, axis=1)
+    cross_shards = cross_sum.result().reshape(4, shard_rows, WIDTH)
+    cross_key_shard, cross_value_shard = from_pairs(jnp.concatenate([cross_shards[2], cross_shards[3]], axis=1), 2)
     query_shard, key_shard, value_shard = from_pairs(qkv_shard, 3)
-    cross_key_shard, cross_value_shard = from_pairs(cross_shard[:, 2 * d :], 2)
     return (
         layer_output,
         tokens_grad,
@@ -517,11 +1287,11 @@
         query_shard,
         key_shard,
         value_shard,
-        self_output_shard,
-        cross_shard[:, d : 2 * d],
+        output_shard,
+        cross_shards[1],
         cross_key_shard,
         cross_value_shard,
-        cross_shard[:, :d],
+        cross_shards[0],
         expand_shard,
         reduce_shard,
         *[norm_shards[n] for n in range(6)],

time: 904 us -> 633 us (0.70)
  waiting for transfers between devices: 305 us -> 9.87 us
  Pallas kernels: 167 us -> 422 us
  matrix products: 191 us -> 41.6 us
  other arithmetic: 67.9 us -> 28 us
  starting transfers between devices: 52 us -> 31.8 us
  local copies, waits for them, and re-layouts: 92.8 us -> 74.8 us
    pallas_call x0 -> x6, Pallas kernels: none -> 277 us  [the longest x1 119 us: early_gather(): pl.pallas_call(functools.partial(early_gather_kernel, wide, narrow), in_s...]
    ppermute x42 -> x24, waiting for transfers between devices: 185 us -> 9.86 us  [trade(): return lax.ppermute(value, axis, [(i, i ^ mask) for i in range(size)])]
    dot_general x14 -> x0, matrix products: 134 us -> none  [the longest x7 70.9 us: linear_back(): return jnp.einsum('te,de->td', gradient, weight, preferred_element_type=F32)]
    all_gather x3 -> x1, waiting for transfers between devices: 120 us -> 0.01 us  [on_device(): lax.all_gather(jnp.concatenate([hidden_in.reshape(shard_rows, device_coun...]
    ppermute x42 -> x24, starting transfers between devices: 51.9 us -> 31.8 us  [trade(): return lax.ppermute(value, axis, [(i, i ^ mask) for i in range(size)])]
    reduce_sum x9 -> x1, other arithmetic: 18.5 us -> 0.61 us  [on_device(): live_total = jnp.sum(norms[6]) * 256.0 + jnp.sum(norms[7])]
    dot_general x3 -> x0, local copies, waits for them, and re-layouts: 16 us -> none  [linear_back(): return jnp.einsum('te,de->td', gradient, weight, preferred_element_type=F32)]
    dot_general x7, matrix products: 56.8 us -> 41.6 us  [outer_sum(): jnp.einsum('td,te->de', left_side, gradient, preferred_element_type=F32)]
  transfers between devices with their start and end apart: 45 -> 25, of which waited for: 20 -> 1; matrix products, arithmetic and copies ran while one was open for 24% -> 11% of each run, Pallas kernels for 10% -> 58%
where the time goes in v2:
time: 633 us; the launch traced here: 627 us
  Pallas kernels  422 us (67%)
  local copies, waits for them, and re-layouts  74.8 us (12%)
  matrix products  41.6 us (7%)
  starting transfers between devices  31.8 us (5%)
  other arithmetic  28 us (4%)
  between operations  18.7 us (3%)
  waiting for transfers between devices  9.87 us (2%)
    pallas_call x1, Pallas kernels, early_gather(): pl.pallas_call(functools.partial(early_gather_kernel, wide, narrow), in_s...  119 us
    pallas_call x1, Pallas kernels, tail(): pl.pallas_call(functools.partial(tail_kernel, narrow), in_specs=[anywhere...  59.5 us
    pallas_call x1, Pallas kernels, feed(): pl.pallas_call(feed_kernel, grid=(rows // TB,), in_specs=[smem, smem, til...  56.8 us
    dot_general x7, matrix products, outer_sum(): jnp.einsum('td,te->de', left_side, gradient, preferred_element_type=F32)  41.6 us
    pallas_call x2, Pallas kernels, self_backward(): pl.pallas_call(self_backward_kernel, grid_spec=pltpu.PrefetchScalarGridSp...  41 us
    pallas_call x1, Pallas kernels, self_forward(): pl.pallas_call(self_forward_kernel, grid_spec=pltpu.PrefetchScalarGridSpe...  39.8 us
    pallas_call x1, Pallas kernels, cross_forward(): pl.pallas_call(cross_forward_kernel, grid=(row_count, pairs), in_specs=[p...  33.3 us
    ppermute x24, starting transfers between devices, trade(): return lax.ppermute(value, axis, [(i, i ^ mask) for i in range(size)])  31.8 us
  transfers between devices with their start and end apart: 25, of which 1 were waited for; matrix products, arithmetic and copies ran while one was open for 11% of the time, Pallas kernels for 58%

profile of v2, /device:TPU:0, one launch (start us, length us, event | category | flops | bytes accessed | tf_op | source)
XLA Modules:
  0.0 627.1 jit_solution(3998612336127158937)
XLA Ops:
  14.6 118.7 %early_gather.1.weight_ref.wo_ref.wq_ref.wkv_ref.weight_any = bf16[1024,8320]{1,0:T(8,128)(2,1)} custom-call(bf16[32,8320]{1,0:T(8,128)(2,1)} %copy-done.51), custom_call_target="tpu_custom_call" | custom-call | bytes 209715200 | tf_op jit(solution)/shard_map/early_gather/pallas_call | solution.py:697
  138.4 11.4 %project.1 = (bf16[1024,1024]{1,0:T(8,128)(2,1)S(1)}, bf16[1024,3072]{1,0:T(8,128)(2,1)S(1)}) custom-call(bf16[1024,1024]{1,0:T(8,128)(2,1)S(1)} %copy-done, f32[8,1024]{1,0:T(8,128)S(1)} %convert_bitcast_fusion.2.norms_ref, bf16[1024,8320]{1,0:T(8,128)(2,1)} %early_gather.1.weight_ref.wo_ref.wq_ref.wkv_ref.weight_any), custom_call_target="tpu_custom_call" | custom-call | flops 6442450944 | bytes 16777216 | tf_op jit(solution)/shard_map/project/pallas_call | solution.py:364
  151.1 39.8 %self_forward.1 = (bf16[1024,1024]{1,0:T(8,128)(2,1)S(1)}, f32[1,8,8,1024]{3,2,1,0:T(8,128)S(1)}) custom-call(s32[4]{0:T(128)S(1)} %fusion.52.low_ref, s32[1,1,1024]{2,1,0:T(1,128)S(1)} %get-tuple-element.199.first_ref, bf16[1024,3072]{1,0:T(8,128)(2,1)S(1)} %get-tuple-element.84.qkv_ref), custom_call_target="tpu_custom_call" | custom-call | flops 21474836480 | bytes 8388608 | tf_op jit(solution)/shard_map/self_forward/pallas_call | solution.py:84
  191.0 12.5 %middle.1 = (f32[1024,1024]{1,0:T(8,128)}, bf16[1024,1024]{1,0:T(8,128)(2,1)S(1)}, bf16[1024,1024]{1,0:T(8,128)(2,1)S(1)}, bf16[512,2048]{1,0:T(8,128)(2,1)S(1)}) custom-call(bf16[1024,1024]{1,0:T(8,128)(2,1)S(1)} %get-tuple-element.85.mixed_ref.out_ref, bf16[1024,1024]{1,0:T(8,128)(2,1)S(1)} %copy-done, bf16[512,1024]{1,0:T(8,128)(2,1)S(1)} %copy-done.5, ...), custom_call_target="tpu_custom_call" | custom-call | flops 6442450944 | bytes 20971520 | tf_op jit(solution)/shard_map/middle/pallas_call | solution.py:393
  204.9 33.3 %cross_forward.1 = (bf16[1024,1024]{1,0:T(8,128)(2,1)S(1)}, f32[1,8,8,1024]{3,2,1,0:T(8,128)S(1)}) custom-call(s32[1,8,1024]{2,1,0:T(8,128)S(1)} %pad.14.bounds_ref, bf16[1024,1024]{1,0:T(8,128)(2,1)S(1)} %get-tuple-element.86.q_ref, bf16[512,2048]{1,0:T(8,128)(2,1)S(1)} %get-tuple-element.87.kv_ref), custom_call_target="tpu_custom_call" | custom-call | flops 21474836480 | bytes 6291456 | tf_op jit(solution)/shard_map/cross_forward/pallas_call | solution.py:201
  242.2 56.8 %feed.1 = (bf16[1024,1024]{1,0:T(8,128)(2,1)}, bf16[1024,1024]{1,0:T(8,128)(2,1)}, bf16[1024,4096]{1,0:T(8,128)(2,1)}, bf16[1024,4096]{1,0:T(8,128)(2,1)}, bf16[...) custom-call(s32[1]{0:T(128)} %copy.180.live_ref, ...), custom_call_target="tpu_custom_call" | custom-call | flops 40802189312 | bytes 52428800 | tf_op jit(solution)/shard_map/feed/pallas_call | solution.py:478
  299.0 13.4 %convolution_convert_fusion = bf16[4096,1024]{1,0:T(8,128)(2,1)S(1)} fusion(bf16[1024,4096]{1,0:T(8,128)(2,1)} %get-tuple-element.96, bf16[1024,1024]{1,0:T(8,128)(2,1)} %get-tuple-element.97), kind=kOutput, calls=%fused_computation.5 | convolution fusion | flops 8594128896 | bytes 18874368 | tf_op jit(solution)/shard_map/td,te->de/dot_general | solution.py:838
  312.4 2.8 dynamic-slice_bitcast_fusion.1
  317.2 5.9 collective-permute-start
  323.1 11.7 %convolution_convert_fusion.1 = bf16[1024,4096]{1,0:T(8,128)(2,1)S(1)} fusion(bf16[1024,1024]{1,0:T(8,128)(2,1)S(1)} %copy-done.74, bf16[1024,4096]{1,0:T(8,128)(2,1)} %get-tuple-element.94), kind=kOutput, calls=%fused_computation.6 | convolution fusion | flops 8594128896 | bytes 18874368 | tf_op jit(solution)/shard_map/td,te->de/dot_general | solution.py:838
  337.1 3.9 copy-done.27
  341.1 3.8 convolution_convert_fusion.4
  344.9 4.3 fusion.1
  355.2 31.5 %cross_backward.1 = (bf16[1024,1024]{1,0:T(8,128)(2,1)S(1)}, bf16[512,2048]{1,0:T(8,128)(2,1)S(1)}) custom-call(s32[1,8,1024]{2,1,0:T(8,128)S(1)} %pad.14.bounds_ref, f32[1,8,8,1024]{3,2,1,0:T(8,128)S(1)} %get-tuple-element.91.log_ref, bf16[1024,1024]{1,0:T(8,128)(2,1)S(1)} %copy-done.13, bf16[512,2048]{1,0:T(8,128)(2,1)S(1)} %copy-done.15, ...), custom_call_target="tpu_custom_call" | custom-call | flops 42949672960 | bytes 12582912 | tf_op jit(solution)/shard_map/cross_backward/pallas_call | solution.py:258
  386.8 2.6 convert_bitcast_fusion
  389.4 2.7 convert_bitcast_fusion.1
  392.1 3.8 convolution_convert_fusion.3
  395.9 3.9 copy.122
  399.8 3.1 dynamic-slice_bitcast_fusion.4
  403.0 3.9 copy.123
  406.9 2.9 dynamic-slice_bitcast_fusion.3
  415.3 3.7 fusion
  428.3 17.6 %cross_close.1 = (f32[1024,1024]{1,0:T(8,128)S(1)}, bf16[1024,1024]{1,0:T(8,128)(2,1)S(1)}, bf16[1024,1024]{1,0:T(8,128)(2,1)S(1)}, bf16[512,1024]{1,0:T(8,128)(2,1)}, f32[8,1024]{1,0:T(8,128)S(1)}) custom-call(bf16[1024,1024]{1,0:T(8,128)(2,1)S(1)} %get-tuple-element.107.dq_ref, bf16[512,2048]{1,0:T(8,128)(2,1)S(1)} %copy-done.4, ...), custom_call_target="tpu_custom_call" | custom-call | flops 6442450944 | bytes 25165824 | tf_op jit(solution)/shard_map/cross_close/pallas_call | solution.py:539
  446.0 3.7 convolution_convert_fusion.2
  449.7 9.8 %collective-permute-done.5 = bf16[4,4,32,512]{3,2,0,1:T(8,128)(2,1)S(1)} collective-permute-done((bf16[4,4,32,512]{3,2,0,1:T(8,128)(2,1)}, bf16[4,4,32,512]{3,2,0,1:T(8,128)(2,1)S(1)}, u32[]{:S(2)}, u32[]{:S(2)}) %collective-permute-start.5) | collective-permute-done | bytes 524320 | tf_op jit(solution)/shard_map/ppermute | solution.py:726
  468.6 20.4 %self_backward.2.low_any = bf16[1024,1536]{1,0:T(8,128)(2,1)S(1)} custom-call(s32[4]{0:T(128)S(1)} %copy-done.18, s32[1,1,1024]{2,1,0:T(1,128)S(1)} %get-tuple-element.199.first_ref, f32[1,8,8,1024]{3,2,1,0:T(8,128)S(1)} %get-tuple-element.111.log_ref, bf16[1024,3072]{1,0:T(8,128)(2,1)S(1)} %bitcast.225, bf16[1024,1024]{1,0:T(8,128)(2,1)S(1)} %copy-done.2, ...), custom_call_target="tpu_custom_call" | custom-call | flops 21474836480 | bytes 16777216 | tf_op jit(solution)/shard_map/self_backward/pallas_call | solution.py:154
  489.1 4.9 add_convert_fusion
  499.2 2.4 collective-permute-start.15
  503.5 20.6 %self_backward.3.high_any = bf16[1024,1536]{1,0:T(8,128)(2,1)S(1)} custom-call(s32[4]{0:T(128)S(1)} %copy-done.18, s32[1,1,1024]{2,1,0:T(1,128)S(1)} %get-tuple-element.199.first_ref, f32[1,8,8,1024]{3,2,1,0:T(8,128)S(1)} %get-tuple-element.111.log_ref, bf16[1024,3072]{1,0:T(8,128)(2,1)S(1)} %bitcast.225, bf16[1024,1024]{1,0:T(8,128)(2,1)S(1)} %copy-done.2, ...), custom_call_target="tpu_custom_call" | custom-call | flops 21474836480 | bytes 16777216 | tf_op jit(solution)/shard_map/self_backward/pallas_call | solution.py:154
  533.9 3.2 copy.125
  537.1 4.5 reshape.546
  548.6 59.5 %tail.1 = (bf16[1024,1024]{1,0:T(8,128)(2,1)}, f32[32,4096]{1,0:T(8,128)}, f32[8,1024]{1,0:T(8,128)}) custom-call(bf16[2,2,2,4,32,1024]{5,4,3,2,1,0:T(8,128)(2,1)} %bitcast.269, bf16[1024,1024]{1,0:T(8,128)(2,1)} %copy-done.20, bf16[1024,1536]{1,0:T(8,128)(2,1)} %copy-done.23, bf16[1024,1536]{1,0:T(8,128)(2,1)} %copy-done.24, ...), custom_call_target="tpu_custom_call" | custom-call | flops 12884901888 | bytes 104857600 | tf_op jit(solution)/shard_map/tail/pallas_call | solution.py:1121
  (314 shorter events, 85.2 us)
Async XLA Ops:
  7.2 235.0 %all-gather.2.cloned.1.call-start = ((), (), s32[]{:S(2)}) async-start(), calls=%async_computation | async-start | bytes 17301504 | tf_op jit(solution)/shard_map/all_gather | solution.py:1214
  14.6 119.9 %copy-start.72 = (s32[1,8]{1,0:T(1,128)S(1)}, s32[1,8]{1,0:T(1,128)}, u32[]{:S(2)}) copy-start(s32[1,8]{1,0:T(1,128)} %param.29) | copy-start | bytes 100
  14.6 119.9 %copy-start.64 = (s32[1,8]{1,0:T(1,128)S(1)}, s32[1,8]{1,0:T(1,128)}, u32[]{:S(2)}) copy-start(s32[1,8]{1,0:T(1,128)} %param.28) | copy-start | bytes 100
  14.6 120.4 %copy-start.63 = (s32[9]{0:T(128)S(1)}, s32[9]{0:T(128)}, u32[]{:S(2)}) copy-start(s32[9]{0:T(128)} %param.30) | copy-start | bytes 112
  14.6 120.4 %copy-start.65 = (s32[8]{0:T(128)S(1)}, s32[8]{0:T(128)}, u32[]{:S(2)}) copy-start(s32[8]{0:T(128)} %param.31) | copy-start | bytes 100
  14.6 123.8 %copy-start = (bf16[1024,1024]{1,0:T(8,128)(2,1)S(1)}, bf16[1024,1024]{1,0:T(8,128)(2,1)}, u32[]{:S(2)}) copy-start(bf16[1024,1024]{1,0:T(8,128)(2,1)} %tokens_any.1) | copy-start | bytes 6291460
  136.4 54.6 %copy-start.7 = (f32[8,1024]{1,0:T(8,128)}, f32[8,1024]{1,0:T(8,128)S(1)}, u32[]{:S(2)}) copy-start(f32[8,1024]{1,0:T(8,128)S(1)} %convert_bitcast_fusion.2.norms_ref) | copy-start | bytes 98308
  317.2 27.7 %collective-permute-start = (bf16[4,4,4,32,1024]{4,3,2,1,0:T(8,128)(2,1)}, bf16[4,4,4,32,1024]{4,3,2,1,0:T(8,128)(2,1)}, u32[]{:S(2)}, u32[]{:S(2)}) collective-permute-start(bf16[4,4,4,32,1024]{4,3,2,1,0:T(8,128)(2,1)} %dynamic-slice_bitcast_fusion.1), channel_id=1, source_target_pairs={{0,4},{4,0},{8,12},{12,8},{16,20},{20,16},{24,28},{28,24},{1,5},{5... | collective-permute-start | bytes 12582920 | tf_op jit(solution)/shard_map/ppermute | solution.py:726
  341.0 45.7 %collective-permute-start.3 = (bf16[1,4,4,32,4096]{4,3,2,1,0:T(8,128)(2,1)}, bf16[1,4,4,32,4096]{4,3,2,1,0:T(8,128)(2,1)}, u32[]{:S(2)}, u32[]{:S(2)}) collective-permute-start(bf16[1,4,4,32,4096]{4,3,2,1,0:T(8,128)(2,1)} %dynamic-slice_bitcast_fusion), channel_id=1, source_target_pairs={{0,4},{4,0},{8,12},{12,8},{16,20},{20,16},{24,28},{28,24},{1,5},{5... | collective-permute-start | bytes 12582920 | tf_op jit(solution)/shard_map/ppermute | solution.py:726
  350.8 36.0 %collective-permute-start.2 = (bf16[4,2,4,32,512]{4,3,0,2,1:T(8,128)(2,1)S(1)}, bf16[4,2,4,32,512]{4,3,0,2,1:T(8,128)(2,1)S(1)}, u32[]{:S(2)}, u32[]{:S(2)}) collective-permute-start(bf16[4,2,4,32,512]{4,3,0,2,1:T(8,128)(2,1)S(1)} %bitcast.244), channel_id=1, source_target_pairs={{0,8},{4,12},{8,0},{12,4},{16,24},{20,28},{24,16},{28,20},{1,9},{5... | collective-permute-start | bytes 3145736 | tf_op jit(solution)/shard_map/ppermute | solution.py:726
  353.1 33.7 %collective-permute-start.1 = (bf16[4,2,4,32,512]{4,3,0,2,1:T(8,128)(2,1)S(1)}, bf16[4,2,4,32,512]{4,3,0,2,1:T(8,128)(2,1)S(1)}, u32[]{:S(2)}, u32[]{:S(2)}) collective-permute-start(bf16[4,2,4,32,512]{4,3,0,2,1:T(8,128)(2,1)S(1)} %bitcast.245), channel_id=1, source_target_pairs={{0,16},{4,20},{8,24},{12,28},{16,0},{20,4},{24,8},{28,12},{1,17},{... | collective-permute-start | bytes 3145736 | tf_op jit(solution)/shard_map/ppermute | solution.py:726
  415.3 44.2 %collective-permute-start.8 = (bf16[4,4,4,32,1024]{4,3,2,1,0:T(8,128)(2,1)}, bf16[4,4,4,32,1024]{4,3,2,1,0:T(8,128)(2,1)}, u32[]{:S(2)}, u32[]{:S(2)}) collective-permute-start(bf16[4,4,4,32,1024]{4,3,2,1,0:T(8,128)(2,1)} %pad_maximum_fusion), channel_id=1, source_target_pairs={{0,4},{4,0},{8,12},{12,8},{16,20},{20,16},{24,28},{28,24},{1,5},{5... | collective-permute-start | bytes 12582920 | tf_op jit(solution)/shard_map/ppermute | solution.py:726
  420.6 38.9 %collective-permute-start.7 = (bf16[1,2,4,32,2048]{4,3,2,1,0:T(8,128)(2,1)}, bf16[1,2,4,32,2048]{4,3,2,1,0:T(8,128)(2,1)}, u32[]{:S(2)}, u32[]{:S(2)}) collective-permute-start(bf16[1,2,4,32,2048]{4,3,2,1,0:T(8,128)(2,1)} %dynamic-slice_bitcast_fusion.11), channel_id=1, source_target_pairs={{0,8},{4,12},{8,0},{12,4},{16,24},{20,28},{24,16},{28,20},{1,9},{5... | collective-permute-start | bytes 3145736 | tf_op jit(solution)/shard_map/ppermute | solution.py:726
  421.9 46.7 %slice-start = ((s8[6291456]{0:T(1024)(128)(4,1)}), s8[4194304]{0:T(1024)(128)(4,1)S(1)}, s32[]{:S(2)}) async-start(s8[6291456]{0:T(1024)(128)(4,1)} %bitcast.224), calls=%async_computation.1 | async-start | bytes 8388608
  423.0 36.5 %collective-permute-start.6 = (bf16[1,2,4,32,2048]{4,3,2,1,0:T(8,128)(2,1)}, bf16[1,2,4,32,2048]{4,3,2,1,0:T(8,128)(2,1)}, u32[]{:S(2)}, u32[]{:S(2)}) collective-permute-start(bf16[1,2,4,32,2048]{4,3,2,1,0:T(8,128)(2,1)} %dynamic-slice_bitcast_fusion.12), channel_id=1, source_target_pairs={{0,16},{4,20},{8,24},{12,28},{16,0},{20,4},{24,8},{28,12},{1,17},{... | collective-permute-start | bytes 3145736 | tf_op jit(solution)/shard_map/ppermute | solution.py:726
  424.2 35.2 %collective-permute-start.5 = (bf16[4,4,32,512]{3,2,0,1:T(8,128)(2,1)}, bf16[4,4,32,512]{3,2,0,1:T(8,128)(2,1)S(1)}, u32[]{:S(2)}, u32[]{:S(2)}) collective-permute-start(bf16[4,4,32,512]{3,2,0,1:T(8,128)(2,1)} %dynamic-slice_bitcast_fusion.17), channel_id=1, source_target_pairs={{0,16},{4,20},{8,24},{12,28},{16,0},{20,4},{24,8},{28,12},{1,17},{... | collective-permute-start | bytes 1572872 | tf_op jit(solution)/shard_map/ppermute | solution.py:726
  427.5 32.0 %collective-permute-start.4 = (bf16[4,4,32,512]{3,2,0,1:T(8,128)(2,1)}, bf16[4,4,32,512]{3,2,0,1:T(8,128)(2,1)S(1)}, u32[]{:S(2)}, u32[]{:S(2)}) collective-permute-start(bf16[4,4,32,512]{3,2,0,1:T(8,128)(2,1)} %dynamic-slice_bitcast_fusion.18), channel_id=1, source_target_pairs={{0,8},{4,12},{8,0},{12,4},{16,24},{20,28},{24,16},{28,20},{1,9},{5... | collective-permute-start | bytes 1572872 | tf_op jit(solution)/shard_map/ppermute | solution.py:726
  461.4 37.2 %collective-permute-start.13 = (bf16[1,4,32,2048]{3,2,1,0:T(8,128)(2,1)S(1)}, bf16[1,4,32,2048]{3,2,1,0:T(8,128)(2,1)S(1)}, u32[]{:S(2)}, u32[]{:S(2)}) collective-permute-start(bf16[1,4,32,2048]{3,2,1,0:T(8,128)(2,1)S(1)} %dynamic-slice_bitcast_fusion.15), channel_id=1, source_target_pairs={{0,16},{4,20},{8,24},{12,28},{16,0},{20,4},{24,8},{28,12},{1,17},{... | collective-permute-start | bytes 1572872 | tf_op jit(solution)/shard_map/ppermute | solution.py:726
  463.4 35.2 %collective-permute-start.12 = (bf16[1,4,32,2048]{3,2,1,0:T(8,128)(2,1)S(1)}, bf16[1,4,32,2048]{3,2,1,0:T(8,128)(2,1)S(1)}, u32[]{:S(2)}, u32[]{:S(2)}) collective-permute-start(bf16[1,4,32,2048]{3,2,1,0:T(8,128)(2,1)S(1)} %dynamic-slice_bitcast_fusion.16), channel_id=1, source_target_pairs={{0,8},{4,12},{8,0},{12,4},{16,24},{20,28},{24,16},{28,20},{1,9},{5... | collective-permute-start | bytes 1572872 | tf_op jit(solution)/shard_map/ppermute | solution.py:726
  465.0 29.8 %collective-permute-start.10 = (bf16[4,32,1024]{2,1,0:T(8,128)(2,1)S(1)}, bf16[4,32,1024]{2,1,0:T(8,128)(2,1)S(1)}, u32[]{:S(2)}, u32[]{:S(2)}) collective-permute-start(bf16[4,32,1024]{2,1,0:T(8,128)(2,1)S(1)} %get-tuple-element.188), channel_id=1, source_target_pairs={{0,2},{1,3},{2,0},{3,1},{4,6},{5,7},{6,4},{7,5},{8,10},{9,11},{10,... | collective-permute-start | bytes 786440 | tf_op jit(solution)/shard_map/ppermute | solution.py:726
  466.6 30.0 %collective-permute-start.11 = (bf16[4,32,1024]{2,1,0:T(8,128)(2,1)S(1)}, bf16[4,32,1024]{2,1,0:T(8,128)(2,1)S(1)}, u32[]{:S(2)}, u32[]{:S(2)}) collective-permute-start(bf16[4,32,1024]{2,1,0:T(8,128)(2,1)S(1)} %get-tuple-element.186), channel_id=1, source_target_pairs={{0,3},{1,2},{2,1},{3,0},{4,7},{5,6},{6,5},{7,4},{8,11},{9,10},{10,... | collective-permute-start | bytes 786440 | tf_op jit(solution)/shard_map/ppermute | solution.py:726
  466.6 32.0 %collective-permute-start.9 = (bf16[4,32,1024]{2,1,0:T(8,128)(2,1)S(1)}, bf16[4,32,1024]{2,1,0:T(8,128)(2,1)S(1)}, u32[]{:S(2)}, u32[]{:S(2)}) collective-permute-start(bf16[4,32,1024]{2,1,0:T(8,128)(2,1)S(1)} %get-tuple-element.187), channel_id=1, source_target_pairs={{0,1},{1,0},{2,3},{3,2},{4,5},{5,4},{6,7},{7,6},{8,9},{9,8},{10,11... | collective-permute-start | bytes 786440 | tf_op jit(solution)/shard_map/ppermute | solution.py:726
  494.8 30.4 %collective-permute-start.17 = (bf16[4,2,4,32,512]{4,3,2,0,1:T(8,128)(2,1)S(1)}, bf16[4,2,4,32,512]{4,3,2,0,1:T(8,128)(2,1)S(1)}, u32[]{:S(2)}, u32[]{:S(2)}) collective-permute-start(bf16[4,2,4,32,512]{4,3,2,0,1:T(8,128)(2,1)S(1)} %bitcast.243), channel_id=1, source_target_pairs={{0,16},{4,20},{8,24},{12,28},{16,0},{20,4},{24,8},{28,12},{1,17},{... | collective-permute-start | bytes 3145736 | tf_op jit(solution)/shard_map/ppermute | solution.py:726
  496.7 28.6 %collective-permute-start.18 = (bf16[4,2,4,32,512]{4,3,2,1,0:T(8,128)(2,1)S(1)}, bf16[4,2,4,32,512]{4,3,2,1,0:T(8,128)(2,1)S(1)}, u32[]{:S(2)}, u32[]{:S(2)}) collective-permute-start(bf16[4,2,4,32,512]{4,3,2,1,0:T(8,128)(2,1)S(1)} %dynamic-slice_bitcast_fusion.2), channel_id=1, source_target_pairs={{0,8},{4,12},{8,0},{12,4},{16,24},{20,28},{24,16},{28,20},{1,9},{5... | collective-permute-start | bytes 3145736 | tf_op jit(solution)/shard_map/ppermute | solution.py:726
  499.0 26.2 %collective-permute-start.14 = (bf16[1,32,4096]{2,1,0:T(8,128)(2,1)S(1)}, bf16[1,32,4096]{2,1,0:T(8,128)(2,1)S(1)}, u32[]{:S(2)}, u32[]{:S(2)}) collective-permute-start(bf16[1,32,4096]{2,1,0:T(8,128)(2,1)S(1)} %get-tuple-element.184), channel_id=1, source_target_pairs={{0,1},{1,0},{2,3},{3,2},{4,5},{5,4},{6,7},{7,6},{8,9},{9,8},{10,11... | collective-permute-start | bytes 786440 | tf_op jit(solution)/shard_map/ppermute | solution.py:726
  499.2 26.1 %collective-permute-start.15 = (bf16[1,32,4096]{2,1,0:T(8,128)(2,1)S(1)}, bf16[1,32,4096]{2,1,0:T(8,128)(2,1)S(1)}, u32[]{:S(2)}, u32[]{:S(2)}) collective-permute-start(bf16[1,32,4096]{2,1,0:T(8,128)(2,1)S(1)} %get-tuple-element.185), channel_id=1, source_target_pairs={{0,2},{1,3},{2,0},{3,1},{4,6},{5,7},{6,4},{7,5},{8,10},{9,11},{10,... | collective-permute-start | bytes 786440 | tf_op jit(solution)/shard_map/ppermute | solution.py:726
  501.6 23.6 %collective-permute-start.16 = (bf16[1,32,4096]{2,1,0:T(8,128)(2,1)S(1)}, bf16[1,32,4096]{2,1,0:T(8,128)(2,1)S(1)}, u32[]{:S(2)}, u32[]{:S(2)}) collective-permute-start(bf16[1,32,4096]{2,1,0:T(8,128)(2,1)S(1)} %get-tuple-element.183), channel_id=1, source_target_pairs={{0,3},{1,2},{2,1},{3,0},{4,7},{5,6},{6,5},{7,4},{8,11},{9,10},{10,... | collective-permute-start | bytes 786440 | tf_op jit(solution)/shard_map/ppermute | solution.py:726
  526.8 14.8 %collective-permute-start.20 = (bf16[4,4,32,512]{3,2,1,0:T(8,128)(2,1)}, bf16[4,4,32,512]{3,2,1,0:T(8,128)(2,1)}, u32[]{:S(2)}, u32[]{:S(2)}) collective-permute-start(bf16[4,4,32,512]{3,2,1,0:T(8,128)(2,1)} %dynamic-slice_bitcast_fusion.13), channel_id=1, source_target_pairs={{0,16},{4,20},{8,24},{12,28},{16,0},{20,4},{24,8},{28,12},{1,17},{... | collective-permute-start | bytes 1572872 | tf_op jit(solution)/shard_map/ppermute | solution.py:726
  530.1 11.5 %collective-permute-start.19 = (bf16[4,4,32,512]{3,2,1,0:T(8,128)(2,1)}, bf16[4,4,32,512]{3,2,1,0:T(8,128)(2,1)}, u32[]{:S(2)}, u32[]{:S(2)}) collective-permute-start(bf16[4,4,32,512]{3,2,1,0:T(8,128)(2,1)} %dynamic-slice_bitcast_fusion.14), channel_id=1, source_target_pairs={{0,8},{4,12},{8,0},{12,4},{16,24},{20,28},{24,16},{28,20},{1,9},{5... | collective-permute-start | bytes 1572872 | tf_op jit(solution)/shard_map/ppermute | solution.py:726
  544.1 71.2 %collective-permute-start.21 = (bf16[4,32,1024]{2,1,0:T(8,128)(2,1)S(1)}, bf16[4,32,1024]{2,1,0:T(8,128)(2,1)S(1)}, u32[]{:S(2)}, u32[]{:S(2)}) collective-permute-start(bf16[4,32,1024]{2,1,0:T(8,128)(2,1)S(1)} %get-tuple-element.180), channel_id=1, source_target_pairs={{0,1},{1,0},{2,3},{3,2},{4,5},{5,4},{6,7},{7,6},{8,9},{9,8},{10,11... | collective-permute-start | bytes 786440 | tf_op jit(solution)/shard_map/ppermute | solution.py:726
  544.7 70.5 %collective-permute-start.22 = (bf16[4,32,1024]{2,1,0:T(8,128)(2,1)S(1)}, bf16[4,32,1024]{2,1,0:T(8,128)(2,1)S(1)}, u32[]{:S(2)}, u32[]{:S(2)}) collective-permute-start(bf16[4,32,1024]{2,1,0:T(8,128)(2,1)S(1)} %get-tuple-element.181), channel_id=1, source_target_pairs={{0,2},{1,3},{2,0},{3,1},{4,6},{5,7},{6,4},{7,5},{8,10},{9,11},{10,... | collective-permute-start | bytes 786440 | tf_op jit(solution)/shard_map/ppermute | solution.py:726
  547.0 68.3 %collective-permute-start.23 = (bf16[4,32,1024]{2,1,0:T(8,128)(2,1)S(1)}, bf16[4,32,1024]{2,1,0:T(8,128)(2,1)S(1)}, u32[]{:S(2)}, u32[]{:S(2)}) collective-permute-start(bf16[4,32,1024]{2,1,0:T(8,128)(2,1)S(1)} %get-tuple-element.182), channel_id=1, source_target_pairs={{0,3},{1,2},{2,1},{3,0},{4,7},{5,6},{6,5},{7,4},{8,11},{9,10},{10,... | collective-permute-start | bytes 786440 | tf_op jit(solution)/shard_map/ppermute | solution.py:726
  (74 other events, 489.2 us)
Sparse Core Ops, SparseCore 0:
  11.6 151.9 all-gather.1

commit v3 on v2

--- a/solution.py
+++ b/solution.py
@@ -23,260 +23,228 @@
     return jnp.dot(a, b, preferred_element_type=F32)
 
 
+def mm_t(a, b):
+    return lax.dot_general(a, b, (((1,), (1,)), ((), ())), preferred_element_type=F32)
+
+
 def halves(x):
     low = lax.broadcasted_iota(jnp.int32, x.shape, 1) < HEAD_DIM
     zero = jnp.zeros_like(x)
     return (jnp.where(low, x, zero), jnp.where(low, zero, x))
 
 
-def self_allowed_of(i, j, first_row):
-    shape = (BQ, BQ)
+def in_turn(tasks, front, back, ahead):
+    waiting = []
+    for task in tasks:
+        waiting.append((task, front(*task)))
+        if len(waiting) > ahead:
+            task, held = waiting.pop(0)
+            back(*task, *held)
+    for task, held in waiting:
+        back(*task, *held)
+
+
+BLOCKS = [slice(i * BQ, (i + 1) * BQ) for i in range(SEQ // BQ)]
+TASKS = [(i, h) for i in range(SEQ // BQ) for h in range(2)]
+
+
+def self_extent(i):
+    return (i + 1) * BQ
+
+
+def cross_extent(i):
+    return MEM
+
+
+def self_visible(first_ref, i):
+    shape = (self_extent(i), BQ)
     key = lax.broadcasted_iota(jnp.int32, shape, 0)
-    allowed = key >= first_row - j * BQ
-    if i == j:
-        allowed = allowed & (key <= lax.broadcasted_iota(jnp.int32, shape, 1))
-    return allowed
-
-
-def self_forward_kernel(low_ref, first_ref, qkv_ref, out_ref, log_ref, m_ref, l_ref, acc_ref):
-    row = pl.program_id(0)
-    blocks = SEQ // BQ
-    for i in range(blocks):
-        rows = slice(i * BQ, (i + 1) * BQ)
-        q_t = qkv_ref[rows, 0:128].T
-        first_row = first_ref[0, :, rows]
-
-        def step(j, fresh):
-            keys = slice(j * BQ, (j + 1) * BQ)
-            k_parts = halves(qkv_ref[keys, 128:256])
-            v_t = qkv_ref[keys, 256:384].T
-            allowed = self_allowed_of(i, j, first_row)
-            for h in range(2):
-                feats = slice(h * 64, (h + 1) * 64)
-                s = jnp.where(allowed, mm(k_parts[h], q_t) * SCALE2, FILLER)
-                peak = jnp.max(s, axis=0, keepdims=True)
-                if fresh:
-                    p = jnp.exp2(s - peak)
-                    m_ref[h : h + 1, :] = peak
-                    l_ref[h : h + 1, :] = jnp.sum(p, axis=0, keepdims=True)
-                    acc_ref[feats, :] = mm(v_t[feats, :], p.astype(BF16))
-                else:
-                    old = m_ref[h : h + 1, :]
-                    peak = jnp.maximum(old, peak)
-                    p = jnp.exp2(s - peak)
-                    fade = jnp.exp2(old - peak)
-                    m_ref[h : h + 1, :] = peak
-                    l_ref[h : h + 1, :] = l_ref[h : h + 1, :] * fade + jnp.sum(p, axis=0, keepdims=True)
-                    acc_ref[feats, :] = acc_ref[feats, :] * fade + mm(v_t[feats, :], p.astype(BF16))
-
-        step(i, True)
-        for j in reversed(range(i)):
-            pl.when(j >= low_ref[row * blocks + i])(functools.partial(step, j, False))
-        total = l_ref[0:2, :]
-        log_ref[0, 0, 0:2, rows] = m_ref[0:2, :] + jnp.log2(total)
-        inv = 1.0 / total
-        o_t = jnp.concatenate([acc_ref[0:64, :] * inv[0:1], acc_ref[64:128, :] * inv[1:2]], axis=0)
-        out_ref[rows, :] = o_t.T.astype(BF16)
-
-
-def self_forward(low, first, qkv, row_count):
-    pairs = HEADS // 2
-    return pl.pallas_call(
-        self_forward_kernel,
-        grid_spec=pltpu.PrefetchScalarGridSpec(
-            num_scalar_prefetch=1,
-            grid=(row_count, pairs),
-            in_specs=[
-                pl.BlockSpec((1, 1, SEQ), lambda r, p, low: (r, 0, 0)),
-                pl.BlockSpec((SEQ, 384), lambda r, p, low: (r, p)),
-            ],
-            out_specs=[
-                pl.BlockSpec((SEQ, 128), lambda r, p, low: (r, p)),
-                pl.BlockSpec((1, 1, 8, SEQ), lambda r, p, low: (r, p, 0, 0)),
-            ],
-            scratch_shapes=[pltpu.VMEM((8, BQ), F32), pltpu.VMEM((8, BQ), F32), pltpu.VMEM((128, BQ), F32)],
-        ),
-        out_shape=[
-            jax.ShapeDtypeStruct((row_count * SEQ, HEADS * HEAD_DIM), BF16),
-            jax.ShapeDtypeStruct((row_count, pairs, 8, SEQ), F32),
-        ],
-        name="self_forward",
-        compiler_params=pltpu.CompilerParams(vmem_limit_bytes=32 << 20),
-        cost_estimate=pl.CostEstimate(flops=20 << 30, bytes_accessed=row_count * (8 << 20), transcendentals=8 << 20),
-    )(low, first, qkv)
-
-
-def self_backward_kernel(low_ref, first_ref, log_ref, qkv_ref, out_ref, grad_ref, dqkv_ref, dk_ref, dv_ref, dq_ref):
-    row = pl.program_id(0)
-    blocks = SEQ // BQ
+    return (key >= first_ref[0, :, BLOCKS[i]]) & (key <= lax.broadcasted_iota(jnp.int32, shape, 1) + i * BQ)
+
+
+def cross_visible(bounds_ref, i):
+    key = lax.broadcasted_iota(jnp.int32, (MEM, BQ), 0)
+    return (key >= bounds_ref[0, 0:1, BLOCKS[i]]) & (key < bounds_ref[0, 1:2, BLOCKS[i]])
+
+
+def attend(q_of, k, v, visible, extent, out_ref, log_ref):
+    k_parts, v_t = halves(k), v.T
+    outs = {}
+
+    def front(i, h):
+        s = jnp.where(visible(i), mm_t(k_parts[h][: extent(i)], q_of(BLOCKS[i])) * SCALE2, FILLER)
+        return s, jnp.max(s, axis=0, keepdims=True)
+
+    def back(i, h, s, peak):
+        p = jnp.exp2(s - peak)
+        total = jnp.sum(p, axis=0, keepdims=True)
+        log_ref[0, 0, h : h + 1, BLOCKS[i]] = peak + jnp.log2(total)
+        outs[h] = mm(v_t[h * 64 : (h + 1) * 64, : extent(i)], p.astype(BF16)) * (1.0 / total)
+        if h == 1:
+            out_ref[BLOCKS[i], :] = jnp.concatenate([outs[0], outs[1]], axis=0).T.astype(BF16)
+
+    in_turn(TASKS, front, back, 3)
+
+
+def attend_back(q_of, k, v, g_ref, out_ref, log_ref, visible, extent, keep_dq, dk_ref, dv_ref):
+    k_parts, k_t, v_parts = halves(k), k.T, halves(v)
+    deltas, dq = {}, {}
     dk_ref[...] = jnp.zeros_like(dk_ref)
     dv_ref[...] = jnp.zeros_like(dv_ref)
-    for i in range(blocks):
-        rows = slice(i * BQ, (i + 1) * BQ)
-        q, g = qkv_ref[rows, 0:128], grad_ref[rows, :]
-        q_t, g_t = q.T, g.T
-        prod = g_t.astype(F32) * out_ref[rows, :].T.astype(F32)
-        delta = [jnp.sum(prod[h * 64 : (h + 1) * 64], axis=0, keepdims=True) for h in range(2)]
-        q_parts, g_parts = halves(q), halves(g)
-        first_row = first_ref[0, :, rows]
-
-        def step(j, fresh):
-            keys = slice(j * BQ, (j + 1) * BQ)
-            k = qkv_ref[keys, 128:256]
-            k_parts, k_t = halves(k), k.T
-            v_parts = halves(qkv_ref[keys, 256:384])
-            allowed = self_allowed_of(i, j, first_row)
-            dv, dk = [], []
-            for h in range(2):
-                feats = slice(h * 64, (h + 1) * 64)
-                s = jnp.where(allowed, mm(k_parts[h], q_t) * SCALE2, FILLER)
-                p = jnp.exp2(s - log_ref[0, 0, h : h + 1, rows])
-                dp = mm(v_parts[h], g_t)
-                ds = (p * (dp - delta[h])).astype(BF16)
-                dv.append(mm(p.astype(BF16), g_parts[h]))
-                dk.append(mm(ds, q_parts[h]))
-                part = mm(k_t[feats, :], ds)
-                dq_ref[feats, :] = part if fresh else dq_ref[feats, :] + part
-            dv_ref[keys, :] += dv[0] + dv[1]
-            dk_ref[keys, :] += dk[0] + dk[1]
-
-        step(i, True)
-        for j in reversed(range(i)):
-            pl.when(j >= low_ref[row * blocks + i])(functools.partial(step, j, False))
-        dqkv_ref[rows, 0:128] = (dq_ref[...] * HEAD_DIM**-0.5).T.astype(BF16)
+
+    def front(i, h):
+        q, g = q_of(BLOCKS[i]), g_ref[BLOCKS[i], :]
+        if h == 0:
+            prod = (g.astype(F32) * out_ref[BLOCKS[i], :].astype(F32)).T
+            deltas[i] = [jnp.sum(prod[n * 64 : (n + 1) * 64], axis=0, keepdims=True) for n in range(2)]
+        s = jnp.where(visible(i), mm_t(k_parts[h][: extent(i)], q) * SCALE2, FILLER)
+        p = jnp.exp2(s - log_ref[0, 0, h : h + 1, BLOCKS[i]])
+        dp = mm_t(v_parts[h][: extent(i)], g)
+        return p.astype(BF16), (p * (dp - deltas[i][h])).astype(BF16)
+
+    def back(i, h, p, ds):
+        n = extent(i)
+        dv_ref[:n, :] += mm(p, halves(g_ref[BLOCKS[i], :])[h])
+        dk_ref[:n, :] += mm(ds, halves(q_of(BLOCKS[i]))[h])
+        dq[h] = mm(k_t[h * 64 : (h + 1) * 64, :n], ds)
+        if h == 1:
+            keep_dq(BLOCKS[i], (jnp.concatenate([dq[0], dq[1]], axis=0) * HEAD_DIM**-0.5).T.astype(BF16))
+
+    in_turn(TASKS, front, back, 2)
+
+
+def self_forward_kernel(first_ref, qkv_ref, out_ref, log_ref):
+    attend(
+        lambda rows: qkv_ref[rows, 0:128],
+        qkv_ref[:, 128:256],
+        qkv_ref[:, 256:384],
+        functools.partial(self_visible, first_ref),
+        self_extent,
+        out_ref,
+        log_ref,
+    )
+
+
+def cross_forward_kernel(bounds_ref, q_ref, kv_ref, out_ref, log_ref):
+    attend(
+        lambda rows: q_ref[rows, :],
+        kv_ref[:, 0:128],
+        kv_ref[:, 128:256],
+        functools.partial(cross_visible, bounds_ref),
+        cross_extent,
+        out_ref,
+        log_ref,
+    )
+
+
+PAIRS = HEADS // 2
+LOG_SPEC = pl.BlockSpec((1, 1, 8, SEQ), lambda r, p: (r, p, 0, 0))
+ROW_SPEC = pl.BlockSpec((SEQ, 128), lambda r, p: (r, p))
+QKV_SPEC = pl.BlockSpec((SEQ, 384), lambda r, p: (r, p))
+KV_SPEC = pl.BlockSpec((MEM, 256), lambda r, p: (r, p))
+FIRST_SPEC = pl.BlockSpec((1, 1, SEQ), lambda r, p: (r, 0, 0))
+BOUNDS_SPEC = pl.BlockSpec((1, 8, SEQ), lambda r, p: (r, 0, 0))
+
+
+def attention_call(kernel, name, in_specs, args, row_count):
+    return pl.pallas_call(
+        kernel,
+        grid=(row_count, PAIRS),
+        in_specs=in_specs,
+        out_specs=[ROW_SPEC, LOG_SPEC],
+        out_shape=[
+            jax.ShapeDtypeStruct((row_count * SEQ, WIDTH), BF16),
+            jax.ShapeDtypeStruct((row_count, PAIRS, 8, SEQ), F32),
+        ],
+        name=name,
+        compiler_params=pltpu.CompilerParams(vmem_limit_bytes=40 << 20),
+        cost_estimate=pl.CostEstimate(flops=20 << 30, bytes_accessed=row_count * (8 << 20), transcendentals=8 << 20),
+    )(*args)
+
+
+def self_forward(first, qkv, row_count):
+    return attention_call(self_forward_kernel, "self_forward", [FIRST_SPEC, QKV_SPEC], (first, qkv), row_count)
+
+
+def cross_forward(bounds, q, kv, row_count):
+    return attention_call(
+        cross_forward_kernel, "cross_forward", [BOUNDS_SPEC, ROW_SPEC, KV_SPEC], (bounds, q, kv), row_count
+    )
+
+
+def self_backward_kernel(first_ref, log_ref, qkv_ref, out_ref, grad_ref, dqkv_ref, dk_ref, dv_ref):
+    def keep_dq(rows, value):
+        dqkv_ref[rows, 0:128] = value
+
+    attend_back(
+        lambda rows: qkv_ref[rows, 0:128],
+        qkv_ref[:, 128:256],
+        qkv_ref[:, 256:384],
+        grad_ref,
+        out_ref,
+        log_ref,
+        functools.partial(self_visible, first_ref),
+        self_extent,
+        keep_dq,
+        dk_ref,
+        dv_ref,
+    )
     dqkv_ref[:, 128:256] = (dk_ref[...] * HEAD_DIM**-0.5).astype(BF16)
     dqkv_ref[:, 256:384] = dv_ref[...].astype(BF16)
 
 
-def self_backward(low, first, logs, qkv, out, grad, row_count, part):
-    pairs = HEADS // 4
-    skip = part * pairs
+def self_backward(first, logs, qkv, out, grad, row_count):
     return pl.pallas_call(
         self_backward_kernel,
-        grid_spec=pltpu.PrefetchScalarGridSpec(
-            num_scalar_prefetch=1,
-            grid=(row_count, pairs),
-            in_specs=[
-                pl.BlockSpec((1, 1, SEQ), lambda r, p, low: (r, 0, 0)),
-                pl.BlockSpec((1, 1, 8, SEQ), lambda r, p, low: (r, p + skip, 0, 0)),
-                pl.BlockSpec((SEQ, 384), lambda r, p, low: (r, p + skip)),
-                pl.BlockSpec((SEQ, 128), lambda r, p, low: (r, p + skip)),
-                pl.BlockSpec((SEQ, 128), lambda r, p, low: (r, p + skip)),
-            ],
-            out_specs=pl.BlockSpec((SEQ, 384), lambda r, p, low: (r, p)),
-            scratch_shapes=[pltpu.VMEM((SEQ, 128), F32), pltpu.VMEM((SEQ, 128), F32), pltpu.VMEM((128, BQ), F32)],
-        ),
-        out_shape=jax.ShapeDtypeStruct((row_count * SEQ, pairs * 384), BF16),
+        grid=(row_count, PAIRS),
+        in_specs=[FIRST_SPEC, LOG_SPEC, QKV_SPEC, ROW_SPEC, ROW_SPEC],
+        out_specs=QKV_SPEC,
+        scratch_shapes=[pltpu.VMEM((SEQ, 128), F32), pltpu.VMEM((SEQ, 128), F32)],
+        out_shape=jax.ShapeDtypeStruct((row_count * SEQ, 3 * WIDTH), BF16),
         name="self_backward",
-        compiler_params=pltpu.CompilerParams(vmem_limit_bytes=32 << 20),
-        cost_estimate=pl.CostEstimate(flops=(5 << 30) * pairs, bytes_accessed=row_count * (16 << 20), transcendentals=8 << 20),
-    )(low, first, logs, qkv, out, grad)
-
-
-def cross_allowed_of(bounds_ref, rows):
-    key = lax.broadcasted_iota(jnp.int32, (MEM, BQ), 0)
-    return (key >= bounds_ref[0, 0:1, rows]) & (key < bounds_ref[0, 1:2, rows])
-
-
-def cross_forward_kernel(bounds_ref, q_ref, kv_ref, out_ref, log_ref):
-    k_parts = halves(kv_ref[:, 0:128])
-    v_t = kv_ref[:, 128:256].T
-    for i in range(SEQ // BQ):
-        rows = slice(i * BQ, (i + 1) * BQ)
-        q_t = q_ref[rows, :].T
-        allowed = cross_allowed_of(bounds_ref, rows)
-        outs = []
-        for h in range(2):
-            s = jnp.where(allowed, mm(k_parts[h], q_t) * SCALE2, FILLER)
-            peak = jnp.max(s, axis=0, keepdims=True)
-            p = jnp.exp2(s - peak)
-            total = jnp.sum(p, axis=0, keepdims=True)
-            log_ref[0, 0, h : h + 1, rows] = peak + jnp.log2(total)
-            outs.append(mm(v_t[h * 64 : (h + 1) * 64, :], p.astype(BF16)) * (1.0 / total))
-        out_ref[rows, :] = jnp.concatenate(outs, axis=0).T.astype(BF16)
-
-
-def cross_forward(bounds, q, kv, row_count):
-    pairs = HEADS // 2
-    return pl.pallas_call(
-        cross_forward_kernel,
-        grid=(row_count, pairs),
-        in_specs=[
-            pl.BlockSpec((1, 8, SEQ), lambda r, p: (r, 0, 0)),
-            pl.BlockSpec((SEQ, 128), lambda r, p: (r, p)),
-            pl.BlockSpec((MEM, 256), lambda r, p: (r, p)),
-        ],
-        out_specs=[
-            pl.BlockSpec((SEQ, 128), lambda r, p: (r, p)),
-            pl.BlockSpec((1, 1, 8, SEQ), lambda r, p: (r, p, 0, 0)),
-        ],
-        out_shape=[
-            jax.ShapeDtypeStruct((row_count * SEQ, HEADS * HEAD_DIM), BF16),
-            jax.ShapeDtypeStruct((row_count, pairs, 8, SEQ), F32),
-        ],
-        name="cross_forward",
-        compiler_params=pltpu.CompilerParams(vmem_limit_bytes=32 << 20),
-        cost_estimate=pl.CostEstimate(flops=20 << 30, bytes_accessed=row_count * (6 << 20), transcendentals=8 << 20),
-    )(bounds, q, kv)
+        compiler_params=pltpu.CompilerParams(vmem_limit_bytes=40 << 20),
+        cost_estimate=pl.CostEstimate(flops=40 << 30, bytes_accessed=row_count * (16 << 20), transcendentals=8 << 20),
+    )(first, logs, qkv, out, grad)
+
+
+def cross_backward_pair(bounds_ref, log_ref, q_ref, kv_ref, out_ref, grad_ref, keep_dq, dkv_ref, dk_ref, dv_ref):
+    attend_back(
+        lambda rows: q_ref[rows, :],
+        kv_ref[:, 0:128],
+        kv_ref[:, 128:256],
+        grad_ref,
+        out_ref,
+        log_ref,
+        functools.partial(cross_visible, bounds_ref),
+        cross_extent,
+        keep_dq,
+        dk_ref,
+        dv_ref,
+    )
 
 
 def cross_backward_kernel(bounds_ref, log_ref, q_ref, kv_ref, out_ref, grad_ref, dq_ref, dkv_ref, dk_ref, dv_ref):
-    k = kv_ref[:, 0:128]
-    k_parts, k_t = halves(k), k.T
-    v_parts = halves(kv_ref[:, 128:256])
-    for i in range(SEQ // BQ):
-        rows = slice(i * BQ, (i + 1) * BQ)
-        q, g = q_ref[rows, :], grad_ref[rows, :]
-        q_t, g_t = q.T, g.T
-        prod = g_t.astype(F32) * out_ref[rows, :].T.astype(F32)
-        q_parts, g_parts = halves(q), halves(g)
-        allowed = cross_allowed_of(bounds_ref, rows)
-        dv, dk, dq = [], [], []
-        for h in range(2):
-            feats = slice(h * 64, (h + 1) * 64)
-            delta = jnp.sum(prod[feats], axis=0, keepdims=True)
-            s = jnp.where(allowed, mm(k_parts[h], q_t) * SCALE2, FILLER)
-            p = jnp.exp2(s - log_ref[0, 0, h : h + 1, rows])
-            dp = mm(v_parts[h], g_t)
-            ds = (p * (dp - delta)).astype(BF16)
-            dv.append(mm(p.astype(BF16), g_parts[h]))
-            dk.append(mm(ds, q_parts[h]))
-            dq.append(mm(k_t[feats, :], ds))
-        if i == 0:
-            dv_ref[...] = dv[0] + dv[1]
-            dk_ref[...] = dk[0] + dk[1]
-        else:
-            dv_ref[...] += dv[0] + dv[1]
-            dk_ref[...] += dk[0] + dk[1]
-        dq_ref[rows, :] = (jnp.concatenate(dq, axis=0) * HEAD_DIM**-0.5).T.astype(BF16)
+    def keep_dq(rows, value):
+        dq_ref[rows, :] = value
+
+    cross_backward_pair(bounds_ref, log_ref, q_ref, kv_ref, out_ref, grad_ref, keep_dq, dkv_ref, dk_ref, dv_ref)
     dkv_ref[:, 0:128] = (dk_ref[...] * HEAD_DIM**-0.5).astype(BF16)
     dkv_ref[:, 128:256] = dv_ref[...].astype(BF16)
 
 
 def cross_backward(bounds, logs, q, kv, out, grad, row_count):
-    pairs = HEADS // 2
     return pl.pallas_call(
         cross_backward_kernel,
-        grid=(row_count, pairs),
-        in_specs=[
-            pl.BlockSpec((1, 8, SEQ), lambda r, p: (r, 0, 0)),
-            pl.BlockSpec((1, 1, 8, SEQ), lambda r, p: (r, p, 0, 0)),
-            pl.BlockSpec((SEQ, 128), lambda r, p: (r, p)),
-            pl.BlockSpec((MEM, 256), lambda r, p: (r, p)),
-            pl.BlockSpec((SEQ, 128), lambda r, p: (r, p)),
-            pl.BlockSpec((SEQ, 128), lambda r, p: (r, p)),
-        ],
-        out_specs=[
-            pl.BlockSpec((SEQ, 128), lambda r, p: (r, p)),
-            pl.BlockSpec((MEM, 256), lambda r, p: (r, p)),
-        ],
+        grid=(row_count, PAIRS),
+        in_specs=[BOUNDS_SPEC, LOG_SPEC, ROW_SPEC, KV_SPEC, ROW_SPEC, ROW_SPEC],
+        out_specs=[ROW_SPEC, KV_SPEC],
         scratch_shapes=[pltpu.VMEM((MEM, 128), F32), pltpu.VMEM((MEM, 128), F32)],
         out_shape=[
-            jax.ShapeDtypeStruct((row_count * SEQ, HEADS * HEAD_DIM), BF16),
-            jax.ShapeDtypeStruct((row_count * MEM, 2 * HEADS * HEAD_DIM), BF16),
+            jax.ShapeDtypeStruct((row_count * SEQ, WIDTH), BF16),
+            jax.ShapeDtypeStruct((row_count * MEM, 2 * WIDTH), BF16),
         ],
         name="cross_backward",
-        compiler_params=pltpu.CompilerParams(vmem_limit_bytes=32 << 20),
+        compiler_params=pltpu.CompilerParams(vmem_limit_bytes=40 << 20),
         cost_estimate=pl.CostEstimate(flops=40 << 30, bytes_accessed=row_count * (12 << 20), transcendentals=8 << 20),
     )(bounds, logs, q, kv, out, grad)
 
@@ -295,15 +263,10 @@
     start = jnp.where(live, start, 0)
     end = jnp.where(live, end, MEM)
     bounds = jnp.pad(jnp.stack([start, end], axis=1), ((0, 0), (0, 6), (0, 0)))
-    low = (first[:, ::BQ] // BQ).reshape(-1)
-    return low, first[:, None, :], bounds
+    return first[:, None, :], bounds
 
 
 TB = 256
-
-
-def mm_t(a, b):
-    return lax.dot_general(a, b, (((1,), (1,)), ((), ())), preferred_element_type=F32)
 
 
 def norm_parts(values):
@@ -842,18 +805,18 @@
 
 
 class Scatter:
-    def __init__(self, share, buffers, out_ref, send_sems, recv_sems, narrow, base=0):
-        self.share, self.out_ref = share, out_ref
+    def __init__(self, own, theirs, buffers, out_ref, send_sems, recv_sems, narrow):
+        self.own, self.theirs, self.out_ref = own, theirs, out_ref
         self.from_core, self.a1, self.b1, self.a2, self.b2, self.from_line = buffers
-        self.send_sems, self.recv_sems, self.base = send_sems, recv_sems, base
+        self.send_sems, self.recv_sems = send_sems, recv_sems
         self.narrow = narrow
-        self.half = share.shape[-1] // 2
+        self.half = self.a1.shape[-1]
         self.w, self.z = lax.axis_index("wide"), lax.axis_index("narrow")
         self.c, self.x, self.y = self.w & 1, (self.w >> 1) & 1, (self.w >> 2) & 1
         self.per_chunk = 4 + narrow
 
     def move(self, i, number, src, dst, target):
-        at = self.base + i * self.per_chunk + number
+        at = i * self.per_chunk + number
         return pltpu.make_async_remote_copy(
             src_ref=src,
             dst_ref=dst,
@@ -864,28 +827,22 @@
         )
 
     def to_core(self, i):
-        return self.move(i, 0, self.share.at[i, :, :, 1 - self.c], self.from_core.at[i], (self.w ^ 1, self.z))
+        return self.move(i, 0, self.theirs(i), self.from_core.at[i], (self.w ^ 1, self.z))
 
     def first(self, i):
         left, right = pl.ds(0, self.half), pl.ds(self.half, self.half)
+        to_x, to_y = (self.w ^ 2, self.z), (self.w ^ 4, self.z)
         return (
-            self.move(
-                i, 1, self.share.at[i, :, 1 - self.x, self.c, :, :, left], self.a1.at[i], (self.w ^ 2, self.z)
-            ),
-            self.move(
-                i, 2, self.share.at[i, 1 - self.y, :, self.c, :, :, right], self.b1.at[i], (self.w ^ 4, self.z)
-            ),
+            self.move(i, 1, self.own.at[i, :, 1 - self.x, :, :, left], self.a1.at[i], to_x),
+            self.move(i, 2, self.own.at[i, 1 - self.y, :, :, :, right], self.b1.at[i], to_y),
         )
 
     def second(self, i):
         left, right = pl.ds(0, self.half), pl.ds(self.half, self.half)
+        to_x, to_y = (self.w ^ 2, self.z), (self.w ^ 4, self.z)
         return (
-            self.move(
-                i, 3, self.share.at[i, 1 - self.y, self.x, self.c, :, :, left], self.a2.at[i], (self.w ^ 4, self.z)
-            ),
-            self.move(
-                i, 4, self.share.at[i, self.y, 1 - self.x, self.c, :, :, right], self.b2.at[i], (self.w ^ 2, self.z)
-            ),
+            self.move(i, 3, self.own.at[i, 1 - self.y, self.x, :, :, left], self.a2.at[i], to_y),
+            self.move(i, 4, self.own.at[i, self.y, 1 - self.x, :, :, right], self.b2.at[i], to_x),
         )
 
     def along(self, i):
@@ -893,7 +850,7 @@
             self.move(
                 i,
                 4 + mask,
-                self.share.at[i, self.y, self.x, self.c, self.z ^ mask],
+                self.own.at[i, self.y, self.x, self.z ^ mask],
                 self.from_line.at[i, mask - 1],
                 (self.w, self.z ^ mask),
             )
@@ -903,9 +860,9 @@
     def begin(self, i):
         self.to_core(i).start()
 
-    def add(self, place, columns, piece):
-        now = self.share[(*place, slice(None), slice(None), columns)]
-        self.share[(*place, slice(None), slice(None), columns)] = (now.astype(F32) + piece.astype(F32)).astype(BF16)
+    def add(self, i, y, x, columns, piece):
+        now = self.own[i, y, x, :, :, columns]
+        self.own[i, y, x, :, :, columns] = (now.astype(F32) + piece.astype(F32)).astype(BF16)
 
     def step(self, i, stage):
         both, left, right = slice(None), slice(0, self.half), slice(self.half, None)
@@ -913,32 +870,31 @@
             self.to_core(i).wait_recv()
             for a in range(2):
                 for b in range(2):
-                    self.add((i, a, b, self.c), both, self.from_core[i, a, b])
+                    self.add(i, a, b, both, self.from_core[i, a, b])
             for copy in self.first(i):
                 copy.start()
         elif stage == 1:
             for copy in self.first(i):
                 copy.wait_recv()
             for a in range(2):
-                self.add((i, a, self.x, self.c), left, self.a1[i, a])
-                self.add((i, self.y, a, self.c), right, self.b1[i, a])
+                self.add(i, a, self.x, left, self.a1[i, a])
+                self.add(i, self.y, a, right, self.b1[i, a])
             for copy in self.second(i):
                 copy.start()
         elif stage == 2:
             for copy in self.second(i):
                 copy.wait_recv()
-            self.add((i, self.y, self.x, self.c), left, self.a2[i])
-            self.add((i, self.y, self.x, self.c), right, self.b2[i])
+            self.add(i, self.y, self.x, left, self.a2[i])
+            self.add(i, self.y, self.x, right, self.b2[i])
             for copy in self.along(i):
                 copy.start()
         else:
             for copy in self.along(i):
                 copy.wait_recv()
-            total = self.share[i, self.y, self.x, self.c, self.z].astype(F32)
+            total = self.own[i, self.y, self.x, self.z].astype(F32)
             for mask in range(1, self.narrow):
                 total = total + self.from_line[i, mask - 1].astype(F32)
-            width = 2 * self.half
-            self.out_ref[:, i * width : (i + 1) * width] = total
+            self.out_ref[i] = total
 
     def close(self, i):
         for copy in (self.to_core(i), *self.first(i), *self.second(i), *self.along(i)):
@@ -946,22 +902,323 @@
 
 
 def scatter_scratch(chunks, narrow, rows, width):
+    copies = chunks * (4 + narrow)
     return [
+        pltpu.VMEM((chunks, 2, 2, narrow, rows, width), BF16),
         pltpu.VMEM((chunks, 2, 2, narrow, rows, width), BF16),
         pltpu.VMEM((chunks, 2, narrow, rows, width // 2), BF16),
         pltpu.VMEM((chunks, 2, narrow, rows, width // 2), BF16),
         pltpu.VMEM((chunks, narrow, rows, width // 2), BF16),
         pltpu.VMEM((chunks, narrow, rows, width // 2), BF16),
         pltpu.VMEM((chunks, narrow - 1, rows, width), BF16),
+        pltpu.SemaphoreType.DMA((copies,)),
+        pltpu.SemaphoreType.DMA((copies,)),
+        pltpu.SemaphoreType.DMA((chunks,)),
     ]
+
+
+class Carried:
+    def __init__(self, shares, scratch, out_ref, narrow):
+        own, *buffers, send_sems, recv_sems, self.load_sems = scratch
+        self.shares = shares
+        self.scatter = Scatter(own, lambda i: self.part(i, 1 - self.scatter.c), buffers, out_ref, send_sems, recv_sems, narrow)
+        self.chunks = own.shape[0]
+
+    def part(self, i, core):
+        ref, at, width = self.shares[i]
+        return ref.at[:, :, core, :, :, pl.ds(at, width)]
+
+    def load(self, i):
+        return pltpu.make_async_copy(self.part(i, self.scatter.c), self.scatter.own.at[i], self.load_sems.at[i])
+
+    def open(self):
+        for i in range(self.chunks):
+            self.load(i).start()
+        greet_all(self.scatter.narrow)
+        for i in range(self.chunks):
+            self.scatter.begin(i)
+
+    def steps(self, plan):
+        for i, stage in plan:
+            if stage == 0:
+                self.load(i).wait()
+            self.scatter.step(i, stage)
+
+    def close(self):
+        for i in range(self.chunks):
+            self.scatter.close(i)
+
+
+def share_views(array, narrow, rows):
+    return array.reshape(2, 2, 2, narrow, rows, array.shape[1])
+
+
+CROSS_PLAN = (
+    ((0, 0), (1, 0)),
+    ((2, 0),),
+    ((0, 1),),
+    ((3, 0),),
+    ((1, 1),),
+    ((2, 1), (0, 2)),
+    ((1, 2),),
+    ((3, 1),),
+    ((2, 2), (0, 3)),
+    ((1, 3),),
+    ((3, 2),),
+    ((2, 3), (3, 3)),
+)
+
+
+def cross_back_kernel(
+    narrow,
+    bounds_ref,
+    log_ref,
+    q_ref,
+    kv_ref,
+    mixed_ref,
+    grad_ref,
+    before_ref,
+    total_ref,
+    norms_ref,
+    early_any,
+    share_any,
+    dq_ref,
+    dkv_ref,
+    out_ref,
+    b1_ref,
+    next_ref,
+    mem_ref,
+    ngrad_ref,
+    shard_ref,
+    dk_ref,
+    dv_ref,
+    wq,
+    wkv,
+    wo,
+    weight_sems,
+    *scratch,
+):
+    step = pl.program_id(0)
+    d = wq.shape[0]
+    width = shard_ref.shape[-1]
+    chunks = shard_ref.shape[0]
+    carried = Carried([(share_any.at[i], 0, width) for i in range(chunks)], scratch, shard_ref, narrow)
+    loads = [
+        pltpu.make_async_copy(early_any.at[:, pl.ds(QUERY_CROSS * d, d)], wq, weight_sems.at[0]),
+        pltpu.make_async_copy(early_any.at[:, pl.ds(2 * KV_CROSS * d, 2 * d)], wkv, weight_sems.at[1]),
+        pltpu.make_async_copy(early_any.at[:, pl.ds(OUT_SELF * d, d)], wo, weight_sems.at[2]),
+    ]
+
+    @pl.when(step == 0)
+    def _():
+        carried.open()
+        for load in loads:
+            load.start()
+
+    @pl.when(step < PAIRS)
+    def _():
+        def keep_dq(rows, value):
+            dq_ref[rows, pl.ds(pl.multiple_of(step * 128, 128), 128)] = value
+
+        cross_backward_pair(bounds_ref, log_ref, q_ref, kv_ref, mixed_ref, grad_ref, keep_dq, None, dk_ref, dv_ref)
+        at = pl.multiple_of(step * 256, 256)
+        dkv_ref[:, pl.ds(at, 128)] = (dk_ref[...] * HEAD_DIM**-0.5).astype(BF16)
+        dkv_ref[:, pl.ds(pl.multiple_of(at + 128, 128), 128)] = dv_ref[...].astype(BF16)
+
+    @pl.when(step == PAIRS)
+    def _():
+        for load in loads:
+            load.wait()
+        ngrad_ref[...] = jnp.zeros_like(ngrad_ref)
+
+    @pl.when(step >= PAIRS)
+    def _():
+        t = step - PAIRS
+        mb = mem_ref.shape[0]
+        gradient = mm_t(dq_ref[pl.ds(pl.multiple_of(t * TB, TB), TB), :], wq[...])
+        mem_ref[...] = mm_t(dkv_ref[pl.ds(pl.multiple_of(t * mb, mb), mb), :], wkv[...]).astype(BF16)
+        unit, inverse = norm_parts(before_ref[...])
+        total = total_ref[...] + norm_back(unit, inverse, norms_ref[2:3, :], gradient)
+        out_ref[...] = total
+        b1 = total.astype(BF16)
+        b1_ref[...] = b1
+        next_ref[...] = mm_t(b1, wo[...]).astype(BF16)
+        ngrad_ref[0:1, :] += jnp.sum(gradient * unit, axis=0, keepdims=True)
+        ngrad_ref[1:2, :] += jnp.sum(gradient, axis=0, keepdims=True)
+
+    for number, plan in enumerate(CROSS_PLAN):
+        pl.when(step == number)(functools.partial(carried.steps, plan))
+    pl.when(step == len(CROSS_PLAN) - 1)(carried.close)
+
+
+def cross_back(bounds, logs, q, kv, mixed, grad, before, total, norms, early, share, narrow):
+    rows, d = q.shape
+    mem_rows = kv.shape[0]
+    chunks = share.shape[0] // d
+    shard_rows = d // (8 * narrow)
+    steps = rows // TB
+    mb = mem_rows // steps
+
+    def pair(s):
+        return jnp.minimum(s, PAIRS - 1)
+
+    def token(s):
+        return jnp.maximum(s - PAIRS, 0)
+
+    anywhere = pl.BlockSpec(memory_space=pl.ANY)
+    by_pair = pl.BlockSpec((SEQ, 128), lambda s: (0, pair(s)))
+    by_token = pl.BlockSpec((TB, d), lambda s: (token(s), 0))
+    return pl.pallas_call(
+        functools.partial(cross_back_kernel, narrow),
+        grid=(PAIRS + steps,),
+        in_specs=[
+            pl.BlockSpec((1, 8, SEQ), lambda s: (0, 0, 0)),
+            pl.BlockSpec((1, 1, 8, SEQ), lambda s: (0, pair(s), 0, 0)),
+            by_pair,
+            pl.BlockSpec((MEM, 256), lambda s: (0, pair(s))),
+            by_pair,
+            by_pair,
+            by_token,
+            by_token,
+            whole(8, d),
+            anywhere,
+            anywhere,
+        ],
+        out_specs=[
+            whole(rows, d),
+            whole(mem_rows, 2 * d),
+            by_token,
+            by_token,
+            by_token,
+            pl.BlockSpec((mb, d), lambda s: (token(s), 0)),
+            whole(8, d),
+            pl.BlockSpec((chunks, shard_rows, d), lambda s: (0, 0, 0), pipeline_mode=pl.Buffered(1)),
+        ],
+        out_shape=[
+            shape(rows, d, BF16),
+            shape(mem_rows, 2 * d, BF16),
+            shape(rows, d, F32),
+            shape(rows, d, BF16),
+            shape(rows, d, BF16),
+            shape(mem_rows, d, BF16),
+            shape(8, d, F32),
+            jax.ShapeDtypeStruct((chunks, shard_rows, d), F32),
+        ],
+        scratch_shapes=[
+            pltpu.VMEM((MEM, 128), F32),
+            pltpu.VMEM((MEM, 128), F32),
+            pltpu.VMEM((d, d), BF16),
+            pltpu.VMEM((d, 2 * d), BF16),
+            pltpu.VMEM((d, d), BF16),
+            pltpu.SemaphoreType.DMA((3,)),
+            *scatter_scratch(chunks, narrow, shard_rows, d),
+        ],
+        name="cross_back",
+        compiler_params=pltpu.CompilerParams(collective_id=2, has_side_effects=True, vmem_limit_bytes=58 << 20),
+        cost_estimate=cost(40 * rows * d * d, 100 << 20),
+    )(
+        bounds,
+        logs,
+        q,
+        kv,
+        mixed,
+        grad,
+        before,
+        total,
+        norms,
+        early,
+        share.reshape(chunks, 2, 2, 2, narrow, shard_rows, d),
+    )
+
+
+SELF_PLAN = (
+    ((0, 0), (1, 0)),
+    ((2, 0),),
+    ((0, 1),),
+    ((3, 0), (1, 1)),
+    ((4, 0),),
+    ((2, 1), (0, 2)),
+    ((5, 0), (1, 2)),
+    (
+        ((3, 1), (2, 2), (6, 0), (0, 3), (4, 1), (3, 2), (1, 3), (7, 0), (5, 1), (4, 2), (2, 3))
+        + ((6, 1), (5, 2), (3, 3), (7, 1), (6, 2), (4, 3), (7, 2), (5, 3), (6, 3), (7, 3))
+    ),
+)
+
+
+def self_back_kernel(
+    narrow,
+    first_ref,
+    log_ref,
+    qkv_ref,
+    mixed_ref,
+    grad_ref,
+    wide_any,
+    a_any,
+    b_any,
+    c_any,
+    d_any,
+    dqkv_ref,
+    shard_ref,
+    dk_ref,
+    dv_ref,
+    *scratch,
+):
+    step = pl.program_id(0)
+    width = shard_ref.shape[-1]
+    shares = [(wide_any, i * width, width) for i in range(4)]
+    shares += [(ref, 0, width) for ref in (a_any, b_any, c_any, d_any)]
+    carried = Carried(shares, scratch, shard_ref, narrow)
+    pl.when(step == 0)(carried.open)
+    self_backward_kernel(first_ref, log_ref, qkv_ref, mixed_ref, grad_ref, dqkv_ref, dk_ref, dv_ref)
+    for number, plan in enumerate(SELF_PLAN):
+        pl.when(step == number)(functools.partial(carried.steps, plan))
+    pl.when(step == len(SELF_PLAN) - 1)(carried.close)
+
+
+def self_back(first, logs, qkv, mixed, grad, wide_share, shares, narrow):
+    rows, d = mixed.shape
+    shard_rows = d // (8 * narrow)
+    anywhere = pl.BlockSpec(memory_space=pl.ANY)
+    by_pair = pl.BlockSpec((SEQ, 128), lambda s: (0, s))
+    qkv_pair = pl.BlockSpec((SEQ, 384), lambda s: (0, s))
+    return pl.pallas_call(
+        functools.partial(self_back_kernel, narrow),
+        grid=(PAIRS,),
+        in_specs=[
+            pl.BlockSpec((1, 1, SEQ), lambda s: (0, 0, 0)),
+            pl.BlockSpec((1, 1, 8, SEQ), lambda s: (0, s, 0, 0)),
+            qkv_pair,
+            by_pair,
+            by_pair,
+            *[anywhere] * 5,
+        ],
+        out_specs=[qkv_pair, pl.BlockSpec((8, shard_rows, d), lambda s: (0, 0, 0), pipeline_mode=pl.Buffered(1))],
+        out_shape=[shape(rows, 3 * d, BF16), jax.ShapeDtypeStruct((8, shard_rows, d), F32)],
+        scratch_shapes=[
+            pltpu.VMEM((SEQ, 128), F32),
+            pltpu.VMEM((SEQ, 128), F32),
+            *scatter_scratch(8, narrow, shard_rows, d),
+        ],
+        name="self_back",
+        compiler_params=pltpu.CompilerParams(collective_id=3, has_side_effects=True, vmem_limit_bytes=58 << 20),
+        cost_estimate=cost(40 * rows * d * d, 100 << 20),
+    )(
+        first,
+        logs,
+        qkv,
+        mixed,
+        grad,
+        share_views(wide_share, narrow, shard_rows),
+        *[share_views(s, narrow, shard_rows) for s in shares],
+    )
 
 
 def tail_kernel(
     narrow,
     share_any,
     normed_any,
-    low_any,
-    high_any,
+    grads_any,
     weight_any,
     tokens_any,
     total_any,
@@ -984,29 +1241,42 @@
     a2,
     b2,
     from_line,
+    send_sems,
+    recv_sems,
     nval,
     nin,
-    send_sems,
-    recv_sems,
+    norm_send_sems,
+    norm_recv_sems,
     load_sems,
 ):
     d = normed.shape[1]
     width = share.shape[-1]
-    part = low_any.shape[1]
     loads = [
         pltpu.make_async_copy(share_any, share.at[0], load_sems.at[0]),
         pltpu.make_async_copy(normed_any, normed, load_sems.at[1]),
-        pltpu.make_async_copy(low_any, grads.at[:, pl.ds(0, part)], load_sems.at[2]),
-        pltpu.make_async_copy(high_any, grads.at[:, pl.ds(part, part)], load_sems.at[3]),
-        pltpu.make_async_copy(weight_any.at[:, pl.ds(0, 3 * d)], weight, load_sems.at[4]),
-        pltpu.make_async_copy(tokens_any, tokens, load_sems.at[5]),
-        pltpu.make_async_copy(total_any, total, load_sems.at[6]),
+        *[
+            pltpu.make_async_copy(
+                grads_any.at[:, pl.ds(i * width, width)], grads.at[:, pl.ds(i * width, width)], load_sems.at[2 + i]
+            )
+            for i in range(3)
+        ],
+        pltpu.make_async_copy(weight_any.at[:, pl.ds(0, 3 * d)], weight, load_sems.at[5]),
+        pltpu.make_async_copy(tokens_any, tokens, load_sems.at[6]),
+        pltpu.make_async_copy(total_any, total, load_sems.at[7]),
     ]
     for load in loads:
         load.start()
     greet_all(narrow)
-    scatter = Scatter(share, (from_core, a1, b1, a2, b2, from_line), shard_ref, send_sems, recv_sems, narrow)
-    w, z = scatter.w, scatter.z
+    w, z = lax.axis_index("wide"), lax.axis_index("narrow")
+    scatter = Scatter(
+        share.at[:, :, :, w & 1],
+        lambda i: share.at[i, :, :, 1 - (w & 1)],
+        (from_core, a1, b1, a2, b2, from_line),
+        shard_ref,
+        send_sems,
+        recv_sems,
+        narrow,
+    )
     rows = share.shape[5]
     group = 2 * narrow * rows
 
@@ -1017,8 +1287,7 @@
         normed_t[:, t * TB : (t + 1) * TB] = normed[t * TB : (t + 1) * TB, :].T
 
     def multiply(i):
-        if i < 3:
-            loads[1 + i].wait()
+        loads[1 + i].wait()
         for a in range(2):
             for b in range(2):
                 at = (2 * a + b) * group
@@ -1028,7 +1297,7 @@
 
     def close_tokens(t):
         if t == 0:
-            for load in loads[4:]:
+            for load in loads[5:]:
                 load.wait()
         at = slice(t * TB, (t + 1) * TB)
         gradient = mm_t(grads[at, :], weight[...])
@@ -1042,14 +1311,12 @@
             nval[0, 0:1, :] += gain
             nval[0, 1:2, :] += shift
 
-    first_sem = CHUNKS * scatter.per_chunk
-
     def norm_copy(stage, number, target):
         return pltpu.make_async_remote_copy(
             src_ref=nval.at[stage],
             dst_ref=nin.at[number],
-            send_sem=send_sems.at[first_sem + number],
-            recv_sem=recv_sems.at[first_sem + number],
+            send_sem=norm_send_sems.at[number],
+            recv_sem=norm_recv_sems.at[number],
             device_id=target,
             device_id_type=pl.DeviceIdType.MESH,
         )
@@ -1111,18 +1378,17 @@
             copy.wait_send()
 
 
-def tail(output_share, normed, low_grads, high_grads, tokens, total, norms, norm_two, norm_three, early, mesh_axes):
+def tail(output_share, normed, grads, tokens, total, norms, norm_two, norm_three, early, mesh_axes):
     (_, wide), (_, narrow) = mesh_axes
     rows, d = tokens.shape
     shard_rows = d // (wide * narrow)
     width = 4 * d // CHUNKS
     anywhere, vmem = pl.BlockSpec(memory_space=pl.ANY), pl.BlockSpec(memory_space=pltpu.VMEM)
-    copies = CHUNKS * (4 + narrow) + 2 + narrow
     return pl.pallas_call(
         functools.partial(tail_kernel, narrow),
-        in_specs=[anywhere] * 7 + [vmem] * 3,
+        in_specs=[anywhere] * 6 + [vmem] * 3,
         out_specs=[vmem] * 3,
-        out_shape=[shape(rows, d, BF16), shape(shard_rows, 4 * d, F32), shape(8, d, F32)],
+        out_shape=[shape(rows, d, BF16), jax.ShapeDtypeStruct((CHUNKS, shard_rows, d), F32), shape(8, d, F32)],
         scratch_shapes=[
             pltpu.VMEM((rows, d), BF16),
             pltpu.VMEM((d, rows), BF16),
@@ -1131,12 +1397,12 @@
             pltpu.VMEM((rows, d), BF16),
             pltpu.VMEM((rows, d), F32),
             pltpu.VMEM((CHUNKS, 2, 2, 2, narrow, shard_rows, width), BF16),
-            *scatter_scratch(CHUNKS, narrow, shard_rows, width),
+            *scatter_scratch(CHUNKS, narrow, shard_rows, width)[1:-1],
             pltpu.VMEM((4, 8, d), F32),
             pltpu.VMEM((2 + narrow, 8, d), F32),
-            pltpu.SemaphoreType.DMA((copies,)),
-            pltpu.SemaphoreType.DMA((copies,)),
-            pltpu.SemaphoreType.DMA((7,)),
+            pltpu.SemaphoreType.DMA((2 + narrow,)),
+            pltpu.SemaphoreType.DMA((2 + narrow,)),
+            pltpu.SemaphoreType.DMA((8,)),
         ],
         name="tail",
         compiler_params=pltpu.CompilerParams(collective_id=1, has_side_effects=True, vmem_limit_bytes=58 << 20),
@@ -1144,8 +1410,7 @@
     )(
         output_share.reshape(2, 2, 2, narrow, shard_rows, d),
         normed,
-        low_grads,
-        high_grads,
+        grads,
         early,
         tokens,
         total,
@@ -1229,57 +1494,70 @@
     pair_tokens = jnp.sum(jnp.where(member, group_counts, 0))
     token_all = row_count * SEQ * device_count
     row_weight = pair_tokens.astype(F32) * (token_all / 1000.0) / live_total
-    low, first, bounds = row_bounds(pair_starts, source_starts, live_length)
+    first, bounds = row_bounds(pair_starts, source_starts, live_length)
 
     normed_one, qkv = project(tokens, norms, early)
-    self_mixed, self_logs = self_forward(low, first, qkv, row_count)
+    self_mixed, self_logs = self_forward(first, qkv, row_count)
     after_self, normed_two, cross_q, cross_kv = middle(self_mixed, tokens, memory, norms, early)
     cross_mixed, cross_logs = cross_forward(bounds, cross_q, cross_kv, row_count)
     layer_output, normed_three, activated, hidden_grad, branch_three, cross_total, branch_two, mixed_grad, norm_three = feed(
         live_length, row_weight[None], cross_mixed, after_self, cotangent, norms, early, late
     )
 
-    reduce_sum = staged(outer_sum(activated, branch_three))
-    mixed_grad, expand_share = lax.optimization_barrier((mixed_grad, outer_sum(normed_three, hidden_grad)))
-    mixed_grad = fence(mixed_grad, reduce_sum)
-    expand_sum = staged(expand_share)
-    cq_grad, ckv_grad = cross_backward(bounds, cross_logs, cross_q, cross_kv, cross_mixed, mixed_grad, row_count)
-    cq_grad, ckv_grad = fence((cq_grad, ckv_grad), reduce_sum, expand_sum)
-    shares = [outer_sum(cross_mixed, branch_two), outer_sum(normed_two, cq_grad)]
-    shares += [outer_sum(memory, part) for part in (ckv_grad[:, :WIDTH], ckv_grad[:, WIDTH:])]
-    cq_grad, shares = lax.optimization_barrier((cq_grad, shares))
-    cross_sum = staged(*shares)
-    self_total, branch_one, mixed_grad, memory_grad, norm_two = cross_close(
-        cq_grad, ckv_grad, after_self, cross_total, norms, early
-    )
-    mixed_grad = fence(mixed_grad, reduce_sum, expand_sum, cross_sum)
-    output_share = outer_sum(self_mixed, branch_one)
-    low_grads = self_backward(low, first, self_logs, qkv, self_mixed, mixed_grad, row_count, 0)
-    low_grads, mixed_grad = fence((low_grads, mixed_grad), reduce_sum, expand_sum)
-    high_grads = self_backward(low, first, self_logs, qkv, self_mixed, mixed_grad, row_count, 1)
-    high_grads = fence(high_grads, expand_sum, cross_sum)
-    if mesh_axes[0][1] == 8 and row_count == 1:
-        high_grads = fence(high_grads, cross_sum)
-        tokens_grad, last_shard, norm_grads = tail(
-            output_share, normed_one, low_grads, high_grads, tokens, self_total, norms, norm_two, norm_three, early, mesh_axes
+    reduce_share, expand_share = outer_sum(activated, branch_three), outer_sum(normed_three, hidden_grad)
+    if mesh_axes[0][1] == 8 and row_count == 1 and quarters == 4 and shard_rows % 32 == 0:
+        narrow = mesh_axes[1][1]
+        cq_grad, ckv_grad, self_total, branch_one, mixed_grad, memory_grad, norm_two, reduce_shard = cross_back(
+            bounds, cross_logs, cross_q, cross_kv, cross_mixed, mixed_grad, after_self, cross_total, norms, early, reduce_share, narrow
         )
-        output_shard, qkv_shard = last_shard[:, :WIDTH], last_shard[:, WIDTH:]
+        cross_shares = [outer_sum(cross_mixed, branch_two), outer_sum(normed_two, cq_grad)]
+        cross_shares += [outer_sum(memory, part) for part in (ckv_grad[:, :WIDTH], ckv_grad[:, WIDTH:])]
+        qkv_grad, shards = self_back(first, self_logs, qkv, self_mixed, mixed_grad, expand_share, cross_shares, narrow)
+        expand_shards, cross_shards = shards[:4], shards[4:]
+        tokens_grad, last_shards, norm_grads = tail(
+            outer_sum(self_mixed, branch_one),
+            normed_one,
+            qkv_grad,
+            tokens,
+            self_total,
+            norms,
+            norm_two,
+            norm_three,
+            early,
+            mesh_axes,
+        )
     else:
-        qkv_grad = jnp.concatenate([low_grads, high_grads], axis=1)
-        last_sum = staged(output_share, *[outer_sum(normed_one, qkv_grad[:, n * WIDTH : (n + 1) * WIDTH]) for n in range(3)])
+        reduce_sum, expand_sum = staged(reduce_share), staged(expand_share)
+        cq_grad, ckv_grad = cross_backward(bounds, cross_logs, cross_q, cross_kv, cross_mixed, mixed_grad, row_count)
+        cq_grad, ckv_grad = fence((cq_grad, ckv_grad), reduce_sum, expand_sum)
+        cross_shares = [outer_sum(cross_mixed, branch_two), outer_sum(normed_two, cq_grad)]
+        cross_shares += [outer_sum(memory, part) for part in (ckv_grad[:, :WIDTH], ckv_grad[:, WIDTH:])]
+        cross_sum = staged(*cross_shares)
+        self_total, branch_one, mixed_grad, memory_grad, norm_two = cross_close(
+            cq_grad, ckv_grad, after_self, cross_total, norms, early
+        )
+        mixed_grad = fence(mixed_grad, reduce_sum, expand_sum, cross_sum)
+        qkv_grad = self_backward(first, self_logs, qkv, self_mixed, mixed_grad, row_count)
+        qkv_grad = fence(qkv_grad, reduce_sum, expand_sum, cross_sum)
+        last_sum = staged(
+            outer_sum(self_mixed, branch_one),
+            *[outer_sum(normed_one, qkv_grad[:, n * WIDTH : (n + 1) * WIDTH]) for n in range(3)],
+        )
         tokens_grad, norm_one = self_close(qkv_grad, tokens, self_total, norms, early)
         norm_grads = sum_everywhere(jnp.concatenate([norm_one[:2], norm_two[:2], norm_three[:2]]), mesh_axes)
-        output_shard, *qkv_shards = last_sum.result().reshape(4, shard_rows, WIDTH)
-        qkv_shard = jnp.concatenate(qkv_shards, axis=1)
+        last_shards = last_sum.result().reshape(4, shard_rows, WIDTH)
+        reduce_shard = reduce_sum.result()
+        expand_shards = expand_sum.result().reshape(shard_rows, 4, -1).transpose(1, 0, 2)
+        cross_shards = cross_sum.result().reshape(4, shard_rows, WIDTH)
+
     norm_shards = lax.dynamic_slice_in_dim(norm_grads, device * shard_rows, shard_rows, axis=1)
-    reduce_shard = reduce_sum.result()
-    expand_shard = expand_sum.result()
+    reduce_shard = reduce_shard.reshape(-1, WIDTH)
     expand_shard = (
-        expand_shard.reshape(shard_rows, quarters, device_count, -1).transpose(0, 2, 1, 3).reshape(shard_rows, -1)
+        expand_shards.reshape(quarters, shard_rows, device_count, -1).transpose(1, 2, 0, 3).reshape(shard_rows, -1)
     )
-    cross_shards = cross_sum.result().reshape(4, shard_rows, WIDTH)
+    output_shard = last_shards[0]
+    query_shard, key_shard, value_shard = from_pairs(jnp.concatenate(list(last_shards[1:]), axis=1), 3)
     cross_key_shard, cross_value_shard = from_pairs(jnp.concatenate([cross_shards[2], cross_shards[3]], axis=1), 2)
-    query_shard, key_shard, value_shard = from_pairs(qkv_shard, 3)
     return (
         layer_output,
         tokens_grad,

time: 633 us -> 559 us (0.88)
  local copies, waits for them, and re-layouts: 74.8 us -> 36 us
  starting transfers between devices: 31.8 us -> 0.04 us
  Pallas kernels: 422 us -> 453 us
  other arithmetic: 28 us -> 2.42 us
  waiting for transfers between devices: 9.87 us -> 0.02 us
    ppermute x24 -> x0, starting transfers between devices: 31.8 us -> none  [trade(): return lax.ppermute(value, axis, [(i, i ^ mask) for i in range(size)])]
    pallas_call x6 -> x4, Pallas kernels: 163 us -> 189 us  [the longest x1 89.8 us: self_back(): pl.pallas_call(functools.partial(self_back_kernel, narrow), grid=(PAIRS,)...]
    convert_element_type x15 -> x0, other arithmetic: 21 us -> none  [the longest x3 13 us: sum_steps(): value = value.astype(BF16)]
    squeeze x15 -> x1, local copies, waits for them, and re-layouts: 19.2 us -> 0.7 us  [on_device(): output_shard = last_shards[0]]
    ppermute x24 -> x0, waiting for transfers between devices: 9.86 us -> none  [trade(): return lax.ppermute(value, axis, [(i, i ^ mask) for i in range(size)])]
    optimization_barrier x2 -> x0, local copies, waits for them, and re-layouts: 7.87 us -> none  [on_device(): cq_grad, shares = lax.optimization_barrier((cq_grad, shares))]
    unnamed x182 -> x117, local copies, waits for them, and re-layouts: 22.9 us -> 15.6 us
  transfers between devices with their start and end apart: 25 -> 1, of which waited for: 1 -> 0; matrix products, arithmetic and copies ran while one was open for 11% -> 1% of each run, Pallas kernels for 58% -> 34%
where the time goes in v3:
time: 559 us; the launch traced here: 554 us
  Pallas kernels  453 us (81%)
  matrix products  44.6 us (8%)
  local copies, waits for them, and re-layouts  36 us (6%)
  between operations  17.8 us (3%)
    pallas_call x1, Pallas kernels, early_gather(): pl.pallas_call(functools.partial(early_gather_kernel, wide, narrow), in_s...  124 us
    pallas_call x1, Pallas kernels, self_back(): pl.pallas_call(functools.partial(self_back_kernel, narrow), grid=(PAIRS,)...  89.8 us
    pallas_call x1, Pallas kernels, cross_back(): pl.pallas_call(functools.partial(cross_back_kernel, narrow), grid=(PAIRS...  61.5 us
    pallas_call x1, Pallas kernels, tail(): pl.pallas_call(functools.partial(tail_kernel, narrow), in_specs=[anywhere...  59.5 us
    pallas_call x1, Pallas kernels, feed(): pl.pallas_call(feed_kernel, grid=(rows // TB,), in_specs=[smem, smem, til...  56.8 us
    dot_general x7, matrix products, outer_sum(): jnp.einsum('td,te->de', left_side, gradient, preferred_element_type=F32)  44.6 us
    pallas_call x2, Pallas kernels, attention_call(): pl.pallas_call(kernel, grid=(row_count, PAIRS), in_specs=in_specs, out_sp...  37.5 us
    unnamed x117, local copies, waits for them, and re-layouts  15.6 us
  transfers between devices with their start and end apart: 1, of which 0 were waited for; matrix products, arithmetic and copies ran while one was open for 1% of the time, Pallas kernels for 34%

profile of v3, /device:TPU:0, one launch (start us, length us, event | category | flops | bytes accessed | tf_op | source)
XLA Modules:
  0.0 554.3 jit_solution(15769620163356092544)
XLA Ops:
  7.2 1.7 reshape.405
  9.4 1.1 reshape.406
  16.4 124.3 %early_gather.1.weight_ref.wo_ref.wq_ref.wkv_ref.early_any.weight_any = bf16[1024,8320]{1,0:T(8,128)(2,1)} custom-call(bf16[32,8320]{1,0:T(8,128)(2,1)} %copy-done.20), custom_call_target="tpu_custom_call" | custom-call | bytes 209715200 | tf_op jit(solution)/shard_map/early_gather/pallas_call | solution.py:660
  140.7 1.0 slice.98
  143.8 11.4 %project.1 = (bf16[1024,1024]{1,0:T(8,128)(2,1)S(1)}, bf16[1024,3072]{1,0:T(8,128)(2,1)S(1)}) custom-call(bf16[1024,1024]{1,0:T(8,128)(2,1)S(1)} %copy-done, f32[8,1024]{1,0:T(8,128)S(1)} %convert_bitcast_fusion.norms_ref, bf16[1024,8320]{1,0:T(8,128)(2,1)} %early_gather.1.weight_ref.wo_ref.wq_ref.wkv_ref.early_any.weight_any), custom_call_target="tpu_custom_call" | custom-call | flops 6442450944 | bytes 16777216 | tf_op jit(solution)/shard_map/project/pallas_call | solution.py:327
  155.2 19.2 %self_forward.1 = (bf16[1024,1024]{1,0:T(8,128)(2,1)S(1)}, f32[1,8,8,1024]{3,2,1,0:T(8,128)S(1)}) custom-call(s32[1,1,1024]{2,1,0:T(1,128)S(1)} %get-tuple-element.108.first_ref, bf16[1024,3072]{1,0:T(8,128)(2,1)S(1)} %get-tuple-element.51.qkv_ref), custom_call_target="tpu_custom_call" | custom-call | flops 21474836480 | bytes 8388608 | tf_op jit(solution)/shard_map/self_forward/pallas_call | solution.py:150
  174.5 12.6 %middle.1 = (f32[1024,1024]{1,0:T(8,128)}, bf16[1024,1024]{1,0:T(8,128)(2,1)S(1)}, bf16[1024,1024]{1,0:T(8,128)(2,1)S(1)}, bf16[512,2048]{1,0:T(8,128)(2,1)S(1)}) custom-call(bf16[1024,1024]{1,0:T(8,128)(2,1)S(1)} %get-tuple-element.52.mixed_ref, bf16[1024,1024]{1,0:T(8,128)(2,1)S(1)} %copy-done, bf16[512,1024]{1,0:T(8,128)(2,1)S(1)} %copy-done.3, ...), custom_call_target="tpu_custom_call" | custom-call | flops 6442450944 | bytes 20971520 | tf_op jit(solution)/shard_map/middle/pallas_call | solution.py:356
  187.1 1.3 copy-done.7
  188.4 18.3 %cross_forward.1 = (bf16[1024,1024]{1,0:T(8,128)(2,1)S(1)}, f32[1,8,8,1024]{3,2,1,0:T(8,128)S(1)}) custom-call(s32[1,8,1024]{2,1,0:T(8,128)S(1)} %pad.14.bounds_ref, bf16[1024,1024]{1,0:T(8,128)(2,1)S(1)} %get-tuple-element.53.q_ref, bf16[512,2048]{1,0:T(8,128)(2,1)S(1)} %get-tuple-element.54.kv_ref), custom_call_target="tpu_custom_call" | custom-call | flops 21474836480 | bytes 8388608 | tf_op jit(solution)/shard_map/cross_forward/pallas_call | solution.py:150
  206.7 1.3 copy-done.9
  208.0 1.5 copy-done.10
  209.5 1.3 copy-done.13
  211.5 56.8 %feed.1 = (bf16[1024,1024]{1,0:T(8,128)(2,1)}, bf16[1024,1024]{1,0:T(8,128)(2,1)}, bf16[1024,4096]{1,0:T(8,128)(2,1)}, bf16[1024,4096]{1,0:T(8,128)(2,1)}, bf16[...) custom-call(s32[1]{0:T(128)} %copy.120.live_ref, ...), custom_call_target="tpu_custom_call" | custom-call | flops 40802189312 | bytes 52428800 | tf_op jit(solution)/shard_map/feed/pallas_call | solution.py:441
  268.3 15.5 %convolution_convert_fusion.1 = bf16[4096,1024]{1,0:T(8,128)(2,1)} fusion(bf16[1024,4096]{1,0:T(8,128)(2,1)} %get-tuple-element.61, bf16[1024,1024]{1,0:T(8,128)(2,1)} %get-tuple-element.62), kind=kOutput, calls=%fused_computation.1 | convolution fusion | flops 8594128896 | bytes 18874368 | tf_op jit(solution)/shard_map/td,te->de/dot_general | solution.py:801
  283.8 61.5 %cross_back.1 = (bf16[1024,1024]{1,0:T(8,128)(2,1)}, bf16[512,2048]{1,0:T(8,128)(2,1)}, f32[1024,1024]{1,0:T(8,128)}, bf16[1024,1024]{1,0:T(8,128)(2,1)}, bf16[1...) custom-call(s32[1,8,1024]{2,1,0:T(8,128)} %copy-done.5, ...), custom_call_target="tpu_custom_call" | custom-call | flops 42949672960 | bytes 104857600 | tf_op jit(solution)/shard_map/cross_back/pallas_call | solution.py:1071
  345.3 4.1 convolution_convert_fusion.2
  349.4 2.6 convolution_convert_fusion.3
  352.0 3.8 convolution_convert_fusion.5
  355.8 3.8 convolution_convert_fusion.4
  359.6 11.2 %convolution_convert_fusion = bf16[1024,4096]{1,0:T(8,128)(2,1)} fusion(bf16[1024,1024]{1,0:T(8,128)(2,1)S(1)} %copy-done.46, bf16[1024,4096]{1,0:T(8,128)(2,1)S(1)} %bitcast.127), kind=kOutput, calls=%fused_computation | convolution fusion | flops 8594128896 | bytes 18874368 | tf_op jit(solution)/shard_map/td,te->de/dot_general | solution.py:801
  370.8 89.8 %self_back.1 = (bf16[1024,3072]{1,0:T(8,128)(2,1)}, f32[8,32,1024]{2,1,0:T(8,128)}) custom-call(s32[1,1,1024]{2,1,0:T(1,128)} %copy-done.6, f32[1,8,8,1024]{3,2,1,0:T(8,128)} %copy-done.15, bf16[1024,3072]{1,0:T(8,128)(2,1)} %copy-done.11, bf16[1024,1024]{1,0:T(8,128)(2,1)} %copy-done.1, bf16[1024,1024]{1,0:T(8,128)(2,1)} %get-tuple-element.66.grad_ref, ...), custom_call_target="tpu_custom_call" | custom-call | flops 42949672960 | bytes 104857600 | tf_op jit(solution)/shard_map/self_back/pallas_call | solution.py:1185
  460.6 1.2 slice.118
  461.9 1.8 slice_bitcast_fusion
  463.7 3.7 convolution_convert_fusion.6
  467.4 59.5 %tail.1 = (bf16[1024,1024]{1,0:T(8,128)(2,1)}, f32[4,32,1024]{2,1,0:T(8,128)}, f32[8,1024]{1,0:T(8,128)}) custom-call(bf16[2,2,2,4,32,1024]{5,4,3,2,1,0:T(8,128)(2,1)} %bitcast.125, bf16[1024,1024]{1,0:T(8,128)(2,1)} %copy-done.12, bf16[1024,3072]{1,0:T(8,128)(2,1)} %get-tuple-element.73.grads_any, ...), custom_call_target="tpu_custom_call" | custom-call | flops 12884901888 | bytes 104857600 | tf_op jit(solution)/shard_map/tail/pallas_call | solution.py:1387
  527.0 0.8 constant_dynamic-slice_fusion
  531.7 1.0 slice_reduce_fusion.2
  535.4 3.1 copy.88
  538.5 4.6 reshape.416
  543.1 1.3 copy.121
  545.1 1.0 copy.122
  546.5 0.8 copy.123
  (150 shorter events, 13.7 us)
Async XLA Ops:
  7.2 204.3 %all-gather.2.cloned.1.call-start = ((), (), s32[]{:S(2)}) async-start(), calls=%async_computation | async-start | bytes 17301504 | tf_op jit(solution)/shard_map/all_gather | solution.py:1479
  9.0 4.5 copy-start.41
  9.0 4.6 copy-start.35
  9.0 4.6 copy-start.36
  9.0 4.6 copy-start.37
  9.0 4.6 copy-start.38
  9.0 4.6 copy-start.39
  9.1 4.6 copy-start.40
  9.1 4.8 copy-start.34
  9.1 5.0 copy-start.24
  9.3 4.9 copy-start.25
  9.3 4.9 copy-start.26
  9.3 5.6 %copy-start.27 = (bf16[32,1024]{1,0:T(8,128)(2,1)S(1)}, bf16[32,1024]{1,0:T(8,128)(2,1)}, u32[]{:S(2)}) copy-start(bf16[32,1024]{1,0:T(8,128)(2,1)} %param.37) | copy-start | bytes 196612
  10.5 4.6 copy-start.28
  10.6 5.0 copy-start.29
  10.6 5.0 copy-start.30
  10.6 5.0 copy-start.31
  14.1 141.1 %copy-start.6 = (s32[1,1,1024]{2,1,0:T(1,128)}, s32[1,1,1024]{2,1,0:T(1,128)S(1)}, u32[]{:S(2)}) copy-start(s32[1,1,1024]{2,1,0:T(1,128)S(1)} %get-tuple-element.108.first_ref) | copy-start | bytes 12292
  14.1 174.3 %copy-start.5 = (s32[1,8,1024]{2,1,0:T(8,128)}, s32[1,8,1024]{2,1,0:T(8,128)S(1)}, u32[]{:S(2)}) copy-start(s32[1,8,1024]{2,1,0:T(8,128)S(1)} %pad.14.bounds_ref) | copy-start | bytes 98308
  16.4 127.4 %copy-start = (bf16[1024,1024]{1,0:T(8,128)(2,1)S(1)}, bf16[1024,1024]{1,0:T(8,128)(2,1)}, u32[]{:S(2)}) copy-start(bf16[1024,1024]{1,0:T(8,128)(2,1)} %tokens_any.1) | copy-start | bytes 6291460
  141.8 32.6 %copy-start.4 = (f32[8,1024]{1,0:T(8,128)}, f32[8,1024]{1,0:T(8,128)S(1)}, u32[]{:S(2)}) copy-start(f32[8,1024]{1,0:T(8,128)S(1)} %convert_bitcast_fusion.norms_ref) | copy-start | bytes 98308
  155.2 19.2 %copy-start.11 = (bf16[1024,3072]{1,0:T(8,128)(2,1)}, bf16[1024,3072]{1,0:T(8,128)(2,1)S(1)}, u32[]{:S(2)}) copy-start(bf16[1024,3072]{1,0:T(8,128)(2,1)S(1)} %get-tuple-element.51.qkv_ref) | copy-start | bytes 18874372
  155.2 19.2 %copy-start.12 = (bf16[1024,1024]{1,0:T(8,128)(2,1)}, bf16[1024,1024]{1,0:T(8,128)(2,1)S(1)}, u32[]{:S(2)}) copy-start(bf16[1024,1024]{1,0:T(8,128)(2,1)S(1)} %get-tuple-element.64.normed_any) | copy-start | bytes 6291460
  155.2 19.2 %copy-start.3 = (bf16[512,1024]{1,0:T(8,128)(2,1)S(1)}, bf16[512,1024]{1,0:T(8,128)(2,1)}, u32[]{:S(2)}) copy-start(bf16[512,1024]{1,0:T(8,128)(2,1)} %memory_ref.1) | copy-start | bytes 3145732
  174.4 12.6 %copy-start.1 = (bf16[1024,1024]{1,0:T(8,128)(2,1)}, bf16[1024,1024]{1,0:T(8,128)(2,1)S(1)}, u32[]{:S(2)}) copy-start(bf16[1024,1024]{1,0:T(8,128)(2,1)S(1)} %get-tuple-element.52.mixed_ref) | copy-start | bytes 6291460
  174.4 12.6 %copy-start.15 = (f32[1,8,8,1024]{3,2,1,0:T(8,128)}, f32[1,8,8,1024]{3,2,1,0:T(8,128)S(1)}, u32[]{:S(2)}) copy-start(f32[1,8,8,1024]{3,2,1,0:T(8,128)S(1)} %get-tuple-element.65.log_ref) | copy-start | bytes 786436
  345.3 4.1 copy-start.42
  352.0 7.6 %slice-start = ((s8[8388608]{0:T(1024)(128)(4,1)}), s8[4194304]{0:T(1024)(128)(4,1)S(1)}, s32[]{:S(2)}) async-start(s8[8388608]{0:T(1024)(128)(4,1)} %bitcast.126), calls=%async_computation.1 | async-start | bytes 8388608
  355.8 3.8 slice-start.1
  355.8 3.8 copy-start.46
  370.8 92.9 %copy-start.43 = (bf16[1024,1024]{1,0:T(8,128)(2,1)S(1)}, bf16[1024,1024]{1,0:T(8,128)(2,1)}, u32[]{:S(2)}) copy-start(bf16[1024,1024]{1,0:T(8,128)(2,1)} %get-tuple-element.63) | copy-start | bytes 6291460
  538.5 4.6 copy-start.17
  (18 other events, 38.6 us)
Sparse Core Ops, SparseCore 0:
  11.6 155.6 all-gather.1

commit v4 on v3

--- a/solution.py
+++ b/solution.py
@@ -420,9 +420,9 @@
         act = (x * half).astype(BF16)
         slope = half + (0.5 * GELU_A) * x * (1.0 - t * t) * (1.0 + (3.0 * GELU_B) * square)
         act_ref[:, at] = act
-        hid = (mm_t(branch, wout_ref[:, at]) * slope).astype(BF16)
+        hid = (mm_t(branch, wout_ref[at, :]) * slope).astype(BF16)
         hid_ref[:, at] = hid
-        result = result + mm(act, wout_ref[:, at])
+        result = result + mm(act, wout_ref[at, :])
         term = mm_t(hid, win_ref[:, at])
         back = term if back is None else back + term
     out_ref[...] = result.astype(BF16)
@@ -436,7 +436,7 @@
 
 def feed(live_length, row_weight, mixed, before, cotangent, norms, early, late):
     rows, d = cotangent.shape
-    ff = late.shape[1] // 2
+    ff = late[0].shape[1]
     smem = pl.BlockSpec(memory_space=pltpu.SMEM)
     return pl.pallas_call(
         feed_kernel,
@@ -449,8 +449,8 @@
             tile(TB, d),
             whole(8, d),
             whole(d, d, OUT_CROSS),
-            whole(d, ff, 0),
-            whole(d, ff, 1),
+            whole(d, ff),
+            whole(ff, d),
         ],
         out_specs=[
             tile(TB, d),
@@ -477,7 +477,7 @@
         name="feed",
         compiler_params=params(58),
         cost_estimate=cost(38 * rows * d * d, 50 << 20),
-    )(live_length, row_weight, mixed, before, cotangent, norms, early, late, late)
+    )(live_length, row_weight, mixed, before, cotangent, norms, early, *late)
 
 
 def cross_close_kernel(
@@ -805,8 +805,8 @@
 
 
 class Scatter:
-    def __init__(self, own, theirs, buffers, out_ref, send_sems, recv_sems, narrow):
-        self.own, self.theirs, self.out_ref = own, theirs, out_ref
+    def __init__(self, own, theirs, buffers, keep, send_sems, recv_sems, narrow):
+        self.own, self.theirs, self.keep = own, theirs, keep
         self.from_core, self.a1, self.b1, self.a2, self.b2, self.from_line = buffers
         self.send_sems, self.recv_sems = send_sems, recv_sems
         self.narrow = narrow
@@ -862,7 +862,7 @@
 
     def add(self, i, y, x, columns, piece):
         now = self.own[i, y, x, :, :, columns]
-        self.own[i, y, x, :, :, columns] = (now.astype(F32) + piece.astype(F32)).astype(BF16)
+        self.own[i, y, x, :, :, columns] = now + piece
 
     def step(self, i, stage):
         both, left, right = slice(None), slice(0, self.half), slice(self.half, None)
@@ -894,7 +894,7 @@
             total = self.own[i, self.y, self.x, self.z].astype(F32)
             for mask in range(1, self.narrow):
                 total = total + self.from_line[i, mask - 1].astype(F32)
-            self.out_ref[i] = total
+            self.keep(i, total)
 
     def close(self, i):
         for copy in (self.to_core(i), *self.first(i), *self.second(i), *self.along(i)):
@@ -918,15 +918,17 @@
 
 
 class Carried:
-    def __init__(self, shares, scratch, out_ref, narrow):
+    def __init__(self, shares, scratch, keep, narrow):
         own, *buffers, send_sems, recv_sems, self.load_sems = scratch
         self.shares = shares
-        self.scatter = Scatter(own, lambda i: self.part(i, 1 - self.scatter.c), buffers, out_ref, send_sems, recv_sems, narrow)
+        self.scatter = Scatter(own, self.other, buffers, keep, send_sems, recv_sems, narrow)
         self.chunks = own.shape[0]
 
     def part(self, i, core):
-        ref, at, width = self.shares[i]
-        return ref.at[:, :, core, :, :, pl.ds(at, width)]
+        return self.shares[i](core)
+
+    def other(self, i):
+        return self.part(i, 1 - self.scatter.c)
 
     def load(self, i):
         return pltpu.make_async_copy(self.part(i, self.scatter.c), self.scatter.own.at[i], self.load_sems.at[i])
@@ -935,7 +937,7 @@
         for i in range(self.chunks):
             self.load(i).start()
         greet_all(self.scatter.narrow)
-        for i in range(self.chunks):
+        for i in range(2):
             self.scatter.begin(i)
 
     def steps(self, plan):
@@ -943,6 +945,8 @@
             if stage == 0:
                 self.load(i).wait()
             self.scatter.step(i, stage)
+            if stage == 0 and i + 2 < self.chunks:
+                self.scatter.begin(i + 2)
 
     def close(self):
         for i in range(self.chunks):
@@ -951,6 +955,23 @@
 
 def share_views(array, narrow, rows):
     return array.reshape(2, 2, 2, narrow, rows, array.shape[1])
+
+
+def share_views(array, narrow, rows):
+    return array.reshape(2, 2, 2, narrow, rows, array.shape[1])
+
+
+def columns_of(ref, at, width):
+    return lambda core: ref.at[:, :, core, :, :, pl.ds(at, width)]
+
+
+def tn(a, b):
+    return lax.dot_general(a, b, (((0,), (0,)), ((), ())), preferred_element_type=F32)
+
+
+def outer_into(out_ref, left_ref, right):
+    for at in range(0, left_ref.shape[1], 256):
+        out_ref[at : at + 256, :] = tn(left_ref[:, at : at + 256], right).astype(BF16)
 
 
 CROSS_PLAN = (
@@ -959,14 +980,20 @@
     ((0, 1),),
     ((3, 0),),
     ((1, 1),),
-    ((2, 1), (0, 2)),
+    ((0, 2), (4, 0)),
+    ((2, 1),),
     ((1, 2),),
-    ((3, 1),),
-    ((2, 2), (0, 3)),
-    ((1, 3),),
+    ((0, 3), (3, 1), (5, 0)),
+    ((2, 2),),
+    ((1, 3), (4, 1)),
     ((3, 2),),
-    ((2, 3), (3, 3)),
+    ((2, 3),),
+    ((5, 1),),
+    ((4, 2),),
+    ((3, 3),),
+    ((5, 2), (4, 3), (5, 3)),
 )
+CROSS_WIDE = 2
 
 
 def cross_back_kernel(
@@ -975,23 +1002,31 @@
     log_ref,
     q_ref,
     kv_ref,
-    mixed_ref,
+    mixed_pair_ref,
     grad_ref,
     before_ref,
     total_ref,
     norms_ref,
+    mixed_ref,
+    b2_ref,
+    normed_ref,
+    memory_ref,
+    self_mixed_ref,
     early_any,
     share_any,
-    dq_ref,
-    dkv_ref,
+    wide_any,
     out_ref,
-    b1_ref,
     next_ref,
     mem_ref,
     ngrad_ref,
+    shares_ref,
     shard_ref,
+    wide_ref,
     dk_ref,
     dv_ref,
+    dq_ref,
+    dkv_ref,
+    b1_ref,
     wq,
     wkv,
     wo,
@@ -1000,9 +1035,19 @@
 ):
     step = pl.program_id(0)
     d = wq.shape[0]
-    width = shard_ref.shape[-1]
-    chunks = shard_ref.shape[0]
-    carried = Carried([(share_any.at[i], 0, width) for i in range(chunks)], scratch, shard_ref, narrow)
+    rows = shard_ref.shape[0] // 4
+
+    def keep(i, value):
+        if i < 4:
+            shard_ref[i * rows : (i + 1) * rows, :] = value
+        else:
+            wide_ref[:, (i - 4) * d : (i - 3) * d] = value
+
+    def piece(i):
+        return lambda core: share_any.at[:, :, core, :, i]
+
+    pieces = [piece(i) for i in range(4)] + [columns_of(wide_any, i * d, d) for i in range(CROSS_WIDE)]
+    carried = Carried(pieces, scratch, keep, narrow)
     loads = [
         pltpu.make_async_copy(early_any.at[:, pl.ds(QUERY_CROSS * d, d)], wq, weight_sems.at[0]),
         pltpu.make_async_copy(early_any.at[:, pl.ds(2 * KV_CROSS * d, 2 * d)], wkv, weight_sems.at[1]),
@@ -1020,7 +1065,7 @@
         def keep_dq(rows, value):
             dq_ref[rows, pl.ds(pl.multiple_of(step * 128, 128), 128)] = value
 
-        cross_backward_pair(bounds_ref, log_ref, q_ref, kv_ref, mixed_ref, grad_ref, keep_dq, None, dk_ref, dv_ref)
+        cross_backward_pair(bounds_ref, log_ref, q_ref, kv_ref, mixed_pair_ref, grad_ref, keep_dq, None, dk_ref, dv_ref)
         at = pl.multiple_of(step * 256, 256)
         dkv_ref[:, pl.ds(at, 128)] = (dk_ref[...] * HEAD_DIM**-0.5).astype(BF16)
         dkv_ref[:, pl.ds(pl.multiple_of(at + 128, 128), 128)] = dv_ref[...].astype(BF16)
@@ -1031,30 +1076,38 @@
             load.wait()
         ngrad_ref[...] = jnp.zeros_like(ngrad_ref)
 
-    @pl.when(step >= PAIRS)
+    tokens_end = PAIRS + SEQ // TB
+
+    @pl.when((step >= PAIRS) & (step < tokens_end))
     def _():
         t = step - PAIRS
         mb = mem_ref.shape[0]
-        gradient = mm_t(dq_ref[pl.ds(pl.multiple_of(t * TB, TB), TB), :], wq[...])
+        at = pl.ds(pl.multiple_of(t * TB, TB), TB)
+        gradient = mm_t(dq_ref[at, :], wq[...])
         mem_ref[...] = mm_t(dkv_ref[pl.ds(pl.multiple_of(t * mb, mb), mb), :], wkv[...]).astype(BF16)
         unit, inverse = norm_parts(before_ref[...])
         total = total_ref[...] + norm_back(unit, inverse, norms_ref[2:3, :], gradient)
         out_ref[...] = total
         b1 = total.astype(BF16)
-        b1_ref[...] = b1
+        b1_ref[at, :] = b1
         next_ref[...] = mm_t(b1, wo[...]).astype(BF16)
         ngrad_ref[0:1, :] += jnp.sum(gradient * unit, axis=0, keepdims=True)
         ngrad_ref[1:2, :] += jnp.sum(gradient, axis=0, keepdims=True)
 
+    pl.when(step == tokens_end)(lambda: outer_into(shares_ref, mixed_ref, b2_ref[...]))
+    pl.when(step == tokens_end + 1)(lambda: outer_into(shares_ref, normed_ref, dq_ref[...]))
+    pl.when(step == tokens_end + 2)(lambda: outer_into(shares_ref, memory_ref, dkv_ref[:, :d]))
+    pl.when(step == tokens_end + 3)(lambda: outer_into(shares_ref, memory_ref, dkv_ref[:, d:]))
+    pl.when(step == tokens_end + 4)(lambda: outer_into(shares_ref, self_mixed_ref, b1_ref[...]))
+
     for number, plan in enumerate(CROSS_PLAN):
         pl.when(step == number)(functools.partial(carried.steps, plan))
     pl.when(step == len(CROSS_PLAN) - 1)(carried.close)
 
 
-def cross_back(bounds, logs, q, kv, mixed, grad, before, total, norms, early, share, narrow):
+def cross_back(bounds, logs, q, kv, mixed, grad, before, total, norms, b2, normed, memory, self_mixed, early, share, wide_share, narrow):
     rows, d = q.shape
     mem_rows = kv.shape[0]
-    chunks = share.shape[0] // d
     shard_rows = d // (8 * narrow)
     steps = rows // TB
     mb = mem_rows // steps
@@ -1063,14 +1116,14 @@
         return jnp.minimum(s, PAIRS - 1)
 
     def token(s):
-        return jnp.maximum(s - PAIRS, 0)
+        return jnp.clip(s - PAIRS, 0, steps - 1)
 
     anywhere = pl.BlockSpec(memory_space=pl.ANY)
     by_pair = pl.BlockSpec((SEQ, 128), lambda s: (0, pair(s)))
     by_token = pl.BlockSpec((TB, d), lambda s: (token(s), 0))
     return pl.pallas_call(
         functools.partial(cross_back_kernel, narrow),
-        grid=(PAIRS + steps,),
+        grid=(PAIRS + steps + 5,),
         in_specs=[
             pl.BlockSpec((1, 8, SEQ), lambda s: (0, 0, 0)),
             pl.BlockSpec((1, 1, 8, SEQ), lambda s: (0, pair(s), 0, 0)),
@@ -1081,40 +1134,47 @@
             by_token,
             by_token,
             whole(8, d),
+            whole(rows, d),
+            whole(rows, d),
+            whole(rows, d),
+            whole(mem_rows, d),
+            whole(rows, d),
             anywhere,
             anywhere,
+            anywhere,
         ],
         out_specs=[
-            whole(rows, d),
-            whole(mem_rows, 2 * d),
-            by_token,
             by_token,
             by_token,
             pl.BlockSpec((mb, d), lambda s: (token(s), 0)),
             whole(8, d),
-            pl.BlockSpec((chunks, shard_rows, d), lambda s: (0, 0, 0), pipeline_mode=pl.Buffered(1)),
+            pl.BlockSpec((d, d), lambda s: (jnp.maximum(s - PAIRS - steps, 0), 0)),
+            whole(4 * shard_rows, d),
+            whole(shard_rows, CROSS_WIDE * d),
         ],
         out_shape=[
-            shape(rows, d, BF16),
-            shape(mem_rows, 2 * d, BF16),
             shape(rows, d, F32),
-            shape(rows, d, BF16),
             shape(rows, d, BF16),
             shape(mem_rows, d, BF16),
             shape(8, d, F32),
-            jax.ShapeDtypeStruct((chunks, shard_rows, d), F32),
+            shape(5 * d, d, BF16),
+            shape(4 * shard_rows, d, F32),
+            shape(shard_rows, CROSS_WIDE * d, F32),
         ],
         scratch_shapes=[
             pltpu.VMEM((MEM, 128), F32),
             pltpu.VMEM((MEM, 128), F32),
+            pltpu.VMEM((rows, d), BF16),
+            pltpu.VMEM((mem_rows, 2 * d), BF16),
+            pltpu.VMEM((rows, d), BF16),
             pltpu.VMEM((d, d), BF16),
             pltpu.VMEM((d, 2 * d), BF16),
             pltpu.VMEM((d, d), BF16),
             pltpu.SemaphoreType.DMA((3,)),
-            *scatter_scratch(chunks, narrow, shard_rows, d),
+            *scatter_scratch(4 + CROSS_WIDE, narrow, shard_rows, d),
         ],
         name="cross_back",
-        compiler_params=pltpu.CompilerParams(collective_id=2, has_side_effects=True, vmem_limit_bytes=58 << 20),
+        compiler_params=pltpu.CompilerParams(collective_id=2, has_side_effects=True, vmem_limit_bytes=60 << 20),
         cost_estimate=cost(40 * rows * d * d, 100 << 20),
     )(
         bounds,
@@ -1126,8 +1186,14 @@
         before,
         total,
         norms,
+        mixed,
+        b2,
+        normed,
+        memory,
+        self_mixed,
         early,
-        share.reshape(chunks, 2, 2, 2, narrow, shard_rows, d),
+        share.reshape(2, 2, 2, narrow, 4, shard_rows, d),
+        share_views(wide_share, narrow, shard_rows),
     )
 
 
@@ -1135,15 +1201,21 @@
     ((0, 0), (1, 0)),
     ((2, 0),),
     ((0, 1),),
-    ((3, 0), (1, 1)),
-    ((4, 0),),
-    ((2, 1), (0, 2)),
-    ((5, 0), (1, 2)),
-    (
-        ((3, 1), (2, 2), (6, 0), (0, 3), (4, 1), (3, 2), (1, 3), (7, 0), (5, 1), (4, 2), (2, 3))
-        + ((6, 1), (5, 2), (3, 3), (7, 1), (6, 2), (4, 3), (7, 2), (5, 3), (6, 3), (7, 3))
-    ),
+    ((3, 0),),
+    ((1, 1),),
+    ((0, 2), (4, 0)),
+    ((2, 1),),
+    ((1, 2), (5, 0), (3, 1)),
+    ((0, 3),),
+    ((2, 2), (6, 0)),
+    ((1, 3), (4, 1)),
+    ((3, 2),),
+    ((2, 3), (5, 1)),
+    ((4, 2),),
+    ((3, 3), (6, 1), (5, 2), (4, 3), (6, 2), (5, 3), (6, 3)),
 )
+SELF_WIDE = 4 - CROSS_WIDE
+SELF_CHUNKS = SELF_WIDE + 5
 
 
 def self_back_kernel(
@@ -1153,55 +1225,162 @@
     qkv_ref,
     mixed_ref,
     grad_ref,
+    normed_ref,
+    tokens_ref,
+    total_ref,
+    norms_ref,
+    early_any,
     wide_any,
-    a_any,
-    b_any,
-    c_any,
-    d_any,
-    dqkv_ref,
-    shard_ref,
+    shares_any,
+    qkv_share_ref,
+    out_ref,
+    ngrad_ref,
+    expand_ref,
+    cross_output_ref,
+    cross_query_ref,
+    cross_key_ref,
+    cross_value_ref,
+    self_output_ref,
     dk_ref,
     dv_ref,
+    dqkv,
+    weight,
+    weight_sem,
     *scratch,
 ):
     step = pl.program_id(0)
-    width = shard_ref.shape[-1]
-    shares = [(wide_any, i * width, width) for i in range(4)]
-    shares += [(ref, 0, width) for ref in (a_any, b_any, c_any, d_any)]
-    carried = Carried(shares, scratch, shard_ref, narrow)
-    pl.when(step == 0)(carried.open)
-    self_backward_kernel(first_ref, log_ref, qkv_ref, mixed_ref, grad_ref, dqkv_ref, dk_ref, dv_ref)
+    d = normed_ref.shape[1]
+
+    def keep(i, value):
+        i -= SELF_WIDE
+        if i < 0:
+            expand_ref[:, (i + SELF_WIDE) * d : (i + SELF_WIDE + 1) * d] = value
+        elif i == 0:
+            cross_output_ref[...] = value
+        elif i == 1:
+            cross_query_ref[...] = value
+        elif i == 4:
+            self_output_ref[...] = value
+        else:
+            for n in range(d // 256):
+                at = (i - 2) * d // 2 + n * 128
+                cross_key_ref[:, at : at + 128] = value[:, n * 256 : n * 256 + 128]
+                cross_value_ref[:, at : at + 128] = value[:, n * 256 + 128 : n * 256 + 256]
+
+    def piece(i):
+        return lambda core: shares_any.at[i, :, :, core]
+
+    pieces = [columns_of(wide_any, (CROSS_WIDE + i) * d, d) for i in range(SELF_WIDE)] + [piece(i) for i in range(5)]
+    carried = Carried(pieces, scratch, keep, narrow)
+    load = pltpu.make_async_copy(early_any.at[:, pl.ds(0, 3 * d)], weight, weight_sem)
+
+    @pl.when(step == 0)
+    def _():
+        carried.open()
+        load.start()
+
+    @pl.when(step < PAIRS)
+    def _():
+        base = step * 384
+
+        def keep_dq(rows, value):
+            dqkv[rows, pl.ds(pl.multiple_of(base, 128), 128)] = value
+
+        attend_back(
+            lambda rows: qkv_ref[rows, 0:128],
+            qkv_ref[:, 128:256],
+            qkv_ref[:, 256:384],
+            grad_ref,
+            mixed_ref,
+            log_ref,
+            functools.partial(self_visible, first_ref),
+            self_extent,
+            keep_dq,
+            dk_ref,
+            dv_ref,
+        )
+        dqkv[:, pl.ds(pl.multiple_of(base + 128, 128), 128)] = (dk_ref[...] * HEAD_DIM**-0.5).astype(BF16)
+        dqkv[:, pl.ds(pl.multiple_of(base + 256, 128), 128)] = dv_ref[...].astype(BF16)
+
+    @pl.when((step >= PAIRS) & (step < PAIRS + 3))
+    def _():
+        at = pl.ds(pl.multiple_of((step - PAIRS) * d, d), d)
+        outer_into(qkv_share_ref, normed_ref, dqkv[:, at])
+
+    @pl.when(step == PAIRS + 3)
+    def _():
+        load.wait()
+        ngrad_ref[...] = jnp.zeros_like(ngrad_ref)
+
+    @pl.when(step >= PAIRS + 3)
+    def _():
+        at = pl.ds(pl.multiple_of((step - PAIRS - 3) * TB, TB), TB)
+        gradient = mm_t(dqkv[at, :], weight[...])
+        unit, inverse = norm_parts(tokens_ref[...].astype(F32))
+        total = total_ref[...] + norm_back(unit, inverse, norms_ref[0:1, :], gradient)
+        out_ref[...] = total.astype(BF16)
+        ngrad_ref[0:1, :] += jnp.sum(gradient * unit, axis=0, keepdims=True)
+        ngrad_ref[1:2, :] += jnp.sum(gradient, axis=0, keepdims=True)
+
     for number, plan in enumerate(SELF_PLAN):
         pl.when(step == number)(functools.partial(carried.steps, plan))
     pl.when(step == len(SELF_PLAN) - 1)(carried.close)
 
 
-def self_back(first, logs, qkv, mixed, grad, wide_share, shares, narrow):
+def self_back(first, logs, qkv, mixed, grad, normed, tokens, total, norms, early, wide_share, shares, narrow):
     rows, d = mixed.shape
     shard_rows = d // (8 * narrow)
+
+    def pair(s):
+        return jnp.minimum(s, PAIRS - 1)
+
+    def token(s):
+        return jnp.maximum(s - PAIRS - 3, 0)
+
     anywhere = pl.BlockSpec(memory_space=pl.ANY)
-    by_pair = pl.BlockSpec((SEQ, 128), lambda s: (0, s))
-    qkv_pair = pl.BlockSpec((SEQ, 384), lambda s: (0, s))
+    by_pair = pl.BlockSpec((SEQ, 128), lambda s: (0, pair(s)))
+    by_token = pl.BlockSpec((TB, d), lambda s: (token(s), 0))
     return pl.pallas_call(
         functools.partial(self_back_kernel, narrow),
-        grid=(PAIRS,),
+        grid=(PAIRS + 3 + rows // TB,),
         in_specs=[
             pl.BlockSpec((1, 1, SEQ), lambda s: (0, 0, 0)),
-            pl.BlockSpec((1, 1, 8, SEQ), lambda s: (0, s, 0, 0)),
-            qkv_pair,
+            pl.BlockSpec((1, 1, 8, SEQ), lambda s: (0, pair(s), 0, 0)),
+            pl.BlockSpec((SEQ, 384), lambda s: (0, pair(s))),
             by_pair,
             by_pair,
-            *[anywhere] * 5,
-        ],
-        out_specs=[qkv_pair, pl.BlockSpec((8, shard_rows, d), lambda s: (0, 0, 0), pipeline_mode=pl.Buffered(1))],
-        out_shape=[shape(rows, 3 * d, BF16), jax.ShapeDtypeStruct((8, shard_rows, d), F32)],
+            whole(rows, d),
+            by_token,
+            by_token,
+            whole(8, d),
+            anywhere,
+            anywhere,
+            anywhere,
+        ],
+        out_specs=[
+            pl.BlockSpec((d, d), lambda s: (0, jnp.clip(s - PAIRS, 0, 2))),
+            by_token,
+            whole(8, d),
+            whole(shard_rows, SELF_WIDE * d),
+            *[whole(shard_rows, d)] * 5,
+        ],
+        out_shape=[
+            shape(d, 3 * d, BF16),
+            shape(rows, d, BF16),
+            shape(8, d, F32),
+            shape(shard_rows, SELF_WIDE * d, F32),
+            *[shape(shard_rows, d, F32)] * 5,
+        ],
         scratch_shapes=[
             pltpu.VMEM((SEQ, 128), F32),
             pltpu.VMEM((SEQ, 128), F32),
-            *scatter_scratch(8, narrow, shard_rows, d),
+            pltpu.VMEM((rows, 3 * d), BF16),
+            pltpu.VMEM((d, 3 * d), BF16),
+            pltpu.SemaphoreType.DMA,
+            *scatter_scratch(SELF_CHUNKS, narrow, shard_rows, d),
         ],
         name="self_back",
-        compiler_params=pltpu.CompilerParams(collective_id=3, has_side_effects=True, vmem_limit_bytes=58 << 20),
+        compiler_params=pltpu.CompilerParams(collective_id=3, has_side_effects=True, vmem_limit_bytes=60 << 20),
         cost_estimate=cost(40 * rows * d * d, 100 << 20),
     )(
         first,
@@ -1209,107 +1388,49 @@
         qkv,
         mixed,
         grad,
+        normed,
+        tokens,
+        total,
+        norms,
+        early,
         share_views(wide_share, narrow, shard_rows),
-        *[share_views(s, narrow, shard_rows) for s in shares],
+        shares.reshape(5, 2, 2, 2, narrow, shard_rows, d),
     )
+
+
+TAIL_CHUNKS = 6
+TAIL_PLAN = [(0, 0), (1, 0)]
+for _k in range(TAIL_CHUNKS + 5):
+    TAIL_PLAN += [(_k + 2, 0)] if _k + 2 < TAIL_CHUNKS else []
+    TAIL_PLAN += [(_k, 1)] if _k < TAIL_CHUNKS else []
+    TAIL_PLAN += [(_k - 1, 2)] if 0 <= _k - 1 < TAIL_CHUNKS else []
+    TAIL_PLAN += [(_k - 3, 3)] if 0 <= _k - 3 < TAIL_CHUNKS else []
 
 
 def tail_kernel(
     narrow,
-    share_any,
-    normed_any,
-    grads_any,
-    weight_any,
-    tokens_any,
-    total_any,
-    norms_ref,
-    norm_two_ref,
-    norm_three_ref,
-    out_ref,
-    shard_ref,
+    norm_refs,
+    qkv_any,
+    query_ref,
+    key_ref,
+    value_ref,
     norm_out_ref,
-    normed,
-    normed_t,
-    grads,
-    weight,
-    tokens,
-    total,
-    share,
-    from_core,
-    a1,
-    b1,
-    a2,
-    b2,
-    from_line,
-    send_sems,
-    recv_sems,
     nval,
     nin,
     norm_send_sems,
     norm_recv_sems,
-    load_sems,
+    *scratch,
 ):
-    d = normed.shape[1]
-    width = share.shape[-1]
-    loads = [
-        pltpu.make_async_copy(share_any, share.at[0], load_sems.at[0]),
-        pltpu.make_async_copy(normed_any, normed, load_sems.at[1]),
-        *[
-            pltpu.make_async_copy(
-                grads_any.at[:, pl.ds(i * width, width)], grads.at[:, pl.ds(i * width, width)], load_sems.at[2 + i]
-            )
-            for i in range(3)
-        ],
-        pltpu.make_async_copy(weight_any.at[:, pl.ds(0, 3 * d)], weight, load_sems.at[5]),
-        pltpu.make_async_copy(tokens_any, tokens, load_sems.at[6]),
-        pltpu.make_async_copy(total_any, total, load_sems.at[7]),
-    ]
-    for load in loads:
-        load.start()
-    greet_all(narrow)
-    w, z = lax.axis_index("wide"), lax.axis_index("narrow")
-    scatter = Scatter(
-        share.at[:, :, :, w & 1],
-        lambda i: share.at[i, :, :, 1 - (w & 1)],
-        (from_core, a1, b1, a2, b2, from_line),
-        shard_ref,
-        send_sems,
-        recv_sems,
-        narrow,
-    )
-    rows = share.shape[5]
-    group = 2 * narrow * rows
-
-    loads[0].wait()
-    scatter.begin(0)
-    loads[1].wait()
-    for t in range(d // TB):
-        normed_t[:, t * TB : (t + 1) * TB] = normed[t * TB : (t + 1) * TB, :].T
-
-    def multiply(i):
-        loads[1 + i].wait()
-        for a in range(2):
-            for b in range(2):
-                at = (2 * a + b) * group
-                product = mm(normed_t[at : at + group, :], grads[:, (i - 1) * width : i * width])
-                share[i, a, b] = product.astype(BF16).reshape(2, narrow, rows, width)
-        scatter.begin(i)
-
-    def close_tokens(t):
-        if t == 0:
-            for load in loads[5:]:
-                load.wait()
-        at = slice(t * TB, (t + 1) * TB)
-        gradient = mm_t(grads[at, :], weight[...])
-        unit, inverse = norm_parts(tokens[at, :].astype(F32))
-        out_ref[at, :] = (total[at, :] + norm_back(unit, inverse, norms_ref[0:1, :], gradient)).astype(BF16)
-        gain, shift = jnp.sum(gradient * unit, axis=0, keepdims=True), jnp.sum(gradient, axis=0, keepdims=True)
-        if t == 0:
-            nval[0, 0:1, :] = gain
-            nval[0, 1:2, :] = shift
-        else:
-            nval[0, 0:1, :] += gain
-            nval[0, 1:2, :] += shift
+    width = scratch[0].shape[-1]
+    outs = (query_ref, key_ref, value_ref)
+
+    def keep(i, value):
+        for n in range(width // 128):
+            pair, kind = divmod(i * width // 128 + n, 3)
+            outs[kind][:, pair * 128 : (pair + 1) * 128] = value[:, n * 128 : (n + 1) * 128]
+
+    carried = Carried([columns_of(qkv_any, i * width, width) for i in range(TAIL_CHUNKS)], scratch, keep, narrow)
+    w, z = carried.scatter.w, carried.scatter.z
 
     def norm_copy(stage, number, target):
         return pltpu.make_async_remote_copy(
@@ -1326,9 +1447,9 @@
 
     def norm_step(stage):
         if stage == 0:
-            nval[0, 2:4, :] = norm_two_ref[0:2, :]
-            nval[0, 4:6, :] = norm_three_ref[0:2, :]
-            nval[0, 6:8, :] = jnp.zeros_like(norm_two_ref[0:2, :])
+            for n, ref in enumerate(norm_refs):
+                nval[0, 2 * n : 2 * n + 2, :] = ref[0:2, :]
+            nval[0, 6:8, :] = jnp.zeros_like(norm_refs[0][0:2, :])
         else:
             for copy in norm_copies[stage - 1]:
                 copy.wait_recv()
@@ -1343,81 +1464,42 @@
             for copy in norm_copies[stage]:
                 copy.start()
 
-    multiply(1)
-    scatter.step(0, 0)
-    multiply(2)
-    scatter.step(1, 0)
-    multiply(3)
-    scatter.step(2, 0)
-    scatter.step(0, 1)
-    close_tokens(0)
-    scatter.step(3, 0)
-    scatter.step(1, 1)
-    scatter.step(0, 2)
-    close_tokens(1)
-    scatter.step(2, 1)
-    scatter.step(1, 2)
-    close_tokens(2)
-    scatter.step(3, 1)
-    scatter.step(0, 3)
-    close_tokens(3)
-    norm_step(0)
-    scatter.step(2, 2)
-    norm_step(1)
-    scatter.step(1, 3)
-    norm_step(2)
-    scatter.step(3, 2)
-    norm_step(3)
-    scatter.step(2, 3)
-    norm_step(4)
-    scatter.step(3, 3)
-    for i in range(CHUNKS):
-        scatter.close(i)
+    carried.open()
+    for number, action in enumerate(TAIL_PLAN):
+        carried.steps([action])
+        if number % 4 == 0 and number // 4 <= 4:
+            norm_step(number // 4)
+    carried.close()
     for copies in norm_copies:
         for copy in copies:
             copy.wait_send()
 
 
-def tail(output_share, normed, grads, tokens, total, norms, norm_two, norm_three, early, mesh_axes):
-    (_, wide), (_, narrow) = mesh_axes
-    rows, d = tokens.shape
-    shard_rows = d // (wide * narrow)
-    width = 4 * d // CHUNKS
+def tail(qkv_share, norm_grads, narrow):
+    d = qkv_share.shape[0]
+    shard_rows = d // (8 * narrow)
+    width = 3 * d // TAIL_CHUNKS
     anywhere, vmem = pl.BlockSpec(memory_space=pl.ANY), pl.BlockSpec(memory_space=pltpu.VMEM)
+
+    def kernel(one, two, three, *refs):
+        tail_kernel(narrow, (one, two, three), *refs)
+
     return pl.pallas_call(
-        functools.partial(tail_kernel, narrow),
-        in_specs=[anywhere] * 6 + [vmem] * 3,
-        out_specs=[vmem] * 3,
-        out_shape=[shape(rows, d, BF16), jax.ShapeDtypeStruct((CHUNKS, shard_rows, d), F32), shape(8, d, F32)],
+        kernel,
+        in_specs=[vmem] * 3 + [anywhere],
+        out_specs=[vmem] * 4,
+        out_shape=[*[shape(shard_rows, d, F32)] * 3, shape(8, d, F32)],
         scratch_shapes=[
-            pltpu.VMEM((rows, d), BF16),
-            pltpu.VMEM((d, rows), BF16),
-            pltpu.VMEM((rows, 3 * d), BF16),
-            pltpu.VMEM((d, 3 * d), BF16),
-            pltpu.VMEM((rows, d), BF16),
-            pltpu.VMEM((rows, d), F32),
-            pltpu.VMEM((CHUNKS, 2, 2, 2, narrow, shard_rows, width), BF16),
-            *scatter_scratch(CHUNKS, narrow, shard_rows, width)[1:-1],
             pltpu.VMEM((4, 8, d), F32),
             pltpu.VMEM((2 + narrow, 8, d), F32),
             pltpu.SemaphoreType.DMA((2 + narrow,)),
             pltpu.SemaphoreType.DMA((2 + narrow,)),
-            pltpu.SemaphoreType.DMA((8,)),
+            *scatter_scratch(TAIL_CHUNKS, narrow, shard_rows, width),
         ],
         name="tail",
-        compiler_params=pltpu.CompilerParams(collective_id=1, has_side_effects=True, vmem_limit_bytes=58 << 20),
-        cost_estimate=cost(12 * rows * d * d, 100 << 20),
-    )(
-        output_share.reshape(2, 2, 2, narrow, shard_rows, d),
-        normed,
-        grads,
-        early,
-        tokens,
-        total,
-        norms,
-        norm_two,
-        norm_three,
-    )
+        compiler_params=pltpu.CompilerParams(collective_id=1, has_side_effects=True, vmem_limit_bytes=40 << 20),
+        cost_estimate=cost(4 * d * d * d, 100 << 20),
+    )(*norm_grads, share_views(qkv_share, narrow, shard_rows))
 
 
 def on_device(
@@ -1475,17 +1557,7 @@
         ),
         mesh_axes,
     )
-    quarters = hidden_out.shape[0] // shard_rows
-    late = lax.all_gather(
-        jnp.concatenate(
-            [hidden_in.reshape(shard_rows, device_count, quarters, -1).transpose(0, 2, 1, 3).reshape(shard_rows, -1)]
-            + [hidden_out[n * shard_rows : (n + 1) * shard_rows] for n in range(quarters)],
-            axis=1,
-        ),
-        names,
-        axis=0,
-        tiled=True,
-    )
+    late = [lax.all_gather(part, names, axis=0, tiled=True) for part in (hidden_in, hidden_out)]
 
     norms = early[:, EXTRA * 128 : EXTRA * 128 + 8].astype(F32).T
     live_total = jnp.sum(norms[6]) * 256.0 + jnp.sum(norms[7])
@@ -1505,27 +1577,54 @@
     )
 
     reduce_share, expand_share = outer_sum(activated, branch_three), outer_sum(normed_three, hidden_grad)
-    if mesh_axes[0][1] == 8 and row_count == 1 and quarters == 4 and shard_rows % 32 == 0:
+    if mesh_axes[0][1] == 8 and row_count == 1 and shard_rows % 32 == 0:
         narrow = mesh_axes[1][1]
-        cq_grad, ckv_grad, self_total, branch_one, mixed_grad, memory_grad, norm_two, reduce_shard = cross_back(
-            bounds, cross_logs, cross_q, cross_kv, cross_mixed, mixed_grad, after_self, cross_total, norms, early, reduce_share, narrow
+        self_total, mixed_grad, memory_grad, norm_two, shares, reduce_shard, expand_low = cross_back(
+            bounds,
+            cross_logs,
+            cross_q,
+            cross_kv,
+            cross_mixed,
+            mixed_grad,
+            after_self,
+            cross_total,
+            norms,
+            branch_two,
+            normed_two,
+            memory,
+            self_mixed,
+            early,
+            reduce_share,
+            expand_share,
+            narrow,
         )
-        cross_shares = [outer_sum(cross_mixed, branch_two), outer_sum(normed_two, cq_grad)]
-        cross_shares += [outer_sum(memory, part) for part in (ckv_grad[:, :WIDTH], ckv_grad[:, WIDTH:])]
-        qkv_grad, shards = self_back(first, self_logs, qkv, self_mixed, mixed_grad, expand_share, cross_shares, narrow)
-        expand_shards, cross_shards = shards[:4], shards[4:]
-        tokens_grad, last_shards, norm_grads = tail(
-            outer_sum(self_mixed, branch_one),
+        (
+            qkv_share,
+            tokens_grad,
+            norm_one,
+            expand_high,
+            cross_output_shard,
+            cross_query_shard,
+            cross_key_shard,
+            cross_value_shard,
+            output_shard,
+        ) = self_back(
+            first,
+            self_logs,
+            qkv,
+            self_mixed,
+            mixed_grad,
             normed_one,
-            qkv_grad,
             tokens,
             self_total,
             norms,
-            norm_two,
-            norm_three,
             early,
-            mesh_axes,
+            expand_share,
+            shares,
+            narrow,
         )
+        query_shard, key_shard, value_shard, norm_grads = tail(qkv_share, (norm_one, norm_two, norm_three), narrow)
+        expand_shard = jnp.concatenate([expand_low, expand_high], axis=1)
     else:
         reduce_sum, expand_sum = staged(reduce_share), staged(expand_share)
         cq_grad, ckv_grad = cross_backward(bounds, cross_logs, cross_q, cross_kv, cross_mixed, mixed_grad, row_count)
@@ -1545,19 +1644,14 @@
         )
         tokens_grad, norm_one = self_close(qkv_grad, tokens, self_total, norms, early)
         norm_grads = sum_everywhere(jnp.concatenate([norm_one[:2], norm_two[:2], norm_three[:2]]), mesh_axes)
-        last_shards = last_sum.result().reshape(4, shard_rows, WIDTH)
+        output_shard, *qkv_shards = last_sum.result().reshape(4, shard_rows, WIDTH)
+        query_shard, key_shard, value_shard = from_pairs(jnp.concatenate(qkv_shards, axis=1), 3)
         reduce_shard = reduce_sum.result()
-        expand_shards = expand_sum.result().reshape(shard_rows, 4, -1).transpose(1, 0, 2)
-        cross_shards = cross_sum.result().reshape(4, shard_rows, WIDTH)
+        expand_shard = expand_sum.result()
+        cross_output_shard, cross_query_shard, *cross_shards = cross_sum.result().reshape(4, shard_rows, WIDTH)
+        cross_key_shard, cross_value_shard = from_pairs(jnp.concatenate(cross_shards, axis=1), 2)
 
     norm_shards = lax.dynamic_slice_in_dim(norm_grads, device * shard_rows, shard_rows, axis=1)
-    reduce_shard = reduce_shard.reshape(-1, WIDTH)
-    expand_shard = (
-        expand_shards.reshape(quarters, shard_rows, device_count, -1).transpose(1, 2, 0, 3).reshape(shard_rows, -1)
-    )
-    output_shard = last_shards[0]
-    query_shard, key_shard, value_shard = from_pairs(jnp.concatenate(list(last_shards[1:]), axis=1), 3)
-    cross_key_shard, cross_value_shard = from_pairs(jnp.concatenate([cross_shards[2], cross_shards[3]], axis=1), 2)
     return (
         layer_output,
         tokens_grad,
@@ -1566,10 +1660,10 @@
         key_shard,
         value_shard,
         output_shard,
-        cross_shards[1],
+        cross_query_shard,
         cross_key_shard,
         cross_value_shard,
-        cross_shards[0],
+        cross_output_shard,
         expand_shard,
         reduce_shard,
         *[norm_shards[n] for n in range(6)],

time: 559 us -> 514 us (0.919)
  Pallas kernels: 453 us -> 427 us
  matrix products: 44.6 us -> 26.8 us
  local copies, waits for them, and re-layouts: 36 us -> 27.7 us
    pallas_call x2, Pallas kernels: 149 us -> 126 us  [the longest x1 83.1 us: self_back(): pl.pallas_call(functools.partial(self_back_kernel, narrow), grid=(PAIRS +...]
    pallas_call x1, Pallas kernels: 124 us -> 104 us  [early_gather(): pl.pallas_call(functools.partial(early_gather_kernel, wide, narrow), in_s...]
    dot_general x7 -> x2, matrix products: 44.6 us -> 26.8 us  [outer_sum(): jnp.einsum('td,te->de', left_side, gradient, preferred_element_type=F32)]
    pallas_call x1, Pallas kernels: 61.5 us -> 78.6 us  [cross_back(): pl.pallas_call(functools.partial(cross_back_kernel, narrow), grid=(PAIRS...]
    reshape x6 -> x0, local copies, waits for them, and re-layouts: 8.54 us -> none  [the longest x2 5.23 us: on_device(): expand_shards.reshape(quarters, shard_rows, device_count, -1)]
    unnamed x117 -> x83, local copies, waits for them, and re-layouts: 15.6 us -> 19.8 us
  transfers between devices with their start and end apart: 1 -> 2, of which waited for: 0 -> 0; matrix products, arithmetic and copies ran while one was open for 1% -> 3% of each run, Pallas kernels for 34% -> 33%
where the time goes in v4:
time: 514 us; the launch traced here: 506 us
  Pallas kernels  427 us (83%)
  local copies, waits for them, and re-layouts  27.7 us (5%)
  matrix products  26.8 us (5%)
  between operations  17.6 us (3%)
  other arithmetic  5.27 us (1%)
    pallas_call x1, Pallas kernels, early_gather(): pl.pallas_call(functools.partial(early_gather_kernel, wide, narrow), in_s...  104 us
    pallas_call x1, Pallas kernels, self_back(): pl.pallas_call(functools.partial(self_back_kernel, narrow), grid=(PAIRS +...  83.1 us
    pallas_call x1, Pallas kernels, cross_back(): pl.pallas_call(functools.partial(cross_back_kernel, narrow), grid=(PAIRS...  78.6 us
    pallas_call x1, Pallas kernels, feed(): pl.pallas_call(feed_kernel, grid=(rows // TB,), in_specs=[smem, smem, til...  56.8 us
    pallas_call x1, Pallas kernels, tail(): pl.pallas_call(kernel, in_specs=[vmem] * 3 + [anywhere], out_specs=[vmem]...  42.7 us
    pallas_call x2, Pallas kernels, attention_call(): pl.pallas_call(kernel, grid=(row_count, PAIRS), in_specs=in_specs, out_sp...  37.5 us
    dot_general x2, matrix products, outer_sum(): jnp.einsum('td,te->de', left_side, gradient, preferred_element_type=F32)  26.8 us
    unnamed x83, local copies, waits for them, and re-layouts  19.8 us
  transfers between devices with their start and end apart: 2, of which 0 were waited for; matrix products, arithmetic and copies ran while one was open for 3% of the time, Pallas kernels for 33%

profile of v4, /device:TPU:0, one launch (start us, length us, event | category | flops | bytes accessed | tf_op | source)
XLA Modules:
  0.0 505.5 jit_solution(6596551865492103097)
XLA Ops:
  9.4 1.4 fusion.6
  12.2 0.8 concatenate.23
  13.1 0.8 select_reduce_fusion
  14.8 0.9 stack_reshape.20
  15.7 0.9 stack_reshape.21
  16.6 0.9 stack_reshape.22
  18.1 0.9 stack_reshape.23
  19.0 0.9 stack_reshape.24
  20.3 0.8 constant_dynamic-update-slice_fusion.4
  21.2 0.8 copy-done.20
  22.0 104.3 %early_gather.1.weight_ref.wo_ref.wq_ref.wkv_ref.early_any = bf16[1024,8320]{1,0:T(8,128)(2,1)} custom-call(bf16[32,8320]{1,0:T(8,128)(2,1)} %copy-done.20), custom_call_target="tpu_custom_call" | custom-call | bytes 209715200 | tf_op jit(solution)/shard_map/early_gather/pallas_call | solution.py:660
  126.3 1.0 slice.38
  129.4 11.2 %project.1 = (bf16[1024,1024]{1,0:T(8,128)(2,1)S(1)}, bf16[1024,3072]{1,0:T(8,128)(2,1)S(1)}) custom-call(bf16[1024,1024]{1,0:T(8,128)(2,1)S(1)} %copy-done, f32[8,1024]{1,0:T(8,128)S(1)} %convert_bitcast_fusion.norms_ref, bf16[1024,8320]{1,0:T(8,128)(2,1)} %early_gather.1.weight_ref.wo_ref.wq_ref.wkv_ref.early_any), custom_call_target="tpu_custom_call" | custom-call | flops 6442450944 | bytes 16777216 | tf_op jit(solution)/shard_map/project/pallas_call | solution.py:327
  140.6 19.2 %self_forward.1 = (bf16[1024,1024]{1,0:T(8,128)(2,1)S(1)}, f32[1,8,8,1024]{3,2,1,0:T(8,128)S(1)}) custom-call(s32[1,1,1024]{2,1,0:T(1,128)S(1)} %get-tuple-element.109.first_ref, bf16[1024,3072]{1,0:T(8,128)(2,1)S(1)} %get-tuple-element.58.qkv_ref), custom_call_target="tpu_custom_call" | custom-call | flops 21474836480 | bytes 8388608 | tf_op jit(solution)/shard_map/self_forward/pallas_call | solution.py:150
  159.9 12.6 %middle.1 = (f32[1024,1024]{1,0:T(8,128)}, bf16[1024,1024]{1,0:T(8,128)(2,1)S(1)}, bf16[1024,1024]{1,0:T(8,128)(2,1)S(1)}, bf16[512,2048]{1,0:T(8,128)(2,1)S(1)}) custom-call(bf16[1024,1024]{1,0:T(8,128)(2,1)S(1)} %get-tuple-element.59.mixed_ref.self_mixed_ref, bf16[1024,1024]{1,0:T(8,128)(2,1)S(1)} %copy-done, bf16[512,1024]{1,0:T(8,128)(2,1)S(1)} %copy-done.2, ...), custom_call_target="tpu_custom_call" | custom-call | flops 6442450944 | bytes 20971520 | tf_op jit(solution)/shard_map/middle/pallas_call | solution.py:356
  172.5 1.4 copy-done.6
  173.9 18.3 %cross_forward.1 = (bf16[1024,1024]{1,0:T(8,128)(2,1)S(1)}, f32[1,8,8,1024]{3,2,1,0:T(8,128)S(1)}) custom-call(s32[1,8,1024]{2,1,0:T(8,128)S(1)} %pad.14.bounds_ref, bf16[1024,1024]{1,0:T(8,128)(2,1)S(1)} %get-tuple-element.60.q_ref, bf16[512,2048]{1,0:T(8,128)(2,1)S(1)} %get-tuple-element.61.kv_ref), custom_call_target="tpu_custom_call" | custom-call | flops 21474836480 | bytes 8388608 | tf_op jit(solution)/shard_map/cross_forward/pallas_call | solution.py:150
  192.2 1.3 copy-done.7
  193.5 1.3 copy-done.8
  194.8 1.3 copy-done.12
  196.8 56.8 %feed.1 = (bf16[1024,1024]{1,0:T(8,128)(2,1)}, bf16[1024,1024]{1,0:T(8,128)(2,1)}, bf16[1024,4096]{1,0:T(8,128)(2,1)}, bf16[1024,4096]{1,0:T(8,128)(2,1)}, bf16[...) custom-call(s32[1]{0:T(128)} %copy.98.live_ref, ...), custom_call_target="tpu_custom_call" | custom-call | flops 40802189312 | bytes 52428800 | tf_op jit(solution)/shard_map/feed/pallas_call | solution.py:441
  253.7 15.6 %convolution_convert_fusion.1 = bf16[4096,1024]{1,0:T(8,128)(2,1)} fusion(bf16[1024,4096]{1,0:T(8,128)(2,1)} %get-tuple-element.71, bf16[1024,1024]{1,0:T(8,128)(2,1)} %get-tuple-element.72), kind=kOutput, calls=%fused_computation.1 | convolution fusion | flops 8594128896 | bytes 18874368 | tf_op jit(solution)/shard_map/td,te->de/dot_general | solution.py:801
  269.3 11.2 %convolution_convert_fusion = bf16[1024,4096]{1,0:T(8,128)(2,1)} fusion(bf16[1024,1024]{1,0:T(8,128)(2,1)S(1)} %copy-done.32, bf16[1024,4096]{1,0:T(8,128)(2,1)S(1)} %copy-done.31), kind=kOutput, calls=%fused_computation | convolution fusion | flops 8594128896 | bytes 18874368 | tf_op jit(solution)/shard_map/td,te->de/dot_general | solution.py:801
  280.5 78.6 %cross_back.1 = (f32[1024,1024]{1,0:T(8,128)}, bf16[1024,1024]{1,0:T(8,128)(2,1)}, bf16[512,1024]{1,0:T(8,128)(2,1)}, f32[8,1024]{1,0:T(8,128)}, bf16[5120,1024]...) custom-call(s32[1,8,1024]{2,1,0:T(8,128)} %copy-done.4, f32[1,8,8,1024]{3,2,1,0:T(8,128)} %copy-done.17, ...), custom_call_target="tpu_custom_call" | custom-call | flops 42949672960 | bytes 104857600 | tf_op jit(solution)/shard_map/cross_back/pallas_call | solution.py:1124
  359.1 83.1 %self_back.1 = (bf16[1024,3072]{1,0:T(8,128)(2,1)}, bf16[1024,1024]{1,0:T(8,128)(2,1)}, f32[8,1024]{1,0:T(8,128)}, f32[32,2048]{1,0:T(8,128)}, f32[32,1024]{1,0:...) custom-call(s32[1,1,1024]{2,1,0:T(1,128)} %copy-done.5, ...), custom_call_target="tpu_custom_call" | custom-call | flops 42949672960 | bytes 104857600 | tf_op jit(solution)/shard_map/self_back/pallas_call | solution.py:1343
  442.2 2.8 copy-done.9
  445.0 0.8 copy-done.15
  445.7 42.7 %tail.1 = (f32[32,1024]{1,0:T(8,128)S(1)}, f32[32,1024]{1,0:T(8,128)S(1)}, f32[32,1024]{1,0:T(8,128)S(1)}, f32[8,1024]{1,0:T(8,128)S(1)}) custom-call(f32[8,1024]{1,0:T(8,128)S(1)} %copy-done.15, f32[8,1024]{1,0:T(8,128)S(1)} %copy-done.14, f32[8,1024]{1,0:T(8,128)S(1)} %copy-done.13, bf16[2,2,2,4,32,3072]{5,4,3,2,1,0:T(8,128)(2,1)S(1)} %bitcast.41), custom_call_target="tpu_custom_call" | custom-call | flops 4294967296 | bytes 104857600 | tf_op jit(solution)/shard_map/tail/pallas_call | solution.py:1487
  489.1 0.8 pad_maximum_fusion
  489.9 1.3 copy.99
  491.3 1.0 copy.100
  497.5 0.8 copy.109
  (97 shorter events, 11.6 us)
Async XLA Ops:
  7.2 14.0 %copy-start.29 = (bf16[32,1024]{1,0:T(8,128)(2,1)S(1)}, bf16[32,1024]{1,0:T(8,128)(2,1)}, u32[]{:S(2)}) copy-start(bf16[32,1024]{1,0:T(8,128)(2,1)} %param.36) | copy-start | bytes 196612
  7.2 14.0 %copy-start.30 = (bf16[32,1024]{1,0:T(8,128)(2,1)S(1)}, bf16[32,1024]{1,0:T(8,128)(2,1)}, u32[]{:S(2)}) copy-start(bf16[32,1024]{1,0:T(8,128)(2,1)} %param.39) | copy-start | bytes 196612
  7.2 189.6 %all-gather.3.cloned.1.call-start = ((), (), s32[]{:S(2)}) async-start(), calls=%async_computation | async-start | bytes 8650752 | tf_op jit(solution)/shard_map/all_gather | solution.py:1560
  7.9 188.9 %all-gather.5.cloned.1.call-start = ((), (), s32[]{:S(2)}) async-start(), calls=%async_computation.1 | async-start | bytes 8650752 | tf_op jit(solution)/shard_map/all_gather | solution.py:1560
  14.7 125.9 %copy-start.5 = (s32[1,1,1024]{2,1,0:T(1,128)}, s32[1,1,1024]{2,1,0:T(1,128)S(1)}, u32[]{:S(2)}) copy-start(s32[1,1,1024]{2,1,0:T(1,128)S(1)} %get-tuple-element.109.first_ref) | copy-start | bytes 12292
  14.7 159.1 %copy-start.4 = (s32[1,8,1024]{2,1,0:T(8,128)}, s32[1,8,1024]{2,1,0:T(8,128)S(1)}, u32[]{:S(2)}) copy-start(s32[1,8,1024]{2,1,0:T(8,128)S(1)} %pad.14.bounds_ref) | copy-start | bytes 98308
  22.0 107.4 %copy-start = (bf16[1024,1024]{1,0:T(8,128)(2,1)S(1)}, bf16[1024,1024]{1,0:T(8,128)(2,1)}, u32[]{:S(2)}) copy-start(bf16[1024,1024]{1,0:T(8,128)(2,1)} %tokens_ref.5) | copy-start | bytes 6291460
  127.4 32.4 %copy-start.3 = (f32[8,1024]{1,0:T(8,128)}, f32[8,1024]{1,0:T(8,128)S(1)}, u32[]{:S(2)}) copy-start(f32[8,1024]{1,0:T(8,128)S(1)} %convert_bitcast_fusion.norms_ref) | copy-start | bytes 98308
  140.6 19.2 %copy-start.10 = (bf16[1024,3072]{1,0:T(8,128)(2,1)}, bf16[1024,3072]{1,0:T(8,128)(2,1)S(1)}, u32[]{:S(2)}) copy-start(bf16[1024,3072]{1,0:T(8,128)(2,1)S(1)} %get-tuple-element.58.qkv_ref) | copy-start | bytes 18874372
  140.6 19.2 %copy-start.11 = (bf16[1024,1024]{1,0:T(8,128)(2,1)}, bf16[1024,1024]{1,0:T(8,128)(2,1)S(1)}, u32[]{:S(2)}) copy-start(bf16[1024,1024]{1,0:T(8,128)(2,1)S(1)} %get-tuple-element.76.normed_ref) | copy-start | bytes 6291460
  140.6 19.3 %copy-start.2 = (bf16[512,1024]{1,0:T(8,128)(2,1)S(1)}, bf16[512,1024]{1,0:T(8,128)(2,1)}, u32[]{:S(2)}) copy-start(bf16[512,1024]{1,0:T(8,128)(2,1)} %memory_ref.3) | copy-start | bytes 3145732
  159.8 12.6 %copy-start.1 = (bf16[1024,1024]{1,0:T(8,128)(2,1)}, bf16[1024,1024]{1,0:T(8,128)(2,1)S(1)}, u32[]{:S(2)}) copy-start(bf16[1024,1024]{1,0:T(8,128)(2,1)S(1)} %get-tuple-element.59.mixed_ref.self_mixed_ref) | copy-start | bytes 6291460
  159.9 12.6 %copy-start.16 = (f32[1,8,8,1024]{3,2,1,0:T(8,128)}, f32[1,8,8,1024]{3,2,1,0:T(8,128)S(1)}, u32[]{:S(2)}) copy-start(f32[1,8,8,1024]{3,2,1,0:T(8,128)S(1)} %get-tuple-element.65.log_ref) | copy-start | bytes 786436
  172.5 1.4 copy-start.6
  192.1 1.3 copy-start.7
  193.5 1.3 copy-start.8
  194.8 1.3 copy-start.12
  253.6 15.7 %copy-start.31 = (bf16[1024,4096]{1,0:T(8,128)(2,1)S(1)}, bf16[1024,4096]{1,0:T(8,128)(2,1)}, u32[]{:S(2)}) copy-start(bf16[1024,4096]{1,0:T(8,128)(2,1)} %get-tuple-element.74) | copy-start | bytes 25165828
  253.6 15.6 %copy-start.32 = (bf16[1024,1024]{1,0:T(8,128)(2,1)S(1)}, bf16[1024,1024]{1,0:T(8,128)(2,1)}, u32[]{:S(2)}) copy-start(bf16[1024,1024]{1,0:T(8,128)(2,1)} %get-tuple-element.73) | copy-start | bytes 6291460
  359.1 83.1 %copy-start.13 = (f32[8,1024]{1,0:T(8,128)S(1)}, f32[8,1024]{1,0:T(8,128)}, u32[]{:S(2)}) copy-start(f32[8,1024]{1,0:T(8,128)} %get-tuple-element.83.three) | copy-start | bytes 98308
  359.1 83.1 %copy-start.14 = (f32[8,1024]{1,0:T(8,128)S(1)}, f32[8,1024]{1,0:T(8,128)}, u32[]{:S(2)}) copy-start(f32[8,1024]{1,0:T(8,128)} %get-tuple-element.82.two) | copy-start | bytes 98308
  442.2 2.8 copy-start.9
  445.7 43.4 %copy-start.22 = (f32[32,2048]{1,0:T(8,128)S(1)}, f32[32,2048]{1,0:T(8,128)}, u32[]{:S(2)}) copy-start(f32[32,2048]{1,0:T(8,128)} %get-tuple-element.93) | copy-start | bytes 786436
  445.7 43.4 %copy-start.23 = (f32[32,2048]{1,0:T(8,128)S(1)}, f32[32,2048]{1,0:T(8,128)}, u32[]{:S(2)}) copy-start(f32[32,2048]{1,0:T(8,128)} %get-tuple-element.94) | copy-start | bytes 786436
  445.7 44.2 %copy-start.18 = (bf16[1024,1024]{1,0:T(8,128)(2,1)S(1)}, bf16[1024,1024]{1,0:T(8,128)(2,1)}, u32[]{:S(2)}) copy-start(bf16[1024,1024]{1,0:T(8,128)(2,1)} %get-tuple-element.131) | copy-start | bytes 6291460
  488.4 2.8 copy-start.19
  488.5 5.8 %copy-start.28 = (f32[32,1024]{1,0:T(8,128)S(1)}, f32[32,1024]{1,0:T(8,128)}, u32[]{:S(2)}) copy-start(f32[32,1024]{1,0:T(8,128)} %get-tuple-element.136) | copy-start | bytes 393220
  489.1 5.8 %copy-start.27 = (f32[32,1024]{1,0:T(8,128)S(1)}, f32[32,1024]{1,0:T(8,128)}, u32[]{:S(2)}) copy-start(f32[32,1024]{1,0:T(8,128)} %get-tuple-element.137) | copy-start | bytes 393220
  489.1 6.4 %copy-start.26 = (f32[32,1024]{1,0:T(8,128)S(1)}, f32[32,1024]{1,0:T(8,128)}, u32[]{:S(2)}) copy-start(f32[32,1024]{1,0:T(8,128)} %get-tuple-element.138) | copy-start | bytes 393220
  489.9 6.2 %copy-start.25 = (f32[32,1024]{1,0:T(8,128)S(1)}, f32[32,1024]{1,0:T(8,128)}, u32[]{:S(2)}) copy-start(f32[32,1024]{1,0:T(8,128)} %get-tuple-element.139) | copy-start | bytes 393220
  489.9 6.9 %copy-start.24 = (f32[32,1024]{1,0:T(8,128)S(1)}, f32[32,1024]{1,0:T(8,128)}, u32[]{:S(2)}) copy-start(f32[32,1024]{1,0:T(8,128)} %get-tuple-element.140) | copy-start | bytes 393220
  489.9 7.6 %copy-start.21 = (f32[128,1024]{1,0:T(8,128)S(1)}, f32[128,1024]{1,0:T(8,128)}, u32[]{:S(2)}) copy-start(f32[128,1024]{1,0:T(8,128)} %get-tuple-element.142) | copy-start | bytes 1572868
  (3 other events, 2.3 us)
Sparse Core Ops, SparseCore 0:
  11.0 107.1 all-gather.2
  121.1 75.5 all-gather.4

commit v5 on v4

--- a/solution.py
+++ b/solution.py
@@ -67,7 +67,7 @@
     return (key >= bounds_ref[0, 0:1, BLOCKS[i]]) & (key < bounds_ref[0, 1:2, BLOCKS[i]])
 
 
-def attend(q_of, k, v, visible, extent, out_ref, log_ref):
+def attend(q_of, k, v, visible, extent, keep_out, keep_log):
     k_parts, v_t = halves(k), v.T
     outs = {}
 
@@ -78,10 +78,10 @@
     def back(i, h, s, peak):
         p = jnp.exp2(s - peak)
         total = jnp.sum(p, axis=0, keepdims=True)
-        log_ref[0, 0, h : h + 1, BLOCKS[i]] = peak + jnp.log2(total)
+        keep_log(h, BLOCKS[i], peak + jnp.log2(total))
         outs[h] = mm(v_t[h * 64 : (h + 1) * 64, : extent(i)], p.astype(BF16)) * (1.0 / total)
         if h == 1:
-            out_ref[BLOCKS[i], :] = jnp.concatenate([outs[0], outs[1]], axis=0).T.astype(BF16)
+            keep_out(BLOCKS[i], jnp.concatenate([outs[0], outs[1]], axis=0).T.astype(BF16))
 
     in_turn(TASKS, front, back, 3)
 
@@ -113,6 +113,16 @@
     in_turn(TASKS, front, back, 2)
 
 
+def keepers(out_ref, log_ref):
+    def keep_out(rows, value):
+        out_ref[rows, :] = value
+
+    def keep_log(h, rows, value):
+        log_ref[0, 0, h : h + 1, rows] = value
+
+    return keep_out, keep_log
+
+
 def self_forward_kernel(first_ref, qkv_ref, out_ref, log_ref):
     attend(
         lambda rows: qkv_ref[rows, 0:128],
@@ -120,8 +130,7 @@
         qkv_ref[:, 256:384],
         functools.partial(self_visible, first_ref),
         self_extent,
-        out_ref,
-        log_ref,
+        *keepers(out_ref, log_ref),
     )
 
 
@@ -132,8 +141,7 @@
         kv_ref[:, 128:256],
         functools.partial(cross_visible, bounds_ref),
         cross_extent,
-        out_ref,
-        log_ref,
+        *keepers(out_ref, log_ref),
     )
 
 
@@ -375,6 +383,16 @@
 
 GELU_A = 0.7978845608028654
 GELU_B = 0.044715
+
+
+def hidden_parts(win_ref, wout_ref, part, d):
+    if len(win_ref.shape) == 2:
+        at = slice(part * d, (part + 1) * d)
+        return win_ref[:, at], wout_ref[at, :]
+    devices, quad, _ = win_ref.shape
+    rows, share = quad // 4, devices // 4
+    win = win_ref[:, part * rows : (part + 1) * rows, :].reshape(d, d)
+    return win, wout_ref[part * share : (part + 1) * share].reshape(d, d)
 
 
 def feed_kernel(
@@ -411,19 +429,20 @@
     normed_ref[...] = normed
     d = normed.shape[1]
     result, back = after, None
-    for part in range(win_ref.shape[1] // d):
+    for part in range(act_ref.shape[1] // d):
         at = slice(part * d, (part + 1) * d)
-        x = mm(normed, win_ref[:, at])
+        win, wout = hidden_parts(win_ref, wout_ref, part, d)
+        x = mm(normed, win)
         square = x * x
         t = jnp.tanh(GELU_A * x * (1.0 + GELU_B * square))
         half = 0.5 * (1.0 + t)
         act = (x * half).astype(BF16)
         slope = half + (0.5 * GELU_A) * x * (1.0 - t * t) * (1.0 + (3.0 * GELU_B) * square)
         act_ref[:, at] = act
-        hid = (mm_t(branch, wout_ref[at, :]) * slope).astype(BF16)
+        hid = (mm_t(branch, wout) * slope).astype(BF16)
         hid_ref[:, at] = hid
-        result = result + mm(act, wout_ref[at, :])
-        term = mm_t(hid, win_ref[:, at])
+        result = result + mm(act, wout)
+        term = mm_t(hid, win)
         back = term if back is None else back + term
     out_ref[...] = result.astype(BF16)
     total = out_grad + norm_back(unit, inverse, norms_ref[4:5, :], back)
@@ -436,7 +455,15 @@
 
 def feed(live_length, row_weight, mixed, before, cotangent, norms, early, late):
     rows, d = cotangent.shape
-    ff = late[0].shape[1]
+    ff = 4 * d
+    if len(late) == 1:
+        devices, block, _ = late[0].shape
+        late = late * 2
+        late_specs = [
+            pl.BlockSpec((devices, block // 2, d), lambda b, n=n: (0, n, 0), pipeline_mode=pl.Buffered(1)) for n in range(2)
+        ]
+    else:
+        late_specs = [whole(d, ff), whole(ff, d)]
     smem = pl.BlockSpec(memory_space=pltpu.SMEM)
     return pl.pallas_call(
         feed_kernel,
@@ -449,8 +476,7 @@
             tile(TB, d),
             whole(8, d),
             whole(d, d, OUT_CROSS),
-            whole(d, ff),
-            whole(ff, d),
+            *late_specs,
         ],
         out_specs=[
             tile(TB, d),
@@ -548,7 +574,7 @@
     )(dqkv, before, total, norms, early)
 
 
-OUT_SELF, KV_CROSS, QUERY_CROSS, OUT_CROSS, EXTRA = 3, 2, 6, 7, 64
+OUT_SELF, QUERY_CROSS, KV_CROSS, OUT_CROSS = 0, 1, 1, 4
 
 
 def greet_all(narrow):
@@ -560,117 +586,385 @@
     pl.semaphore_wait(barrier, len(others))
 
 
-def early_gather_kernel(wide, narrow, shard_ref, out_ref, send_sems, recv_sems, own_sem):
-    rows = shard_ref.shape[0]
-    half = rows // 2
-    w, z = lax.axis_index("wide"), lax.axis_index("narrow")
-    core, x, y = w ^ 1, w ^ 2, w ^ 4
-    up, down, to_x, to_y, on_y, on_x, to_core = [k * narrow for k in range(7)]
-
-    def start_of(holder, s):
-        return pl.multiple_of((holder * narrow + s) * rows, rows)
-
-    def move(holder, s, number, target, first=0, count=rows, own=False):
-        at = pl.multiple_of(start_of(holder, s) + first, half)
-        place = out_ref.at[pl.ds(at, count)]
+class Gather:
+    def __init__(self, shard_ref, out_ref, send_sems, recv_sems, narrow):
+        self.shard_ref, self.out_ref = shard_ref, out_ref
+        self.send_sems, self.recv_sems = send_sems, recv_sems
+        self.narrow = narrow
+        self.rows = shard_ref.shape[0]
+        self.half = self.rows // 2
+        self.w, self.z = w, z = lax.axis_index("wide"), lax.axis_index("narrow")
+        self.core, self.x, self.y, self.xy = w ^ 1, w ^ 2, w ^ 4, w ^ 6
+        self.above, self.below = (w, z + 1), (w, z - 1)
+        self.at_core, self.at_x, self.at_y = (self.core, z), (self.x, z), (self.y, z)
+        self.up, self.down, self.to_x, self.to_y, self.on_y, self.on_x, self.to_core = [k * narrow for k in range(7)]
+
+    def move(self, holder, s, number, target, first=0, count=None, own=False):
+        count = self.rows if count is None else count
+        at = pl.multiple_of((holder * self.narrow + s) * self.rows + first, self.half)
+        place = self.out_ref.at[pl.ds(at, count)]
         return pltpu.make_async_remote_copy(
-            src_ref=shard_ref.at[pl.ds(first, count)] if own else place,
+            src_ref=self.shard_ref.at[pl.ds(first, count)] if own else place,
             dst_ref=place,
-            send_sem=send_sems.at[number],
-            recv_sem=recv_sems.at[number],
+            send_sem=self.send_sems.at[number],
+            recv_sem=self.recv_sems.at[number],
             device_id=target,
             device_id_type=pl.DeviceIdType.MESH,
         )
 
-    above, below = (w, z + 1), (w, z - 1)
+    def own_place(self):
+        return self.out_ref.at[pl.ds(pl.multiple_of((self.w * self.narrow + self.z) * self.rows, self.rows), self.rows)]
+
+    def spread(self, s, own=False):
+        self.move(self.w, s, self.to_x + s, self.at_x, own=own).start()
+        self.move(self.w, s, self.to_y + s, self.at_y, own=own).start()
+        self.move(self.w, s, self.to_core + s, self.at_core, own=own).start()
+
+    def relay(self, s):
+        half = self.half
+        self.move(self.x, s, self.to_x + s, self.at_x).wait_recv()
+        self.move(self.x, s, self.on_y + s, self.at_y, 0, half).start()
+        self.move(self.x, s, self.to_core + self.narrow + s, self.at_core).start()
+        self.move(self.y, s, self.to_y + s, self.at_y).wait_recv()
+        self.move(self.y, s, self.on_x + s, self.at_x, half, half).start()
+        self.move(self.y, s, self.to_core + 2 * self.narrow + s, self.at_core).start()
+
+    def corner(self, s):
+        self.move(self.xy, s, self.on_y + s, self.at_y, 0, self.half).wait_recv()
+        self.move(self.xy, s, self.on_x + s, self.at_x, self.half, self.half).wait_recv()
+        self.move(self.xy, s, self.to_core + 3 * self.narrow + s, self.at_core).start()
+
+    def at_distance(self, r, action):
+        if r == 0:
+            action(self.z)
+        else:
+            pl.when(self.z - r >= 0)(lambda: action(self.z - r))
+            pl.when(self.z + r < self.narrow)(lambda: action(self.z + r))
+
+    def begin_line(self):
+        z = self.z
+        pl.when(z < self.narrow - 1)(lambda: self.move(self.w, z, self.up + z, self.above, own=True).start())
+        pl.when(z > 0)(lambda: self.move(self.w, z, self.down + z, self.below, own=True).start())
+
+    def begin_spread(self):
+        self.spread(self.z, own=True)
+
+    def round(self, r):
+        z = self.z
+
+        def from_below():
+            s = z - r
+            self.move(self.w, s, self.up + s, self.above).wait_recv()
+            pl.when(z < self.narrow - 1)(lambda: self.move(self.w, s, self.up + s, self.above).start())
+            self.spread(s)
+
+        def from_above():
+            s = z + r
+            self.move(self.w, s, self.down + s, self.below).wait_recv()
+            pl.when(z > 0)(lambda: self.move(self.w, s, self.down + s, self.below).start())
+            self.spread(s)
+
+        if r < self.narrow:
+            pl.when(z - r >= 0)(from_below)
+            pl.when(z + r < self.narrow)(from_above)
+        self.at_distance(r - 1, self.relay)
+
+    def corners(self):
+        for r in range(self.narrow):
+            self.at_distance(r, self.corner)
+
+    def arrive(self):
+        for s in range(self.narrow):
+            for k, holder in enumerate((self.w, self.x, self.y, self.xy)):
+                self.move(holder ^ 1, s, self.to_core + k * self.narrow + s, self.at_core).wait_recv()
+
+    def close(self):
+        z, half = self.z, self.half
+        for s in range(self.narrow):
+            up, down = self.move(self.w, s, self.up + s, self.above), self.move(self.w, s, self.down + s, self.below)
+            pl.when((s <= z) & (z < self.narrow - 1))(up.wait_send)
+            pl.when((s >= z) & (z > 0))(down.wait_send)
+            self.move(self.w, s, self.to_x + s, self.at_x).wait_send()
+            self.move(self.w, s, self.to_y + s, self.at_y).wait_send()
+            self.move(self.x, s, self.on_y + s, self.at_y, 0, half).wait_send()
+            self.move(self.y, s, self.on_x + s, self.at_x, half, half).wait_send()
+            for k, holder in enumerate((self.w, self.x, self.y, self.xy)):
+                self.move(holder, s, self.to_core + k * self.narrow + s, self.at_core).wait_send()
+
+
+def place_bounds(live_ref, pairs_ref, sources_ref, first_ref, bounds_ref):
+    place = lax.broadcasted_iota(jnp.int32, (1, SEQ), 1)
+    live = place < live_ref[0]
+    count = pairs_ref.shape[1]
+    first, start, end = jnp.zeros_like(place), jnp.zeros_like(place), jnp.zeros_like(place)
+    for n in range(count):
+        begun = place >= pairs_ref[0, n]
+        first = jnp.where(begun, pairs_ref[0, n], first)
+        start = jnp.where(begun, sources_ref[0, n], start)
+        end = jnp.where(begun, sources_ref[0, n + 1] if n + 1 < count else MEM, end)
+    first_ref[0] = jnp.where(live, first, live_ref[0])
+    bounds_ref[0, 0:1, :] = jnp.where(live, start, 0)
+    bounds_ref[0, 1:2, :] = jnp.where(live, end, MEM)
+    bounds_ref[0, 2:8, :] = jnp.zeros((6, SEQ), jnp.int32)
+
+
+def front_kernel(
+    narrow,
+    live_ref,
+    pairs_ref,
+    sources_ref,
+    wq_ref,
+    wk_ref,
+    wv_ref,
+    ck_ref,
+    cv_ref,
+    others_refs,
+    hidden_in_ref,
+    hidden_out_ref,
+    extra_ref,
+    tokens_ref,
+    memory_ref,
+    wide_any,
+    later_any,
+    late_any,
+    normed_any,
+    qkv_any,
+    mixed_ref,
+    log_ref,
+    norms_ref,
+    first_ref,
+    bounds_ref,
+    after_ref,
+    normed_two_ref,
+    cross_q_ref,
+    cross_kv_ref,
+    cross_mixed_ref,
+    cross_log_ref,
+    shard_a,
+    shard_b,
+    shard_c,
+    weight,
+    later,
+    normed,
+    qkv,
+    a_send,
+    a_recv,
+    b_send,
+    b_recv,
+    c_send,
+    c_recv,
+    local_sems,
+):
+    d = tokens_ref.shape[1]
+    rows = wq_ref.shape[0]
+    for p in range(PAIRS):
+        lanes = slice(p * 128, (p + 1) * 128)
+        for n, ref in enumerate((wq_ref, wk_ref, wv_ref)):
+            shard_a[:, (3 * p + n) * 128 : (3 * p + n + 1) * 128] = ref[:, lanes]
+        for n, ref in enumerate((ck_ref, cv_ref)):
+            at = KV_CROSS * 2 * d + (2 * p + n) * 128
+            shard_b[:, at : at + 128] = ref[:, lanes]
+    shard_a[:, 3 * d :] = extra_ref[...]
+
+    one = Gather(shard_a, weight, a_send, a_recv, narrow)
+    two = Gather(shard_b, later, b_send, b_recv, narrow)
+    three = Gather(shard_c, late_any, c_send, c_recv, narrow)
+    keeps = [
+        pltpu.make_async_copy(gather.shard_ref, gather.own_place(), local_sems.at[n])
+        for n, gather in enumerate((one, two, three))
+    ]
     greet_all(narrow)
-
-    keep = pltpu.make_async_copy(shard_ref, out_ref.at[pl.ds(start_of(w, z), rows)], own_sem)
-    keep.start()
-
-    def spread(s, own=False):
-        move(w, s, to_x + s, (x, z), own=own).start()
-        move(w, s, to_y + s, (y, z), own=own).start()
-        move(w, s, to_core + s, (core, z), own=own).start()
-
-    def relay(s):
-        move(x, s, to_x + s, (x, z)).wait_recv()
-        move(x, s, on_y + s, (y, z), 0, half).start()
-        move(x, s, to_core + narrow + s, (core, z)).start()
-        move(y, s, to_y + s, (y, z)).wait_recv()
-        move(y, s, on_x + s, (x, z), half, half).start()
-        move(y, s, to_core + 2 * narrow + s, (core, z)).start()
-
-    def at_distance(r, action):
-        if r == 0:
-            action(z)
-        else:
-            pl.when(z - r >= 0)(lambda: action(z - r))
-            pl.when(z + r < narrow)(lambda: action(z + r))
-
-    pl.when(z < narrow - 1)(lambda: move(w, z, up + z, above, own=True).start())
-    pl.when(z > 0)(lambda: move(w, z, down + z, below, own=True).start())
-    spread(z, own=True)
-    for r in range(1, narrow):
-
-        def from_below(r=r):
-            s = z - r
-            move(w, s, up + s, above).wait_recv()
-            pl.when(z < narrow - 1)(lambda: move(w, s, up + s, above).start())
-            spread(s)
-
-        def from_above(r=r):
-            s = z + r
-            move(w, s, down + s, below).wait_recv()
-            pl.when(z > 0)(lambda: move(w, s, down + s, below).start())
-            spread(s)
-
-        pl.when(z - r >= 0)(from_below)
-        pl.when(z + r < narrow)(from_above)
-        at_distance(r - 1, relay)
-    at_distance(narrow - 1, relay)
-
-    def corner(s):
-        move(x ^ 4, s, on_y + s, (y, z), 0, half).wait_recv()
-        move(x ^ 4, s, on_x + s, (x, z), half, half).wait_recv()
-        move(x ^ 4, s, to_core + 3 * narrow + s, (core, z)).start()
-
-    for r in range(narrow):
-        at_distance(r, corner)
-    for s in range(narrow):
-        for k, holder in enumerate((w, x, y, x ^ 4)):
-            move(holder ^ 1, s, to_core + k * narrow + s, (core, z)).wait_recv()
-    for s in range(narrow):
-        pl.when((s <= z) & (z < narrow - 1))(lambda s=s: move(w, s, up + s, above).wait_send())
-        pl.when((s >= z) & (z > 0))(lambda s=s: move(w, s, down + s, below).wait_send())
-        move(w, s, to_x + s, (x, z)).wait_send()
-        move(w, s, to_y + s, (y, z)).wait_send()
-        move(x, s, on_y + s, (y, z), 0, half).wait_send()
-        move(y, s, on_x + s, (x, z), half, half).wait_send()
-        for k, holder in enumerate((w, x, y, x ^ 4)):
-            move(holder, s, to_core + k * narrow + s, (core, z)).wait_send()
-    keep.wait()
-
-
-def early_gather(shard, mesh_axes):
-    (_, wide), (_, narrow) = mesh_axes
-    rows, columns = shard.shape
-    if wide != 8 or rows % 32:
-        return lax.all_gather(shard, tuple(axis for axis, _ in mesh_axes), axis=0, tiled=True)
+    one.begin_line()
+    one.begin_spread()
+    keeps[0].start()
+    for at, ref in zip((OUT_SELF, QUERY_CROSS, OUT_CROSS), others_refs):
+        shard_b[:, at * d : (at + 1) * d] = ref[...]
+    for n in range(4):
+        shard_c[n * rows : (n + 1) * rows, :] = hidden_in_ref[:, n * d : (n + 1) * d]
+    shard_c[4 * rows :, :] = hidden_out_ref[...]
+    keeps[1].start()
+    keeps[2].start()
+    place_bounds(live_ref, pairs_ref, sources_ref, first_ref, bounds_ref)
+    one.round(1)
+    one.round(2)
+    two.begin_line()
+    for r in range(3, narrow + 1):
+        one.round(r)
+    two.begin_spread()
+    one.corners()
+    one.arrive()
+    keeps[0].wait()
+    out_wide = pltpu.make_async_copy(weight, wide_any, local_sems.at[3])
+    out_wide.start()
+
+    norms_ref[...] = weight[:, 3 * d :].astype(F32).T[0:8, :]
+
+    def project_block(t, carry):
+        at = pl.ds(pl.multiple_of(t * TB, TB), TB)
+        unit, _ = norm_parts(tokens_ref[at, :].astype(F32))
+        value = (unit * norms_ref[0:1, :] + norms_ref[1:2, :]).astype(BF16)
+        normed[at, :] = value
+        for part in range(3):
+            lanes = slice(part * d, (part + 1) * d)
+            qkv[at, lanes] = mm(value, weight[:, lanes]).astype(BF16)
+        return carry
+
+    def pair_block(p, carry):
+        def lanes(n):
+            return pl.ds(pl.multiple_of(p * 384 + n * 128, 128), 128)
+
+        attend(
+            lambda at: qkv[at, lanes(0)],
+            qkv[:, lanes(1)],
+            qkv[:, lanes(2)],
+            functools.partial(self_visible, first_ref),
+            self_extent,
+            *pair_keepers(mixed_ref, log_ref, p),
+        )
+        return carry
+
+    def middle_block(t, carry):
+        at = pl.ds(pl.multiple_of(t * TB, TB), TB)
+        mb = memory_ref.shape[0] * TB // tokens_ref.shape[0]
+        mem_at = pl.ds(pl.multiple_of(t * mb, mb), mb)
+        after = tokens_ref[at, :].astype(F32) + mm(mixed_ref[at, :], later[:, OUT_SELF * d : (OUT_SELF + 1) * d])
+        after_ref[at, :] = after
+        for n in range(2):
+            lanes = slice((2 * KV_CROSS + n) * d, (2 * KV_CROSS + n + 1) * d)
+            cross_kv_ref[mem_at, n * d : (n + 1) * d] = mm(memory_ref[mem_at, :], later[:, lanes]).astype(BF16)
+        unit, _ = norm_parts(after)
+        value = (unit * norms_ref[2:3, :] + norms_ref[3:4, :]).astype(BF16)
+        normed_two_ref[at, :] = value
+        cross_q_ref[at, :] = mm(value, later[:, QUERY_CROSS * d : (QUERY_CROSS + 1) * d]).astype(BF16)
+        return carry
+
+    def cross_block(p, carry):
+        def lanes(n):
+            return pl.ds(pl.multiple_of(p * 256 + n * 128, 128), 128)
+
+        q_lanes = pl.ds(pl.multiple_of(p * 128, 128), 128)
+        attend(
+            lambda at: cross_q_ref[at, q_lanes],
+            cross_kv_ref[:, lanes(0)],
+            cross_kv_ref[:, lanes(1)],
+            functools.partial(cross_visible, bounds_ref),
+            cross_extent,
+            *pair_keepers(cross_mixed_ref, cross_log_ref, p),
+        )
+        return carry
+
+    lax.fori_loop(0, 4, project_block, 0)
+    out_normed = pltpu.make_async_copy(normed, normed_any, local_sems.at[4])
+    out_qkv = pltpu.make_async_copy(qkv, qkv_any, local_sems.at[5])
+    out_normed.start()
+    out_qkv.start()
+    two.round(1)
+    lax.fori_loop(0, 2, pair_block, 0)
+    two.round(2)
+    lax.fori_loop(2, 5, pair_block, 0)
+    for r in range(3, narrow):
+        two.round(r)
+    three.begin_line()
+    lax.fori_loop(5, 8, pair_block, 0)
+    two.round(narrow)
+    three.begin_spread()
+    two.corners()
+    two.arrive()
+    keeps[1].wait()
+    out_later = pltpu.make_async_copy(later, later_any, local_sems.at[6])
+    out_later.start()
+    lax.fori_loop(0, 4, middle_block, 0)
+    three.round(1)
+    lax.fori_loop(0, 4, cross_block, 0)
+    three.round(2)
+    lax.fori_loop(4, 8, cross_block, 0)
+    for r in range(3, narrow + 1):
+        three.round(r)
+    three.corners()
+    three.arrive()
+    keeps[2].wait()
+    for gather in (one, two, three):
+        gather.close()
+    for copy in (out_wide, out_normed, out_qkv, out_later):
+        copy.wait()
+
+
+def pair_keepers(out_ref, log_ref, p):
+    def keep_out(at, value):
+        out_ref[at, pl.ds(pl.multiple_of(p * 128, 128), 128)] = value
+
+    def keep_log(h, at, value):
+        log_ref[0, p, h : h + 1, at] = value
+
+    return keep_out, keep_log
+
+
+def front(live_length, pair_starts, source_starts, weights, hidden_in, hidden_out, extra, tokens, memory, narrow):
+    self_query, self_key, self_value, self_output, cross_query, cross_key, cross_value, cross_output = weights
+    shard_rows, d = self_query.shape
+    rows, mem_rows = tokens.shape[0], memory.shape[0]
+    block = 4 * shard_rows + hidden_out.shape[0]
+    anywhere, vmem = pl.BlockSpec(memory_space=pl.ANY), pl.BlockSpec(memory_space=pltpu.VMEM)
+    smem = pl.BlockSpec(memory_space=pltpu.SMEM)
+    logs = jax.ShapeDtypeStruct((1, PAIRS, 8, SEQ), F32)
+
+    def kernel(*refs):
+        front_kernel(narrow, *refs[:8], refs[8:11], *refs[11:])
+
     return pl.pallas_call(
-        functools.partial(early_gather_kernel, wide, narrow),
-        in_specs=[pl.BlockSpec(memory_space=pl.ANY)],
-        out_specs=pl.BlockSpec(memory_space=pl.ANY),
-        out_shape=jax.ShapeDtypeStruct((rows * wide * narrow, columns), BF16),
+        kernel,
+        in_specs=[smem] * 3 + [vmem] * 13,
+        out_specs=[anywhere] * 5 + [vmem] * 11,
+        out_shape=[
+            shape(d, 3 * d + 128, BF16),
+            shape(d, 5 * d, BF16),
+            shape(8 * narrow * block, d, BF16),
+            shape(rows, d, BF16),
+            shape(rows, 3 * d, BF16),
+            shape(rows, d, BF16),
+            logs,
+            shape(8, d, F32),
+            jax.ShapeDtypeStruct((1, 1, SEQ), jnp.int32),
+            jax.ShapeDtypeStruct((1, 8, SEQ), jnp.int32),
+            shape(rows, d, F32),
+            shape(rows, d, BF16),
+            shape(rows, d, BF16),
+            shape(mem_rows, 2 * d, BF16),
+            shape(rows, d, BF16),
+            logs,
+        ],
         scratch_shapes=[
-            pltpu.SemaphoreType.DMA((10 * narrow,)),
-            pltpu.SemaphoreType.DMA((10 * narrow,)),
-            pltpu.SemaphoreType.DMA,
+            pltpu.VMEM((shard_rows, 3 * d + 128), BF16),
+            pltpu.VMEM((shard_rows, 5 * d), BF16),
+            pltpu.VMEM((block, d), BF16),
+            pltpu.VMEM((d, 3 * d + 128), BF16),
+            pltpu.VMEM((d, 5 * d), BF16),
+            pltpu.VMEM((rows, d), BF16),
+            pltpu.VMEM((rows, 3 * d), BF16),
+            *[pltpu.SemaphoreType.DMA((10 * narrow,))] * 6,
+            pltpu.SemaphoreType.DMA((7,)),
         ],
-        name="early_gather",
-        compiler_params=pltpu.CompilerParams(collective_id=0, has_side_effects=True),
-        cost_estimate=pl.CostEstimate(flops=0, bytes_accessed=200 << 20, transcendentals=0),
-    )(shard)
+        name="front",
+        compiler_params=pltpu.CompilerParams(collective_id=0, has_side_effects=True, vmem_limit_bytes=60 << 20),
+        cost_estimate=cost(30 * rows * d * d, 200 << 20),
+    )(
+        live_length,
+        pair_starts,
+        source_starts,
+        self_query,
+        self_key,
+        self_value,
+        cross_key,
+        cross_value,
+        self_output,
+        cross_query,
+        cross_output,
+        hidden_in,
+        hidden_out,
+        extra,
+        tokens,
+        memory,
+    )
 
 
 def stages_of(mesh_axes):
@@ -1543,41 +1837,64 @@
     digits = jnp.pad(digits, ((0, shard_rows - row_count), (0, 0)))
     norms = jnp.stack([first_gain, first_shift, second_gain, second_shift, third_gain, third_shift], axis=1)
     extra = jnp.pad(jnp.concatenate([norms, digits], axis=1), ((0, 0), (0, 120)))
-    early = early_gather(
-        jnp.concatenate(
-            [
-                by_pairs(self_query, self_key, self_value),
-                self_output,
-                by_pairs(cross_key, cross_value),
-                cross_query,
-                cross_output,
-                extra,
-            ],
-            axis=1,
-        ),
-        mesh_axes,
-    )
-    late = [lax.all_gather(part, names, axis=0, tiled=True) for part in (hidden_in, hidden_out)]
-
-    norms = early[:, EXTRA * 128 : EXTRA * 128 + 8].astype(F32).T
+    weights = (self_query, self_key, self_value, self_output, cross_query, cross_key, cross_value, cross_output)
+    fast = mesh_axes[0][1] == 8 and row_count == 1 and shard_rows % 32 == 0
+    if fast:
+        (
+            early,
+            later,
+            late,
+            normed_one,
+            qkv,
+            self_mixed,
+            self_logs,
+            norms,
+            first,
+            bounds,
+            after_self,
+            normed_two,
+            cross_q,
+            cross_kv,
+            cross_mixed,
+            cross_logs,
+        ) = front(
+            live_length,
+            pair_starts,
+            source_starts,
+            weights,
+            hidden_in,
+            hidden_out,
+            extra,
+            tokens,
+            memory,
+            mesh_axes[1][1],
+        )
+        late = [late.reshape(device_count, -1, WIDTH)]
+    else:
+        shard = [by_pairs(self_query, self_key, self_value), extra, self_output, cross_query]
+        shard += [by_pairs(cross_key, cross_value), cross_output]
+        early = lax.all_gather(jnp.concatenate(shard, axis=1), names, axis=0, tiled=True)
+        late = [lax.all_gather(part, names, axis=0, tiled=True) for part in (hidden_in, hidden_out)]
+        early, later = early[:, : 3 * WIDTH + 128], early[:, 3 * WIDTH + 128 :]
+        norms = early[:, 3 * WIDTH : 3 * WIDTH + 8].astype(F32).T
+        first, bounds = row_bounds(pair_starts, source_starts, live_length)
+        normed_one, qkv = project(tokens, norms, early)
+        self_mixed, self_logs = self_forward(first, qkv, row_count)
+        after_self, normed_two, cross_q, cross_kv = middle(self_mixed, tokens, memory, norms, later)
+        cross_mixed, cross_logs = cross_forward(bounds, cross_q, cross_kv, row_count)
+
     live_total = jnp.sum(norms[6]) * 256.0 + jnp.sum(norms[7])
     device = lax.axis_index(names)
     member = (group_bounds[:-1] <= device) & (device < group_bounds[1:])
     pair_tokens = jnp.sum(jnp.where(member, group_counts, 0))
     token_all = row_count * SEQ * device_count
     row_weight = pair_tokens.astype(F32) * (token_all / 1000.0) / live_total
-    first, bounds = row_bounds(pair_starts, source_starts, live_length)
-
-    normed_one, qkv = project(tokens, norms, early)
-    self_mixed, self_logs = self_forward(first, qkv, row_count)
-    after_self, normed_two, cross_q, cross_kv = middle(self_mixed, tokens, memory, norms, early)
-    cross_mixed, cross_logs = cross_forward(bounds, cross_q, cross_kv, row_count)
     layer_output, normed_three, activated, hidden_grad, branch_three, cross_total, branch_two, mixed_grad, norm_three = feed(
-        live_length, row_weight[None], cross_mixed, after_self, cotangent, norms, early, late
+        live_length, row_weight[None], cross_mixed, after_self, cotangent, norms, later, late
     )
 
     reduce_share, expand_share = outer_sum(activated, branch_three), outer_sum(normed_three, hidden_grad)
-    if mesh_axes[0][1] == 8 and row_count == 1 and shard_rows % 32 == 0:
+    if fast:
         narrow = mesh_axes[1][1]
         self_total, mixed_grad, memory_grad, norm_two, shares, reduce_shard, expand_low = cross_back(
             bounds,
@@ -1593,7 +1910,7 @@
             normed_two,
             memory,
             self_mixed,
-            early,
+            later,
             reduce_share,
             expand_share,
             narrow,
@@ -1633,7 +1950,7 @@
         cross_shares += [outer_sum(memory, part) for part in (ckv_grad[:, :WIDTH], ckv_grad[:, WIDTH:])]
         cross_sum = staged(*cross_shares)
         self_total, branch_one, mixed_grad, memory_grad, norm_two = cross_close(
-            cq_grad, ckv_grad, after_self, cross_total, norms, early
+            cq_grad, ckv_grad, after_self, cross_total, norms, later
         )
         mixed_grad = fence(mixed_grad, reduce_sum, expand_sum, cross_sum)
         qkv_grad = self_backward(first, self_logs, qkv, self_mixed, mixed_grad, row_count)

time: 514 us -> 479 us (0.932)
  between operations: 17.6 us -> 3.88 us
  local copies, waits for them, and re-layouts: 27.7 us -> 14 us
  Pallas kernels: 427 us -> 421 us
    unnamed x83 -> x41, local copies, waits for them, and re-layouts: 19.8 us -> 11.9 us
    pallas_call x5 -> x1, Pallas kernels: 166 us -> 161 us  [front(): pl.pallas_call(kernel, in_specs=[smem] * 3 + [vmem] * 13, out_specs=[anyw...]
  transfers between devices with their start and end apart: 2 -> 0, of which waited for: 0 -> 0; matrix products, arithmetic and copies ran while one was open for 3% -> 0% of each run, Pallas kernels for 33% -> 0%
where the time goes in v5:
time: 479 us; the launch traced here: 470 us
  Pallas kernels  421 us (88%)
  matrix products  26.7 us (6%)
  local copies, waits for them, and re-layouts  14 us (3%)
    pallas_call x1, Pallas kernels, front(): pl.pallas_call(kernel, in_specs=[smem] * 3 + [vmem] * 13, out_specs=[anyw...  161 us
    pallas_call x1, Pallas kernels, self_back(): pl.pallas_call(functools.partial(self_back_kernel, narrow), grid=(PAIRS +...  83.4 us
    pallas_call x1, Pallas kernels, cross_back(): pl.pallas_call(functools.partial(cross_back_kernel, narrow), grid=(PAIRS...  77.9 us
    pallas_call x1, Pallas kernels, feed(): pl.pallas_call(feed_kernel, grid=(rows // TB,), in_specs=[smem, smem, til...  56.3 us
    pallas_call x1, Pallas kernels, tail(): pl.pallas_call(kernel, in_specs=[vmem] * 3 + [anywhere], out_specs=[vmem]...  42.3 us
    dot_general x2, matrix products, outer_sum(): jnp.einsum('td,te->de', left_side, gradient, preferred_element_type=F32)  26.7 us
    unnamed x41, local copies, waits for them, and re-layouts  11.9 us

profile of v5, /device:TPU:0, one launch (start us, length us, event | category | flops | bytes accessed | tf_op | source)
XLA Modules:
  0.0 470.4 jit_solution(14091117250338711638)
XLA Ops:
  1.4 1.4 fusion.3
  3.5 0.8 concatenate.15
  4.2 0.1 copy.49
  4.3 0.6 pad.9.refs_13_
  4.9 161.2 %front.1 = (bf16[1024,3200]{1,0:T(8,128)(2,1)}, bf16[1024,5120]{1,0:T(8,128)(2,1)}, bf16[8192,1024]{1,0:T(8,128)(2,1)}, bf16[1024,1024]{1,0:T(8,128)(2,1)}, bf16...) custom-call(s32[1]{0:T(128)S(6)} %copy.61.refs_0_.live_ref, ...), custom_call_target="tpu_custom_call" | custom-call | flops 32212254720 | bytes 209715200 | tf_op jit(solution)/shard_map/front/pallas_call | solution.py:914
  166.2 1.5 slice_reduce_fusion
  169.0 56.3 %feed.1 = (bf16[1024,1024]{1,0:T(8,128)(2,1)}, bf16[1024,1024]{1,0:T(8,128)(2,1)}, bf16[1024,4096]{1,0:T(8,128)(2,1)}, bf16[1024,4096]{1,0:T(8,128)(2,1)}, bf16[...) custom-call(s32[1]{0:T(128)S(6)} %copy.61.refs_0_.live_ref, ...), custom_call_target="tpu_custom_call" | custom-call | flops 40802189312 | bytes 52428800 | tf_op jit(solution)/shard_map/feed/pallas_call | solution.py:468
  225.3 0.0 copy-start.14
  225.3 15.6 %convolution_convert_fusion.1 = bf16[4096,1024]{1,0:T(8,128)(2,1)} fusion(bf16[1024,4096]{1,0:T(8,128)(2,1)} %get-tuple-element.82, bf16[1024,1024]{1,0:T(8,128)(2,1)} %get-tuple-element.83), kind=kOutput, calls=%fused_computation.1 | convolution fusion | flops 8594128896 | bytes 18874368 | tf_op jit(solution)/shard_map/td,te->de/dot_general | solution.py:1095
  240.9 0.0 copy-done.13
  241.0 11.1 %convolution_convert_fusion = bf16[1024,4096]{1,0:T(8,128)(2,1)} fusion(bf16[1024,1024]{1,0:T(8,128)(2,1)S(1)} %copy-done.14, bf16[1024,4096]{1,0:T(8,128)(2,1)S(1)} %copy-done.13), kind=kOutput, calls=%fused_computation | convolution fusion | flops 8594128896 | bytes 18874368 | tf_op jit(solution)/shard_map/td,te->de/dot_general | solution.py:1095
  252.0 77.9 %cross_back.1 = (f32[1024,1024]{1,0:T(8,128)}, bf16[1024,1024]{1,0:T(8,128)(2,1)}, bf16[512,1024]{1,0:T(8,128)(2,1)}, f32[8,1024]{1,0:T(8,128)}, bf16[5120,1024]...) custom-call(s32[1,8,1024]{2,1,0:T(8,128)} %get-tuple-element.74.bounds_ref, ...), custom_call_target="tpu_custom_call" | custom-call | flops 42949672960 | bytes 104857600 | tf_op jit(solution)/shard_map/cross_back/pallas_call | solution.py:1418
  330.0 0.0 copy-start.1
  330.0 0.0 copy-start.2
  330.0 83.4 %self_back.1 = (bf16[1024,3072]{1,0:T(8,128)(2,1)}, bf16[1024,1024]{1,0:T(8,128)(2,1)}, f32[8,1024]{1,0:T(8,128)}, f32[32,2048]{1,0:T(8,128)}, f32[32,1024]{1,0:...) custom-call(s32[1,1,1024]{2,1,0:T(1,128)} %get-tuple-element.70.first_ref, ...), custom_call_target="tpu_custom_call" | custom-call | flops 42949672960 | bytes 104857600 | tf_op jit(solution)/shard_map/self_back/pallas_call | solution.py:1637
  413.4 1.8 pad_maximum_fusion
  415.2 2.8 copy-done
  418.0 0.8 copy-done.3
  418.7 42.3 %tail.1 = (f32[32,1024]{1,0:T(8,128)S(1)}, f32[32,1024]{1,0:T(8,128)S(1)}, f32[32,1024]{1,0:T(8,128)S(1)}, f32[8,1024]{1,0:T(8,128)S(1)}) custom-call(f32[8,1024]{1,0:T(8,128)S(1)} %copy-done.3, f32[8,1024]{1,0:T(8,128)S(1)} %copy-done.2, f32[8,1024]{1,0:T(8,128)S(1)} %copy-done.1, bf16[2,2,2,4,32,3072]{5,4,3,2,1,0:T(8,128)(2,1)S(1)} %bitcast.30), custom_call_target="tpu_custom_call" | custom-call | flops 4294967296 | bytes 104857600 | tf_op jit(solution)/shard_map/tail/pallas_call | solution.py:1781
  461.1 0.1 constant_dynamic-slice_fusion
  461.2 0.5 slice_bitcast_fusion
  461.7 1.3 copy.62
  463.0 1.0 copy.63
  464.0 0.7 copy.64
  464.6 0.7 copy.65
  465.3 0.7 copy.66
  466.0 0.7 copy.67
  466.6 0.7 copy.68
  467.3 0.7 copy.69
  467.9 0.7 copy.70
  468.6 0.7 copy.71
  469.2 0.8 copy.72
  (25 shorter events, 0.1 us)
Async XLA Ops:
  225.3 15.6 %copy-start.13 = (bf16[1024,4096]{1,0:T(8,128)(2,1)S(1)}, bf16[1024,4096]{1,0:T(8,128)(2,1)}, u32[]{:S(2)}) copy-start(bf16[1024,4096]{1,0:T(8,128)(2,1)} %get-tuple-element.85) | copy-start | bytes 25165828
  225.3 15.6 %copy-start.14 = (bf16[1024,1024]{1,0:T(8,128)(2,1)S(1)}, bf16[1024,1024]{1,0:T(8,128)(2,1)}, u32[]{:S(2)}) copy-start(bf16[1024,1024]{1,0:T(8,128)(2,1)} %get-tuple-element.84) | copy-start | bytes 6291460
  330.0 83.4 %copy-start.7 = (f32[32,2048]{1,0:T(8,128)S(1)}, f32[32,2048]{1,0:T(8,128)}, u32[]{:S(2)}) copy-start(f32[32,2048]{1,0:T(8,128)} %get-tuple-element.105) | copy-start | bytes 786436
  330.0 85.2 %copy-start.1 = (f32[8,1024]{1,0:T(8,128)S(1)}, f32[8,1024]{1,0:T(8,128)}, u32[]{:S(2)}) copy-start(f32[8,1024]{1,0:T(8,128)} %get-tuple-element.95.three) | copy-start | bytes 98308
  330.0 85.2 %copy-start.2 = (f32[8,1024]{1,0:T(8,128)S(1)}, f32[8,1024]{1,0:T(8,128)}, u32[]{:S(2)}) copy-start(f32[8,1024]{1,0:T(8,128)} %get-tuple-element.94.two) | copy-start | bytes 98308
  415.2 2.8 copy-start
  418.0 0.8 copy-start.3
  418.7 43.0 %copy-start.4 = (bf16[1024,1024]{1,0:T(8,128)(2,1)S(1)}, bf16[1024,1024]{1,0:T(8,128)(2,1)}, u32[]{:S(2)}) copy-start(bf16[1024,1024]{1,0:T(8,128)(2,1)} %get-tuple-element.137) | copy-start | bytes 6291460
  461.0 2.0 copy-start.5
  461.0 4.9 %copy-start.12 = (f32[32,1024]{1,0:T(8,128)S(1)}, f32[32,1024]{1,0:T(8,128)}, u32[]{:S(2)}) copy-start(f32[32,1024]{1,0:T(8,128)} %get-tuple-element.142) | copy-start | bytes 393220
  461.0 5.6 %copy-start.11 = (f32[32,1024]{1,0:T(8,128)S(1)}, f32[32,1024]{1,0:T(8,128)}, u32[]{:S(2)}) copy-start(f32[32,1024]{1,0:T(8,128)} %get-tuple-element.143) | copy-start | bytes 393220
  461.0 6.2 %copy-start.10 = (f32[32,1024]{1,0:T(8,128)S(1)}, f32[32,1024]{1,0:T(8,128)}, u32[]{:S(2)}) copy-start(f32[32,1024]{1,0:T(8,128)} %get-tuple-element.144) | copy-start | bytes 393220
  461.1 6.9 %copy-start.9 = (f32[32,1024]{1,0:T(8,128)S(1)}, f32[32,1024]{1,0:T(8,128)}, u32[]{:S(2)}) copy-start(f32[32,1024]{1,0:T(8,128)} %get-tuple-element.145) | copy-start | bytes 393220
  461.1 7.5 %copy-start.8 = (f32[32,1024]{1,0:T(8,128)S(1)}, f32[32,1024]{1,0:T(8,128)}, u32[]{:S(2)}) copy-start(f32[32,1024]{1,0:T(8,128)} %get-tuple-element.146) | copy-start | bytes 393220
  461.7 7.6 %copy-start.6 = (f32[128,1024]{1,0:T(8,128)S(1)}, f32[128,1024]{1,0:T(8,128)}, u32[]{:S(2)}) copy-start(f32[128,1024]{1,0:T(8,128)} %get-tuple-element.148) | copy-start | bytes 1572868

commit v6 on v5

--- a/solution.py
+++ b/solution.py
@@ -1104,6 +1104,7 @@
         self.from_core, self.a1, self.b1, self.a2, self.b2, self.from_line = buffers
         self.send_sems, self.recv_sems = send_sems, recv_sems
         self.narrow = narrow
+        self.slots = own.shape[0]
         self.half = self.a1.shape[-1]
         self.w, self.z = lax.axis_index("wide"), lax.axis_index("narrow")
         self.c, self.x, self.y = self.w & 1, (self.w >> 1) & 1, (self.w >> 2) & 1
@@ -1121,22 +1122,22 @@
         )
 
     def to_core(self, i):
-        return self.move(i, 0, self.theirs(i), self.from_core.at[i], (self.w ^ 1, self.z))
+        return self.move(i, 0, self.theirs(i), self.from_core.at[i % self.slots], (self.w ^ 1, self.z))
 
     def first(self, i):
         left, right = pl.ds(0, self.half), pl.ds(self.half, self.half)
         to_x, to_y = (self.w ^ 2, self.z), (self.w ^ 4, self.z)
         return (
-            self.move(i, 1, self.own.at[i, :, 1 - self.x, :, :, left], self.a1.at[i], to_x),
-            self.move(i, 2, self.own.at[i, 1 - self.y, :, :, :, right], self.b1.at[i], to_y),
+            self.move(i, 1, self.own.at[i % self.slots, :, 1 - self.x, :, :, left], self.a1.at[i % self.slots], to_x),
+            self.move(i, 2, self.own.at[i % self.slots, 1 - self.y, :, :, :, right], self.b1.at[i % self.slots], to_y),
         )
 
     def second(self, i):
         left, right = pl.ds(0, self.half), pl.ds(self.half, self.half)
         to_x, to_y = (self.w ^ 2, self.z), (self.w ^ 4, self.z)
         return (
-            self.move(i, 3, self.own.at[i, 1 - self.y, self.x, :, :, left], self.a2.at[i], to_y),
-            self.move(i, 4, self.own.at[i, self.y, 1 - self.x, :, :, right], self.b2.at[i], to_x),
+            self.move(i, 3, self.own.at[i % self.slots, 1 - self.y, self.x, :, :, left], self.a2.at[i % self.slots], to_y),
+            self.move(i, 4, self.own.at[i % self.slots, self.y, 1 - self.x, :, :, right], self.b2.at[i % self.slots], to_x),
         )
 
     def along(self, i):
@@ -1144,8 +1145,8 @@
             self.move(
                 i,
                 4 + mask,
-                self.own.at[i, self.y, self.x, self.z ^ mask],
-                self.from_line.at[i, mask - 1],
+                self.own.at[i % self.slots, self.y, self.x, self.z ^ mask],
+                self.from_line.at[i % self.slots, mask - 1],
                 (self.w, self.z ^ mask),
             )
             for mask in range(1, self.narrow)
@@ -1155,8 +1156,8 @@
         self.to_core(i).start()
 
     def add(self, i, y, x, columns, piece):
-        now = self.own[i, y, x, :, :, columns]
-        self.own[i, y, x, :, :, columns] = now + piece
+        now = self.own[i % self.slots, y, x, :, :, columns]
+        self.own[i % self.slots, y, x, :, :, columns] = now + piece
 
     def step(self, i, stage):
         both, left, right = slice(None), slice(0, self.half), slice(self.half, None)
@@ -1164,30 +1165,30 @@
             self.to_core(i).wait_recv()
             for a in range(2):
                 for b in range(2):
-                    self.add(i, a, b, both, self.from_core[i, a, b])
+                    self.add(i, a, b, both, self.from_core[i % self.slots, a, b])
             for copy in self.first(i):
                 copy.start()
         elif stage == 1:
             for copy in self.first(i):
                 copy.wait_recv()
             for a in range(2):
-                self.add(i, a, self.x, left, self.a1[i, a])
-                self.add(i, self.y, a, right, self.b1[i, a])
+                self.add(i, a, self.x, left, self.a1[i % self.slots, a])
+                self.add(i, self.y, a, right, self.b1[i % self.slots, a])
             for copy in self.second(i):
                 copy.start()
         elif stage == 2:
             for copy in self.second(i):
                 copy.wait_recv()
-            self.add(i, self.y, self.x, left, self.a2[i])
-            self.add(i, self.y, self.x, right, self.b2[i])
+            self.add(i, self.y, self.x, left, self.a2[i % self.slots])
+            self.add(i, self.y, self.x, right, self.b2[i % self.slots])
             for copy in self.along(i):
                 copy.start()
         else:
             for copy in self.along(i):
                 copy.wait_recv()
-            total = self.own[i, self.y, self.x, self.z].astype(F32)
+            total = self.own[i % self.slots, self.y, self.x, self.z].astype(F32)
             for mask in range(1, self.narrow):
-                total = total + self.from_line[i, mask - 1].astype(F32)
+                total = total + self.from_line[i % self.slots, mask - 1].astype(F32)
             self.keep(i, total)
 
     def close(self, i):
@@ -1195,8 +1196,8 @@
             copy.wait_send()
 
 
-def scatter_scratch(chunks, narrow, rows, width):
-    copies = chunks * (4 + narrow)
+def scatter_scratch(chunks, narrow, rows, width, more=0):
+    copies = (chunks + more) * (4 + narrow)
     return [
         pltpu.VMEM((chunks, 2, 2, narrow, rows, width), BF16),
         pltpu.VMEM((chunks, 2, 2, narrow, rows, width), BF16),
@@ -1207,7 +1208,7 @@
         pltpu.VMEM((chunks, narrow - 1, rows, width), BF16),
         pltpu.SemaphoreType.DMA((copies,)),
         pltpu.SemaphoreType.DMA((copies,)),
-        pltpu.SemaphoreType.DMA((chunks,)),
+        pltpu.SemaphoreType.DMA((chunks + more,)),
     ]
 
 
@@ -1216,34 +1217,38 @@
         own, *buffers, send_sems, recv_sems, self.load_sems = scratch
         self.shares = shares
         self.scatter = Scatter(own, self.other, buffers, keep, send_sems, recv_sems, narrow)
-        self.chunks = own.shape[0]
-
-    def part(self, i, core):
-        return self.shares[i](core)
+        self.chunks, self.slots = len(shares), own.shape[0]
 
     def other(self, i):
-        return self.part(i, 1 - self.scatter.c)
+        return self.shares[i](1 - self.scatter.c)
 
     def load(self, i):
-        return pltpu.make_async_copy(self.part(i, self.scatter.c), self.scatter.own.at[i], self.load_sems.at[i])
+        return pltpu.make_async_copy(
+            self.shares[i](self.scatter.c), self.scatter.own.at[i % self.slots], self.load_sems.at[i]
+        )
 
     def open(self):
-        for i in range(self.chunks):
+        for i in range(self.slots):
             self.load(i).start()
         greet_all(self.scatter.narrow)
         for i in range(2):
             self.scatter.begin(i)
+
+    def reuse(self, i):
+        self.scatter.close(i - self.slots)
+        self.load(i).start()
+        self.scatter.begin(i)
 
     def steps(self, plan):
         for i, stage in plan:
             if stage == 0:
                 self.load(i).wait()
             self.scatter.step(i, stage)
-            if stage == 0 and i + 2 < self.chunks:
+            if stage == 0 and i + 2 < self.slots:
                 self.scatter.begin(i + 2)
 
     def close(self):
-        for i in range(self.chunks):
+        for i in range(self.chunks - self.slots, self.chunks):
             self.scatter.close(i)
 
 
@@ -1269,23 +1274,23 @@
 
 
 CROSS_PLAN = (
-    ((0, 0), (1, 0)),
-    ((2, 0),),
-    ((0, 1),),
-    ((3, 0),),
-    ((1, 1),),
-    ((0, 2), (4, 0)),
-    ((2, 1),),
+    ((0, 0),),
+    ((1, 0),),
+    (),
+    ((0, 1), (1, 1)),
+    ((2, 0), (3, 0)),
     ((1, 2),),
-    ((0, 3), (3, 1), (5, 0)),
-    ((2, 2),),
-    ((1, 3), (4, 1)),
-    ((3, 2),),
-    ((2, 3),),
+    ((0, 2),),
+    ((2, 1), (4, 0)),
+    ((1, 3),),
+    ((2, 2), (3, 1), (4, 1)),
+    ((3, 2), (5, 0)),
+    ((4, 2),),
     ((5, 1),),
-    ((4, 2),),
-    ((3, 3),),
-    ((5, 2), (4, 3), (5, 3)),
+    ((5, 2),),
+    ((0, 3),),
+    (),
+    ((2, 3), (3, 3), (4, 3), (5, 3)),
 )
 CROSS_WIDE = 2
 
@@ -1492,22 +1497,23 @@
 
 
 SELF_PLAN = (
-    ((0, 0), (1, 0)),
+    ((0, 0),),
+    ((1, 0),),
     ((2, 0),),
-    ((0, 1),),
-    ((3, 0),),
+    ((0, 1), (2, 1), (3, 0), (4, 0)),
     ((1, 1),),
-    ((0, 2), (4, 0)),
-    ((2, 1),),
-    ((1, 2), (5, 0), (3, 1)),
-    ((0, 3),),
-    ((2, 2), (6, 0)),
-    ((1, 3), (4, 1)),
-    ((3, 2),),
-    ((2, 3), (5, 1)),
-    ((4, 2),),
-    ((3, 3), (6, 1), (5, 2), (4, 3), (6, 2), (5, 3), (6, 3)),
+    ((0, 2), (2, 2)),
+    ((3, 1), (5, 0)),
+    ((4, 1), (6, 0)),
+    ((0, 3), (2, 3), (1, 2), (3, 2), (5, 1)),
+    ((1, 3),),
+    ((3, 3), (4, 2), (6, 1), (7, 0)),
+    ((8, 0),),
+    ((5, 2), (5, 3), (6, 2), (7, 1), (8, 1), (9, 0)),
+    ((7, 2), (8, 2), (9, 1), (9, 2)),
+    ((4, 3), (6, 3), (7, 3), (8, 3), (9, 3)),
 )
+SELF_REUSE = {9: 7, 10: 8, 11: 9}
 SELF_WIDE = 4 - CROSS_WIDE
 SELF_CHUNKS = SELF_WIDE + 5
 
@@ -1523,27 +1529,38 @@
     tokens_ref,
     total_ref,
     norms_ref,
+    norm_two_ref,
+    norm_three_ref,
     early_any,
     wide_any,
     shares_any,
-    qkv_share_ref,
     out_ref,
-    ngrad_ref,
+    norm_out_ref,
     expand_ref,
     cross_output_ref,
     cross_query_ref,
     cross_key_ref,
     cross_value_ref,
     self_output_ref,
+    query_ref,
+    key_ref,
+    value_ref,
     dk_ref,
     dv_ref,
     dqkv,
     weight,
     weight_sem,
+    stage,
+    nval,
+    nin,
+    norm_send_sems,
+    norm_recv_sems,
     *scratch,
 ):
     step = pl.program_id(0)
     d = normed_ref.shape[1]
+
+    outs = (query_ref, key_ref, value_ref)
 
     def keep(i, value):
         i -= SELF_WIDE
@@ -1555,6 +1572,10 @@
             cross_query_ref[...] = value
         elif i == 4:
             self_output_ref[...] = value
+        elif i > 4:
+            for n in range(d // 128):
+                pair, kind = divmod((i - 5) * d // 128 + n, 3)
+                outs[kind][:, pair * 128 : (pair + 1) * 128] = value[:, n * 128 : (n + 1) * 128]
         else:
             for n in range(d // 256):
                 at = (i - 2) * d // 2 + n * 128
@@ -1564,7 +1585,11 @@
     def piece(i):
         return lambda core: shares_any.at[i, :, :, core]
 
+    def staged_piece(i):
+        return lambda core: stage.at[i, :, :, core]
+
     pieces = [columns_of(wide_any, (CROSS_WIDE + i) * d, d) for i in range(SELF_WIDE)] + [piece(i) for i in range(5)]
+    pieces += [staged_piece(i) for i in range(3)]
     carried = Carried(pieces, scratch, keep, narrow)
     load = pltpu.make_async_copy(early_any.at[:, pl.ds(0, 3 * d)], weight, weight_sem)
 
@@ -1596,15 +1621,25 @@
         dqkv[:, pl.ds(pl.multiple_of(base + 128, 128), 128)] = (dk_ref[...] * HEAD_DIM**-0.5).astype(BF16)
         dqkv[:, pl.ds(pl.multiple_of(base + 256, 128), 128)] = dv_ref[...].astype(BF16)
 
-    @pl.when((step >= PAIRS) & (step < PAIRS + 3))
-    def _():
-        at = pl.ds(pl.multiple_of((step - PAIRS) * d, d), d)
-        outer_into(qkv_share_ref, normed_ref, dqkv[:, at])
+    rows = stage.shape[5]
+    group = 2 * narrow * rows
+
+    def multiply(m):
+        for a in range(2):
+            for b in range(2):
+                at = (2 * a + b) * group
+                product = tn(normed_ref[:, at : at + group], dqkv[:, m * d : (m + 1) * d])
+                stage[m, a, b] = product.astype(BF16).reshape(2, narrow, rows, d)
+
+    for m in range(3):
+        pl.when(step == PAIRS + m)(functools.partial(multiply, m))
 
     @pl.when(step == PAIRS + 3)
     def _():
         load.wait()
-        ngrad_ref[...] = jnp.zeros_like(ngrad_ref)
+        nval[0] = jnp.zeros_like(nval[0])
+        nval[0, 2:4, :] = norm_two_ref[0:2, :]
+        nval[0, 4:6, :] = norm_three_ref[0:2, :]
 
     @pl.when(step >= PAIRS + 3)
     def _():
@@ -1613,15 +1648,58 @@
         unit, inverse = norm_parts(tokens_ref[...].astype(F32))
         total = total_ref[...] + norm_back(unit, inverse, norms_ref[0:1, :], gradient)
         out_ref[...] = total.astype(BF16)
-        ngrad_ref[0:1, :] += jnp.sum(gradient * unit, axis=0, keepdims=True)
-        ngrad_ref[1:2, :] += jnp.sum(gradient, axis=0, keepdims=True)
-
-    for number, plan in enumerate(SELF_PLAN):
+        nval[0, 0:1, :] += jnp.sum(gradient * unit, axis=0, keepdims=True)
+        nval[0, 1:2, :] += jnp.sum(gradient, axis=0, keepdims=True)
+
+    w, z = carried.scatter.w, carried.scatter.z
+
+    def norm_copy(stage_number, number, target):
+        return pltpu.make_async_remote_copy(
+            src_ref=nval.at[stage_number],
+            dst_ref=nin.at[number],
+            send_sem=norm_send_sems.at[number],
+            recv_sem=norm_recv_sems.at[number],
+            device_id=target,
+            device_id_type=pl.DeviceIdType.MESH,
+        )
+
+    norm_copies = [[norm_copy(0, 0, (w ^ 1, z))], [norm_copy(1, 1, (w ^ 2, z))], [norm_copy(2, 2, (w ^ 4, z))]]
+    norm_copies.append([norm_copy(3, 2 + mask, (w, z ^ mask)) for mask in range(1, narrow)])
+
+    def norm_step(number):
+        if number > 0:
+            for copy in norm_copies[number - 1]:
+                copy.wait_recv()
+            value = nval[number - 1]
+            if number < 4:
+                nval[number] = value + nin[number - 1]
+            else:
+                for mask in range(1, narrow):
+                    value = value + nin[2 + mask]
+                norm_out_ref[...] = value
+        if number < 4:
+            for copy in norm_copies[number]:
+                copy.start()
+
+    last = len(SELF_PLAN) - 1
+    for number, plan in enumerate(SELF_PLAN[:last]):
         pl.when(step == number)(functools.partial(carried.steps, plan))
-    pl.when(step == len(SELF_PLAN) - 1)(carried.close)
-
-
-def self_back(first, logs, qkv, mixed, grad, normed, tokens, total, norms, early, wide_share, shares, narrow):
+        if number in SELF_REUSE:
+            pl.when(step == number)(functools.partial(carried.reuse, SELF_REUSE[number]))
+
+    @pl.when(step == last)
+    def _():
+        for number in range(5):
+            norm_step(number)
+            if number < len(SELF_PLAN[last]):
+                carried.steps(SELF_PLAN[last][number : number + 1])
+        carried.close()
+        for copies in norm_copies:
+            for copy in copies:
+                copy.wait_send()
+
+
+def self_back(first, logs, qkv, mixed, grad, normed, tokens, total, norms, norm_two, norm_three, early, wide_share, shares, narrow):
     rows, d = mixed.shape
     shard_rows = d // (8 * narrow)
 
@@ -1647,23 +1725,23 @@
             by_token,
             by_token,
             whole(8, d),
+            whole(8, d),
+            whole(8, d),
             anywhere,
             anywhere,
             anywhere,
         ],
         out_specs=[
-            pl.BlockSpec((d, d), lambda s: (0, jnp.clip(s - PAIRS, 0, 2))),
             by_token,
             whole(8, d),
             whole(shard_rows, SELF_WIDE * d),
-            *[whole(shard_rows, d)] * 5,
+            *[whole(shard_rows, d)] * 8,
         ],
         out_shape=[
-            shape(d, 3 * d, BF16),
             shape(rows, d, BF16),
             shape(8, d, F32),
             shape(shard_rows, SELF_WIDE * d, F32),
-            *[shape(shard_rows, d, F32)] * 5,
+            *[shape(shard_rows, d, F32)] * 8,
         ],
         scratch_shapes=[
             pltpu.VMEM((SEQ, 128), F32),
@@ -1671,7 +1749,12 @@
             pltpu.VMEM((rows, 3 * d), BF16),
             pltpu.VMEM((d, 3 * d), BF16),
             pltpu.SemaphoreType.DMA,
-            *scatter_scratch(SELF_CHUNKS, narrow, shard_rows, d),
+            pltpu.VMEM((3, 2, 2, 2, narrow, shard_rows, d), BF16),
+            pltpu.VMEM((4, 8, d), F32),
+            pltpu.VMEM((2 + narrow, 8, d), F32),
+            pltpu.SemaphoreType.DMA((2 + narrow,)),
+            pltpu.SemaphoreType.DMA((2 + narrow,)),
+            *scatter_scratch(SELF_CHUNKS, narrow, shard_rows, d, 3),
         ],
         name="self_back",
         compiler_params=pltpu.CompilerParams(collective_id=3, has_side_effects=True, vmem_limit_bytes=60 << 20),
@@ -1686,114 +1769,12 @@
         tokens,
         total,
         norms,
+        norm_two,
+        norm_three,
         early,
         share_views(wide_share, narrow, shard_rows),
         shares.reshape(5, 2, 2, 2, narrow, shard_rows, d),
     )
-
-
-TAIL_CHUNKS = 6
-TAIL_PLAN = [(0, 0), (1, 0)]
-for _k in range(TAIL_CHUNKS + 5):
-    TAIL_PLAN += [(_k + 2, 0)] if _k + 2 < TAIL_CHUNKS else []
-    TAIL_PLAN += [(_k, 1)] if _k < TAIL_CHUNKS else []
-    TAIL_PLAN += [(_k - 1, 2)] if 0 <= _k - 1 < TAIL_CHUNKS else []
-    TAIL_PLAN += [(_k - 3, 3)] if 0 <= _k - 3 < TAIL_CHUNKS else []
-
-
-def tail_kernel(
-    narrow,
-    norm_refs,
-    qkv_any,
-    query_ref,
-    key_ref,
-    value_ref,
-    norm_out_ref,
-    nval,
-    nin,
-    norm_send_sems,
-    norm_recv_sems,
-    *scratch,
-):
-    width = scratch[0].shape[-1]
-    outs = (query_ref, key_ref, value_ref)
-
-    def keep(i, value):
-        for n in range(width // 128):
-            pair, kind = divmod(i * width // 128 + n, 3)
-            outs[kind][:, pair * 128 : (pair + 1) * 128] = value[:, n * 128 : (n + 1) * 128]
-
-    carried = Carried([columns_of(qkv_any, i * width, width) for i in range(TAIL_CHUNKS)], scratch, keep, narrow)
-    w, z = carried.scatter.w, carried.scatter.z
-
-    def norm_copy(stage, number, target):
-        return pltpu.make_async_remote_copy(
-            src_ref=nval.at[stage],
-            dst_ref=nin.at[number],
-            send_sem=norm_send_sems.at[number],
-            recv_sem=norm_recv_sems.at[number],
-            device_id=target,
-            device_id_type=pl.DeviceIdType.MESH,
-        )
-
-    norm_copies = [[norm_copy(0, 0, (w ^ 1, z))], [norm_copy(1, 1, (w ^ 2, z))], [norm_copy(2, 2, (w ^ 4, z))]]
-    norm_copies.append([norm_copy(3, 2 + mask, (w, z ^ mask)) for mask in range(1, narrow)])
-
-    def norm_step(stage):
-        if stage == 0:
-            for n, ref in enumerate(norm_refs):
-                nval[0, 2 * n : 2 * n + 2, :] = ref[0:2, :]
-            nval[0, 6:8, :] = jnp.zeros_like(norm_refs[0][0:2, :])
-        else:
-            for copy in norm_copies[stage - 1]:
-                copy.wait_recv()
-            value = nval[stage - 1]
-            if stage < 4:
-                nval[stage] = value + nin[stage - 1]
-            else:
-                for mask in range(1, narrow):
-                    value = value + nin[2 + mask]
-                norm_out_ref[...] = value
-        if stage < 4:
-            for copy in norm_copies[stage]:
-                copy.start()
-
-    carried.open()
-    for number, action in enumerate(TAIL_PLAN):
-        carried.steps([action])
-        if number % 4 == 0 and number // 4 <= 4:
-            norm_step(number // 4)
-    carried.close()
-    for copies in norm_copies:
-        for copy in copies:
-            copy.wait_send()
-
-
-def tail(qkv_share, norm_grads, narrow):
-    d = qkv_share.shape[0]
-    shard_rows = d // (8 * narrow)
-    width = 3 * d // TAIL_CHUNKS
-    anywhere, vmem = pl.BlockSpec(memory_space=pl.ANY), pl.BlockSpec(memory_space=pltpu.VMEM)
-
-    def kernel(one, two, three, *refs):
-        tail_kernel(narrow, (one, two, three), *refs)
-
-    return pl.pallas_call(
-        kernel,
-        in_specs=[vmem] * 3 + [anywhere],
-        out_specs=[vmem] * 4,
-        out_shape=[*[shape(shard_rows, d, F32)] * 3, shape(8, d, F32)],
-        scratch_shapes=[
-            pltpu.VMEM((4, 8, d), F32),
-            pltpu.VMEM((2 + narrow, 8, d), F32),
-            pltpu.SemaphoreType.DMA((2 + narrow,)),
-            pltpu.SemaphoreType.DMA((2 + narrow,)),
-            *scatter_scratch(TAIL_CHUNKS, narrow, shard_rows, width),
-        ],
-        name="tail",
-        compiler_params=pltpu.CompilerParams(collective_id=1, has_side_effects=True, vmem_limit_bytes=40 << 20),
-        cost_estimate=cost(4 * d * d * d, 100 << 20),
-    )(*norm_grads, share_views(qkv_share, narrow, shard_rows))
 
 
 def on_device(
@@ -1916,15 +1897,17 @@
             narrow,
         )
         (
-            qkv_share,
             tokens_grad,
-            norm_one,
+            norm_grads,
             expand_high,
             cross_output_shard,
             cross_query_shard,
             cross_key_shard,
             cross_value_shard,
             output_shard,
+            query_shard,
+            key_shard,
+            value_shard,
         ) = self_back(
             first,
             self_logs,
@@ -1935,12 +1918,13 @@
             tokens,
             self_total,
             norms,
+            norm_two,
+            norm_three,
             early,
             expand_share,
             shares,
             narrow,
         )
-        query_shard, key_shard, value_shard, norm_grads = tail(qkv_share, (norm_one, norm_two, norm_three), narrow)
         expand_shard = jnp.concatenate([expand_low, expand_high], axis=1)
     else:
         reduce_sum, expand_sum = staged(reduce_share), staged(expand_share)

time: 479 us -> 459 us (0.958)
  Pallas kernels: 421 us -> 402 us
    pallas_call x1 -> x0, Pallas kernels: 42.3 us -> none  [tail(): pl.pallas_call(kernel, in_specs=[vmem] * 3 + [anywhere], out_specs=[vmem]...]
    pallas_call x1, Pallas kernels: 83.4 us -> 111 us  [self_back(): pl.pallas_call(functools.partial(self_back_kernel, narrow), grid=(PAIRS +...]
    unnamed x41 -> x37, local copies, waits for them, and re-layouts: 11.9 us -> 10.2 us
where the time goes in v6:
time: 459 us; the launch traced here: 451 us
  Pallas kernels  402 us (88%)
  matrix products  26.9 us (6%)
  local copies, waits for them, and re-layouts  13.1 us (3%)
  other arithmetic  4.73 us (1%)
    pallas_call x1, Pallas kernels, front(): pl.pallas_call(kernel, in_specs=[smem] * 3 + [vmem] * 13, out_specs=[anyw...  161 us
    pallas_call x1, Pallas kernels, self_back(): pl.pallas_call(functools.partial(self_back_kernel, narrow), grid=(PAIRS +...  111 us
    pallas_call x1, Pallas kernels, cross_back(): pl.pallas_call(functools.partial(cross_back_kernel, narrow), grid=(PAIRS...  73.5 us
    pallas_call x1, Pallas kernels, feed(): pl.pallas_call(feed_kernel, grid=(rows // TB,), in_specs=[smem, smem, til...  56.3 us
    dot_general x2, matrix products, outer_sum(): jnp.einsum('td,te->de', left_side, gradient, preferred_element_type=F32)  26.9 us
    unnamed x37, local copies, waits for them, and re-layouts  10.2 us

profile of v6, /device:TPU:0, one launch (start us, length us, event | category | flops | bytes accessed | tf_op | source)
XLA Modules:
  0.0 451.0 jit_solution(4727957245400032371)
XLA Ops:
  1.4 1.4 fusion.3
  3.5 0.8 concatenate.15
  4.2 0.1 copy.49
  4.3 0.6 pad.9.refs_13_
  4.9 161.2 %front.1 = (bf16[1024,3200]{1,0:T(8,128)(2,1)}, bf16[1024,5120]{1,0:T(8,128)(2,1)}, bf16[8192,1024]{1,0:T(8,128)(2,1)}, bf16[1024,1024]{1,0:T(8,128)(2,1)}, bf16...) custom-call(s32[1]{0:T(128)S(6)} %copy.61.refs_0_.live_ref, ...), custom_call_target="tpu_custom_call" | custom-call | flops 32212254720 | bytes 209715200 | tf_op jit(solution)/shard_map/front/pallas_call | solution.py:914
  166.2 1.5 slice_reduce_fusion
  169.0 56.3 %feed.1 = (bf16[1024,1024]{1,0:T(8,128)(2,1)}, bf16[1024,1024]{1,0:T(8,128)(2,1)}, bf16[1024,4096]{1,0:T(8,128)(2,1)}, bf16[1024,4096]{1,0:T(8,128)(2,1)}, bf16[...) custom-call(s32[1]{0:T(128)S(6)} %copy.61.refs_0_.live_ref, ...), custom_call_target="tpu_custom_call" | custom-call | flops 40802189312 | bytes 52428800 | tf_op jit(solution)/shard_map/feed/pallas_call | solution.py:468
  225.3 0.0 copy-start.11
  225.3 0.0 copy-start.12
  225.3 15.6 %convolution_convert_fusion.1 = bf16[4096,1024]{1,0:T(8,128)(2,1)} fusion(bf16[1024,4096]{1,0:T(8,128)(2,1)} %get-tuple-element.80, bf16[1024,1024]{1,0:T(8,128)(2,1)} %get-tuple-element.81), kind=kOutput, calls=%fused_computation.1 | convolution fusion | flops 8594128896 | bytes 18874368 | tf_op jit(solution)/shard_map/td,te->de/dot_general | solution.py:1095
  241.0 0.0 copy-done.11
  241.0 0.0 copy-done.12
  241.0 11.3 %convolution_convert_fusion = bf16[1024,4096]{1,0:T(8,128)(2,1)} fusion(bf16[1024,1024]{1,0:T(8,128)(2,1)S(1)} %copy-done.12, bf16[1024,4096]{1,0:T(8,128)(2,1)S(1)} %copy-done.11), kind=kOutput, calls=%fused_computation | convolution fusion | flops 8594128896 | bytes 18874368 | tf_op jit(solution)/shard_map/td,te->de/dot_general | solution.py:1095
  252.2 73.5 %cross_back.1 = (f32[1024,1024]{1,0:T(8,128)}, bf16[1024,1024]{1,0:T(8,128)(2,1)}, bf16[512,1024]{1,0:T(8,128)(2,1)}, f32[8,1024]{1,0:T(8,128)}, bf16[5120,1024]...) custom-call(s32[1,8,1024]{2,1,0:T(8,128)} %get-tuple-element.72.bounds_ref, ...), custom_call_target="tpu_custom_call" | custom-call | flops 42949672960 | bytes 104857600 | tf_op jit(solution)/shard_map/cross_back/pallas_call | solution.py:1423
  325.7 0.0 copy-start.2
  325.7 111.4 %self_back.1 = (bf16[1024,1024]{1,0:T(8,128)(2,1)}, f32[8,1024]{1,0:T(8,128)}, f32[32,2048]{1,0:T(8,128)}, f32[32,1024]{1,0:T(8,128)}, f32[32,1024]{1,0:T(8,128)...) custom-call(s32[1,1,1024]{2,1,0:T(1,128)} %get-tuple-element.68.firs, ...), custom_call_target="tpu_custom_call" | custom-call | flops 42949672960 | bytes 104857600 | tf_op jit(solution)/shard_map/self_back/pallas_call | solution.py:1715
  437.1 0.0 copy-start
  437.2 0.9 constant_dynamic-slice_fusion
  438.0 0.5 slice_bitcast_fusion
  438.6 1.8 pad_maximum_fusion
  440.4 3.1 copy.62
  443.6 1.0 copy.63
  444.5 0.7 copy.64
  445.2 0.7 copy.65
  445.9 0.7 copy.66
  446.5 0.7 copy.67
  447.2 0.7 copy.68
  447.8 0.7 copy.69
  448.5 0.7 copy.70
  449.2 0.7 copy.71
  449.8 0.0 copy-done.1
  449.8 0.8 copy.72
  (20 shorter events, 0.0 us)
Async XLA Ops:
  225.3 15.7 %copy-start.11 = (bf16[1024,4096]{1,0:T(8,128)(2,1)S(1)}, bf16[1024,4096]{1,0:T(8,128)(2,1)}, u32[]{:S(2)}) copy-start(bf16[1024,4096]{1,0:T(8,128)(2,1)} %get-tuple-element.83) | copy-start | bytes 25165828
  225.3 15.6 %copy-start.12 = (bf16[1024,1024]{1,0:T(8,128)(2,1)S(1)}, bf16[1024,1024]{1,0:T(8,128)(2,1)}, u32[]{:S(2)}) copy-start(bf16[1024,1024]{1,0:T(8,128)(2,1)} %get-tuple-element.82) | copy-start | bytes 6291460
  325.7 112.9 %copy-start.2 = (f32[32,2048]{1,0:T(8,128)S(1)}, f32[32,2048]{1,0:T(8,128)}, u32[]{:S(2)}) copy-start(f32[32,2048]{1,0:T(8,128)} %get-tuple-element.101) | copy-start | bytes 786436
  437.1 6.5 %copy-start = (bf16[512,1024]{1,0:T(8,128)(2,1)S(1)}, bf16[512,1024]{1,0:T(8,128)(2,1)}, u32[]{:S(2)}) copy-start(bf16[512,1024]{1,0:T(8,128)(2,1)} %get-tuple-element.134) | copy-start | bytes 3145732
  437.1 7.4 %copy-start.10 = (f32[32,1024]{1,0:T(8,128)S(1)}, f32[32,1024]{1,0:T(8,128)}, u32[]{:S(2)}) copy-start(f32[32,1024]{1,0:T(8,128)} %get-tuple-element.135) | copy-start | bytes 393220
  437.1 8.1 %copy-start.9 = (f32[32,1024]{1,0:T(8,128)S(1)}, f32[32,1024]{1,0:T(8,128)}, u32[]{:S(2)}) copy-start(f32[32,1024]{1,0:T(8,128)} %get-tuple-element.136) | copy-start | bytes 393220
  437.1 8.7 %copy-start.8 = (f32[32,1024]{1,0:T(8,128)S(1)}, f32[32,1024]{1,0:T(8,128)}, u32[]{:S(2)}) copy-start(f32[32,1024]{1,0:T(8,128)} %get-tuple-element.137) | copy-start | bytes 393220
  437.2 9.4 %copy-start.7 = (f32[32,1024]{1,0:T(8,128)S(1)}, f32[32,1024]{1,0:T(8,128)}, u32[]{:S(2)}) copy-start(f32[32,1024]{1,0:T(8,128)} %get-tuple-element.138) | copy-start | bytes 393220
  438.6 8.6 %copy-start.6 = (f32[32,1024]{1,0:T(8,128)S(1)}, f32[32,1024]{1,0:T(8,128)}, u32[]{:S(2)}) copy-start(f32[32,1024]{1,0:T(8,128)} %get-tuple-element.139) | copy-start | bytes 393220
  438.6 9.3 %copy-start.5 = (f32[32,1024]{1,0:T(8,128)S(1)}, f32[32,1024]{1,0:T(8,128)}, u32[]{:S(2)}) copy-start(f32[32,1024]{1,0:T(8,128)} %get-tuple-element.140) | copy-start | bytes 393220
  438.6 9.9 %copy-start.4 = (f32[32,1024]{1,0:T(8,128)S(1)}, f32[32,1024]{1,0:T(8,128)}, u32[]{:S(2)}) copy-start(f32[32,1024]{1,0:T(8,128)} %get-tuple-element.141) | copy-start | bytes 393220
  440.4 8.7 %copy-start.3 = (f32[32,1024]{1,0:T(8,128)S(1)}, f32[32,1024]{1,0:T(8,128)}, u32[]{:S(2)}) copy-start(f32[32,1024]{1,0:T(8,128)} %get-tuple-element.142) | copy-start | bytes 393220
  440.4 9.4 %copy-start.1 = (f32[128,1024]{1,0:T(8,128)S(1)}, f32[128,1024]{1,0:T(8,128)}, u32[]{:S(2)}) copy-start(f32[128,1024]{1,0:T(8,128)} %get-tuple-element.144) | copy-start | bytes 1572868

commit v7 on v6

--- a/solution.py
+++ b/solution.py
@@ -396,8 +396,11 @@
 
 
 def feed_kernel(
+    narrow,
+    token_all,
     live_ref,
-    weight_ref,
+    group_bounds_ref,
+    group_counts_ref,
     mixed_ref,
     before_ref,
     cot_ref,
@@ -420,7 +423,13 @@
     row = block // per_row
     places = lax.broadcasted_iota(jnp.int32, (TB, 1), 0) + (block % per_row) * TB
     live = (places < live_ref[row]).astype(F32)
-    out_grad = cot_ref[...].astype(F32) * live * weight_ref[0]
+    device = lax.axis_index("wide") * narrow + lax.axis_index("narrow")
+    pair_tokens = jnp.int32(0)
+    for g in range(group_counts_ref.shape[0]):
+        member = (group_bounds_ref[g] <= device) & (device < group_bounds_ref[g + 1])
+        pair_tokens += jnp.where(member, group_counts_ref[g], 0)
+    live_total = jnp.sum(norms_ref[6:7, :], keepdims=True) * 256.0 + jnp.sum(norms_ref[7:8, :], keepdims=True)
+    out_grad = cot_ref[...].astype(F32) * live * (pair_tokens.astype(F32) * (token_all / 1000.0) / live_total)
     branch = out_grad.astype(BF16)
     b3_ref[...] = branch
     after = before_ref[...] + mm(mixed_ref[...], wo_ref[...])
@@ -453,8 +462,9 @@
     add_norm_grads(ngrad_ref, unit, back)
 
 
-def feed(live_length, row_weight, mixed, before, cotangent, norms, early, late):
+def feed(live_length, group_bounds, group_counts, mixed, before, cotangent, norms, early, late, mesh_axes):
     rows, d = cotangent.shape
+    (_, wide), (_, narrow) = mesh_axes
     ff = 4 * d
     if len(late) == 1:
         devices, block, _ = late[0].shape
@@ -466,9 +476,10 @@
         late_specs = [whole(d, ff), whole(ff, d)]
     smem = pl.BlockSpec(memory_space=pltpu.SMEM)
     return pl.pallas_call(
-        feed_kernel,
+        functools.partial(feed_kernel, narrow, rows * wide * narrow),
         grid=(rows // TB,),
         in_specs=[
+            smem,
             smem,
             smem,
             tile(TB, d),
@@ -503,7 +514,7 @@
         name="feed",
         compiler_params=params(58),
         cost_estimate=cost(38 * rows * d * d, 50 << 20),
-    )(live_length, row_weight, mixed, before, cotangent, norms, early, *late)
+    )(live_length, group_bounds, group_counts, mixed, before, cotangent, norms, early, *late)
 
 
 def cross_close_kernel(
@@ -873,13 +884,14 @@
     keeps[1].wait()
     out_later = pltpu.make_async_copy(later, later_any, local_sems.at[6])
     out_later.start()
+    three.round(1)
     lax.fori_loop(0, 4, middle_block, 0)
-    three.round(1)
+    three.round(2)
     lax.fori_loop(0, 4, cross_block, 0)
-    three.round(2)
+    for r in range(3, narrow):
+        three.round(r)
     lax.fori_loop(4, 8, cross_block, 0)
-    for r in range(3, narrow + 1):
-        three.round(r)
+    three.round(narrow)
     three.corners()
     three.arrive()
     keeps[2].wait()
@@ -1531,6 +1543,7 @@
     norms_ref,
     norm_two_ref,
     norm_three_ref,
+    expand_low_ref,
     early_any,
     wide_any,
     shares_any,
@@ -1565,7 +1578,7 @@
     def keep(i, value):
         i -= SELF_WIDE
         if i < 0:
-            expand_ref[:, (i + SELF_WIDE) * d : (i + SELF_WIDE + 1) * d] = value
+            expand_ref[:, (i + 4) * d : (i + 5) * d] = value
         elif i == 0:
             cross_output_ref[...] = value
         elif i == 1:
@@ -1597,6 +1610,7 @@
     def _():
         carried.open()
         load.start()
+        expand_ref[:, : CROSS_WIDE * d] = expand_low_ref[...]
 
     @pl.when(step < PAIRS)
     def _():
@@ -1699,7 +1713,7 @@
                 copy.wait_send()
 
 
-def self_back(first, logs, qkv, mixed, grad, normed, tokens, total, norms, norm_two, norm_three, early, wide_share, shares, narrow):
+def self_back(first, logs, qkv, mixed, grad, normed, tokens, total, norms, norm_two, norm_three, expand_low, early, wide_share, shares, narrow):
     rows, d = mixed.shape
     shard_rows = d // (8 * narrow)
 
@@ -1727,6 +1741,7 @@
             whole(8, d),
             whole(8, d),
             whole(8, d),
+            whole(shard_rows, CROSS_WIDE * d),
             anywhere,
             anywhere,
             anywhere,
@@ -1734,13 +1749,13 @@
         out_specs=[
             by_token,
             whole(8, d),
-            whole(shard_rows, SELF_WIDE * d),
+            whole(shard_rows, 4 * d),
             *[whole(shard_rows, d)] * 8,
         ],
         out_shape=[
             shape(rows, d, BF16),
             shape(8, d, F32),
-            shape(shard_rows, SELF_WIDE * d, F32),
+            shape(shard_rows, 4 * d, F32),
             *[shape(shard_rows, d, F32)] * 8,
         ],
         scratch_shapes=[
@@ -1771,6 +1786,7 @@
         norms,
         norm_two,
         norm_three,
+        expand_low,
         early,
         share_views(wide_share, narrow, shard_rows),
         shares.reshape(5, 2, 2, 2, narrow, shard_rows, d),
@@ -1864,14 +1880,9 @@
         after_self, normed_two, cross_q, cross_kv = middle(self_mixed, tokens, memory, norms, later)
         cross_mixed, cross_logs = cross_forward(bounds, cross_q, cross_kv, row_count)
 
-    live_total = jnp.sum(norms[6]) * 256.0 + jnp.sum(norms[7])
     device = lax.axis_index(names)
-    member = (group_bounds[:-1] <= device) & (device < group_bounds[1:])
-    pair_tokens = jnp.sum(jnp.where(member, group_counts, 0))
-    token_all = row_count * SEQ * device_count
-    row_weight = pair_tokens.astype(F32) * (token_all / 1000.0) / live_total
     layer_output, normed_three, activated, hidden_grad, branch_three, cross_total, branch_two, mixed_grad, norm_three = feed(
-        live_length, row_weight[None], cross_mixed, after_self, cotangent, norms, later, late
+        live_length, group_bounds, group_counts, cross_mixed, after_self, cotangent, norms, later, late, mesh_axes
     )
 
     reduce_share, expand_share = outer_sum(activated, branch_three), outer_sum(normed_three, hidden_grad)
@@ -1899,7 +1910,7 @@
         (
             tokens_grad,
             norm_grads,
-            expand_high,
+            expand_shard,
             cross_output_shard,
             cross_query_shard,
             cross_key_shard,
@@ -1920,12 +1931,12 @@
             norms,
             norm_two,
             norm_three,
+            expand_low,
             early,
             expand_share,
             shares,
             narrow,
         )
-        expand_shard = jnp.concatenate([expand_low, expand_high], axis=1)
     else:
         reduce_sum, expand_sum = staged(reduce_share), staged(expand_share)
         cq_grad, ckv_grad = cross_backward(bounds, cross_logs, cross_q, cross_kv, cross_mixed, mixed_grad, row_count)

time: 459 us -> 453 us (0.987)
  other arithmetic: 4.73 us -> 0.01 us
    unnamed x37 -> x38, local copies, waits for them, and re-layouts: 10.2 us -> 11 us
where the time goes in v7:
time: 453 us; the launch traced here: 445 us
  Pallas kernels  402 us (89%)
  matrix products  26.8 us (6%)
  local copies, waits for them, and re-layouts  13.9 us (3%)
    pallas_call x1, Pallas kernels, front(): pl.pallas_call(kernel, in_specs=[smem] * 3 + [vmem] * 13, out_specs=[anyw...  161 us
    pallas_call x1, Pallas kernels, self_back(): pl.pallas_call(functools.partial(self_back_kernel, narrow), grid=(PAIRS +...  112 us
    pallas_call x1, Pallas kernels, cross_back(): pl.pallas_call(functools.partial(cross_back_kernel, narrow), grid=(PAIRS...  73.2 us
    pallas_call x1, Pallas kernels, feed(): pl.pallas_call(functools.partial(feed_kernel, narrow, rows * wide * narro...  56.4 us
    dot_general x2, matrix products, outer_sum(): jnp.einsum('td,te->de', left_side, gradient, preferred_element_type=F32)  26.8 us
    unnamed x38, local copies, waits for them, and re-layouts  11 us

profile of v7, /device:TPU:0, one launch (start us, length us, event | category | flops | bytes accessed | tf_op | source)
XLA Modules:
  0.0 444.8 jit_solution(7753489092893112114)
XLA Ops:
  1.4 0.8 concatenate.12
  2.1 0.1 copy.49
  2.2 0.6 pad.9.refs_13_
  2.8 160.8 %front.1 = (bf16[1024,3200]{1,0:T(8,128)(2,1)}, bf16[1024,5120]{1,0:T(8,128)(2,1)}, bf16[8192,1024]{1,0:T(8,128)(2,1)}, bf16[1024,1024]{1,0:T(8,128)(2,1)}, bf16...) custom-call(s32[1]{0:T(128)S(6)} %copy.62.refs_0_.live_ref, ...), custom_call_target="tpu_custom_call" | custom-call | flops 32212254720 | bytes 209715200 | tf_op jit(solution)/shard_map/front/pallas_call | solution.py:926
  163.7 56.4 %feed.1 = (bf16[1024,1024]{1,0:T(8,128)(2,1)}, bf16[1024,1024]{1,0:T(8,128)(2,1)}, bf16[1024,4096]{1,0:T(8,128)(2,1)}, bf16[1024,4096]{1,0:T(8,128)(2,1)}, bf16[...) custom-call(s32[1]{0:T(128)S(6)} %copy.62.refs_0_.live_ref, ...), custom_call_target="tpu_custom_call" | custom-call | flops 40802189312 | bytes 52428800 | tf_op jit(solution)/shard_map/feed/pallas_call | solution.py:478
  220.0 0.0 copy-start.11
  220.1 0.0 copy-start.12
  220.1 15.6 %convolution_convert_fusion = bf16[1024,4096]{1,0:T(8,128)(2,1)} fusion(bf16[1024,1024]{1,0:T(8,128)(2,1)} %get-tuple-element.82, bf16[1024,4096]{1,0:T(8,128)(2,1)} %get-tuple-element.83), kind=kOutput, calls=%fused_computation | convolution fusion | flops 8594128896 | bytes 18874368 | tf_op jit(solution)/shard_map/td,te->de/dot_general | solution.py:1107
  235.6 0.0 copy-done.11
  235.6 0.0 copy-done.12
  235.6 11.3 %convolution_convert_fusion.1 = bf16[4096,1024]{1,0:T(8,128)(2,1)} fusion(bf16[1024,4096]{1,0:T(8,128)(2,1)S(1)} %copy-done.11, bf16[1024,1024]{1,0:T(8,128)(2,1)S(1)} %copy-done.12), kind=kOutput, calls=%fused_computation.1 | convolution fusion | flops 8594128896 | bytes 18874368 | tf_op jit(solution)/shard_map/td,te->de/dot_general | solution.py:1107
  246.9 73.2 %cross_back.1 = (f32[1024,1024]{1,0:T(8,128)}, bf16[1024,1024]{1,0:T(8,128)(2,1)}, bf16[512,1024]{1,0:T(8,128)(2,1)}, f32[8,1024]{1,0:T(8,128)}, bf16[5120,1024]...) custom-call(s32[1,8,1024]{2,1,0:T(8,128)} %get-tuple-element.72.bounds_ref, ...), custom_call_target="tpu_custom_call" | custom-call | flops 42949672960 | bytes 104857600 | tf_op jit(solution)/shard_map/cross_back/pallas_call | solution.py:1435
  320.1 111.8 %self_back.1 = (bf16[1024,1024]{1,0:T(8,128)(2,1)}, f32[8,1024]{1,0:T(8,128)}, f32[32,4096]{1,0:T(8,128)}, f32[32,1024]{1,0:T(8,128)}, f32[32,1024]{1,0:T(8,128)...) custom-call(s32[1,1,1024]{2,1,0:T(1,128)} %get-tuple-element.68.firs, ...), custom_call_target="tpu_custom_call" | custom-call | flops 42949672960 | bytes 104857600 | tf_op jit(solution)/shard_map/self_back/pallas_call | solution.py:1729
  431.9 0.0 copy-start
  432.0 0.9 constant_dynamic-slice_fusion
  432.9 0.5 slice_bitcast_fusion
  433.4 3.2 copy.63
  436.6 1.0 copy.64
  437.5 0.7 copy.65
  438.2 0.7 copy.66
  438.9 0.7 copy.67
  439.5 0.7 copy.68
  440.2 0.7 copy.69
  440.8 0.0 copy-done.5
  440.8 0.7 copy.70
  441.5 0.0 copy-done.4
  441.5 0.7 copy.71
  442.1 0.0 copy-done.3
  442.2 0.7 copy.72
  442.8 0.0 copy-done.2
  442.8 0.8 copy.73
  443.6 0.8 copy.74
  (18 shorter events, 0.0 us)
Async XLA Ops:
  220.0 15.6 %copy-start.11 = (bf16[1024,4096]{1,0:T(8,128)(2,1)S(1)}, bf16[1024,4096]{1,0:T(8,128)(2,1)}, u32[]{:S(2)}) copy-start(bf16[1024,4096]{1,0:T(8,128)(2,1)} %get-tuple-element.80) | copy-start | bytes 25165828
  220.1 15.6 %copy-start.12 = (bf16[1024,1024]{1,0:T(8,128)(2,1)S(1)}, bf16[1024,1024]{1,0:T(8,128)(2,1)}, u32[]{:S(2)}) copy-start(bf16[1024,1024]{1,0:T(8,128)(2,1)} %get-tuple-element.81) | copy-start | bytes 6291460
  431.9 4.7 %copy-start = (bf16[512,1024]{1,0:T(8,128)(2,1)S(1)}, bf16[512,1024]{1,0:T(8,128)(2,1)}, u32[]{:S(2)}) copy-start(bf16[512,1024]{1,0:T(8,128)(2,1)} %get-tuple-element.132) | copy-start | bytes 3145732
  431.9 5.6 %copy-start.10 = (f32[32,1024]{1,0:T(8,128)S(1)}, f32[32,1024]{1,0:T(8,128)}, u32[]{:S(2)}) copy-start(f32[32,1024]{1,0:T(8,128)} %get-tuple-element.133) | copy-start | bytes 393220
  431.9 6.3 %copy-start.9 = (f32[32,1024]{1,0:T(8,128)S(1)}, f32[32,1024]{1,0:T(8,128)}, u32[]{:S(2)}) copy-start(f32[32,1024]{1,0:T(8,128)} %get-tuple-element.134) | copy-start | bytes 393220
  431.9 6.9 %copy-start.8 = (f32[32,1024]{1,0:T(8,128)S(1)}, f32[32,1024]{1,0:T(8,128)}, u32[]{:S(2)}) copy-start(f32[32,1024]{1,0:T(8,128)} %get-tuple-element.135) | copy-start | bytes 393220
  431.9 7.6 %copy-start.7 = (f32[32,1024]{1,0:T(8,128)S(1)}, f32[32,1024]{1,0:T(8,128)}, u32[]{:S(2)}) copy-start(f32[32,1024]{1,0:T(8,128)} %get-tuple-element.136) | copy-start | bytes 393220
  431.9 8.2 %copy-start.6 = (f32[32,1024]{1,0:T(8,128)S(1)}, f32[32,1024]{1,0:T(8,128)}, u32[]{:S(2)}) copy-start(f32[32,1024]{1,0:T(8,128)} %get-tuple-element.137) | copy-start | bytes 393220
  431.9 8.9 %copy-start.5 = (f32[32,1024]{1,0:T(8,128)S(1)}, f32[32,1024]{1,0:T(8,128)}, u32[]{:S(2)}) copy-start(f32[32,1024]{1,0:T(8,128)} %get-tuple-element.138) | copy-start | bytes 393220
  432.0 9.5 %copy-start.4 = (f32[32,1024]{1,0:T(8,128)S(1)}, f32[32,1024]{1,0:T(8,128)}, u32[]{:S(2)}) copy-start(f32[32,1024]{1,0:T(8,128)} %get-tuple-element.139) | copy-start | bytes 393220
  432.0 10.2 %copy-start.3 = (f32[32,1024]{1,0:T(8,128)S(1)}, f32[32,1024]{1,0:T(8,128)}, u32[]{:S(2)}) copy-start(f32[32,1024]{1,0:T(8,128)} %get-tuple-element.140) | copy-start | bytes 393220
  433.4 9.4 %copy-start.2 = (f32[32,4096]{1,0:T(8,128)S(1)}, f32[32,4096]{1,0:T(8,128)}, u32[]{:S(2)}) copy-start(f32[32,4096]{1,0:T(8,128)} %get-tuple-element.141) | copy-start | bytes 1572868
  433.4 10.2 %copy-start.1 = (f32[128,1024]{1,0:T(8,128)S(1)}, f32[128,1024]{1,0:T(8,128)}, u32[]{:S(2)}) copy-start(f32[128,1024]{1,0:T(8,128)} %get-tuple-element.142) | copy-start | bytes 1572868

commit v8 on v7

--- a/solution.py
+++ b/solution.py
@@ -417,8 +417,32 @@
     b2_ref,
     grad_ref,
     ngrad_ref,
+    *scratch,
 ):
     block = pl.program_id(0)
+    loads = []
+    if scratch:
+        late_any = win_ref
+        win_ref, wout_ref, sems = scratch
+        devices, quad, _ = win_ref.shape
+        rows, share = quad // 4, devices // 4
+        for n in range(4):
+            lane, holders = pl.ds(n * rows, rows), pl.ds(n * share, share)
+            loads.append(
+                (
+                    pltpu.make_async_copy(late_any.at[:, lane], win_ref.at[:, lane], sems.at[2 * n]),
+                    pltpu.make_async_copy(
+                        late_any.at[holders, pl.ds(quad, quad)], wout_ref.at[holders], sems.at[2 * n + 1]
+                    ),
+                )
+            )
+
+        @pl.when(block == 0)
+        def _():
+            for pair in loads:
+                for load in pair:
+                    load.start()
+
     per_row = SEQ // TB
     row = block // per_row
     places = lax.broadcasted_iota(jnp.int32, (TB, 1), 0) + (block % per_row) * TB
@@ -440,6 +464,8 @@
     result, back = after, None
     for part in range(act_ref.shape[1] // d):
         at = slice(part * d, (part + 1) * d)
+        for load in loads[part] if loads else ():
+            pl.when(block == 0)(load.wait)
         win, wout = hidden_parts(win_ref, wout_ref, part, d)
         x = mm(normed, win)
         square = x * x
@@ -469,11 +495,10 @@
     if len(late) == 1:
         devices, block, _ = late[0].shape
         late = late * 2
-        late_specs = [
-            pl.BlockSpec((devices, block // 2, d), lambda b, n=n: (0, n, 0), pipeline_mode=pl.Buffered(1)) for n in range(2)
-        ]
+        late_specs = [pl.BlockSpec(memory_space=pl.ANY)] * 2
+        scratch = [pltpu.VMEM((devices, block // 2, d), BF16)] * 2 + [pltpu.SemaphoreType.DMA((8,))]
     else:
-        late_specs = [whole(d, ff), whole(ff, d)]
+        late_specs, scratch = [whole(d, ff), whole(ff, d)], []
     smem = pl.BlockSpec(memory_space=pltpu.SMEM)
     return pl.pallas_call(
         functools.partial(feed_kernel, narrow, rows * wide * narrow),
@@ -511,6 +536,7 @@
             shape(rows, d, BF16),
             shape(8, d, F32),
         ],
+        scratch_shapes=scratch,
         name="feed",
         compiler_params=params(58),
         cost_estimate=cost(38 * rows * d * d, 50 << 20),
@@ -1318,11 +1344,11 @@
     before_ref,
     total_ref,
     norms_ref,
-    mixed_ref,
-    b2_ref,
-    normed_ref,
-    memory_ref,
-    self_mixed_ref,
+    mixed_any,
+    b2_any,
+    normed_any,
+    memory_any,
+    self_mixed_any,
     early_any,
     share_any,
     wide_any,
@@ -1342,6 +1368,11 @@
     wkv,
     wo,
     weight_sems,
+    mixed_ref,
+    b2_ref,
+    normed_ref,
+    memory_ref,
+    self_mixed_ref,
     *scratch,
 ):
     step = pl.program_id(0)
@@ -1364,11 +1395,23 @@
         pltpu.make_async_copy(early_any.at[:, pl.ds(2 * KV_CROSS * d, 2 * d)], wkv, weight_sems.at[1]),
         pltpu.make_async_copy(early_any.at[:, pl.ds(OUT_SELF * d, d)], wo, weight_sems.at[2]),
     ]
+    later_loads = [
+        pltpu.make_async_copy(source, target, weight_sems.at[3 + n])
+        for n, (source, target) in enumerate(
+            (
+                (mixed_any, mixed_ref),
+                (b2_any, b2_ref),
+                (normed_any, normed_ref),
+                (memory_any, memory_ref),
+                (self_mixed_any, self_mixed_ref),
+            )
+        )
+    ]
 
     @pl.when(step == 0)
     def _():
         carried.open()
-        for load in loads:
+        for load in loads + later_loads:
             load.start()
 
     @pl.when(step < PAIRS)
@@ -1405,7 +1448,12 @@
         ngrad_ref[0:1, :] += jnp.sum(gradient * unit, axis=0, keepdims=True)
         ngrad_ref[1:2, :] += jnp.sum(gradient, axis=0, keepdims=True)
 
-    pl.when(step == tokens_end)(lambda: outer_into(shares_ref, mixed_ref, b2_ref[...]))
+    @pl.when(step == tokens_end)
+    def _():
+        for load in later_loads:
+            load.wait()
+        outer_into(shares_ref, mixed_ref, b2_ref[...])
+
     pl.when(step == tokens_end + 1)(lambda: outer_into(shares_ref, normed_ref, dq_ref[...]))
     pl.when(step == tokens_end + 2)(lambda: outer_into(shares_ref, memory_ref, dkv_ref[:, :d]))
     pl.when(step == tokens_end + 3)(lambda: outer_into(shares_ref, memory_ref, dkv_ref[:, d:]))
@@ -1445,11 +1493,7 @@
             by_token,
             by_token,
             whole(8, d),
-            whole(rows, d),
-            whole(rows, d),
-            whole(rows, d),
-            whole(mem_rows, d),
-            whole(rows, d),
+            *[anywhere] * 5,
             anywhere,
             anywhere,
             anywhere,
@@ -1481,7 +1525,12 @@
             pltpu.VMEM((d, d), BF16),
             pltpu.VMEM((d, 2 * d), BF16),
             pltpu.VMEM((d, d), BF16),
-            pltpu.SemaphoreType.DMA((3,)),
+            pltpu.SemaphoreType.DMA((8,)),
+            pltpu.VMEM((rows, d), BF16),
+            pltpu.VMEM((rows, d), BF16),
+            pltpu.VMEM((rows, d), BF16),
+            pltpu.VMEM((mem_rows, d), BF16),
+            pltpu.VMEM((rows, d), BF16),
             *scatter_scratch(4 + CROSS_WIDE, narrow, shard_rows, d),
         ],
         name="cross_back",

time: 453 us -> 450 us (level)
  no operation moved by 1% of the time
where the time goes in v8:
time: 450 us; the launch traced here: 442 us
  Pallas kernels  399 us (89%)
  matrix products  26.8 us (6%)
  local copies, waits for them, and re-layouts  13.9 us (3%)
    pallas_call x1, Pallas kernels, front(): pl.pallas_call(kernel, in_specs=[smem] * 3 + [vmem] * 13, out_specs=[anyw...  161 us
    pallas_call x1, Pallas kernels, self_back(): pl.pallas_call(functools.partial(self_back_kernel, narrow), grid=(PAIRS +...  112 us
    pallas_call x1, Pallas kernels, cross_back(): pl.pallas_call(functools.partial(cross_back_kernel, narrow), grid=(PAIRS...  70.4 us
    pallas_call x1, Pallas kernels, feed(): pl.pallas_call(functools.partial(feed_kernel, narrow, rows * wide * narro...  56.3 us
    dot_general x2, matrix products, outer_sum(): jnp.einsum('td,te->de', left_side, gradient, preferred_element_type=F32)  26.8 us
    unnamed x38, local copies, waits for them, and re-layouts  11 us

profile of v8, /device:TPU:0, one launch (start us, length us, event | category | flops | bytes accessed | tf_op | source)
XLA Modules:
  0.0 441.9 jit_solution(11180365350069551417)
XLA Ops:
  1.4 0.8 concatenate.12
  2.1 0.1 copy.49
  2.2 0.6 pad.9.refs_13_
  2.8 160.8 %front.1 = (bf16[1024,3200]{1,0:T(8,128)(2,1)}, bf16[1024,5120]{1,0:T(8,128)(2,1)}, bf16[8192,1024]{1,0:T(8,128)(2,1)}, bf16[1024,1024]{1,0:T(8,128)(2,1)}, bf16...) custom-call(s32[1]{0:T(128)S(6)} %copy.62.refs_0_.live_ref, ...), custom_call_target="tpu_custom_call" | custom-call | flops 32212254720 | bytes 209715200 | tf_op jit(solution)/shard_map/front/pallas_call | solution.py:952
  163.7 56.3 %feed.1 = (bf16[1024,1024]{1,0:T(8,128)(2,1)}, bf16[1024,1024]{1,0:T(8,128)(2,1)}, bf16[1024,4096]{1,0:T(8,128)(2,1)}, bf16[1024,4096]{1,0:T(8,128)(2,1)}, bf16[...) custom-call(s32[1]{0:T(128)S(6)} %copy.62.refs_0_.live_ref, ...), custom_call_target="tpu_custom_call" | custom-call | flops 40802189312 | bytes 52428800 | tf_op jit(solution)/shard_map/feed/pallas_call | solution.py:503
  220.0 0.0 copy-start.11
  220.0 15.6 %convolution_convert_fusion = bf16[1024,4096]{1,0:T(8,128)(2,1)} fusion(bf16[1024,1024]{1,0:T(8,128)(2,1)} %get-tuple-element.82, bf16[1024,4096]{1,0:T(8,128)(2,1)} %get-tuple-element.83), kind=kOutput, calls=%fused_computation | convolution fusion | flops 8594128896 | bytes 18874368 | tf_op jit(solution)/shard_map/td,te->de/dot_general | solution.py:1133
  235.6 0.0 copy-done.11
  235.6 11.3 %convolution_convert_fusion.1 = bf16[4096,1024]{1,0:T(8,128)(2,1)} fusion(bf16[1024,4096]{1,0:T(8,128)(2,1)S(1)} %copy-done.11, bf16[1024,1024]{1,0:T(8,128)(2,1)S(1)} %copy-done.12), kind=kOutput, calls=%fused_computation.1 | convolution fusion | flops 8594128896 | bytes 18874368 | tf_op jit(solution)/shard_map/td,te->de/dot_general | solution.py:1133
  246.8 70.4 %cross_back.1 = (f32[1024,1024]{1,0:T(8,128)}, bf16[1024,1024]{1,0:T(8,128)(2,1)}, bf16[512,1024]{1,0:T(8,128)(2,1)}, f32[8,1024]{1,0:T(8,128)}, bf16[5120,1024]...) custom-call(s32[1,8,1024]{2,1,0:T(8,128)} %get-tuple-element.72.bounds_ref, ...), custom_call_target="tpu_custom_call" | custom-call | flops 42949672960 | bytes 104857600 | tf_op jit(solution)/shard_map/cross_back/pallas_call | solution.py:1483
  317.2 111.7 %self_back.1 = (bf16[1024,1024]{1,0:T(8,128)(2,1)}, f32[8,1024]{1,0:T(8,128)}, f32[32,4096]{1,0:T(8,128)}, f32[32,1024]{1,0:T(8,128)}, f32[32,1024]{1,0:T(8,128)...) custom-call(s32[1,1,1024]{2,1,0:T(1,128)} %get-tuple-element.68.firs, ...), custom_call_target="tpu_custom_call" | custom-call | flops 42949672960 | bytes 104857600 | tf_op jit(solution)/shard_map/self_back/pallas_call | solution.py:1778
  429.1 0.9 constant_dynamic-slice_fusion
  429.9 0.5 slice_bitcast_fusion
  430.5 3.2 copy.63
  433.7 0.0 copy-done
  433.7 1.0 copy.64
  434.6 0.7 copy.65
  435.3 0.7 copy.66
  435.9 0.0 copy-done.8
  436.0 0.7 copy.67
  436.6 0.0 copy-done.7
  436.6 0.7 copy.68
  437.3 0.0 copy-done.6
  437.3 0.7 copy.69
  437.9 0.0 copy-done.5
  437.9 0.7 copy.70
  438.6 0.0 copy-done.4
  438.6 0.7 copy.71
  439.2 0.7 copy.72
  439.9 0.8 copy.73
  440.7 0.0 copy-done.1
  440.7 0.8 copy.74
  (18 shorter events, 0.0 us)
Async XLA Ops:
  220.0 15.6 %copy-start.11 = (bf16[1024,4096]{1,0:T(8,128)(2,1)S(1)}, bf16[1024,4096]{1,0:T(8,128)(2,1)}, u32[]{:S(2)}) copy-start(bf16[1024,4096]{1,0:T(8,128)(2,1)} %get-tuple-element.80) | copy-start | bytes 25165828
  220.0 15.6 %copy-start.12 = (bf16[1024,1024]{1,0:T(8,128)(2,1)S(1)}, bf16[1024,1024]{1,0:T(8,128)(2,1)}, u32[]{:S(2)}) copy-start(bf16[1024,1024]{1,0:T(8,128)(2,1)} %get-tuple-element.81) | copy-start | bytes 6291460
  429.0 4.7 %copy-start = (bf16[512,1024]{1,0:T(8,128)(2,1)S(1)}, bf16[512,1024]{1,0:T(8,128)(2,1)}, u32[]{:S(2)}) copy-start(bf16[512,1024]{1,0:T(8,128)(2,1)} %get-tuple-element.132) | copy-start | bytes 3145732
  429.0 5.6 %copy-start.10 = (f32[32,1024]{1,0:T(8,128)S(1)}, f32[32,1024]{1,0:T(8,128)}, u32[]{:S(2)}) copy-start(f32[32,1024]{1,0:T(8,128)} %get-tuple-element.133) | copy-start | bytes 393220
  429.0 6.3 %copy-start.9 = (f32[32,1024]{1,0:T(8,128)S(1)}, f32[32,1024]{1,0:T(8,128)}, u32[]{:S(2)}) copy-start(f32[32,1024]{1,0:T(8,128)} %get-tuple-element.134) | copy-start | bytes 393220
  429.0 6.9 %copy-start.8 = (f32[32,1024]{1,0:T(8,128)S(1)}, f32[32,1024]{1,0:T(8,128)}, u32[]{:S(2)}) copy-start(f32[32,1024]{1,0:T(8,128)} %get-tuple-element.135) | copy-start | bytes 393220
  429.0 7.6 %copy-start.7 = (f32[32,1024]{1,0:T(8,128)S(1)}, f32[32,1024]{1,0:T(8,128)}, u32[]{:S(2)}) copy-start(f32[32,1024]{1,0:T(8,128)} %get-tuple-element.136) | copy-start | bytes 393220
  429.0 8.2 %copy-start.6 = (f32[32,1024]{1,0:T(8,128)S(1)}, f32[32,1024]{1,0:T(8,128)}, u32[]{:S(2)}) copy-start(f32[32,1024]{1,0:T(8,128)} %get-tuple-element.137) | copy-start | bytes 393220
  429.0 8.9 %copy-start.5 = (f32[32,1024]{1,0:T(8,128)S(1)}, f32[32,1024]{1,0:T(8,128)}, u32[]{:S(2)}) copy-start(f32[32,1024]{1,0:T(8,128)} %get-tuple-element.138) | copy-start | bytes 393220
  429.0 9.5 %copy-start.4 = (f32[32,1024]{1,0:T(8,128)S(1)}, f32[32,1024]{1,0:T(8,128)}, u32[]{:S(2)}) copy-start(f32[32,1024]{1,0:T(8,128)} %get-tuple-element.139) | copy-start | bytes 393220
  429.1 10.2 %copy-start.3 = (f32[32,1024]{1,0:T(8,128)S(1)}, f32[32,1024]{1,0:T(8,128)}, u32[]{:S(2)}) copy-start(f32[32,1024]{1,0:T(8,128)} %get-tuple-element.140) | copy-start | bytes 393220
  430.5 9.4 %copy-start.2 = (f32[32,4096]{1,0:T(8,128)S(1)}, f32[32,4096]{1,0:T(8,128)}, u32[]{:S(2)}) copy-start(f32[32,4096]{1,0:T(8,128)} %get-tuple-element.141) | copy-start | bytes 1572868
  430.5 10.2 %copy-start.1 = (f32[128,1024]{1,0:T(8,128)S(1)}, f32[128,1024]{1,0:T(8,128)}, u32[]{:S(2)}) copy-start(f32[128,1024]{1,0:T(8,128)} %get-tuple-element.142) | copy-start | bytes 1572868

commit v9 on v8

--- a/solution.py
+++ b/solution.py
@@ -2012,6 +2012,8 @@
         cross_output_shard, cross_query_shard, *cross_shards = cross_sum.result().reshape(4, shard_rows, WIDTH)
         cross_key_shard, cross_value_shard = from_pairs(jnp.concatenate(cross_shards, axis=1), 2)
 
+    live = (jnp.arange(SEQ, dtype=jnp.int32)[None, :] < live_length[:, None]).reshape(-1, 1)
+    tokens_grad = jnp.where(live, tokens_grad, jnp.zeros_like(tokens_grad))
     norm_shards = lax.dynamic_slice_in_dim(norm_grads, device * shard_rows, shard_rows, axis=1)
     return (
         layer_output,

time: 450 us -> 450 us (level)
    unnamed x38 -> x37, local copies, waits for them, and re-layouts: 11 us -> 7.85 us
where the time goes in v9:
time: 450 us; the launch traced here: 442 us
  Pallas kernels  399 us (89%)
  matrix products  26.8 us (6%)
  local copies, waits for them, and re-layouts  10.7 us (2%)
    pallas_call x1, Pallas kernels, front(): pl.pallas_call(kernel, in_specs=[smem] * 3 + [vmem] * 13, out_specs=[anyw...  161 us
    pallas_call x1, Pallas kernels, self_back(): pl.pallas_call(functools.partial(self_back_kernel, narrow), grid=(PAIRS +...  112 us
    pallas_call x1, Pallas kernels, cross_back(): pl.pallas_call(functools.partial(cross_back_kernel, narrow), grid=(PAIRS...  70.4 us
    pallas_call x1, Pallas kernels, feed(): pl.pallas_call(functools.partial(feed_kernel, narrow, rows * wide * narro...  56.3 us
    dot_general x2, matrix products, outer_sum(): jnp.einsum('td,te->de', left_side, gradient, preferred_element_type=F32)  26.8 us

profile of v9, /device:TPU:0, one launch (start us, length us, event | category | flops | bytes accessed | tf_op | source)
XLA Modules:
  0.0 441.9 jit_solution(12944995775226151614)
XLA Ops:
  1.4 0.8 concatenate.12
  2.1 0.1 copy.49
  2.2 0.6 pad.9.refs_13_
  2.8 160.8 %front.1 = (bf16[1024,3200]{1,0:T(8,128)(2,1)}, bf16[1024,5120]{1,0:T(8,128)(2,1)}, bf16[8192,1024]{1,0:T(8,128)(2,1)}, bf16[1024,1024]{1,0:T(8,128)(2,1)}, bf16...) custom-call(s32[1]{0:T(128)} %copy.61.refs_0_.live_ref, ...), custom_call_target="tpu_custom_call" | custom-call | flops 32212254720 | bytes 209715200 | tf_op jit(solution)/shard_map/front/pallas_call | solution.py:952
  163.7 56.3 %feed.1 = (bf16[1024,1024]{1,0:T(8,128)(2,1)}, bf16[1024,1024]{1,0:T(8,128)(2,1)}, bf16[1024,4096]{1,0:T(8,128)(2,1)}, bf16[1024,4096]{1,0:T(8,128)(2,1)}, bf16[...) custom-call(s32[1]{0:T(128)} %copy.61.refs_0_.live_ref, ...), custom_call_target="tpu_custom_call" | custom-call | flops 40802189312 | bytes 52428800 | tf_op jit(solution)/shard_map/feed/pallas_call | solution.py:503
  220.0 0.0 copy-start.11
  220.0 0.0 copy-start.12
  220.0 15.6 %convolution_convert_fusion = bf16[1024,4096]{1,0:T(8,128)(2,1)} fusion(bf16[1024,1024]{1,0:T(8,128)(2,1)} %get-tuple-element.82, bf16[1024,4096]{1,0:T(8,128)(2,1)} %get-tuple-element.83), kind=kOutput, calls=%fused_computation | convolution fusion | flops 8594128896 | bytes 18874368 | tf_op jit(solution)/shard_map/td,te->de/dot_general | solution.py:1133
  235.6 0.0 copy-done.11
  235.6 0.0 copy-done.12
  235.6 11.3 %convolution_convert_fusion.1 = bf16[4096,1024]{1,0:T(8,128)(2,1)} fusion(bf16[1024,4096]{1,0:T(8,128)(2,1)S(1)} %copy-done.11, bf16[1024,1024]{1,0:T(8,128)(2,1)S(1)} %copy-done.12), kind=kOutput, calls=%fused_computation.1 | convolution fusion | flops 8594128896 | bytes 18874368 | tf_op jit(solution)/shard_map/td,te->de/dot_general | solution.py:1133
  246.8 70.4 %cross_back.1 = (f32[1024,1024]{1,0:T(8,128)}, bf16[1024,1024]{1,0:T(8,128)(2,1)}, bf16[512,1024]{1,0:T(8,128)(2,1)}, f32[8,1024]{1,0:T(8,128)}, bf16[5120,1024]...) custom-call(s32[1,8,1024]{2,1,0:T(8,128)} %get-tuple-element.72.bounds_ref, ...), custom_call_target="tpu_custom_call" | custom-call | flops 42949672960 | bytes 104857600 | tf_op jit(solution)/shard_map/cross_back/pallas_call | solution.py:1483
  317.2 111.7 %self_back.1 = (bf16[1024,1024]{1,0:T(8,128)(2,1)}, f32[8,1024]{1,0:T(8,128)}, f32[32,4096]{1,0:T(8,128)}, f32[32,1024]{1,0:T(8,128)}, f32[32,1024]{1,0:T(8,128)...) custom-call(s32[1,1,1024]{2,1,0:T(1,128)} %get-tuple-element.68.firs, ...), custom_call_target="tpu_custom_call" | custom-call | flops 42949672960 | bytes 104857600 | tf_op jit(solution)/shard_map/self_back/pallas_call | solution.py:1778
  429.0 0.0 copy-start
  429.0 3.2 broadcast_select_fusion
  432.3 0.8 constant_dynamic-slice_fusion
  433.1 0.5 slice_bitcast_fusion
  433.7 1.0 copy.62
  434.6 0.0 copy-done.10
  434.6 0.7 copy.63
  435.3 0.0 copy-done.9
  435.3 0.7 copy.64
  435.9 0.0 copy-done.8
  435.9 0.7 copy.65
  436.6 0.0 copy-done.7
  436.6 0.7 copy.66
  437.3 0.7 copy.67
  437.9 0.7 copy.68
  438.6 0.7 copy.69
  439.2 0.7 copy.70
  439.9 0.8 copy.71
  440.7 0.8 copy.72
  (19 shorter events, 0.0 us)
Async XLA Ops:
  220.0 15.6 %copy-start.11 = (bf16[1024,4096]{1,0:T(8,128)(2,1)S(1)}, bf16[1024,4096]{1,0:T(8,128)(2,1)}, u32[]{:S(2)}) copy-start(bf16[1024,4096]{1,0:T(8,128)(2,1)} %get-tuple-element.80) | copy-start | bytes 25165828
  220.0 15.6 %copy-start.12 = (bf16[1024,1024]{1,0:T(8,128)(2,1)S(1)}, bf16[1024,1024]{1,0:T(8,128)(2,1)}, u32[]{:S(2)}) copy-start(bf16[1024,1024]{1,0:T(8,128)(2,1)} %get-tuple-element.81) | copy-start | bytes 6291460
  429.0 4.7 %copy-start = (bf16[512,1024]{1,0:T(8,128)(2,1)S(1)}, bf16[512,1024]{1,0:T(8,128)(2,1)}, u32[]{:S(2)}) copy-start(bf16[512,1024]{1,0:T(8,128)(2,1)} %get-tuple-element.132) | copy-start | bytes 3145732
  432.2 2.4 copy-start.10
  432.2 3.1 copy-start.9
  432.2 3.7 copy-start.8
  432.2 4.4 copy-start.7
  432.2 5.0 %copy-start.6 = (f32[32,1024]{1,0:T(8,128)S(1)}, f32[32,1024]{1,0:T(8,128)}, u32[]{:S(2)}) copy-start(f32[32,1024]{1,0:T(8,128)} %get-tuple-element.137) | copy-start | bytes 393220
  432.2 5.7 %copy-start.5 = (f32[32,1024]{1,0:T(8,128)S(1)}, f32[32,1024]{1,0:T(8,128)}, u32[]{:S(2)}) copy-start(f32[32,1024]{1,0:T(8,128)} %get-tuple-element.138) | copy-start | bytes 393220
  432.2 6.3 %copy-start.4 = (f32[32,1024]{1,0:T(8,128)S(1)}, f32[32,1024]{1,0:T(8,128)}, u32[]{:S(2)}) copy-start(f32[32,1024]{1,0:T(8,128)} %get-tuple-element.139) | copy-start | bytes 393220
  432.3 7.0 %copy-start.3 = (f32[32,1024]{1,0:T(8,128)S(1)}, f32[32,1024]{1,0:T(8,128)}, u32[]{:S(2)}) copy-start(f32[32,1024]{1,0:T(8,128)} %get-tuple-element.140) | copy-start | bytes 393220
  433.6 6.3 %copy-start.2 = (f32[32,4096]{1,0:T(8,128)S(1)}, f32[32,4096]{1,0:T(8,128)}, u32[]{:S(2)}) copy-start(f32[32,4096]{1,0:T(8,128)} %get-tuple-element.141) | copy-start | bytes 1572868
  433.6 7.0 %copy-start.1 = (f32[128,1024]{1,0:T(8,128)S(1)}, f32[128,1024]{1,0:T(8,128)}, u32[]{:S(2)}) copy-start(f32[128,1024]{1,0:T(8,128)} %get-tuple-element.142) | copy-start | bytes 1572868
